TPU v7x, 32 devices: a whole 2x2x4 slice. The times are simulated.
32 devices in a mesh: fsdp: 8 (over z, y), ctx: 2 (over x), tp: 2 (over core).
Axes of the slice: x: 2, y: 2, z: 4, core: 2. Of those that a mesh axis runs over, the one named last changes fastest.
Arguments:
- tokens: bfloat16 [12288, 1536], P(('fsdp', 'ctx')), may hold values from -6 to 6
- out_cotangent: bfloat16 [12288, 1536], P(('fsdp', 'ctx')), may hold values from -6 to 6
- lengths: int32 [8, 4], P('fsdp'), may hold values from 1 to 1152, 1536 in all within a row
- adapter_of_doc: int32 [8, 4], P('fsdp'), may hold values from 0 to 7
- routes: int32 [12288, 8], P(('fsdp', 'ctx')), may hold values from 0 to 15, all different within a row; in each aligned block of 768 rows (0 to 767, 768 to 1535, ...) at most 576 rows name the same one
- attn_gain: float32 [1536], replicated, may hold values from 0.5 to 1.5
- ffn_gain: float32 [1536], replicated, may hold values from 0.5 to 1.5
- w_query: bfloat16 [1536, 1536], P('fsdp', 'tp'), may hold values from -0.15625 to 0.15625
- key_matrix: bfloat16 [1536, 512], P('fsdp', 'tp'), may hold values from -0.15625 to 0.15625
- value_matrix: bfloat16 [1536, 512], P('fsdp', 'tp'), may hold values from -0.15625 to 0.15625
- w_out: bfloat16 [1536, 1536], P('tp', 'fsdp'), may hold values from -0.625 to 0.625
- w_router: bfloat16 [1536, 16], P('fsdp'), may hold values from -0.078125 to 0.078125
- w_gate: bfloat16 [16, 1536, 512], P('fsdp', None, 'tp'), may hold values from -0.15625 to 0.15625
- w_up: bfloat16 [16, 1536, 512], P('fsdp', None, 'tp'), may hold values from -0.15625 to 0.15625
- w_down: bfloat16 [16, 512, 1536], P('fsdp', 'tp'), may hold values from -0.75 to 0.75
- a_query: bfloat16 [1536, 128], P('fsdp'), may hold values from -0.15625 to 0.15625
- b_query: bfloat16 [128, 1536], P('fsdp'), may hold values from -1.5 to 1.5
- a_key: bfloat16 [1536, 128], P('fsdp'), may hold values from -0.15625 to 0.15625
- key_second_factor: bfloat16 [128, 512], P('fsdp'), may hold values from -1.5 to 1.5
- a_value: bfloat16 [1536, 128], P('fsdp'), may hold values from -0.15625 to 0.15625
- value_second_factor: bfloat16 [128, 512], P('fsdp'), may hold values from -1.5 to 1.5
- a_out: bfloat16 [1536, 128], P('fsdp'), may hold values from -0.15625 to 0.15625
- b_out: bfloat16 [128, 1536], P('fsdp'), may hold values from -6 to 6
- a_router: bfloat16 [1536, 128], P('fsdp'), may hold values from -0.15625 to 0.15625
- b_router: bfloat16 [128, 16], P('fsdp'), may hold values from -0.75 to 0.75
- a_gate: bfloat16 [1536, 128], P('fsdp'), may hold values from -0.15625 to 0.15625
- b_gate: bfloat16 [128, 512], P('fsdp'), may hold values from -1.5 to 1.5
- a_up: bfloat16 [1536, 128], P('fsdp'), may hold values from -0.15625 to 0.15625
- b_up: bfloat16 [128, 512], P('fsdp'), may hold values from -1.5 to 1.5
- a_down: bfloat16 [512, 128], P('fsdp'), may hold values from -0.25 to 0.25
- b_down: bfloat16 [128, 1536], P('fsdp'), may hold values from -4 to 4
Outputs:
- output: bfloat16 [12288, 1536], P(('fsdp', 'ctx'))
- grad_tokens: bfloat16 [12288, 1536], P(('fsdp', 'ctx'))
- grad_a_query: float32 [1536, 128], P('fsdp')
- grad_b_query: float32 [128, 1536], P('fsdp')
- grad_a_key: float32 [1536, 128], P('fsdp')
- grad_b_key: float32 [128, 512], P('fsdp')
- grad_a_value: float32 [1536, 128], P('fsdp')
- grad_b_value: float32 [128, 512], P('fsdp')
- grad_a_out: float32 [1536, 128], P('fsdp')
- grad_b_out: float32 [128, 1536], P('fsdp')
- grad_a_router: float32 [1536, 128], P('fsdp')
- grad_b_router: float32 [128, 16], P('fsdp')
- grad_a_gate: float32 [1536, 128], P('fsdp')
- grad_b_gate: float32 [128, 512], P('fsdp')
- grad_a_up: float32 [1536, 128], P('fsdp')
- grad_b_up: float32 [128, 512], P('fsdp')
- grad_a_down: float32 [512, 128], P('fsdp')
- grad_b_down: float32 [128, 1536], P('fsdp')
Inputs may be any that keep to these rules, and one draw needn't show every extreme that they name: `lengths`: each row sums to 1536; every row has one document of exactly 1152 tokens. `routes`: each row names 8 different experts. Within the 768 rows of one device no expert is named more than 576 times, and some expert reaches 576 in some device's rows.
All inputs are finite; a program needn't handle non-finite values.
Results may differ from a plain program's by a relative error of at most 0.024.
Values may be sent and summed in bfloat16 or wider, within the bound.
A program may use at most 512 MiB of HBM per device.

v0:
```python
import math

import jax
import jax.numpy as jnp
from jax import lax
from jax.sharding import PartitionSpec as P

HEAD_SIZE = 64
ADAPTER_RANK = 16
ADAPTER_COUNT = 8


norm_eps = 1e-05


def passed_along(x, axis, by):
    peers = lax.axis_size(axis)
    pairs = [(i, i + by) for i in range(peers) if 0 <= i + by < peers]
    return lax.ppermute(x, axis, pairs)


def exact_dot(left, right):
    return jnp.dot(left, right, precision=lax.Precision.HIGHEST)


def rms_norm(values, gain):
    return values * lax.rsqrt(jnp.mean(values * values, axis=-1, keepdims=True) + norm_eps) * gain


def norm_back(values, gain, grad):
    unused, pull = jax.vjp(lambda inner: rms_norm(inner, gain), values)
    return pull(grad)[0]


def rotary_apply(values, cosine_table, sine_table):
    half = values.shape[-1] // 2
    first = values[..., :half]
    second = values[..., half:]
    return jnp.concatenate(
        [first * cosine_table - second * sine_table, first * sine_table + second * cosine_table],
        axis=-1,
    )


def doc_layout(lengths, adapter_of_doc, query_group):
    ends = jnp.cumsum(lengths, axis=1)
    starts = ends - lengths
    place = jnp.arange(query_group, dtype=jnp.int32)
    document_index = jnp.sum((place[None, :, None] >= ends[:, None, :]).astype(jnp.int32), axis=2)
    picked = (
        document_index[:, :, None] == jnp.arange(lengths.shape[1], dtype=jnp.int32)[None, None, :]
    ).astype(jnp.int32)
    begin = jnp.sum(picked * starts[:, None, :], axis=2)
    chosen = jnp.sum(picked * adapter_of_doc[:, None, :], axis=2)
    return (document_index, place[None, :] - begin, chosen)


def expert_forward(recv_x, recv_z, recv_c, gate_w, up_w, gate_b, up_b, down_a):
    ranks = recv_z.shape[-1] // 2
    masks = jnp.repeat(recv_c.astype(jnp.float32), ranks // recv_c.shape[-1], axis=-1)
    gate_val = jnp.einsum(
        "necd,edf->necf", recv_x, gate_w, preferred_element_type=jnp.float32
    ) + jnp.einsum("necr,rf->necf", recv_z[..., :ranks], gate_b, preferred_element_type=jnp.float32)
    up_val = jnp.einsum(
        "necd,edf->necf", recv_x, up_w, preferred_element_type=jnp.float32
    ) + jnp.einsum("necr,rf->necf", recv_z[..., ranks:], up_b, preferred_element_type=jnp.float32)
    act = (jax.nn.silu(gate_val) * up_val).astype(jnp.bfloat16)
    down_low = (
        jnp.einsum("necf,fr->necr", act, down_a, preferred_element_type=jnp.float32) * masks
    ).astype(jnp.bfloat16)
    return (gate_val, up_val, act, down_low, masks)


def on_device(
    tokens,
    out_cotangent,
    lengths,
    adapter_of_doc,
    routes,
    attn_gain,
    ffn_gain,
    w_query,
    key_matrix,
    value_matrix,
    w_out,
    w_router,
    w_gate,
    w_up,
    w_down,
    a_query,
    b_query,
    a_key,
    key_second_factor,
    a_value,
    value_second_factor,
    a_out,
    b_out,
    a_router,
    b_router,
    a_gate,
    b_gate,
    a_up,
    b_up,
    a_down,
    b_down,
):
    rows = tokens.shape[0]
    width = tokens.shape[1]
    topk = routes.shape[1]
    tp_at = lax.axis_index("tp")
    ctx_at = lax.axis_index("ctx")
    n_fsdp = lax.axis_size("fsdp")
    query_group = rows * lax.axis_size("ctx")
    (
        query_w,
        key_w,
        value_w,
        out_w,
        router_w,
        query_a,
        query_b,
        key_a,
        key_b,
        value_a,
        value_b,
        out_a,
        out_b,
        router_a,
        router_b,
        gate_a,
        gate_b,
        up_a,
        up_b,
        down_a,
        down_b,
    ) = (
        lax.all_gather(w_query, "fsdp", axis=0, tiled=True),
        lax.all_gather(key_matrix, "fsdp", axis=0, tiled=True),
        lax.all_gather(value_matrix, "fsdp", axis=0, tiled=True),
        lax.all_gather(w_out, "fsdp", axis=1, tiled=True),
        lax.all_gather(w_router, "fsdp", axis=0, tiled=True),
        lax.all_gather(a_query, "fsdp", axis=0, tiled=True),
        lax.all_gather(b_query, "fsdp", axis=0, tiled=True),
        lax.all_gather(a_key, "fsdp", axis=0, tiled=True),
        lax.all_gather(key_second_factor, "fsdp", axis=0, tiled=True),
        lax.all_gather(a_value, "fsdp", axis=0, tiled=True),
        lax.all_gather(value_second_factor, "fsdp", axis=0, tiled=True),
        lax.all_gather(a_out, "fsdp", axis=0, tiled=True),
        lax.all_gather(b_out, "fsdp", axis=0, tiled=True),
        lax.all_gather(a_router, "fsdp", axis=0, tiled=True),
        lax.all_gather(b_router, "fsdp", axis=0, tiled=True),
        lax.all_gather(a_gate, "fsdp", axis=0, tiled=True),
        lax.all_gather(b_gate, "fsdp", axis=0, tiled=True),
        lax.all_gather(a_up, "fsdp", axis=0, tiled=True),
        lax.all_gather(b_up, "fsdp", axis=0, tiled=True),
        lax.all_gather(a_down, "fsdp", axis=0, tiled=True),
        lax.all_gather(b_down, "fsdp", axis=0, tiled=True),
    )
    q_width = query_w.shape[1]
    kv_width = key_w.shape[1]
    ff_width = w_gate.shape[2]
    experts = router_w.shape[1]
    cap = min(rows, 3 * rows * topk // (2 * experts))
    rank_cols = query_a.shape[1]
    query_bt = lax.dynamic_slice_in_dim(query_b, tp_at * q_width, q_width, 1)
    key_bt = lax.dynamic_slice_in_dim(key_b, tp_at * kv_width, kv_width, 1)
    value_bt = lax.dynamic_slice_in_dim(value_b, tp_at * kv_width, kv_width, 1)
    out_at = lax.dynamic_slice_in_dim(out_a, tp_at * q_width, q_width, 0)
    gate_bt = lax.dynamic_slice_in_dim(gate_b, tp_at * ff_width, ff_width, 1)
    up_bt = lax.dynamic_slice_in_dim(up_b, tp_at * ff_width, ff_width, 1)
    down_at = lax.dynamic_slice_in_dim(down_a, tp_at * ff_width, ff_width, 0)
    document_index, position, chosen = doc_layout(lengths, adapter_of_doc, query_group)
    start = ctx_at * rows
    doc_local = lax.dynamic_slice_in_dim(document_index[0], start, rows)
    pos_local = lax.dynamic_slice_in_dim(position[0], start, rows)
    chosen_local = lax.dynamic_slice_in_dim(chosen[0], start, rows)
    query_index = start + jnp.arange(rows, dtype=jnp.int32)
    key_index = jnp.concatenate([query_index - rows, query_index])
    key_doc = jnp.take(document_index[0], jnp.maximum(key_index, 0))
    allowed = (
        (key_doc[None, :] == doc_local[:, None])
        & (key_index[None, :] <= query_index[:, None])
        & (key_index[None, :] >= 0)
    )
    mask = (
        chosen_local[:, None] == (jnp.arange(rank_cols, dtype=jnp.int32) // ADAPTER_RANK)[None, :]
    ).astype(jnp.float32)
    half = HEAD_SIZE // 2
    freq = 10000.0 ** (-jnp.arange(half, dtype=jnp.float32) / half)
    angles = pos_local.astype(jnp.float32)[:, None] * freq[None, :]
    cosine_table = jnp.cos(angles)[:, None, :]
    sine_table = jnp.sin(angles)[:, None, :]
    scale = 1.0 / math.sqrt(HEAD_SIZE)
    heads_kv = kv_width // HEAD_SIZE
    per_group = q_width // kv_width

    def lowrank(inputs, first, second):
        lowered = jnp.dot(inputs, first, preferred_element_type=jnp.float32) * mask
        return (lowered, exact_dot(lowered, second.astype(jnp.float32)))

    xfull = tokens.astype(jnp.float32)
    normed = rms_norm(xfull, attn_gain).astype(jnp.bfloat16)
    query_u, query_extra = lowrank(normed, query_a, query_bt)
    key_u, key_extra = lowrank(normed, key_a, key_bt)
    value_u, value_extra = lowrank(normed, value_a, value_bt)
    query_pre = jnp.dot(normed, query_w, preferred_element_type=jnp.float32) + query_extra
    key_pre = jnp.dot(normed, key_w, preferred_element_type=jnp.float32) + key_extra
    value_state = (
        jnp.dot(normed, value_w, preferred_element_type=jnp.float32) + value_extra
    ).astype(jnp.bfloat16)
    query_state = (
        rotary_apply(query_pre.reshape(rows, -1, HEAD_SIZE), cosine_table, sine_table)
        .reshape(rows, q_width)
        .astype(jnp.bfloat16)
    )
    key = (
        rotary_apply(key_pre.reshape(rows, -1, HEAD_SIZE), cosine_table, sine_table)
        .reshape(rows, kv_width)
        .astype(jnp.bfloat16)
    )
    far_key, far_value = passed_along((key, value_state), "ctx", 1)
    keys_h = jnp.concatenate([far_key, key], axis=0).reshape(2 * rows, heads_kv, HEAD_SIZE)
    values_h = jnp.concatenate([far_value, value_state], axis=0).reshape(
        2 * rows, heads_kv, HEAD_SIZE
    )
    query_h = query_state.reshape(rows, heads_kv, per_group, HEAD_SIZE)

    def score_block():
        raw = (
            jnp.einsum("qgrd,kgd->grqk", query_h, keys_h, preferred_element_type=jnp.float32)
            * scale
        )
        return jnp.where(allowed[None, None], raw, -1e30)

    scores = score_block()
    top = jnp.max(scores, axis=-1, keepdims=True)
    expd = jnp.exp(scores - top)
    total = jnp.sum(expd, axis=-1, keepdims=True)
    probs = expd / total
    log_total = top + jnp.log(total)
    mixed_heads = (
        jnp.einsum(
            "grqk,kgd->qgrd",
            probs.astype(jnp.bfloat16),
            values_h,
            preferred_element_type=jnp.float32,
        )
        .reshape(rows, q_width)
        .astype(jnp.bfloat16)
    )
    out_u, out_extra = lowrank(mixed_heads, out_at, out_b)
    attn_part = jnp.dot(mixed_heads, out_w, preferred_element_type=jnp.float32) + out_extra
    attended = lax.psum(attn_part, "tp")
    hidden = xfull + attended
    normed_two = rms_norm(hidden, ffn_gain).astype(jnp.bfloat16)
    router_u, router_extra = lowrank(normed_two, router_a, router_b)
    logits = jnp.dot(normed_two, router_w, preferred_element_type=jnp.float32) + router_extra
    gates = jax.nn.softmax(jnp.take_along_axis(logits, routes, axis=1), axis=-1)
    gate_u = jnp.dot(normed_two, gate_a, preferred_element_type=jnp.float32) * mask
    up_u = jnp.dot(normed_two, up_a, preferred_element_type=jnp.float32) * mask
    low_in = jnp.concatenate([gate_u, up_u], axis=1).astype(jnp.bfloat16)
    choose = (chosen_local[:, None] == jnp.arange(ADAPTER_COUNT, dtype=jnp.int32)[None, :]).astype(
        jnp.bfloat16
    )
    flat = routes.reshape(-1)
    count = rows * topk
    hot = (flat[:, None] == jnp.arange(experts, dtype=jnp.int32)[None, :]).astype(jnp.int32)
    slot = jnp.sum((jnp.cumsum(hot, axis=0) - hot) * hot, axis=1)
    dest = flat * cap + slot
    owner = (
        jnp.full((experts * cap,), -1, jnp.int32).at[dest].set(jnp.arange(count, dtype=jnp.int32))
    )
    live = (owner >= 0)[:, None]
    safe = jnp.maximum(owner, 0)
    token_of = safe // topk

    def to_slots(values, index):
        picked = jnp.where(live, values[index], jnp.zeros((), values.dtype))
        return picked.reshape(n_fsdp, experts // n_fsdp, cap, values.shape[-1])

    recv_x, recv_z, recv_c = (
        lax.all_to_all(
            to_slots(normed_two, token_of), "fsdp", split_axis=0, concat_axis=0, tiled=True
        ),
        lax.all_to_all(to_slots(low_in, token_of), "fsdp", split_axis=0, concat_axis=0, tiled=True),
        lax.all_to_all(to_slots(choose, token_of), "fsdp", split_axis=0, concat_axis=0, tiled=True),
    )
    ex_gate, ex_up, ex_down = (w_gate, w_up, w_down)
    gate_val, up_val, act, down_low, masks = expert_forward(
        recv_x, recv_z, recv_c, ex_gate, ex_up, gate_bt, up_bt, down_at
    )
    produced = (
        jnp.einsum("necf,efd->necd", act, ex_down, preferred_element_type=jnp.float32)
        + jnp.einsum("necr,rd->necd", down_low, down_b, preferred_element_type=jnp.float32)
    ).astype(jnp.bfloat16)
    returned = lax.all_to_all(produced, "fsdp", split_axis=0, concat_axis=0, tiled=True)
    y_rows = returned.reshape(experts * cap, width)[dest].reshape(rows, topk, width)
    moe_part = jnp.sum(gates[:, :, None] * y_rows.astype(jnp.float32), axis=1)
    moe = lax.psum(moe_part.astype(jnp.bfloat16), "tp").astype(jnp.float32)
    output = (hidden + moe).astype(jnp.bfloat16)
    dout = out_cotangent.astype(jnp.float32)
    dgate_part = jnp.sum(y_rows.astype(jnp.float32) * dout[:, None, :], axis=-1)
    grad_rows = (gates[:, :, None] * dout[:, None, :]).astype(jnp.bfloat16).reshape(count, width)
    dy_slots = to_slots(grad_rows, safe)
    recv_dy = lax.all_to_all(dy_slots, "fsdp", split_axis=0, concat_axis=0, tiled=True)
    down_grad = (
        jnp.einsum("necd,rd->necr", recv_dy, down_b, preferred_element_type=jnp.float32) * masks
    )
    act_grad = jnp.einsum(
        "necd,efd->necf", recv_dy, ex_down, preferred_element_type=jnp.float32
    ) + jnp.einsum(
        "necr,fr->necf", down_grad, down_at.astype(jnp.float32), precision=lax.Precision.HIGHEST
    )
    grad_bd = jnp.einsum("necr,necd->rd", down_low, recv_dy, preferred_element_type=jnp.float32)
    grad_ad_part = jnp.einsum(
        "necf,necr->fr", act.astype(jnp.float32), down_grad, precision=lax.Precision.HIGHEST
    )
    sigma = jax.nn.sigmoid(gate_val)
    silu_val = gate_val * sigma
    gate_grad = (act_grad * up_val * sigma * (1.0 + gate_val * (1.0 - sigma))).astype(jnp.bfloat16)
    up_grad = (act_grad * silu_val).astype(jnp.bfloat16)
    x_grad = (
        jnp.einsum("necf,edf->necd", gate_grad, ex_gate, preferred_element_type=jnp.float32)
        + jnp.einsum("necf,edf->necd", up_grad, ex_up, preferred_element_type=jnp.float32)
    ).astype(jnp.bfloat16)
    z_grad = jnp.concatenate(
        [
            jnp.einsum("necf,rf->necr", gate_grad, gate_bt, preferred_element_type=jnp.float32),
            jnp.einsum("necf,rf->necr", up_grad, up_bt, preferred_element_type=jnp.float32),
        ],
        axis=-1,
    ).astype(jnp.bfloat16)
    grad_bg_part = jnp.einsum(
        "necr,necf->rf", recv_z[..., :rank_cols], gate_grad, preferred_element_type=jnp.float32
    )
    grad_bu_part = jnp.einsum(
        "necr,necf->rf", recv_z[..., rank_cols:], up_grad, preferred_element_type=jnp.float32
    )
    back_x, back_z = (
        lax.all_to_all(x_grad, "fsdp", split_axis=0, concat_axis=0, tiled=True),
        lax.all_to_all(z_grad, "fsdp", split_axis=0, concat_axis=0, tiled=True),
    )
    dx_sum = jnp.sum(
        back_x.reshape(experts * cap, width)[dest].reshape(rows, topk, width).astype(jnp.float32),
        axis=1,
    )
    dz_sum = jnp.sum(
        back_z.reshape(experts * cap, 2 * rank_cols)[dest]
        .reshape(rows, topk, 2 * rank_cols)
        .astype(jnp.float32),
        axis=1,
    )
    gate_du = dz_sum[:, :rank_cols] * mask
    up_du = dz_sum[:, rank_cols:] * mask
    normed_two_full = normed_two.astype(jnp.float32)
    dn2_part = (
        dx_sum
        + exact_dot(gate_du, gate_a.astype(jnp.float32).T)
        + exact_dot(up_du, up_a.astype(jnp.float32).T)
    )
    grad_ag = exact_dot(normed_two_full.T, gate_du)
    grad_au = exact_dot(normed_two_full.T, up_du)
    dn2_experts, dgate = lax.psum((dn2_part, dgate_part), "tp")
    dpicked = gates * (dgate - jnp.sum(gates * dgate, axis=-1, keepdims=True))
    route_hot = (routes[:, :, None] == jnp.arange(experts, dtype=jnp.int32)[None, None, :]).astype(
        jnp.float32
    )
    dlogits = jnp.sum(route_hot * dpicked[:, :, None], axis=1).astype(jnp.bfloat16)
    router_du = jnp.dot(dlogits, router_b.T, preferred_element_type=jnp.float32) * mask
    dn2 = (
        dn2_experts
        + jnp.dot(dlogits, router_w.T, preferred_element_type=jnp.float32)
        + exact_dot(router_du, router_a.astype(jnp.float32).T)
    )
    only_first = (tp_at == 0).astype(jnp.float32)
    grad_br = exact_dot(router_u.T, dlogits.astype(jnp.float32)) * only_first
    grad_ar = exact_dot(normed_two_full.T, router_du) * only_first
    dhidden = dout + norm_back(hidden, ffn_gain, dn2)
    dattn = dhidden.astype(jnp.bfloat16)
    out_du = jnp.dot(dattn, out_b.T, preferred_element_type=jnp.float32) * mask
    dmixed = (
        jnp.dot(dattn, out_w.T, preferred_element_type=jnp.float32)
        + exact_dot(out_du, out_at.astype(jnp.float32).T)
    ).astype(jnp.bfloat16)
    grad_bo = exact_dot(out_u.T, dattn.astype(jnp.float32))
    grad_ao_part = exact_dot(mixed_heads.astype(jnp.float32).T, out_du)
    probs_again = jnp.exp(score_block() - log_total)
    dmixed_h = dmixed.reshape(rows, heads_kv, per_group, HEAD_SIZE)
    dvalues = jnp.einsum(
        "grqk,qgrd->kgd",
        probs_again.astype(jnp.bfloat16),
        dmixed_h,
        preferred_element_type=jnp.float32,
    ).reshape(2 * rows, kv_width)
    dprobs = jnp.einsum("qgrd,kgd->grqk", dmixed_h, values_h, preferred_element_type=jnp.float32)
    dscores = (
        probs_again * (dprobs - jnp.sum(probs_again * dprobs, axis=-1, keepdims=True))
    ).astype(jnp.bfloat16)
    dquery = (
        jnp.einsum("grqk,kgd->qgrd", dscores, keys_h, preferred_element_type=jnp.float32) * scale
    )
    dkeys = (
        jnp.einsum("grqk,qgrd->kgd", dscores, query_h, preferred_element_type=jnp.float32) * scale
    ).reshape(2 * rows, kv_width)
    far_dkey, far_dvalue = (
        passed_along(dkeys[:rows].astype(jnp.bfloat16), "ctx", -1).astype(jnp.float32),
        passed_along(dvalues[:rows].astype(jnp.bfloat16), "ctx", -1).astype(jnp.float32),
    )
    dkey = dkeys[rows:] + far_dkey
    dvalue = (dvalues[rows:] + far_dvalue).astype(jnp.bfloat16)
    dquery_pre = (
        rotary_apply(dquery.reshape(rows, -1, HEAD_SIZE), cosine_table, -sine_table)
        .reshape(rows, q_width)
        .astype(jnp.bfloat16)
    )
    dkey_pre = (
        rotary_apply(dkey.reshape(rows, -1, HEAD_SIZE), cosine_table, -sine_table)
        .reshape(rows, kv_width)
        .astype(jnp.bfloat16)
    )
    query_du = jnp.dot(dquery_pre, query_bt.T, preferred_element_type=jnp.float32) * mask
    key_du = jnp.dot(dkey_pre, key_bt.T, preferred_element_type=jnp.float32) * mask
    value_du = jnp.dot(dvalue, value_bt.T, preferred_element_type=jnp.float32) * mask
    dn1_part = (
        jnp.dot(dquery_pre, query_w.T, preferred_element_type=jnp.float32)
        + jnp.dot(dkey_pre, key_w.T, preferred_element_type=jnp.float32)
        + jnp.dot(dvalue, value_w.T, preferred_element_type=jnp.float32)
    )
    dn1_part = (
        dn1_part
        + exact_dot(query_du, query_a.astype(jnp.float32).T)
        + exact_dot(key_du, key_a.astype(jnp.float32).T)
        + exact_dot(value_du, value_a.astype(jnp.float32).T)
    )
    normed_full = normed.astype(jnp.float32)
    grad_aq = exact_dot(normed_full.T, query_du)
    grad_ak = exact_dot(normed_full.T, key_du)
    grad_av = exact_dot(normed_full.T, value_du)
    grad_bq_part = exact_dot(query_u.T, dquery_pre.astype(jnp.float32))
    grad_bk_part = exact_dot(key_u.T, dkey_pre.astype(jnp.float32))
    grad_bv_part = exact_dot(value_u.T, dvalue.astype(jnp.float32))
    dn1 = lax.psum(dn1_part.astype(jnp.bfloat16), "tp").astype(jnp.float32)
    grad_tokens = (dhidden + norm_back(xfull, attn_gain, dn1)).astype(jnp.bfloat16)

    def place_cols(piece, full_cols):
        blank = jnp.zeros((piece.shape[0], full_cols), jnp.float32)
        return lax.dynamic_update_slice_in_dim(blank, piece, tp_at * piece.shape[1], 1)

    def place_rows(piece, full_rows):
        blank = jnp.zeros((full_rows, piece.shape[1]), jnp.float32)
        return lax.dynamic_update_slice_in_dim(blank, piece, tp_at * piece.shape[0], 0)

    grads = (
        grad_aq,
        place_cols(grad_bq_part, query_b.shape[1]),
        grad_ak,
        place_cols(grad_bk_part, key_b.shape[1]),
        grad_av,
        place_cols(grad_bv_part, value_b.shape[1]),
        place_rows(grad_ao_part, out_a.shape[0]),
        grad_bo,
        grad_ar,
        grad_br,
        grad_ag,
        place_cols(grad_bg_part, gate_b.shape[1]),
        grad_au,
        place_cols(grad_bu_part, up_b.shape[1]),
        place_rows(grad_ad_part, down_a.shape[0]),
        grad_bd,
    )
    shards = (
        lax.psum_scatter(
            grads[0].astype(jnp.bfloat16), "fsdp", scatter_dimension=0, tiled=True
        ).astype(jnp.float32),
        lax.psum_scatter(
            grads[1].astype(jnp.bfloat16), "fsdp", scatter_dimension=0, tiled=True
        ).astype(jnp.float32),
        lax.psum_scatter(
            grads[2].astype(jnp.bfloat16), "fsdp", scatter_dimension=0, tiled=True
        ).astype(jnp.float32),
        lax.psum_scatter(
            grads[3].astype(jnp.bfloat16), "fsdp", scatter_dimension=0, tiled=True
        ).astype(jnp.float32),
        lax.psum_scatter(
            grads[4].astype(jnp.bfloat16), "fsdp", scatter_dimension=0, tiled=True
        ).astype(jnp.float32),
        lax.psum_scatter(
            grads[5].astype(jnp.bfloat16), "fsdp", scatter_dimension=0, tiled=True
        ).astype(jnp.float32),
        lax.psum_scatter(
            grads[6].astype(jnp.bfloat16), "fsdp", scatter_dimension=0, tiled=True
        ).astype(jnp.float32),
        lax.psum_scatter(
            grads[7].astype(jnp.bfloat16), "fsdp", scatter_dimension=0, tiled=True
        ).astype(jnp.float32),
        lax.psum_scatter(
            grads[8].astype(jnp.bfloat16), "fsdp", scatter_dimension=0, tiled=True
        ).astype(jnp.float32),
        lax.psum_scatter(
            grads[9].astype(jnp.bfloat16), "fsdp", scatter_dimension=0, tiled=True
        ).astype(jnp.float32),
        lax.psum_scatter(
            grads[10].astype(jnp.bfloat16), "fsdp", scatter_dimension=0, tiled=True
        ).astype(jnp.float32),
        lax.psum_scatter(
            grads[11].astype(jnp.bfloat16), "fsdp", scatter_dimension=0, tiled=True
        ).astype(jnp.float32),
        lax.psum_scatter(
            grads[12].astype(jnp.bfloat16), "fsdp", scatter_dimension=0, tiled=True
        ).astype(jnp.float32),
        lax.psum_scatter(
            grads[13].astype(jnp.bfloat16), "fsdp", scatter_dimension=0, tiled=True
        ).astype(jnp.float32),
        lax.psum_scatter(
            grads[14].astype(jnp.bfloat16), "fsdp", scatter_dimension=0, tiled=True
        ).astype(jnp.float32),
        lax.psum_scatter(
            grads[15].astype(jnp.bfloat16), "fsdp", scatter_dimension=0, tiled=True
        ).astype(jnp.float32),
    )
    final = (
        lax.psum(shards[0].astype(jnp.bfloat16), ("ctx", "tp")).astype(jnp.float32),
        lax.psum(shards[1].astype(jnp.bfloat16), ("ctx", "tp")).astype(jnp.float32),
        lax.psum(shards[2].astype(jnp.bfloat16), ("ctx", "tp")).astype(jnp.float32),
        lax.psum(shards[3].astype(jnp.bfloat16), ("ctx", "tp")).astype(jnp.float32),
        lax.psum(shards[4].astype(jnp.bfloat16), ("ctx", "tp")).astype(jnp.float32),
        lax.psum(shards[5].astype(jnp.bfloat16), ("ctx", "tp")).astype(jnp.float32),
        lax.psum(shards[6].astype(jnp.bfloat16), ("ctx", "tp")).astype(jnp.float32),
        lax.psum(shards[7].astype(jnp.bfloat16), ("ctx", "tp")).astype(jnp.float32),
        lax.psum(shards[8].astype(jnp.bfloat16), ("ctx", "tp")).astype(jnp.float32),
        lax.psum(shards[9].astype(jnp.bfloat16), ("ctx", "tp")).astype(jnp.float32),
        lax.psum(shards[10].astype(jnp.bfloat16), ("ctx", "tp")).astype(jnp.float32),
        lax.psum(shards[11].astype(jnp.bfloat16), ("ctx", "tp")).astype(jnp.float32),
        lax.psum(shards[12].astype(jnp.bfloat16), ("ctx", "tp")).astype(jnp.float32),
        lax.psum(shards[13].astype(jnp.bfloat16), ("ctx", "tp")).astype(jnp.float32),
        lax.psum(shards[14].astype(jnp.bfloat16), ("ctx", "tp")).astype(jnp.float32),
        lax.psum(shards[15].astype(jnp.bfloat16), ("ctx", "tp")).astype(jnp.float32),
    )
    return (
        output,
        grad_tokens,
        final[0],
        final[1],
        final[2],
        final[3],
        final[4],
        final[5],
        final[6],
        final[7],
        final[8],
        final[9],
        final[10],
        final[11],
        final[12],
        final[13],
        final[14],
        final[15],
    )


def solution(mesh):
    placed = (
        P(("fsdp", "ctx"), None),
        P(("fsdp", "ctx"), None),
        P("fsdp", None),
        P("fsdp", None),
        P(("fsdp", "ctx"), None),
        P(),
        P(),
        P("fsdp", "tp"),
        P("fsdp", "tp"),
        P("fsdp", "tp"),
        P("tp", "fsdp"),
        P("fsdp", None),
        P("fsdp", None, "tp"),
        P("fsdp", None, "tp"),
        P("fsdp", "tp", None),
        P("fsdp", None),
        P("fsdp", None),
        P("fsdp", None),
        P("fsdp", None),
        P("fsdp", None),
        P("fsdp", None),
        P("fsdp", None),
        P("fsdp", None),
        P("fsdp", None),
        P("fsdp", None),
        P("fsdp", None),
        P("fsdp", None),
        P("fsdp", None),
        P("fsdp", None),
        P("fsdp", None),
        P("fsdp", None),
    )
    return jax.shard_map(
        on_device,
        mesh=mesh,
        in_specs=placed,
        out_specs=(
            P(("fsdp", "ctx"), None),
            P(("fsdp", "ctx"), None),
            P("fsdp", None),
            P("fsdp", None),
            P("fsdp", None),
            P("fsdp", None),
            P("fsdp", None),
            P("fsdp", None),
            P("fsdp", None),
            P("fsdp", None),
            P("fsdp", None),
            P("fsdp", None),
            P("fsdp", None),
            P("fsdp", None),
            P("fsdp", None),
            P("fsdp", None),
            P("fsdp", None),
            P("fsdp", None),
        ),
        check_vma=False,
    )
```

profile of v0, /device:TPU:0, one launch (start us, length us, event | category | flops | bytes accessed | tf_op | source)
XLA Modules:
  0.0 4550.8 jit_solution(2840313502084406454)
XLA Ops:
  685.3 57.4 %gather_fusion.1 = bf16[9216,1536]{1,0:T(8,128)(2,1)} fusion(bf16[768,1536]{1,0:T(8,128)(2,1)} %multiply_convert_fusion.4, s32[9216]{0:T(1024)S(1)} %get-tuple-element.56), kind=kCustom, calls=%fused_computation.1 | custom fusion | bytes 56659968 | tf_op jit(solution)/shard_map/gather | solution.py:278
  748.6 49.3 %gather_fusion.8 = f32[6144]{0:T(1024)S(1)} fusion(f32[768,16]{0,1:T(8,128)S(1)} %convolution_add_fusion.4, s32[6144]{0:T(1024)S(1)} %reshape.760), kind=kCustom, calls=%fused_computation.8 | custom fusion | bytes 98304 | tf_op jit(solution)/shard_map/jit(take_along_axis)/gather | solution.py:258
  802.3 37.1 gather_fusion.2
  862.7 64.2 %gather_fusion.5 = bf16[9216,1536]{1,0:T(8,128)(2,1)} fusion(bf16[6144,1536]{1,0:T(8,128)(2,1)} %fusion.8, s32[9216]{0:T(1024)S(1)} %copy-done.92), kind=kCustom, calls=%fused_computation.5 | custom fusion | bytes 56659968 | tf_op jit(solution)/shard_map/gather | solution.py:278
  926.9 37.2 broadcast_select_fusion
  966.9 588.1 %all_to_all.35 = bf16[8,2,576,1536]{3,2,1,0:T(8,128)(2,1)} all-to-all(bf16[8,2,576,1536]{3,2,1,0:T(8,128)(2,1)} %get-tuple-element.58), channel_id=1, replica_groups=mesh['fsdp'=8,'ctx'=2,'tp'=2] {'fsdp'}, dimensions={0} | all-to-all | bytes 56623104 | tf_op jit(solution)/shard_map/all_to_all | solution.py:282
  1555.0 42.6 all-to-all-start.4
  1597.6 543.0 %all_gather.80 = bf16[128,512]{1,0:T(8,128)(2,1)S(1)} all-gather(bf16[16,512]{1,0:T(8,128)(2,1)S(1)} %copy-done.120), channel_id=1, replica_groups=mesh['fsdp'=8,'ctx'=2,'tp'=2] {'fsdp'}, dimensions={0}, use_global_device_ids=true | all-gather | bytes 147456 | tf_op jit(solution)/shard_map/all_gather | solution.py:153
  2428.6 78.0 %all-to-all-start.5 = ((bf16[8,2,576,1536]{3,2,1,0:T(8,128)(2,1)}), bf16[8,2,576,1536]{3,2,1,0:T(8,128)(2,1)}, u32[]{:S(2)}, u32[]{:S(2)}) async-start(bf16[8,2,576,1536]{3,2,1,0:T(8,128)(2,1)} %copy.244), calls=%async_computation.5 | async-start | bytes 56623104 | tf_op jit(solution)/shard_map/all_to_all | solution.py:340
  2585.5 450.7 %all-to-all-done.5 = bf16[8,2,576,1536]{3,2,1,0:T(8,128)(2,1)} async-done(((bf16[8,2,576,1536]{3,2,1,0:T(8,128)(2,1)}), bf16[8,2,576,1536]{3,2,1,0:T(8,128)(2,1)}, u32[]{:S(2)}, u32[]{:S(2)}) %all-to-all-start.5) | async-done | bytes 28311584 | tf_op jit(solution)/shard_map/all_to_all | solution.py:340
  3036.2 78.2 %all-to-all-start.3 = ((bf16[8,2,576,1536]{3,2,1,0:T(8,128)(2,1)}), bf16[8,2,576,1536]{3,2,1,0:T(8,128)(2,1)}, u32[]{:S(2)}, u32[]{:S(2)}) async-start(bf16[8,2,576,1536]{3,2,1,0:T(8,128)(2,1)} %copy.239), calls=%async_computation.3 | async-start | bytes 56623104 | tf_op jit(solution)/shard_map/all_to_all | solution.py:296
  3149.7 50.0 %gather_fusion.6 = bf16[6144,1536]{1,0:T(8,128)(2,1)} fusion(bf16[9216,1536]{1,0:T(8,128)(2,1)} %bitcast.50, s32[6144]{0:T(1024)S(1)} %broadcast_clamp_fusion), kind=kCustom, calls=%fused_computation.6 | custom fusion | bytes 37773312 | tf_op jit(solution)/shard_map/gather | solution.py:344
  3267.2 376.0 %all-to-all-done.3 = bf16[8,2,576,1536]{3,2,1,0:T(8,128)(2,1)} async-done(((bf16[8,2,576,1536]{3,2,1,0:T(8,128)(2,1)}), bf16[8,2,576,1536]{3,2,1,0:T(8,128)(2,1)}, u32[]{:S(2)}, u32[]{:S(2)}) %all-to-all-start.3) | async-done | bytes 28311584 | tf_op jit(solution)/shard_map/all_to_all | solution.py:296
  3643.1 50.1 %gather_fusion.4 = bf16[6144,1536]{1,0:T(8,128)(2,1)} fusion(bf16[9216,1536]{1,0:T(8,128)(2,1)} %bitcast.40, s32[6144]{0:T(1024)S(1)} %broadcast_clamp_fusion), kind=kCustom, calls=%fused_computation.4 | custom fusion | bytes 37773312 | tf_op jit(solution)/shard_map/gather | solution.py:297
  3775.7 36.9 fusion
  3812.6 44.9 fusion.2
  3958.7 58.8 %reduce-scatter.23.cloned.1.call-done = bf16[16,512]{1,0:T(8,128)(2,1)} async-done(((bf16[128,512]{1,0:T(8,128)(2,1)}), bf16[16,512]{1,0:T(8,128)(2,1)}) %reduce-scatter.23.cloned.1.call-update) | async-done | bytes 16400 | tf_op jit(solution)/shard_map/reduce_scatter | solution.py:481
  4017.4 63.1 %reduce-scatter.27.cloned.1.call-done = bf16[16,512]{1,0:T(8,128)(2,1)} async-done(((bf16[128,512]{1,0:T(8,128)(2,1)}), bf16[16,512]{1,0:T(8,128)(2,1)}) %reduce-scatter.27.cloned.1.call-update) | async-done | bytes 16400 | tf_op jit(solution)/shard_map/reduce_scatter | solution.py:487
  4080.6 64.1 %reduce-scatter.17.cloned.1.call-done = bf16[192,128]{1,0:T(8,128)(2,1)} async-done(((bf16[1536,128]{1,0:T(8,128)(2,1)}), bf16[192,128]{1,0:T(8,128)(2,1)}) %reduce-scatter.17.cloned.1.call-update) | async-done | bytes 49168 | tf_op jit(solution)/shard_map/reduce_scatter | solution.py:472
  4144.7 63.6 %reduce-scatter.19.cloned.1.call-done = bf16[16,1536]{1,0:T(8,128)(2,1)} async-done(((bf16[128,1536]{1,0:T(8,128)(2,1)}), bf16[16,1536]{1,0:T(8,128)(2,1)}) %reduce-scatter.19.cloned.1.call-update) | async-done | bytes 49168 | tf_op jit(solution)/shard_map/reduce_scatter | solution.py:475
  4208.3 63.6 %reduce-scatter.29.cloned.1.call-done = bf16[192,128]{1,0:T(8,128)(2,1)} async-done(((bf16[1536,128]{1,0:T(8,128)(2,1)}), bf16[192,128]{1,0:T(8,128)(2,1)}) %reduce-scatter.29.cloned.1.call-update) | async-done | bytes 49168 | tf_op jit(solution)/shard_map/reduce_scatter | solution.py:490
  4271.8 63.5 %reduce-scatter.31.cloned.1.call-done = bf16[16,1536]{1,0:T(8,128)(2,1)} async-done(((bf16[128,1536]{1,0:T(8,128)(2,1)}), bf16[16,1536]{1,0:T(8,128)(2,1)}) %reduce-scatter.31.cloned.1.call-update) | async-done | bytes 49168 | tf_op jit(solution)/shard_map/reduce_scatter | solution.py:493
  4335.4 63.7 %reduce-scatter.21.cloned.1.call-done = bf16[192,128]{1,0:T(8,128)(2,1)} async-done(((bf16[1536,128]{1,0:T(8,128)(2,1)}), bf16[192,128]{1,0:T(8,128)(2,1)}) %reduce-scatter.21.cloned.1.call-update) | async-done | bytes 49168 | tf_op jit(solution)/shard_map/reduce_scatter | solution.py:478
  4399.1 63.5 %reduce-scatter.25.cloned.1.call-done = bf16[192,128]{1,0:T(8,128)(2,1)} async-done(((bf16[1536,128]{1,0:T(8,128)(2,1)}), bf16[192,128]{1,0:T(8,128)(2,1)}) %reduce-scatter.25.cloned.1.call-update) | async-done | bytes 49168 | tf_op jit(solution)/shard_map/reduce_scatter | solution.py:484
  (542 shorter events, 1446.6 us)
Async XLA Ops:
  7.2 358.5 %all-gather.4.cloned.1.call-start = ((), (), s32[]{:S(2)}) async-start(), calls=%async_computation.23 | async-start | bytes 2654208 | tf_op jit(solution)/shard_map/all_gather | solution.py:137
  7.9 424.6 %all-gather.6.cloned.1.call-start = ((), (), s32[]{:S(2)}) async-start(), calls=%async_computation.24 | async-start | bytes 2654208 | tf_op jit(solution)/shard_map/all_gather | solution.py:140
  115.1 246.9 %collective-permute-start = (bf16[768,256]{1,0:T(8,128)(2,1)}, bf16[768,256]{1,0:T(8,128)(2,1)}, u32[]{:S(2)}, u32[]{:S(2)}) collective-permute-start(bf16[768,256]{1,0:T(8,128)(2,1)} %fusion.79), channel_id=1, source_target_pairs={{0,2},{1,3},{4,6},{5,7},{8,10},{9,11},{12,14},{13,15},{16,18},{17,... | collective-permute-start | bytes 1179656 | tf_op jit(solution)/shard_map/ppermute | solution.py:19
  219.7 458.3 %all-reduce.7.cloned.1.call-start = ((), (), s32[]{:S(2)}) async-start(), calls=%async_computation.25 | async-start | bytes 9437184 | tf_op jit(solution)/shard_map/psum | solution.py:253
  508.2 336.9 %all-to-all-start.2 = ((bf16[8,2,576,8]{2,3,1,0:T(8,128)(2,1)}), bf16[8,2,576,8]{2,3,1,0:T(8,128)(2,1)}, u32[]{:S(2)}, u32[]{:S(2)}) async-start(bf16[8,2,576,8]{2,3,1,0:T(8,128)(2,1)} %broadcast_select_fusion.3), calls=%async_computation.2 | async-start | bytes 327680 | tf_op jit(solution)/shard_map/all_to_all | solution.py:286
  1555.0 732.1 %all-to-all-start.4 = ((bf16[8,2,576,1536]{3,2,1,0:T(8,128)(2,1)}), bf16[8,2,576,1536]{3,2,1,0:T(8,128)(2,1)}, u32[]{:S(2)}, u32[]{:S(2)}) async-start(bf16[8,2,576,1536]{3,2,1,0:T(8,128)(2,1)} %get-tuple-element.57), calls=%async_computation.4 | async-start | bytes 56623104 | tf_op jit(solution)/shard_map/all_to_all | solution.py:305
  2428.6 607.6 %all-to-all-start.5 = ((bf16[8,2,576,1536]{3,2,1,0:T(8,128)(2,1)}), bf16[8,2,576,1536]{3,2,1,0:T(8,128)(2,1)}, u32[]{:S(2)}, u32[]{:S(2)}) async-start(bf16[8,2,576,1536]{3,2,1,0:T(8,128)(2,1)} %copy.244), calls=%async_computation.5 | async-start | bytes 56623104 | tf_op jit(solution)/shard_map/all_to_all | solution.py:340
  3036.2 606.9 %all-to-all-start.3 = ((bf16[8,2,576,1536]{3,2,1,0:T(8,128)(2,1)}), bf16[8,2,576,1536]{3,2,1,0:T(8,128)(2,1)}, u32[]{:S(2)}, u32[]{:S(2)}) async-start(bf16[8,2,576,1536]{3,2,1,0:T(8,128)(2,1)} %copy.239), calls=%async_computation.3 | async-start | bytes 56623104 | tf_op jit(solution)/shard_map/all_to_all | solution.py:296
  3114.4 615.9 %all-reduce.9.cloned.1.call-start = ((), (), s32[]{:S(2)}) async-start(), calls=%async_computation.26 | async-start | bytes 9437184 | tf_op jit(solution)/shard_map/psum | solution.py:363
  3219.6 739.0 %reduce-scatter.39.cloned.1.call-start = ((), (), s32[]{:S(2)}) async-start(), calls=%async_computation.38 | async-start | bytes 147456 | tf_op jit(solution)/shard_map/reduce_scatter | solution.py:505
  3224.5 734.1 %reduce-scatter.43.cloned.1.call-start = ((), (), s32[]{:S(2)}) async-start(), calls=%async_computation.40 | async-start | bytes 147456 | tf_op jit(solution)/shard_map/reduce_scatter | solution.py:511
  3230.1 728.4 %reduce-scatter.45.cloned.1.call-start = ((), (), s32[]{:S(2)}) async-start(), calls=%async_computation.41 | async-start | bytes 147456 | tf_op jit(solution)/shard_map/reduce_scatter | solution.py:514
  3240.8 717.7 %reduce-scatter.47.cloned.1.call-start = ((), (), s32[]{:S(2)}) async-start(), calls=%async_computation.42 | async-start | bytes 442368 | tf_op jit(solution)/shard_map/reduce_scatter | solution.py:517
  3255.6 703.0 %reduce-scatter.37.cloned.1.call-start = ((), (), s32[]{:S(2)}) async-start(), calls=%async_computation.37 | async-start | bytes 442368 | tf_op jit(solution)/shard_map/reduce_scatter | solution.py:502
  3260.8 697.8 %reduce-scatter.41.cloned.1.call-start = ((), (), s32[]{:S(2)}) async-start(), calls=%async_computation.39 | async-start | bytes 442368 | tf_op jit(solution)/shard_map/reduce_scatter | solution.py:508
  3266.7 691.9 %reduce-scatter.35.cloned.1.call-start = ((), (), s32[]{:S(2)}) async-start(), calls=%async_computation.36 | async-start | bytes 36864 | tf_op jit(solution)/shard_map/reduce_scatter | solution.py:499
  3730.1 287.3 %reduce-scatter.23.cloned.1.call-start = ((), (), s32[]{:S(2)}) async-start(), calls=%async_computation.30 | async-start | bytes 147456 | tf_op jit(solution)/shard_map/reduce_scatter | solution.py:481
  3910.9 233.8 %reduce-scatter.17.cloned.1.call-start = ((), (), s32[]{:S(2)}) async-start(), calls=%async_computation.27 | async-start | bytes 442368 | tf_op jit(solution)/shard_map/reduce_scatter | solution.py:472
  3916.0 292.3 %reduce-scatter.19.cloned.1.call-start = ((), (), s32[]{:S(2)}) async-start(), calls=%async_computation.28 | async-start | bytes 442368 | tf_op jit(solution)/shard_map/reduce_scatter | solution.py:475
  3919.3 352.6 %reduce-scatter.29.cloned.1.call-start = ((), (), s32[]{:S(2)}) async-start(), calls=%async_computation.33 | async-start | bytes 442368 | tf_op jit(solution)/shard_map/reduce_scatter | solution.py:490
  3922.6 412.8 %reduce-scatter.31.cloned.1.call-start = ((), (), s32[]{:S(2)}) async-start(), calls=%async_computation.34 | async-start | bytes 442368 | tf_op jit(solution)/shard_map/reduce_scatter | solution.py:493
  3927.0 472.1 %reduce-scatter.21.cloned.1.call-start = ((), (), s32[]{:S(2)}) async-start(), calls=%async_computation.29 | async-start | bytes 442368 | tf_op jit(solution)/shard_map/reduce_scatter | solution.py:478
  3937.2 525.4 %reduce-scatter.25.cloned.1.call-start = ((), (), s32[]{:S(2)}) async-start(), calls=%async_computation.31 | async-start | bytes 442368 | tf_op jit(solution)/shard_map/reduce_scatter | solution.py:484
  3946.9 553.5 %all-reduce.11.cloned.1.call-start = ((), (), s32[]{:S(2)}) async-start(), calls=%async_computation.43 | async-start | bytes 1155072 | tf_op jit(solution)/shard_map/psum | solution.py:522
  (136 other events, 11354.7 us)
Sparse Core Ops, SparseCore 0:
  10.2 56.9 all-gather.3
  219.8 57.0 all-gather.5
  440.8 29.3 all-reduce.6
  3219.7 30.3 all-reduce.8
  3253.2 261.1 reduce-scatter.38
  3517.6 61.1 reduce-scatter.42
  3582.1 61.1 reduce-scatter.44
  3646.6 60.3 reduce-scatter.46
  3710.2 60.4 reduce-scatter.36
  3773.8 60.4 reduce-scatter.40
  3838.0 52.5 reduce-scatter.34
  3893.7 60.4 reduce-scatter.32
  3957.5 59.8 reduce-scatter.22
  4020.6 59.9 reduce-scatter.26
  4084.2 60.4 reduce-scatter.16
  4147.8 60.4 reduce-scatter.18
  4211.4 60.4 reduce-scatter.28
  4275.0 60.3 reduce-scatter.30
  4338.7 60.3 reduce-scatter.20
  4402.2 60.3 reduce-scatter.24
  4466.1 34.3 all-reduce.10
  4503.5 29.3 all-reduce.12
where the time goes:
time: 4560 us; the launch traced here: 4550 us
  blocking collectives  1710 us (38%)
  waiting for transfers between devices  1390 us (30%)
  matrix products  505 us (11%)
  local copies, waits for them, and re-layouts  471 us (10%)
  other arithmetic  235 us (5%)
  starting transfers between devices  227 us (5%)
    all_to_all x1, blocking collectives, on_device(): lax.all_to_all(to_slots(normed_two, token_of), 'fsdp', split_axis=0, conc...  588 us
    all_gather x1, blocking collectives, on_device(): lax.all_gather(b_gate, 'fsdp', axis=0, tiled=True)  543 us
    all_to_all x1, waiting for transfers between devices, on_device(): lax.all_to_all(x_grad, 'fsdp', split_axis=0, concat_axis=0, tiled=True)  451 us
    all_to_all x1, waiting for transfers between devices, on_device(): lax.all_to_all(produced, 'fsdp', split_axis=0, concat_axis=0, tiled=True)  376 us
    gather x5, local copies, waits for them, and re-layouts, to_slots(): picked = jnp.where(live, values[index], jnp.zeros((), values.dtype))  194 us
  transfers between devices with their start and end apart: 32, of which 14 were waited for; matrix products, arithmetic and copies ran while one was open for 25% of the time, Pallas kernels for 0%

commit v1 on v0

v1 whole, which is shorter than its diff:
```python
import math

import jax
import jax.numpy as jnp
from jax import lax
from jax.sharding import PartitionSpec as P

HEAD_SIZE = 64
ADAPTER_RANK = 16
LANES = 128
norm_eps = 1e-05
BF = jnp.bfloat16
F32 = jnp.float32


def dot(left, right, dims=((1,), (0,))):
    return lax.dot_general(left, right, (dims, ((), ())), preferred_element_type=F32)


def dot_t(left, right):
    return dot(left, right, ((1,), (1,)))


def t_dot(left, right):
    return dot(left, right, ((0,), (0,)))


def rms_norm(values, gain):
    return values * lax.rsqrt(jnp.mean(values * values, axis=-1, keepdims=True) + norm_eps) * gain


def norm_back(values, gain, grad):
    unused, pull = jax.vjp(lambda inner: rms_norm(inner, gain), values)
    return pull(grad)[0]


def rotary_apply(values, cosine_table, sine_table):
    half = values.shape[-1] // 2
    first = values[..., :half]
    second = values[..., half:]
    return jnp.concatenate(
        [first * cosine_table - second * sine_table, first * sine_table + second * cosine_table],
        axis=-1,
    )


def levels(n):
    outer = 4 if n % 4 == 0 else n
    return outer, n // outer


def spread(block):
    n = lax.axis_size("fsdp")
    outer, inner = levels(n)
    me = lax.axis_index("fsdp")
    held = [block]
    for unused in range(outer - 1):
        held.append(lax.ppermute(held[-1], "fsdp", [(i, (i + inner) % n) for i in range(n)]))
    rows = [held]
    turn = [(i, i // inner * inner + (i % inner + 1) % inner) for i in range(n)]
    for unused in range(inner - 1):
        rows.append([lax.ppermute(h, "fsdp", turn) for h in rows[-1]])
    found = []
    for dj, row in enumerate(rows):
        for do, part in enumerate(row):
            owner = (me // inner - do + outer) % outer * inner + (me % inner - dj + inner) % inner
            found.append((owner, part))
    return found


def gathered(block):
    n = lax.axis_size("fsdp")
    whole = jnp.zeros((n,) + block.shape, block.dtype)
    for owner, part in spread(block):
        whole = lax.dynamic_update_index_in_dim(whole, part, owner, 0)
    return whole


def tiles(matrix):
    rows, cols = matrix.shape
    if cols % LANES:
        matrix = jnp.pad(matrix, ((0, 0), (0, LANES - cols % LANES)))
    return [matrix[:, i : i + LANES] for i in range(0, matrix.shape[1], LANES)]


def on_device(
    tokens, out_cotangent, lengths, adapter_of_doc, routes, attn_gain, ffn_gain,
    w_query, key_matrix, value_matrix, w_out, w_router, w_gate, w_up, w_down,
    a_query, b_query, a_key, key_second_factor, a_value, value_second_factor,
    a_out, b_out, a_router, b_router, a_gate, b_gate, a_up, b_up, a_down, b_down,
):
    rows, width = tokens.shape
    n = lax.axis_size("fsdp")
    n_tp = lax.axis_size("tp")
    tp_at = lax.axis_index("tp")
    ctx_at = lax.axis_index("ctx")
    group = rows * lax.axis_size("ctx")
    q_width = w_query.shape[1]
    kv_width = key_matrix.shape[1]
    ff_width = w_gate.shape[2]
    local_experts = w_gate.shape[0]
    experts = w_router.shape[1]
    ranks = a_query.shape[1]
    share = w_query.shape[0]
    low_rows = b_query.shape[0]

    def tp_cols(matrix, size):
        return lax.dynamic_slice_in_dim(matrix, tp_at * size, size, 1)

    def packed_low(parts, height):
        stack = jnp.concatenate(sum([tiles(p) for p in parts], []), axis=0)
        blocks = -(-stack.shape[0] // height)
        stack = jnp.pad(stack, ((0, blocks * height - stack.shape[0]), (0, 0)))
        return [stack[i * height : (i + 1) * height] for i in range(blocks)]

    first_low = [tp_cols(b_query, q_width), tp_cols(key_second_factor, kv_width), tp_cols(value_second_factor, kv_width)]
    second_low = [tp_cols(b_gate, ff_width), tp_cols(b_up, ff_width), b_out, b_down, b_router]
    base_one = [w_query, key_matrix, value_matrix, a_query, a_key, a_value]
    pack_one = jnp.concatenate(base_one + packed_low(first_low, share), axis=1)
    router_pad = jnp.pad(w_router, ((0, 0), (0, LANES - experts)))
    base_two = [w_out.T, a_router, a_gate, a_up, router_pad, a_out]
    pack_two = jnp.concatenate(base_two + packed_low(second_low + [a_down], share), axis=1)
    expert_block = jnp.concatenate([w_gate, w_up, jnp.swapaxes(w_down, 1, 2)], axis=2)

    one = gathered(pack_one)
    two = gathered(pack_two)
    expert_parts = spread(expert_block)

    def unpack_low(whole, col, parts):
        flat = whole[:, :, col:]
        flat = flat.reshape(n, share, -1, LANES).transpose(0, 2, 1, 3).reshape(n, -1, LANES)
        found = []
        at = 0
        for height, cols in parts:
            count = -(-cols // LANES)
            piece = flat[:, at : at + count * height].reshape(n, count, height, LANES)
            found.append(piece.transpose(0, 2, 1, 3).reshape(n * height, count * LANES))
            at += count * height
        return found

    w_one = one.reshape(n * share, -1)
    cols_one = q_width + 2 * kv_width + 3 * ranks
    query_b, key_b, value_b = unpack_low(one, cols_one, [(low_rows, q_width), (low_rows, kv_width), (low_rows, kv_width)])
    w_two = two.reshape(n * share, -1)
    cols_two = q_width + 5 * ranks
    gate_b, up_b, out_b, down_b, router_b, down_a = unpack_low(
        two,
        cols_two,
        [(low_rows, ff_width), (low_rows, ff_width), (low_rows, width), (low_rows, width), (low_rows, experts), (a_down.shape[0], ranks)],
    )
    out_wt = w_two[:, :q_width]
    router_a = w_two[:, q_width : q_width + ranks]
    gate_a = w_two[:, q_width + ranks : q_width + 2 * ranks]
    up_a = w_two[:, q_width + 2 * ranks : q_width + 3 * ranks]
    router_w = w_two[:, q_width + 3 * ranks : q_width + 4 * ranks]
    out_a = lax.dynamic_slice_in_dim(w_two[:, q_width + 4 * ranks : q_width + 5 * ranks], tp_at * q_width, q_width, 0)
    down_at = lax.dynamic_slice_in_dim(down_a, tp_at * ff_width, ff_width, 0)

    ends = jnp.cumsum(lengths[0])
    starts = ends - lengths[0]
    place = jnp.arange(group, dtype=jnp.int32)
    doc = jnp.sum((place[:, None] >= ends[None, :]).astype(jnp.int32), axis=1)
    picked = (doc[:, None] == jnp.arange(lengths.shape[1], dtype=jnp.int32)[None, :]).astype(jnp.int32)
    begin = jnp.sum(picked * starts[None, :], axis=1)
    chosen = jnp.sum(picked * adapter_of_doc[0][None, :], axis=1)
    start = ctx_at * rows
    query_index = start + jnp.arange(rows, dtype=jnp.int32)
    begin_local = lax.dynamic_slice_in_dim(begin, start, rows)
    chosen_local = lax.dynamic_slice_in_dim(chosen, start, rows)
    key_index = start - rows + jnp.arange(2 * rows, dtype=jnp.int32)
    allowed = (
        (key_index[None, :] <= query_index[:, None])
        & (key_index[None, :] >= begin_local[:, None])
        & (key_index[None, :] >= 0)
    )
    mask = (chosen_local[:, None] == (jnp.arange(ranks, dtype=jnp.int32) // ADAPTER_RANK)[None, :]).astype(F32)
    half = HEAD_SIZE // 2
    freq = 10000.0 ** (-jnp.arange(half, dtype=F32) / half)
    angles = (query_index - begin_local).astype(F32)[:, None] * freq[None, :]
    cosine_table = jnp.cos(angles)[:, None, :]
    sine_table = jnp.sin(angles)[:, None, :]
    scale = 1.0 / math.sqrt(HEAD_SIZE)
    heads_kv = kv_width // HEAD_SIZE
    per_group = q_width // kv_width

    xfull = tokens.astype(F32)
    normed = rms_norm(xfull, attn_gain).astype(BF)
    raw = dot(normed, w_one[:, :cols_one])
    qkv = q_width + 2 * kv_width
    query_u = (raw[:, qkv : qkv + ranks] * mask).astype(BF)
    key_u = (raw[:, qkv + ranks : qkv + 2 * ranks] * mask).astype(BF)
    value_u = (raw[:, qkv + 2 * ranks : qkv + 3 * ranks] * mask).astype(BF)
    query_pre = raw[:, :q_width] + dot(query_u, query_b)
    key_pre = raw[:, q_width : q_width + kv_width] + dot(key_u, key_b)
    value_state = (raw[:, q_width + kv_width : qkv] + dot(value_u, value_b)).astype(BF)
    query_state = (
        rotary_apply(query_pre.reshape(rows, -1, HEAD_SIZE), cosine_table, sine_table).reshape(rows, q_width).astype(BF)
    )
    key = rotary_apply(key_pre.reshape(rows, -1, HEAD_SIZE), cosine_table, sine_table).reshape(rows, kv_width).astype(BF)
    far = lax.ppermute(jnp.concatenate([key, value_state], axis=1), "ctx", [(i, i + 1) for i in range(lax.axis_size("ctx") - 1)])
    keys_h = jnp.concatenate([far[:, :kv_width], key], axis=0).reshape(2 * rows, heads_kv, HEAD_SIZE)
    values_h = jnp.concatenate([far[:, kv_width:], value_state], axis=0).reshape(2 * rows, heads_kv, HEAD_SIZE)
    query_h = query_state.reshape(rows, heads_kv, per_group, HEAD_SIZE)

    def score_block():
        s = jnp.einsum("qgrd,kgd->grqk", query_h, keys_h, preferred_element_type=F32) * scale
        return jnp.where(allowed[None, None], s, -1e30)

    scores = score_block()
    top = jnp.max(scores, axis=-1, keepdims=True)
    expd = jnp.exp(scores - top)
    total = jnp.sum(expd, axis=-1, keepdims=True)
    probs = expd / total
    log_total = top + jnp.log(total)
    mixed_heads = (
        jnp.einsum("grqk,kgd->qgrd", probs.astype(BF), values_h, preferred_element_type=F32).reshape(rows, q_width).astype(BF)
    )
    out_u = dot(mixed_heads, out_a) * mask
    attn_part = dot_t(mixed_heads, out_wt) + dot(out_u.astype(BF), out_b)
    hidden = xfull + lax.psum(attn_part, "tp")
    normed_two = rms_norm(hidden, ffn_gain).astype(BF)
    lows = dot(normed_two, w_two[:, q_width : q_width + 4 * ranks])
    router_u = (lows[:, :ranks] * mask).astype(BF)
    zin_gate = (lows[:, ranks : 2 * ranks] * mask).astype(BF)
    zin_up = (lows[:, 2 * ranks : 3 * ranks] * mask).astype(BF)
    logits = lows[:, 3 * ranks : 3 * ranks + experts] + dot(router_u, router_b)[:, :experts]
    selected = jnp.any(routes[:, :, None] == jnp.arange(experts, dtype=jnp.int32)[None, None, :], axis=1)
    gates = jax.nn.softmax(jnp.where(selected, logits, -jnp.inf), axis=-1)

    cot = out_cotangent
    dout = cot.astype(F32)
    gate_low = dot(zin_gate, gate_b)
    up_low = dot(zin_up, up_b)
    down_back = dot_t(cot, down_b) * mask
    act_low = dot_t(down_back.astype(BF), down_at)
    moe = jnp.zeros((rows, width), F32)
    dn2 = jnp.zeros((rows, width), F32)
    act_sum = jnp.zeros((rows, ff_width), F32)
    dg_sum = jnp.zeros((rows, ff_width), F32)
    du_sum = jnp.zeros((rows, ff_width), F32)
    dgate = jnp.zeros((rows, experts), F32)
    for owner, part in expert_parts:
        for j in range(local_experts):
            e = owner * local_experts + j
            w_gu = part[j][:, : 2 * ff_width]
            w_d = part[j][:, 2 * ff_width :]
            g = lax.dynamic_slice_in_dim(gates, e, 1, 1)
            pre = dot(normed_two, w_gu)
            gv = pre[:, :ff_width] + gate_low
            uv = pre[:, ff_width:] + up_low
            sig = jax.nn.sigmoid(gv)
            silu = gv * sig
            act = silu * uv
            back = dot(cot, w_d) + act_low
            col = jnp.sum(act * back, axis=1, keepdims=True)
            dgate = dgate + jnp.where(jnp.arange(experts)[None, :] == e, col, 0.0)
            act_g = (act * g).astype(BF)
            back = back * g
            dg = (back * uv * sig * (1.0 + gv * (1.0 - sig))).astype(BF)
            du = (back * silu).astype(BF)
            moe = moe + dot_t(act_g, w_d)
            dn2 = dn2 + dot_t(jnp.concatenate([dg, du], axis=1), w_gu)
            act_sum = act_sum + act_g.astype(F32)
            dg_sum = dg_sum + dg.astype(F32)
            du_sum = du_sum + du.astype(F32)
    down_low = (dot(act_sum.astype(BF), down_at) * mask).astype(BF)
    moe = moe + dot(down_low, down_b)
    output = (hidden + lax.psum(moe.astype(BF), "tp").astype(F32)).astype(BF)
    grad_bd = t_dot(down_low, cot)
    grad_ad = t_dot(act_sum.astype(BF), down_back.astype(BF))
    dg_sum = dg_sum.astype(BF)
    du_sum = du_sum.astype(BF)
    grad_bg = t_dot(zin_gate, dg_sum)
    grad_bu = t_dot(zin_up, du_sum)
    gate_du = (dot_t(dg_sum, gate_b) * mask).astype(BF)
    up_du = (dot_t(du_sum, up_b) * mask).astype(BF)
    dn2 = dn2 + dot_t(gate_du, gate_a) + dot_t(up_du, up_a)
    grad_ag = t_dot(normed_two, gate_du)
    grad_au = t_dot(normed_two, up_du)
    dn2, dgate = lax.psum((dn2, dgate), "tp")
    dlogits = (gates * (dgate - jnp.sum(gates * dgate, axis=-1, keepdims=True))).astype(BF)
    dlogits = jnp.pad(dlogits, ((0, 0), (0, LANES - experts)))
    router_du = (dot_t(dlogits, router_b) * mask).astype(BF)
    dn2 = dn2 + dot_t(dlogits, router_w) + dot_t(router_du, router_a)
    grad_br = t_dot(router_u, dlogits)[:, :experts]
    grad_ar = t_dot(normed_two, router_du)
    dhidden = dout + norm_back(hidden, ffn_gain, dn2)
    dattn = dhidden.astype(BF)
    out_du = (dot_t(dattn, out_b) * mask).astype(BF)
    dmixed = (dot(dattn, out_wt) + dot_t(out_du, out_a)).astype(BF)
    grad_bo = t_dot(out_u.astype(BF), dattn)
    grad_ao = t_dot(mixed_heads, out_du)
    probs_again = jnp.exp(score_block() - log_total)
    dmixed_h = dmixed.reshape(rows, heads_kv, per_group, HEAD_SIZE)
    dvalues = jnp.einsum("grqk,qgrd->kgd", probs_again.astype(BF), dmixed_h, preferred_element_type=F32).reshape(2 * rows, kv_width)
    dprobs = jnp.einsum("qgrd,kgd->grqk", dmixed_h, values_h, preferred_element_type=F32)
    dscores = (probs_again * (dprobs - jnp.sum(probs_again * dprobs, axis=-1, keepdims=True))).astype(BF)
    dquery = jnp.einsum("grqk,kgd->qgrd", dscores, keys_h, preferred_element_type=F32) * scale
    dkeys = (jnp.einsum("grqk,qgrd->kgd", dscores, query_h, preferred_element_type=F32) * scale).reshape(2 * rows, kv_width)
    far_back = lax.ppermute(
        jnp.concatenate([dkeys[:rows], dvalues[:rows]], axis=1).astype(BF),
        "ctx",
        [(i + 1, i) for i in range(lax.axis_size("ctx") - 1)],
    ).astype(F32)
    dkey = dkeys[rows:] + far_back[:, :kv_width]
    dvalue = (dvalues[rows:] + far_back[:, kv_width:]).astype(BF)
    dquery_pre = rotary_apply(dquery.reshape(rows, -1, HEAD_SIZE), cosine_table, -sine_table).reshape(rows, q_width).astype(BF)
    dkey_pre = rotary_apply(dkey.reshape(rows, -1, HEAD_SIZE), cosine_table, -sine_table).reshape(rows, kv_width).astype(BF)
    query_du = (dot_t(dquery_pre, query_b) * mask).astype(BF)
    key_du = (dot_t(dkey_pre, key_b) * mask).astype(BF)
    value_du = (dot_t(dvalue, value_b) * mask).astype(BF)
    everything = jnp.concatenate([dquery_pre, dkey_pre, dvalue, query_du, key_du, value_du], axis=1)
    dn1 = dot_t(everything, w_one[:, :cols_one])
    grad_a3 = t_dot(normed, everything[:, qkv:])
    grad_bq = t_dot(query_u, dquery_pre)
    grad_bk = t_dot(key_u, dkey_pre)
    grad_bv = t_dot(value_u, dvalue)
    dn1 = lax.psum(dn1.astype(BF), "tp").astype(F32)
    grad_tokens = (dhidden + norm_back(xfull, attn_gain, dn1)).astype(BF)

    def place_cols(piece, full_cols):
        blank = jnp.zeros((piece.shape[0], full_cols), F32)
        return lax.dynamic_update_slice_in_dim(blank, piece, tp_at * piece.shape[1], 1)

    def place_rows(piece, full_rows):
        blank = jnp.zeros((full_rows, piece.shape[1]), F32)
        return lax.dynamic_update_slice_in_dim(blank, piece, tp_at * piece.shape[0], 0)

    only_first = (tp_at == 0).astype(F32)
    grads = (
        grad_a3[:, :ranks],
        place_cols(grad_bq, q_width * n_tp),
        grad_a3[:, ranks : 2 * ranks],
        place_cols(grad_bk, kv_width * n_tp),
        grad_a3[:, 2 * ranks :],
        place_cols(grad_bv, kv_width * n_tp),
        place_rows(grad_ao, q_width * n_tp),
        grad_bo,
        grad_ar * only_first,
        grad_br * only_first,
        grad_ag,
        place_cols(grad_bg, ff_width * n_tp),
        grad_au,
        place_cols(grad_bu, ff_width * n_tp),
        place_rows(grad_ad, ff_width * n_tp),
        grad_bd,
    )
    flat = []
    for g in grads:
        height, cols = g.shape[0] // n, g.shape[1]
        count = -(-cols // LANES)
        g = jnp.pad(g.astype(BF), ((0, 0), (0, count * LANES - cols)))
        flat.append(g.reshape(n, height, count, LANES).transpose(0, 2, 1, 3).reshape(n, count * height, LANES))
    flat = jnp.concatenate(flat, axis=1)
    mine = lax.psum_scatter(flat, "fsdp", scatter_dimension=0, tiled=False)
    mine = lax.psum(mine, ("ctx", "tp")).astype(F32)
    final = []
    at = 0
    for g in grads:
        height, cols = g.shape[0] // n, g.shape[1]
        count = -(-cols // LANES)
        piece = mine[at : at + count * height].reshape(count, height, LANES).transpose(1, 0, 2).reshape(height, count * LANES)
        final.append(piece[:, :cols])
        at += count * height
    return (output, grad_tokens, *final)


def solution(mesh):
    both = P(("fsdp", "ctx"), None)
    split = P("fsdp", None)
    placed = (
        both, both, split, split, both, P(), P(),
        P("fsdp", "tp"), P("fsdp", "tp"), P("fsdp", "tp"), P("tp", "fsdp"), split,
        P("fsdp", None, "tp"), P("fsdp", None, "tp"), P("fsdp", "tp", None),
    ) + (split,) * 16
    return jax.shard_map(
        on_device, mesh=mesh, in_specs=placed, out_specs=(both, both) + (split,) * 16, check_vma=False
    )
```

time: 4560 us -> 1470 us (0.32)
  blocking collectives: 1710 us -> 3.53 us
  waiting for transfers between devices: 1390 us -> 646 us
  local copies, waits for them, and re-layouts: 471 us -> 186 us
  starting transfers between devices: 227 us -> 22.8 us
  other arithmetic: 235 us -> 136 us
  matrix products: 505 us -> 447 us
    all_gather x19 -> x0, blocking collectives: 1110 us -> none  [the longest x1 543 us: on_device(): lax.all_gather(b_gate, 'fsdp', axis=0, tiled=True)]
    all_to_all x6 -> x0, waiting for transfers between devices: 830 us -> none  [the longest x1 451 us: on_device(): lax.all_to_all(x_grad, 'fsdp', split_axis=0, concat_axis=0, tiled=True)]
    all_to_all x1 -> x0, blocking collectives: 588 us -> none  [on_device(): lax.all_to_all(to_slots(normed_two, token_of), 'fsdp', split_axis=0, conc...]
    ppermute x4 -> x23, waiting for transfers between devices: 18.4 us -> 528 us  [the longest x9 277 us: spread(): lax.ppermute(held[-1], 'fsdp', [(i, (i + inner) % n) for i in range(n)])]
    reduce_scatter x16 -> x1, waiting for transfers between devices: 504 us -> 91.1 us  [on_device(): mine = lax.psum_scatter(flat, 'fsdp', scatter_dimension=0, tiled=False)]
    gather x14 -> x0, local copies, waits for them, and re-layouts: 379 us -> none  [the longest x5 194 us: to_slots(): picked = jnp.where(live, values[index], jnp.zeros((), values.dtype))]
    all_to_all x6 -> x0, starting transfers between devices: 216 us -> none  [the longest x1 78.2 us: on_device(): lax.all_to_all(produced, 'fsdp', split_axis=0, concat_axis=0, tiled=True)]
    unnamed x254 -> x579, local copies, waits for them, and re-layouts: 13.3 us -> 81.7 us
  transfers between devices with their start and end apart: 32 -> 28, of which waited for: 14 -> 16; matrix products, arithmetic and copies ran while one was open for 25% -> 28% of each run, Pallas kernels for 0% -> 0%
where the time goes in v1:
time: 1470 us; the launch traced here: 1460 us
  waiting for transfers between devices  646 us (44%)
  matrix products  447 us (30%)
  local copies, waits for them, and re-layouts  186 us (13%)
  other arithmetic  136 us (9%)
  starting transfers between devices  22.8 us (2%)
  between operations  17.4 us (1%)
    dot_general x107, matrix products, dot(): lax.dot_general(left, right, (dims, ((), ())), preferred_element_type=F32)  320 us
    ppermute x9, waiting for transfers between devices, spread(): lax.ppermute(held[-1], 'fsdp', [(i, (i + inner) % n) for i in range(n)])  277 us
    ppermute x12, waiting for transfers between devices, spread(): rows.append([lax.ppermute(h, 'fsdp', turn) for h in rows[-1]])  232 us
    reduce_scatter x1, waiting for transfers between devices, on_device(): mine = lax.psum_scatter(flat, 'fsdp', scatter_dimension=0, tiled=False)  91.1 us
    unnamed x579, local copies, waits for them, and re-layouts  81.7 us
    convert_element_type x1, other arithmetic, on_device(): (probs_again * (dprobs - jnp.sum(probs_again * dprobs, axis=-1, keepdims=...  44.7 us
    dot_general x1, matrix products, on_device(): jnp.einsum('qgrd,kgd->grqk', dmixed_h, values_h, preferred_element_type=F32)  35.5 us
  transfers between devices with their start and end apart: 28, of which 16 were waited for; matrix products, arithmetic and copies ran while one was open for 28% of the time, Pallas kernels for 0%

profile of v1, /device:TPU:0, one launch (start us, length us, event | category | flops | bytes accessed | tf_op | source)
XLA Modules:
  0.0 1459.6 jit_solution(16098463741452086289)
XLA Ops:
  82.4 107.0 %collective-permute-done.1 = bf16[192,1792]{1,0:T(8,128)(2,1)S(1)} collective-permute-done((bf16[192,1792]{1,0:T(8,128)(2,1)}, bf16[192,1792]{1,0:T(8,128)(2,1)S(1)}, u32[]{:S(2)}, u32[]{:S(2)}) %collective-permute-start.1) | collective-permute-done | bytes 688160 | tf_op jit(solution)/shard_map/ppermute | solution.py:58
  189.4 14.7 %collective-permute-done.9 = bf16[192,1792]{1,0:T(8,128)(2,1)S(1)} collective-permute-done((bf16[192,1792]{1,0:T(8,128)(2,1)}, bf16[192,1792]{1,0:T(8,128)(2,1)S(1)}, u32[]{:S(2)}, u32[]{:S(2)}) %collective-permute-start.9) | collective-permute-done | bytes 688160 | tf_op jit(solution)/shard_map/ppermute | solution.py:58
  206.0 12.9 collective-permute-done.2
  239.3 99.3 %collective-permute-done.4 = bf16[192,1792]{1,0:T(8,128)(2,1)S(1)} collective-permute-done((bf16[192,1792]{1,0:T(8,128)(2,1)}, bf16[192,1792]{1,0:T(8,128)(2,1)S(1)}, u32[]{:S(2)}, u32[]{:S(2)}) %collective-permute-start.4) | collective-permute-done | bytes 688160 | tf_op jit(solution)/shard_map/ppermute | solution.py:62
  340.0 13.3 collective-permute-done.12
  354.8 13.3 collective-permute-done.5
  369.5 13.3 collective-permute-done.13
  383.7 13.8 collective-permute-done.6
  444.9 22.0 %fusion.384 = (f32[4,3,768]{2,1,0:T(4,128)S(1)}, f32[4,3,768,1536]{2,3,1,0:T(8,128)}) fusion(bf16[1536,4,64,1]{0,2,3,1:T(8,128)(2,1)} %bitcast.467, bf16[768,4,3,64]{0,3,2,1:T(8,128)(2,1)S(1)} %bitcast.448, pred[768,1536]{0,1:T(8,128)(4,1)} %and_and_fusion), kind=kOutput, calls=%fused_computation.780 | convolution fusion | flops 1854397440 | bytes 59805696 | tf_op jit(solution)/shard_map/qgrd,kgd->grqk/dot_general | solution.py:206
  466.9 18.1 %fusion.3 = f32[4,3,768]{2,1,0:T(4,128)S(1)} fusion(f32[4,3,768,1536]{2,3,1,0:T(8,128)} %get-tuple-element.209, f32[4,3,768]{2,1,0:T(4,128)S(1)} %get-tuple-element.208), kind=kLoop, calls=%fused_computation.9 | loop fusion | flops 28302336 | bytes 56696832 | tf_op jit(solution)/shard_map/reduce_sum | solution.py:212
  485.0 20.9 %fusion.34 = bf16[4,64,3,768]{3,1,2,0:T(8,128)(2,1)S(1)} fusion(bf16[1536,4,64,1]{0,2,3,1:T(8,128)(2,1)S(1)} %bitcast.463, f32[4,3,768,1536]{2,3,1,0:T(8,128)} %get-tuple-element.209, f32[4,3,768]{2,1,0:T(4,128)S(1)} %fusion.3, f32[4,3,768]{2,1,0:T(4,128)S(1)} %get-tuple-element.208), kind=kOutput, calls=%fused_computation.96 | convolution fusion | flops 1854996480 | bytes 58662912 | tf_op jit(solution)/shard_map/grqk,kgd->qgrd/dot_general | solution.py:216
  573.0 56.6 %collective-permute-done.16 = bf16[2,1536,768]{1,2,0:T(8,128)(2,1)} collective-permute-done((bf16[2,1536,768]{1,2,0:T(8,128)(2,1)}, bf16[2,1536,768]{1,2,0:T(8,128)(2,1)}, u32[]{:S(2)}, u32[]{:S(2)}) %collective-permute-start.16) | collective-permute-done | bytes 4718624 | tf_op jit(solution)/shard_map/ppermute | solution.py:58
  650.4 74.6 %collective-permute-done.17 = bf16[2,1536,768]{1,2,0:T(8,128)(2,1)} collective-permute-done((bf16[2,1536,768]{1,2,0:T(8,128)(2,1)}, bf16[2,1536,768]{1,2,0:T(8,128)(2,1)}, u32[]{:S(2)}, u32[]{:S(2)}) %collective-permute-start.17) | collective-permute-done | bytes 4718624 | tf_op jit(solution)/shard_map/ppermute | solution.py:58
  750.0 74.4 %collective-permute-done.21 = bf16[2,1536,768]{1,2,0:T(8,128)(2,1)} collective-permute-done((bf16[2,1536,768]{1,2,0:T(8,128)(2,1)}, bf16[2,1536,768]{1,2,0:T(8,128)(2,1)}, u32[]{:S(2)}, u32[]{:S(2)}) %collective-permute-start.21) | collective-permute-done | bytes 4718624 | tf_op jit(solution)/shard_map/ppermute | solution.py:62
  841.1 18.5 %add_convert_fusion.5 = (bf16[768,256]{0,1:T(8,128)(2,1)}, bf16[768,256]{0,1:T(8,128)(2,1)}, bf16[768,256]{0,1:T(8,128)(2,1)}, bf16[768,256]{0,1:T(8,128)(2,1)},...) fusion(f32[768,256]{0,1:T(8,128)} %copy-done.11, ...), kind=kLoop, calls=%fused_computation.328 | loop fusion | flops 47185920 | bytes 46055424 | tf_op jit(solution)/shard_map/convert_element_type | solution.py:271
  952.5 28.2 %add_add_fusion.2 = f32[768,1536]{1,0:T(8,128)} fusion(f32[768,1536]{1,0:T(8,128)} %fusion.267, f32[768,1536]{1,0:T(8,128)} %fusion.37, f32[768,1536]{1,0:T(8,128)} %fusion.41, f32[768,1536]{1,0:T(8,128)} %fusion.45, f32[768,1536]{1,0:T(8,128)} %fusion.49, f32[768,1536]{1,0:T(8,128)} %fusion.53, f32[768,1536]{1,0:T(8,128)} %fusion.57, ...), kind=kOutput, calls=%fused_computation.32 | convolution fusion | flops 322043904 | bytes 85524480 | tf_op jit(solution)/shard_map/dot_general | solution.py:17
  1066.4 25.7 %add_convert_fusion.1 = bf16[768,1536]{1,0:T(8,128)(2,1)} fusion(f32[768,1536]{1,0:T(8,128)} %fusion.258, f32[768,1536]{1,0:T(8,128)} %fusion.200, f32[768,1536]{1,0:T(8,128)} %fusion.203, f32[768,1536]{1,0:T(8,128)} %fusion.206, f32[768,1536]{1,0:T(8,128)} %fusion.209, f32[768,1536]{1,0:T(8,128)} %fusion.212, f32[768,1536]{1,0:T(8,128)} %fusion.215, ...), kind=kOutput, calls=%fused_computation.34 | convolution fusion | flops 624033792 | bytes 79036416 | tf_op jit(solution)/shard_map/dot_general | solution.py:17
  1109.6 35.5 %fusion = (f32[4,3,768]{2,1,0:T(4,128)S(1)}, f32[4,1536,768,3]{2,1,3,0:T(8,128)}) fusion(f32[4,3,768,1536]{2,3,1,0:T(8,128)} %get-tuple-element.209, f32[4,3,768]{2,1,0:T(4,128)S(1)} %copy-done.154, bf16[1536,4,64,1]{0,2,3,1:T(8,128)(2,1)S(1)} %bitcast.464, bf16[768,4,3,64]{0,3,2,1:T(8,128)(2,1)S(1)} %bitcast.450), kind=kOutput, calls=%fused_computation.2 | convolution fusion | flops 1854397440 | bytes 115286016 | tf_op jit(solution)/shard_map/qgrd,kgd->grqk/dot_general | solution.py:296
  1145.0 21.6 %fusion.23 = f32[1536,4,64]{0,2,1:T(8,128)} fusion(bf16[768,4,3,64]{0,3,2,1:T(8,128)(2,1)S(1)} %bitcast.451, f32[4,3,768,1536]{2,3,1,0:T(8,128)} %get-tuple-element.209, f32[4,3,768]{2,1,0:T(4,128)S(1)} %copy-done.154), kind=kOutput, calls=%fused_computation.45 | convolution fusion | flops 1840250880 | bytes 59412480 | tf_op jit(solution)/shard_map/grqk,qgrd->kgd/dot_general | solution.py:295
  1166.6 44.7 %fusion.2 = bf16[4,3,768,1536]{2,3,1,0:T(8,128)(2,1)} fusion(f32[4,1536,768,3]{2,1,3,0:T(8,128)} %get-tuple-element.220, f32[4,3,768,1536]{2,3,1,0:T(8,128)} %get-tuple-element.209, f32[4,3,768]{2,1,0:T(4,128)S(1)} %get-tuple-element.219, f32[4,3,768]{2,1,0:T(4,128)S(1)} %copy-done.154), kind=kLoop, calls=%fused_computation.4 | loop fusion | flops 56623104 | bytes 141631488 | tf_op jit(solution)/shard_map/convert_element_type | solution.py:297
  1223.2 15.2 %fusion.27 = f32[1536,4,64]{0,2,1:T(8,128)} fusion(bf16[768,4,3,64]{0,3,2,1:T(8,128)(2,1)S(1)} %bitcast.449, bf16[4,3,768,1536]{2,3,1,0:T(8,128)(2,1)} %fusion.2), kind=kOutput, calls=%fused_computation.48 | convolution fusion | flops 1812332544 | bytes 31064064 | tf_op jit(solution)/shard_map/grqk,qgrd->kgd/dot_general | solution.py:299
  1245.2 17.9 %collective-permute-done.22 = bf16[768,512]{0,1:T(8,128)(2,1)} collective-permute-done((bf16[768,512]{0,1:T(8,128)(2,1)}, bf16[768,512]{0,1:T(8,128)(2,1)}, u32[]{:S(2)}, u32[]{:S(2)}) %collective-permute-start.22) | collective-permute-done | bytes 786464 | tf_op jit(solution)/shard_map/ppermute | solution.py:300
  1317.7 91.1 %reduce-scatter.2.cloned.1.call-done = bf16[1,2256,128]{2,1,0:T(8,128)(2,1)} async-done(((bf16[8,2256,128]{2,1,0:T(8,128)(2,1)}), bf16[1,2256,128]{2,1,0:T(8,128)(2,1)}) %reduce-scatter.2.cloned.1.call-update) | async-done | bytes 577552 | tf_op jit(solution)/shard_map/reduce_scatter | solution.py:355
  1416.4 27.2 %all-reduce.16.cloned.1.call-done = bf16[2256,128]{1,0:T(8,128)(2,1)} async-done(((bf16[2256,128]{1,0:T(8,128)(2,1)}), bf16[2256,128]{1,0:T(8,128)(2,1)}) %all-reduce.16.cloned.1.call-update) | async-done | bytes 577552 | tf_op jit(solution)/shard_map/psum | solution.py:356
  (885 shorter events, 562.1 us)
Async XLA Ops:
  7.3 533.7 %all-reduce.12.cloned.1.call-start = ((), (), s32[]{:S(2)}) async-start(), calls=%async_computation.1 | async-start | bytes 9437184 | tf_op jit(solution)/shard_map/psum | solution.py:220
  33.6 43.0 %collective-permute-start = (bf16[192,1792]{1,0:T(8,128)(2,1)}, bf16[192,1792]{1,0:T(8,128)(2,1)}, u32[]{:S(2)}, u32[]{:S(2)}) collective-permute-start(bf16[192,1792]{1,0:T(8,128)(2,1)} %constant_dynamic-update-slice_fusion.10), channel_id=1, source_target_pairs={{0,8},{4,12},{8,16},{12,20},{16,24},{20,28},{24,0},{28,4},{1,9},{5... | collective-permute-start | bytes 2064392 | tf_op jit(solution)/shard_map/ppermute | solution.py:58
  36.7 196.6 %collective-permute-start.3 = (bf16[192,1792]{1,0:T(8,128)(2,1)}, bf16[192,1792]{1,0:T(8,128)(2,1)}, u32[]{:S(2)}, u32[]{:S(2)}) collective-permute-start(bf16[192,1792]{1,0:T(8,128)(2,1)} %constant_dynamic-update-slice_fusion.10), channel_id=1, source_target_pairs={{0,4},{4,0},{8,12},{12,8},{16,20},{20,16},{24,28},{28,24},{1,5},{5... | collective-permute-start | bytes 2064392 | tf_op jit(solution)/shard_map/ppermute | solution.py:62
  54.7 182.1 %collective-permute-start.11 = (bf16[192,1792]{1,0:T(8,128)(2,1)}, bf16[192,1792]{1,0:T(8,128)(2,1)}, u32[]{:S(2)}, u32[]{:S(2)}) collective-permute-start(bf16[192,1792]{1,0:T(8,128)(2,1)} %constant_dynamic-update-slice_fusion.47), channel_id=1, source_target_pairs={{0,4},{4,0},{8,12},{12,8},{16,20},{20,16},{24,28},{28,24},{1,5},{5... | collective-permute-start | bytes 2064392 | tf_op jit(solution)/shard_map/ppermute | solution.py:62
  62.5 465.4 %collective-permute-start.15 = (bf16[2,1536,768]{1,2,0:T(8,128)(2,1)}, bf16[2,1536,768]{1,2,0:T(8,128)(2,1)}, u32[]{:S(2)}, u32[]{:S(2)}) collective-permute-start(bf16[2,1536,768]{1,2,0:T(8,128)(2,1)} %pad_maximum_fusion), channel_id=1, source_target_pairs={{0,8},{4,12},{8,16},{12,20},{16,24},{20,28},{24,0},{28,4},{1,9},{5... | collective-permute-start | bytes 14155784 | tf_op jit(solution)/shard_map/ppermute | solution.py:58
  76.6 112.8 %collective-permute-start.1 = (bf16[192,1792]{1,0:T(8,128)(2,1)}, bf16[192,1792]{1,0:T(8,128)(2,1)S(1)}, u32[]{:S(2)}, u32[]{:S(2)}) collective-permute-start(bf16[192,1792]{1,0:T(8,128)(2,1)} %collective-permute-done), channel_id=1, source_target_pairs={{0,8},{4,12},{8,16},{12,20},{16,24},{20,28},{24,0},{28,4},{1,9},{5... | collective-permute-start | bytes 2064392 | tf_op jit(solution)/shard_map/ppermute | solution.py:58
  76.6 127.5 %collective-permute-start.9 = (bf16[192,1792]{1,0:T(8,128)(2,1)}, bf16[192,1792]{1,0:T(8,128)(2,1)S(1)}, u32[]{:S(2)}, u32[]{:S(2)}) collective-permute-start(bf16[192,1792]{1,0:T(8,128)(2,1)} %collective-permute-done.8), channel_id=1, source_target_pairs={{0,8},{4,12},{8,16},{12,20},{16,24},{20,28},{24,0},{28,4},{1,9},{5... | collective-permute-start | bytes 2064392 | tf_op jit(solution)/shard_map/ppermute | solution.py:58
  189.4 29.5 %collective-permute-start.2 = (bf16[192,1792]{1,0:T(8,128)(2,1)S(1)}, bf16[192,1792]{1,0:T(8,128)(2,1)S(1)}, u32[]{:S(2)}, u32[]{:S(2)}) collective-permute-start(bf16[192,1792]{1,0:T(8,128)(2,1)S(1)} %collective-permute-done.1), channel_id=1, source_target_pairs={{0,8},{4,12},{8,16},{12,20},{16,24},{20,28},{24,0},{28,4},{1,9},{5... | collective-permute-start | bytes 2064392 | tf_op jit(solution)/shard_map/ppermute | solution.py:58
  218.9 309.6 %collective-permute-start.18 = (bf16[2,1536,768]{1,2,0:T(8,128)(2,1)}, bf16[2,1536,768]{1,2,0:T(8,128)(2,1)}, u32[]{:S(2)}, u32[]{:S(2)}) collective-permute-start(bf16[2,1536,768]{1,2,0:T(8,128)(2,1)} %pad_maximum_fusion), channel_id=1, source_target_pairs={{0,4},{4,0},{8,12},{12,8},{16,20},{20,16},{24,28},{28,24},{1,5},{5... | collective-permute-start | bytes 14155784 | tf_op jit(solution)/shard_map/ppermute | solution.py:62
  231.9 106.7 %collective-permute-start.4 = (bf16[192,1792]{1,0:T(8,128)(2,1)}, bf16[192,1792]{1,0:T(8,128)(2,1)S(1)}, u32[]{:S(2)}, u32[]{:S(2)}) collective-permute-start(bf16[192,1792]{1,0:T(8,128)(2,1)} %collective-permute-done), channel_id=1, source_target_pairs={{0,4},{4,0},{8,12},{12,8},{16,20},{20,16},{24,28},{28,24},{1,5},{5... | collective-permute-start | bytes 2064392 | tf_op jit(solution)/shard_map/ppermute | solution.py:62
  233.3 120.1 %collective-permute-start.12 = (bf16[192,1792]{1,0:T(8,128)(2,1)}, bf16[192,1792]{1,0:T(8,128)(2,1)S(1)}, u32[]{:S(2)}, u32[]{:S(2)}) collective-permute-start(bf16[192,1792]{1,0:T(8,128)(2,1)} %collective-permute-done.8), channel_id=1, source_target_pairs={{0,4},{4,0},{8,12},{12,8},{16,20},{20,16},{24,28},{28,24},{1,5},{5... | collective-permute-start | bytes 2064392 | tf_op jit(solution)/shard_map/ppermute | solution.py:62
  236.8 131.3 %collective-permute-start.5 = (bf16[192,1792]{1,0:T(8,128)(2,1)S(1)}, bf16[192,1792]{1,0:T(8,128)(2,1)S(1)}, u32[]{:S(2)}, u32[]{:S(2)}) collective-permute-start(bf16[192,1792]{1,0:T(8,128)(2,1)S(1)} %collective-permute-done.1), channel_id=1, source_target_pairs={{0,4},{4,0},{8,12},{12,8},{16,20},{20,16},{24,28},{28,24},{1,5},{5... | collective-permute-start | bytes 2064392 | tf_op jit(solution)/shard_map/ppermute | solution.py:62
  338.6 44.2 %collective-permute-start.13 = (bf16[192,1792]{1,0:T(8,128)(2,1)S(1)}, bf16[192,1792]{1,0:T(8,128)(2,1)S(1)}, u32[]{:S(2)}, u32[]{:S(2)}) collective-permute-start(bf16[192,1792]{1,0:T(8,128)(2,1)S(1)} %collective-permute-done.9), channel_id=1, source_target_pairs={{0,4},{4,0},{8,12},{12,8},{16,20},{20,16},{24,28},{28,24},{1,5},{5... | collective-permute-start | bytes 2064392 | tf_op jit(solution)/shard_map/ppermute | solution.py:62
  353.3 44.2 %collective-permute-start.6 = (bf16[192,1792]{1,0:T(8,128)(2,1)S(1)}, bf16[192,1792]{1,0:T(8,128)(2,1)S(1)}, u32[]{:S(2)}, u32[]{:S(2)}) collective-permute-start(bf16[192,1792]{1,0:T(8,128)(2,1)S(1)} %collective-permute-done.2), channel_id=1, source_target_pairs={{0,4},{4,0},{8,12},{12,8},{16,20},{20,16},{24,28},{28,24},{1,5},{5... | collective-permute-start | bytes 2064392 | tf_op jit(solution)/shard_map/ppermute | solution.py:62
  368.1 50.7 %collective-permute-start.14 = (bf16[192,1792]{1,0:T(8,128)(2,1)S(1)}, bf16[192,1792]{1,0:T(8,128)(2,1)}, u32[]{:S(2)}, u32[]{:S(2)}) collective-permute-start(bf16[192,1792]{1,0:T(8,128)(2,1)S(1)} %collective-permute-done.10), channel_id=1, source_target_pairs={{0,4},{4,0},{8,12},{12,8},{16,20},{20,16},{24,28},{28,24},{1,5},{5... | collective-permute-start | bytes 2064392 | tf_op jit(solution)/shard_map/ppermute | solution.py:62
  513.3 578.9 %all-reduce.14.cloned.1.call-start = ((), (), s32[]{:S(2)}) async-start(), calls=%async_computation.2 | async-start | bytes 9437184 | tf_op jit(solution)/shard_map/psum | solution.py:280
  527.9 101.7 %collective-permute-start.16 = (bf16[2,1536,768]{1,2,0:T(8,128)(2,1)}, bf16[2,1536,768]{1,2,0:T(8,128)(2,1)}, u32[]{:S(2)}, u32[]{:S(2)}) collective-permute-start(bf16[2,1536,768]{1,2,0:T(8,128)(2,1)} %collective-permute-done.15), channel_id=1, source_target_pairs={{0,8},{4,12},{8,16},{12,20},{16,24},{20,28},{24,0},{28,4},{1,9},{5... | collective-permute-start | bytes 14155784 | tf_op jit(solution)/shard_map/ppermute | solution.py:58
  528.1 102.4 %collective-permute-start.19 = (bf16[2,1536,768]{1,2,0:T(8,128)(2,1)}, bf16[2,1536,768]{1,2,0:T(8,128)(2,1)}, u32[]{:S(2)}, u32[]{:S(2)}) collective-permute-start(bf16[2,1536,768]{1,2,0:T(8,128)(2,1)} %collective-permute-done.15), channel_id=1, source_target_pairs={{0,4},{4,0},{8,12},{12,8},{16,20},{20,16},{24,28},{28,24},{1,5},{5... | collective-permute-start | bytes 14155784 | tf_op jit(solution)/shard_map/ppermute | solution.py:62
  629.6 95.3 %collective-permute-start.17 = (bf16[2,1536,768]{1,2,0:T(8,128)(2,1)}, bf16[2,1536,768]{1,2,0:T(8,128)(2,1)}, u32[]{:S(2)}, u32[]{:S(2)}) collective-permute-start(bf16[2,1536,768]{1,2,0:T(8,128)(2,1)} %collective-permute-done.16), channel_id=1, source_target_pairs={{0,8},{4,12},{8,16},{12,20},{16,24},{20,28},{24,0},{28,4},{1,9},{5... | collective-permute-start | bytes 14155784 | tf_op jit(solution)/shard_map/ppermute | solution.py:58
  630.0 100.3 %collective-permute-start.20 = (bf16[2,1536,768]{1,2,0:T(8,128)(2,1)}, bf16[2,1536,768]{1,2,0:T(8,128)(2,1)}, u32[]{:S(2)}, u32[]{:S(2)}) collective-permute-start(bf16[2,1536,768]{1,2,0:T(8,128)(2,1)} %collective-permute-done.16), channel_id=1, source_target_pairs={{0,4},{4,0},{8,12},{12,8},{16,20},{20,16},{24,28},{28,24},{1,5},{5... | collective-permute-start | bytes 14155784 | tf_op jit(solution)/shard_map/ppermute | solution.py:62
  725.0 99.4 %collective-permute-start.21 = (bf16[2,1536,768]{1,2,0:T(8,128)(2,1)}, bf16[2,1536,768]{1,2,0:T(8,128)(2,1)}, u32[]{:S(2)}, u32[]{:S(2)}) collective-permute-start(bf16[2,1536,768]{1,2,0:T(8,128)(2,1)} %collective-permute-done.17), channel_id=1, source_target_pairs={{0,4},{4,0},{8,12},{12,8},{16,20},{20,16},{24,28},{28,24},{1,5},{5... | collective-permute-start | bytes 14155784 | tf_op jit(solution)/shard_map/ppermute | solution.py:62
  980.7 334.5 %all-reduce.18.cloned.1.call-start = ((), (), s32[]{:S(2)}) async-start(), calls=%async_computation.5 | async-start | bytes 9437184 | tf_op jit(solution)/shard_map/psum | solution.py:268
  1279.8 129.1 %reduce-scatter.2.cloned.1.call-start = ((), (), s32[]{:S(2)}) async-start(), calls=%async_computation.3 | async-start | bytes 5197824 | tf_op jit(solution)/shard_map/reduce_scatter | solution.py:355
  1315.1 128.5 %all-reduce.16.cloned.1.call-start = ((), (), s32[]{:S(2)}) async-start(), calls=%async_computation.4 | async-start | bytes 1155072 | tf_op jit(solution)/shard_map/psum | solution.py:356
  (254 other events, 4858.5 us)
Sparse Core Ops, SparseCore 0:
  513.4 25.6 all-reduce.11
  980.8 28.3 all-reduce.13
  1279.9 28.5 all-reduce.17
  1315.2 93.5 reduce-scatter.1
  1411.2 32.4 all-reduce.15

commit v2 on v1

--- a/solution.py
+++ b/solution.py
@@ -1,8 +1,10 @@
-import math
+import functools
 
 import jax
 import jax.numpy as jnp
 from jax import lax
+from jax.experimental import pallas as pl
+from jax.experimental.pallas import tpu as pltpu
 from jax.sharding import PartitionSpec as P
 
 HEAD_SIZE = 64
@@ -13,8 +15,11 @@
 F32 = jnp.float32
 
 
-def dot(left, right, dims=((1,), (0,))):
-    return lax.dot_general(left, right, (dims, ((), ())), preferred_element_type=F32)
+MESH = pl.DeviceIdType.MESH
+
+
+def dot(left, right, dims=((1,), (0,)), precision=None):
+    return lax.dot_general(left, right, (dims, ((), ())), preferred_element_type=F32, precision=precision)
 
 
 def dot_t(left, right):
@@ -74,6 +79,260 @@
     for owner, part in spread(block):
         whole = lax.dynamic_update_index_in_dim(whole, part, owner, 0)
     return whole
+
+
+def fill_bias(bias, start_ref, begin_ref, rows):
+    step = rows // 3
+    for at in range(0, 2 * rows, step):
+        key = start_ref[0] - rows + at + lax.broadcasted_iota(jnp.int32, (step, rows), 0)
+        query = start_ref[0] + lax.broadcasted_iota(jnp.int32, (step, rows), 1)
+        ok = (key <= query) & (key >= begin_ref[...]) & (key >= 0)
+        bias[pl.ds(at, step), :] = jnp.where(ok, 0.0, -1e30)
+
+
+def split_heads(ref, out, count, rows, at=0):
+    for h in range(count):
+        out[h, pl.ds(at, rows), :] = ref[:, h * HEAD_SIZE : (h + 1) * HEAD_SIZE]
+
+
+def attend_kernel(group, q_blocks, start_ref, begin_ref, q_ref, ko_ref, vo_ref, kf_ref, vf_ref, o_ref, lse_ref, bias, ks, vts, qs, ots):
+    rows = q_ref.shape[0]
+    width = rows // q_blocks
+    heads = 2 * group
+    @pl.when(pl.program_id(0) == 0)
+    def _():
+        fill_bias(bias, start_ref, begin_ref, rows)
+    split_heads(kf_ref, ks, 2, rows, 0)
+    split_heads(ko_ref, ks, 2, rows, rows)
+    split_heads(q_ref, qs, heads, rows, 0)
+    vts[:, pl.ds(0, rows)] = vf_ref[...].astype(F32).T.astype(BF)
+    vts[:, pl.ds(rows, rows)] = vo_ref[...].astype(F32).T.astype(BF)
+    for b in range(q_blocks):
+        keys = rows + (b + 1) * width
+        def one(h, _):
+            g = h // group
+            s = dot_t(ks[g, pl.ds(0, keys), :], qs[h, pl.ds(b * width, width), :]) + bias[pl.ds(0, keys), pl.ds(b * width, width)]
+            top = jnp.max(s, axis=0, keepdims=True)
+            p = jnp.exp(s - top)
+            total = jnp.sum(p, axis=0, keepdims=True)
+            lse_ref[0, pl.ds(h, 1), pl.ds(b * width, width)] = top + jnp.log(total)
+            vt = vts[pl.ds(pl.multiple_of(g * HEAD_SIZE, HEAD_SIZE), HEAD_SIZE), pl.ds(0, keys)]
+            o = dot(vt, p.astype(BF)) / total
+            ots[pl.ds(pl.multiple_of(h * HEAD_SIZE, HEAD_SIZE), HEAD_SIZE), pl.ds(b * width, width)] = o
+            return 0
+        lax.fori_loop(0, heads, one, 0)
+    for j in range(group):
+        o_ref[:, j * LANES : (j + 1) * LANES] = ots[pl.ds(j * LANES, LANES), :].T.astype(BF)
+
+
+def attend(q, kv, far, begin, start, q_blocks=3):
+    rows, q_width = q.shape
+    kv_width = kv.shape[1] // 2
+    pairs = kv_width // LANES
+    group = q_width // kv_width
+    spec = lambda off: pl.BlockSpec((rows, LANES), lambda i: (0, i + off))
+    return pl.pallas_call(
+        functools.partial(attend_kernel, group, q_blocks),
+        grid=(pairs,),
+        in_specs=[pl.BlockSpec(memory_space=pltpu.SMEM), pl.BlockSpec((1, rows), lambda i: (0, 0)),
+                  pl.BlockSpec((rows, group * LANES), lambda i: (0, i)), spec(0), spec(pairs), spec(0), spec(pairs)],
+        out_specs=[pl.BlockSpec((rows, group * LANES), lambda i: (0, i)), pl.BlockSpec((1, 8, rows), lambda i: (i, 0, 0))],
+        out_shape=[jax.ShapeDtypeStruct((rows, q_width), BF), jax.ShapeDtypeStruct((pairs, 8, rows), F32)],
+        scratch_shapes=[pltpu.VMEM((2 * rows, rows), F32), pltpu.VMEM((2, 2 * rows, HEAD_SIZE), BF), pltpu.VMEM((LANES, 2 * rows), BF),
+                        pltpu.VMEM((2 * group, rows, HEAD_SIZE), BF), pltpu.VMEM((2 * group * HEAD_SIZE, rows), F32)],
+        compiler_params=pltpu.CompilerParams(vmem_limit_bytes=50 << 20),
+        cost_estimate=pl.CostEstimate(flops=8 * rows * rows * q_width, bytes_accessed=8 << 20, transcendentals=2 * rows * rows * 12),
+    )(start, begin, q, kv, kv, far, far)
+
+
+def attend_back_kernel(group, q_blocks, start_ref, begin_ref, q_ref, ko_ref, vo_ref, kf_ref, vf_ref, o_ref, do_ref, lse_ref,
+                       dq_ref, dko_ref, dvo_ref, dkf_ref, dvf_ref, bias, ks, vs, kts, qs, dos, dqts, dks, dvs, deltas):
+    rows = q_ref.shape[0]
+    width = rows // q_blocks
+    heads = 2 * group
+    @pl.when(pl.program_id(0) == 0)
+    def _():
+        fill_bias(bias, start_ref, begin_ref, rows)
+    split_heads(kf_ref, ks, 2, rows, 0)
+    split_heads(ko_ref, ks, 2, rows, rows)
+    split_heads(vf_ref, vs, 2, rows, 0)
+    split_heads(vo_ref, vs, 2, rows, rows)
+    split_heads(q_ref, qs, heads, rows, 0)
+    split_heads(do_ref, dos, heads, rows, 0)
+    kts[:, pl.ds(0, rows)] = kf_ref[...].astype(F32).T.astype(BF)
+    kts[:, pl.ds(rows, rows)] = ko_ref[...].astype(F32).T.astype(BF)
+    cols = heads * HEAD_SIZE
+    pick = (lax.broadcasted_iota(jnp.int32, (8, cols), 1) // HEAD_SIZE == lax.broadcasted_iota(jnp.int32, (8, cols), 0)).astype(F32)
+    prod = o_ref[...].astype(F32) * do_ref[...].astype(F32)
+    deltas[...] = dot(pick, prod, ((1,), (1,)), lax.Precision.HIGHEST)
+    dks[...] = jnp.zeros_like(dks)
+    dvs[...] = jnp.zeros_like(dvs)
+    for b in range(q_blocks):
+        keys = rows + (b + 1) * width
+        def one(h, _):
+            g = h // group
+            at = pl.ds(b * width, width)
+            qb = qs[h, at, :]
+            dob = dos[h, at, :]
+            s = dot_t(ks[g, pl.ds(0, keys), :], qb) + bias[pl.ds(0, keys), at]
+            p = jnp.exp(s - lse_ref[0, pl.ds(h, 1), at])
+            dp = dot_t(vs[g, pl.ds(0, keys), :], dob)
+            ds = (p * (dp - deltas[pl.ds(h, 1), at])).astype(BF)
+            dvs[g, pl.ds(0, keys), :] += dot(p.astype(BF), dob)
+            dks[g, pl.ds(0, keys), :] += dot(ds, qb)
+            kt = kts[pl.ds(pl.multiple_of(g * HEAD_SIZE, HEAD_SIZE), HEAD_SIZE), pl.ds(0, keys)]
+            dqts[pl.ds(pl.multiple_of(h * HEAD_SIZE, HEAD_SIZE), HEAD_SIZE), at] = dot(kt, ds) * 0.125
+            return 0
+        lax.fori_loop(0, heads, one, 0)
+    for j in range(group):
+        dq_ref[:, j * LANES : (j + 1) * LANES] = dqts[pl.ds(j * LANES, LANES), :].T
+    for g in range(2):
+        at = slice(g * HEAD_SIZE, (g + 1) * HEAD_SIZE)
+        dkf_ref[:, at] = dks[g, pl.ds(0, rows), :].astype(BF)
+        dko_ref[:, at] = dks[g, pl.ds(rows, rows), :]
+        dvf_ref[:, at] = dvs[g, pl.ds(0, rows), :].astype(BF)
+        dvo_ref[:, at] = dvs[g, pl.ds(rows, rows), :]
+
+
+def attend_back(q, kv, far, begin, start, o, do, lse, q_blocks=3):
+    rows, q_width = q.shape
+    kv_width = kv.shape[1] // 2
+    pairs = kv_width // LANES
+    group = q_width // kv_width
+    spec = lambda off: pl.BlockSpec((rows, LANES), lambda i: (0, i + off))
+    wide = pl.BlockSpec((rows, group * LANES), lambda i: (0, i))
+    sd = jax.ShapeDtypeStruct
+    return pl.pallas_call(
+        functools.partial(attend_back_kernel, group, q_blocks),
+        grid=(pairs,),
+        in_specs=[pl.BlockSpec(memory_space=pltpu.SMEM), pl.BlockSpec((1, rows), lambda i: (0, 0)),
+                  wide, spec(0), spec(pairs), spec(0), spec(pairs), wide, wide, pl.BlockSpec((1, 8, rows), lambda i: (i, 0, 0))],
+        out_specs=[wide, spec(0), spec(0), spec(0), spec(0)],
+        out_shape=[sd((rows, q_width), F32), sd((rows, kv_width), F32), sd((rows, kv_width), F32), sd((rows, kv_width), BF), sd((rows, kv_width), BF)],
+        scratch_shapes=[pltpu.VMEM((2 * rows, rows), F32), pltpu.VMEM((2, 2 * rows, HEAD_SIZE), BF), pltpu.VMEM((2, 2 * rows, HEAD_SIZE), BF), pltpu.VMEM((LANES, 2 * rows), BF),
+                        pltpu.VMEM((2 * group, rows, HEAD_SIZE), BF), pltpu.VMEM((2 * group, rows, HEAD_SIZE), BF), pltpu.VMEM((2 * group * HEAD_SIZE, rows), F32),
+                        pltpu.VMEM((2, 2 * rows, HEAD_SIZE), F32), pltpu.VMEM((2, 2 * rows, HEAD_SIZE), F32), pltpu.VMEM((8, rows), F32)],
+        compiler_params=pltpu.CompilerParams(vmem_limit_bytes=56 << 20),
+        cost_estimate=pl.CostEstimate(flops=20 * rows * rows * q_width, bytes_accessed=16 << 20, transcendentals=2 * rows * rows * 12),
+    )(start, begin, q, kv, kv, far, far, o, do, lse)
+
+
+def gather_kernel(n, count, *refs):
+    ins, outs = refs[:count], refs[count : 2 * count]
+    own_sem, z_send, z_recv, y_send, y_recv, x_send, x_recv = refs[2 * count :]
+    outer, inner = levels(n)
+    me = lax.axis_index("fsdp")
+    ctx = lax.axis_index("ctx")
+    z, y = me // inner, me % inner
+    right = (z + 1) % outer * inner + y
+    left = (z + outer - 1) % outer * inner + y
+
+    def shard(do, dj):
+        return (z + outer - do) % outer * inner + (y + inner - dj) % inner
+
+    barrier = pltpu.get_barrier_semaphore()
+    peers = [right, left] + [z * inner + (y + dj) % inner for dj in range(1, inner)]
+    for peer in peers:
+        pl.semaphore_signal(barrier, inc=1, device_id={"fsdp": peer}, device_id_type=MESH)
+    pl.semaphore_signal(barrier, inc=1, device_id={"ctx": 1 - ctx}, device_id_type=MESH)
+    pl.semaphore_wait(barrier, len(peers) + 1)
+
+    def slab(a):
+        third = ins[a].shape[0] // 3
+        if third % 16:
+            return pl.ds(0, ins[a].shape[0])
+        return pl.ds(pl.multiple_of(ctx * third, 16), 2 * third)
+
+    def tricked(a):
+        return ins[a].shape[0] // 3 % 16 == 0
+
+    def block(a, k, rows):
+        return ins[a].at[rows] if k is None else outs[a].at[k, rows]
+
+    def z_copy(a, k):
+        src = shard(k - 1, 0)
+        return pltpu.make_async_remote_copy(
+            src_ref=block(a, None if k == 1 else src, slab(a)), dst_ref=outs[a].at[src, slab(a)],
+            send_sem=z_send.at[a, k - 1], recv_sem=z_recv.at[a, k - 1], device_id={"fsdp": right}, device_id_type=MESH)
+
+    def y_copy(a, do, dj):
+        src = shard(do, 0)
+        return pltpu.make_async_remote_copy(
+            src_ref=block(a, None if do == 0 else src, slab(a)), dst_ref=outs[a].at[src, slab(a)],
+            send_sem=y_send.at[a, do, dj - 1], recv_sem=y_recv.at[a, do, dj - 1],
+            device_id={"fsdp": z * inner + (y + dj) % inner}, device_id_type=MESH)
+
+    def x_copy(a, do, dj):
+        src = shard(do, dj)
+        third = ins[a].shape[0] // 3
+        rows = pl.ds(pl.multiple_of(ctx * 2 * third, 16), third)
+        return pltpu.make_async_remote_copy(
+            src_ref=outs[a].at[src, rows], dst_ref=outs[a].at[src, rows],
+            send_sem=x_send.at[a, do, dj], recv_sem=x_recv.at[a, do, dj], device_id={"ctx": 1 - ctx}, device_id_type=MESH)
+
+    started = []
+
+    def go(copy):
+        copy.start()
+        started.append(copy)
+
+    own = [pltpu.make_async_copy(ins[a], outs[a].at[me], own_sem.at[a]) for a in range(count)]
+    for a in range(count):
+        go(z_copy(a, 1))
+        for dj in range(1, inner):
+            go(y_copy(a, 0, dj))
+    for c in own:
+        c.start()
+    for do in range(1, outer + 1):
+        if do < outer:
+            for a in range(count):
+                z_copy(a, do).wait_recv()
+                if do + 1 < outer:
+                    go(z_copy(a, do + 1))
+                for dj in range(1, inner):
+                    go(y_copy(a, do, dj))
+                if tricked(a):
+                    go(x_copy(a, do, 0))
+        for a in range(count):
+            for dj in range(1, inner):
+                y_copy(a, do - 1, dj).wait_recv()
+                if tricked(a):
+                    go(x_copy(a, do - 1, dj))
+    for a in range(count):
+        if tricked(a):
+            for do in range(outer):
+                for dj in range(inner):
+                    if do or dj:
+                        x_copy(a, do, dj).wait_recv()
+    for c in started:
+        c.wait_send()
+    for c in own:
+        c.wait()
+
+
+def gather_now(arrays, collective_id):
+    n = lax.axis_size("fsdp")
+    outer, inner = levels(n)
+    count = len(arrays)
+    dma = pltpu.SemaphoreType.DMA
+    return pl.pallas_call(
+        functools.partial(gather_kernel, n, count),
+        in_specs=[pl.BlockSpec(memory_space=pl.ANY)] * count,
+        out_specs=[pl.BlockSpec(memory_space=pl.ANY)] * count,
+        out_shape=[jax.ShapeDtypeStruct((n,) + a.shape, a.dtype) for a in arrays],
+        scratch_shapes=[
+            dma((count,)), dma((count, outer - 1)), dma((count, outer - 1)),
+            dma((count, outer, max(inner - 1, 1))), dma((count, outer, max(inner - 1, 1))),
+            dma((count, outer, inner)), dma((count, outer, inner)),
+        ],
+        compiler_params=pltpu.CompilerParams(collective_id=collective_id, has_side_effects=True),
+    )(*arrays)
+
+
+def tp_sum(value):
+    if lax.axis_size("tp") != 2:
+        return lax.psum(value, "tp")
+    return value + lax.ppermute(value, "tp", [(0, 1), (1, 0)])
 
 
 def tiles(matrix):
@@ -122,8 +381,9 @@
     pack_two = jnp.concatenate(base_two + packed_low(second_low + [a_down], share), axis=1)
     expert_block = jnp.concatenate([w_gate, w_up, jnp.swapaxes(w_down, 1, 2)], axis=2)
 
-    one = gathered(pack_one)
-    two = gathered(pack_two)
+    (one,) = gather_now([pack_one], 0)
+    one, pack_two, expert_block = lax.optimization_barrier((one, pack_two, expert_block))
+    two = lax.all_gather(pack_two, "fsdp", axis=0, tiled=False)
     expert_parts = spread(expert_block)
 
     def unpack_low(whole, col, parts):
@@ -167,21 +427,12 @@
     query_index = start + jnp.arange(rows, dtype=jnp.int32)
     begin_local = lax.dynamic_slice_in_dim(begin, start, rows)
     chosen_local = lax.dynamic_slice_in_dim(chosen, start, rows)
-    key_index = start - rows + jnp.arange(2 * rows, dtype=jnp.int32)
-    allowed = (
-        (key_index[None, :] <= query_index[:, None])
-        & (key_index[None, :] >= begin_local[:, None])
-        & (key_index[None, :] >= 0)
-    )
     mask = (chosen_local[:, None] == (jnp.arange(ranks, dtype=jnp.int32) // ADAPTER_RANK)[None, :]).astype(F32)
     half = HEAD_SIZE // 2
     freq = 10000.0 ** (-jnp.arange(half, dtype=F32) / half)
     angles = (query_index - begin_local).astype(F32)[:, None] * freq[None, :]
     cosine_table = jnp.cos(angles)[:, None, :]
     sine_table = jnp.sin(angles)[:, None, :]
-    scale = 1.0 / math.sqrt(HEAD_SIZE)
-    heads_kv = kv_width // HEAD_SIZE
-    per_group = q_width // kv_width
 
     xfull = tokens.astype(F32)
     normed = rms_norm(xfull, attn_gain).astype(BF)
@@ -198,26 +449,14 @@
     )
     key = rotary_apply(key_pre.reshape(rows, -1, HEAD_SIZE), cosine_table, sine_table).reshape(rows, kv_width).astype(BF)
     far = lax.ppermute(jnp.concatenate([key, value_state], axis=1), "ctx", [(i, i + 1) for i in range(lax.axis_size("ctx") - 1)])
-    keys_h = jnp.concatenate([far[:, :kv_width], key], axis=0).reshape(2 * rows, heads_kv, HEAD_SIZE)
-    values_h = jnp.concatenate([far[:, kv_width:], value_state], axis=0).reshape(2 * rows, heads_kv, HEAD_SIZE)
-    query_h = query_state.reshape(rows, heads_kv, per_group, HEAD_SIZE)
-
-    def score_block():
-        s = jnp.einsum("qgrd,kgd->grqk", query_h, keys_h, preferred_element_type=F32) * scale
-        return jnp.where(allowed[None, None], s, -1e30)
-
-    scores = score_block()
-    top = jnp.max(scores, axis=-1, keepdims=True)
-    expd = jnp.exp(scores - top)
-    total = jnp.sum(expd, axis=-1, keepdims=True)
-    probs = expd / total
-    log_total = top + jnp.log(total)
-    mixed_heads = (
-        jnp.einsum("grqk,kgd->qgrd", probs.astype(BF), values_h, preferred_element_type=F32).reshape(rows, q_width).astype(BF)
-    )
+    kv = jnp.concatenate([key, value_state], axis=1)
+    begin_row = begin_local[None, :]
+    start_at = jnp.reshape(start, (1,)).astype(jnp.int32)
+    query_state = (query_state.astype(F32) * 0.125).astype(BF)
+    mixed_heads, log_total = attend(query_state, kv, far, begin_row, start_at)
     out_u = dot(mixed_heads, out_a) * mask
     attn_part = dot_t(mixed_heads, out_wt) + dot(out_u.astype(BF), out_b)
-    hidden = xfull + lax.psum(attn_part, "tp")
+    hidden = xfull + tp_sum(attn_part)
     normed_two = rms_norm(hidden, ffn_gain).astype(BF)
     lows = dot(normed_two, w_two[:, q_width : q_width + 4 * ranks])
     router_u = (lows[:, :ranks] * mask).astype(BF)
@@ -265,7 +504,7 @@
             du_sum = du_sum + du.astype(F32)
     down_low = (dot(act_sum.astype(BF), down_at) * mask).astype(BF)
     moe = moe + dot(down_low, down_b)
-    output = (hidden + lax.psum(moe.astype(BF), "tp").astype(F32)).astype(BF)
+    output = (hidden + tp_sum(moe.astype(BF).astype(F32))).astype(BF)
     grad_bd = t_dot(down_low, cot)
     grad_ad = t_dot(act_sum.astype(BF), down_back.astype(BF))
     dg_sum = dg_sum.astype(BF)
@@ -277,7 +516,7 @@
     dn2 = dn2 + dot_t(gate_du, gate_a) + dot_t(up_du, up_a)
     grad_ag = t_dot(normed_two, gate_du)
     grad_au = t_dot(normed_two, up_du)
-    dn2, dgate = lax.psum((dn2, dgate), "tp")
+    dn2, dgate = tp_sum(dn2), tp_sum(dgate)
     dlogits = (gates * (dgate - jnp.sum(gates * dgate, axis=-1, keepdims=True))).astype(BF)
     dlogits = jnp.pad(dlogits, ((0, 0), (0, LANES - experts)))
     router_du = (dot_t(dlogits, router_b) * mask).astype(BF)
@@ -290,20 +529,16 @@
     dmixed = (dot(dattn, out_wt) + dot_t(out_du, out_a)).astype(BF)
     grad_bo = t_dot(out_u.astype(BF), dattn)
     grad_ao = t_dot(mixed_heads, out_du)
-    probs_again = jnp.exp(score_block() - log_total)
-    dmixed_h = dmixed.reshape(rows, heads_kv, per_group, HEAD_SIZE)
-    dvalues = jnp.einsum("grqk,qgrd->kgd", probs_again.astype(BF), dmixed_h, preferred_element_type=F32).reshape(2 * rows, kv_width)
-    dprobs = jnp.einsum("qgrd,kgd->grqk", dmixed_h, values_h, preferred_element_type=F32)
-    dscores = (probs_again * (dprobs - jnp.sum(probs_again * dprobs, axis=-1, keepdims=True))).astype(BF)
-    dquery = jnp.einsum("grqk,kgd->qgrd", dscores, keys_h, preferred_element_type=F32) * scale
-    dkeys = (jnp.einsum("grqk,qgrd->kgd", dscores, query_h, preferred_element_type=F32) * scale).reshape(2 * rows, kv_width)
+    dquery, dkey_own, dvalue_own, dkey_far, dvalue_far = attend_back(
+        query_state, kv, far, begin_row, start_at, mixed_heads, dmixed, log_total
+    )
     far_back = lax.ppermute(
-        jnp.concatenate([dkeys[:rows], dvalues[:rows]], axis=1).astype(BF),
+        jnp.concatenate([dkey_far, dvalue_far], axis=1),
         "ctx",
         [(i + 1, i) for i in range(lax.axis_size("ctx") - 1)],
     ).astype(F32)
-    dkey = dkeys[rows:] + far_back[:, :kv_width]
-    dvalue = (dvalues[rows:] + far_back[:, kv_width:]).astype(BF)
+    dkey = dkey_own + far_back[:, :kv_width]
+    dvalue = (dvalue_own + far_back[:, kv_width:]).astype(BF)
     dquery_pre = rotary_apply(dquery.reshape(rows, -1, HEAD_SIZE), cosine_table, -sine_table).reshape(rows, q_width).astype(BF)
     dkey_pre = rotary_apply(dkey.reshape(rows, -1, HEAD_SIZE), cosine_table, -sine_table).reshape(rows, kv_width).astype(BF)
     query_du = (dot_t(dquery_pre, query_b) * mask).astype(BF)
@@ -315,7 +550,7 @@
     grad_bq = t_dot(query_u, dquery_pre)
     grad_bk = t_dot(key_u, dkey_pre)
     grad_bv = t_dot(value_u, dvalue)
-    dn1 = lax.psum(dn1.astype(BF), "tp").astype(F32)
+    dn1 = tp_sum(dn1)
     grad_tokens = (dhidden + norm_back(xfull, attn_gain, dn1)).astype(BF)
 
     def place_cols(piece, full_cols):
@@ -345,23 +580,27 @@
         place_rows(grad_ad, ff_width * n_tp),
         grad_bd,
     )
-    flat = []
-    for g in grads:
-        height, cols = g.shape[0] // n, g.shape[1]
-        count = -(-cols // LANES)
-        g = jnp.pad(g.astype(BF), ((0, 0), (0, count * LANES - cols)))
-        flat.append(g.reshape(n, height, count, LANES).transpose(0, 2, 1, 3).reshape(n, count * height, LANES))
-    flat = jnp.concatenate(flat, axis=1)
-    mine = lax.psum_scatter(flat, "fsdp", scatter_dimension=0, tiled=False)
-    mine = lax.psum(mine, ("ctx", "tp")).astype(F32)
-    final = []
-    at = 0
-    for g in grads:
-        height, cols = g.shape[0] // n, g.shape[1]
-        count = -(-cols // LANES)
-        piece = mine[at : at + count * height].reshape(count, height, LANES).transpose(1, 0, 2).reshape(height, count * LANES)
-        final.append(piece[:, :cols])
-        at += count * height
+    def reduce_grads(some):
+        flat = []
+        for g in some:
+            height, cols = g.shape[0] // n, g.shape[1]
+            count = -(-cols // LANES)
+            g = jnp.pad(g.astype(BF), ((0, 0), (0, count * LANES - cols)))
+            flat.append(g.reshape(n, height, count, LANES).transpose(0, 2, 1, 3).reshape(n, count * height, LANES))
+        flat = jnp.concatenate(flat, axis=1)
+        mine = lax.psum_scatter(flat, "fsdp", scatter_dimension=0, tiled=False)
+        mine = lax.psum(mine, ("ctx", "tp")).astype(F32)
+        found = []
+        at = 0
+        for g in some:
+            height, cols = g.shape[0] // n, g.shape[1]
+            count = -(-cols // LANES)
+            piece = mine[at : at + count * height].reshape(count, height, LANES).transpose(1, 0, 2).reshape(height, count * LANES)
+            found.append(piece[:, :cols])
+            at += count * height
+        return found
+
+    final = reduce_grads(grads[:6]) + reduce_grads(grads[6:])
     return (output, grad_tokens, *final)
 
 

time: 1470 us -> 1140 us (0.78)
  waiting for transfers between devices: 646 us -> 378 us
  Pallas kernels: 0 us -> 133 us
  matrix products: 447 us -> 326 us
  other arithmetic: 136 us -> 85.5 us
    ppermute x12 -> x4, waiting for transfers between devices: 232 us -> 23.2 us  [spread(): rows.append([lax.ppermute(h, 'fsdp', turn) for h in rows[-1]])]
    pallas_call x0 -> x3, Pallas kernels: none -> 133 us  [the longest x1 54.4 us: gather_now(): pl.pallas_call(functools.partial(gather_kernel, n, count), in_specs=[pl.B...]
    dot_general x113 -> x107, matrix products: 447 us -> 326 us  [dot(): lax.dot_general(left, right, (dims, ((), ())), preferred_element_type=F32...]
    convert_element_type x3, other arithmetic: 46.1 us -> 3.71 us  [the longest x1 1.33 us: on_device(): far_back = lax.ppermute(jnp.concatenate([dkey_far, dvalue_far], axis=1),...]
    ppermute x9 -> x3, waiting for transfers between devices: 277 us -> 238 us  [spread(): lax.ppermute(held[-1], 'fsdp', [(i, (i + inner) % n) for i in range(n)])]
    dynamic_update_slice x16 -> x0, local copies, waits for them, and re-layouts: 20.3 us -> none  [gathered(): whole = lax.dynamic_update_index_in_dim(whole, part, owner, 0)]
    reduce_sum x2 -> x1, other arithmetic: 18.2 us -> 0.1 us  [on_device(): chosen = jnp.sum(picked * adapter_of_doc[0][None, :], axis=1)]
    reduce_scatter x1 -> x2, waiting for transfers between devices: 91.1 us -> 74.7 us  [reduce_grads(): mine = lax.psum_scatter(flat, 'fsdp', scatter_dimension=0, tiled=False)]
  transfers between devices with their start and end apart: 28 -> 18, of which waited for: 16 -> 11; matrix products, arithmetic and copies ran while one was open for 28% -> 25% of each run, Pallas kernels for 0% -> 3%
where the time goes in v2:
time: 1140 us; the launch traced here: 1130 us
  waiting for transfers between devices  378 us (33%)
  matrix products  326 us (29%)
  local copies, waits for them, and re-layouts  176 us (15%)
  Pallas kernels  133 us (12%)
  other arithmetic  85.5 us (8%)
  between operations  17 us (1%)
  starting transfers between devices  14.1 us (1%)
    dot_general x107, matrix products, dot(): lax.dot_general(left, right, (dims, ((), ())), preferred_element_type=F32...  326 us
    ppermute x3, waiting for transfers between devices, spread(): lax.ppermute(held[-1], 'fsdp', [(i, (i + inner) % n) for i in range(n)])  238 us
    unnamed x550, local copies, waits for them, and re-layouts  77.8 us
    reduce_scatter x2, waiting for transfers between devices, reduce_grads(): mine = lax.psum_scatter(flat, 'fsdp', scatter_dimension=0, tiled=False)  74.7 us
    pallas_call x1, Pallas kernels, gather_now(): pl.pallas_call(functools.partial(gather_kernel, n, count), in_specs=[pl.B...  54.4 us
    pallas_call x1, Pallas kernels, attend_back(): pl.pallas_call(functools.partial(attend_back_kernel, group, q_blocks), gr...  43.9 us
    pallas_call x1, Pallas kernels, attend(): pl.pallas_call(functools.partial(attend_kernel, group, q_blocks), grid=(p...  34.8 us
    squeeze x8, local copies, waits for them, and re-layouts, on_device(): w_gu = part[j][:, :2 * ff_width]  32.7 us
  transfers between devices with their start and end apart: 18, of which 11 were waited for; matrix products, arithmetic and copies ran while one was open for 25% of the time, Pallas kernels for 3%

profile of v2, /device:TPU:0, one launch (start us, length us, event | category | flops | bytes accessed | tf_op | source)
XLA Modules:
  0.0 1128.8 jit_solution(13983444597626342776)
XLA Ops:
  38.4 54.4 %shard_map.430 = bf16[8,192,1792]{2,1,0:T(8,128)(2,1)} custom-call(bf16[192,1792]{1,0:T(8,128)(2,1)} %copy-done.123), custom_call_target="tpu_custom_call" | custom-call | tf_op jit(solution)/shard_map/pallas_call | solution.py:318
  109.7 6.9 fusion.9
  120.7 154.0 %collective-permute-done.2 = bf16[2,1536,768]{1,2,0:T(8,128)(2,1)} collective-permute-done((bf16[2,1536,768]{1,2,0:T(8,128)(2,1)}, bf16[2,1536,768]{1,2,0:T(8,128)(2,1)}, u32[]{:S(2)}, u32[]{:S(2)}) %collective-permute-start.2) | collective-permute-done | bytes 4718624 | tf_op jit(solution)/shard_map/ppermute | solution.py:63
  306.6 34.8 %shard_map.431 = (bf16[768,768]{1,0:T(8,128)(2,1)S(1)}, f32[2,8,768]{2,1,0:T(8,128)S(1)}) custom-call(s32[1]{0:T(128)} %bitcast.start_ref, s32[1,768]{1,0:T(1,128)S(1)} %broadcast_in_dim.263.begin_ref, bf16[768,768]{1,0:T(8,128)(2,1)S(1)} %copy.174.q_ref, bf16[768,512]{1,0:T(8,128)(2,1)S(1)} %pad_maximum_fusion.1.ko_ref.vo_ref, ...), custom_call_target="tpu_custom_call" | custom-call | flops 3623878656 | bytes 8388608 | tf_op jit(solution)/shard_map/pallas_call | solution.py:134
  341.4 5.2 slice_bitcast_fusion.12
  351.4 25.2 %collective-permute-done.3 = bf16[2,1536,768]{1,2,0:T(8,128)(2,1)} collective-permute-done((bf16[2,1536,768]{1,2,0:T(8,128)(2,1)}, bf16[2,1536,768]{1,2,0:T(8,128)(2,1)}, u32[]{:S(2)}, u32[]{:S(2)}) %collective-permute-start.3) | collective-permute-done | bytes 4718624 | tf_op jit(solution)/shard_map/ppermute | solution.py:63
  386.4 4.9 slice_bitcast_fusion.5
  418.8 58.7 %collective-permute-done.4 = bf16[2,1536,768]{1,2,0:T(8,128)(2,1)} collective-permute-done((bf16[2,1536,768]{1,2,0:T(8,128)(2,1)}, bf16[2,1536,768]{1,2,0:T(8,128)(2,1)}, u32[]{:S(2)}, u32[]{:S(2)}) %collective-permute-start.4) | collective-permute-done | bytes 4718624 | tf_op jit(solution)/shard_map/ppermute | solution.py:63
  563.6 20.2 %collective-permute-done.8 = bf16[2,1536,768]{1,2,0:T(8,128)(2,1)} collective-permute-done((bf16[2,1536,768]{1,2,0:T(8,128)(2,1)}, bf16[2,1536,768]{1,2,0:T(8,128)(2,1)}, u32[]{:S(2)}, u32[]{:S(2)}) %collective-permute-start.8) | collective-permute-done | bytes 4718624 | tf_op jit(solution)/shard_map/ppermute | solution.py:67
  594.8 5.1 multiply_reduce_fusion.17
  603.0 6.4 add_convert_fusion.6
  609.4 11.9 %add_convert_fusion.5 = (bf16[768,256]{0,1:T(8,128)(2,1)}, bf16[768,256]{0,1:T(8,128)(2,1)}, bf16[768,256]{0,1:T(8,128)(2,1)}, bf16[768,256]{0,1:T(8,128)(2,1)},...) fusion(f32[768,256]{0,1:T(8,128)S(1)} %copy-done.22, ...), kind=kLoop, calls=%fused_computation.303 | loop fusion | flops 47185920 | bytes 46055424 | tf_op jit(solution)/shard_map/convert_element_type | solution.py:510
  621.4 9.7 add_convert_fusion.4
  743.8 28.3 %add_add_fusion.2 = f32[768,1536]{1,0:T(8,128)} fusion(f32[768,1536]{1,0:T(8,128)} %fusion.252, f32[768,1536]{1,0:T(8,128)} %fusion.254, f32[768,1536]{1,0:T(8,128)} %fusion.26, f32[768,1536]{1,0:T(8,128)} %fusion.30, f32[768,1536]{1,0:T(8,128)} %fusion.34, f32[768,1536]{1,0:T(8,128)} %fusion.38, f32[768,1536]{1,0:T(8,128)} %fusion.42, ...), kind=kOutput, calls=%fused_computation.18 | convolution fusion | flops 1229586432 | bytes 87293952 | tf_op jit(solution)/shard_map/dot_general | solution.py:22
  772.3 27.0 %fusion.12 = f32[768,1536]{1,0:T(8,128)} fusion(f32[768,1536]{1,0:T(8,128)} %fusion.243, f32[768,1536]{1,0:T(8,128)} %fusion.185, f32[768,1536]{1,0:T(8,128)} %fusion.188, f32[768,1536]{1,0:T(8,128)} %fusion.191, f32[768,1536]{1,0:T(8,128)} %fusion.194, f32[768,1536]{1,0:T(8,128)} %fusion.197, f32[768,1536]{1,0:T(8,128)} %fusion.200, ...), kind=kOutput, calls=%fused_computation.55 | convolution fusion | flops 625213440 | bytes 81395712 | tf_op jit(solution)/shard_map/dot_general | solution.py:22
  809.9 11.3 %multiply_reduce_fusion = (f32[768]{0:T(1024)S(1)}, f32[768,1536]{1,0:T(8,128)}) fusion(f32[768,1536]{1,0:T(8,128)} %copy-done.10, f32[1536]{0:T(1024)S(1)} %copy-done.210, f32[768,1536]{1,0:T(8,128)} %fusion.248, f32[768,1536]{1,0:T(8,128)} %fusion.250, f32[768,1536]{1,0:T(8,128)} %add_add_fusion.2, f32[768,1536]{1,0:T(8,128)} %collective-permute-done.10), kind=kLoop, calls=%fused_computation.16 | loop fusion | flops 7077120 | bytes 28320768 | tf_op jit(solution)/shard_map/transpose(jvp())/reduce_sum | solution.py:34
  821.2 8.7 fusion
  836.4 43.9 %shard_map.432 = (f32[768,768]{1,0:T(8,128)}, f32[768,256]{1,0:T(8,128)}, f32[768,256]{1,0:T(8,128)}, bf16[768,256]{1,0:T(8,128)(2,1)}, bf16[768,256]{1,0:T(8,128)(2,1)}) custom-call(s32[1]{0:T(128)} %bitcast.start_ref, s32[1,768]{1,0:T(1,128)} %copy-done.4, bf16[768,768]{1,0:T(8,128)(2,1)} %copy-done.2, bf16[768,512]{1,0:T(8,128)(2,1)} %copy-done.3, ...), custom_call_target="tpu_custom_call" | custom-call | flops 9059696640 | bytes 16777216 | tf_op jit(solution)/shard_map/pallas_call | solution.py:205
  898.5 5.7 collective-permute-done.12
  983.7 7.5 fusion.7
  991.4 7.9 collective-permute-done.13
  1001.5 74.7 %reduce-scatter.5.cloned.1.call-done = bf16[1,1360,128]{2,1,0:T(8,128)(2,1)} async-done(((bf16[8,1360,128]{2,1,0:T(8,128)(2,1)}), bf16[1,1360,128]{2,1,0:T(8,128)(2,1)}) %reduce-scatter.5.cloned.1.call-update) | async-done | bytes 348176 | tf_op jit(solution)/shard_map/reduce_scatter | solution.py:591
  1076.2 7.3 fusion.2
  1083.5 27.0 %all-reduce.9.cloned.1.call-done = (bf16[896,128]{1,0:T(8,128)(2,1)}, bf16[1360,128]{1,0:T(8,128)(2,1)}) async-done(((bf16[896,128]{1,0:T(8,128)(2,1)}, bf16[1360,128]{1,0:T(8,128)(2,1)}), (bf16[896,128]{1,0:T(8,128)(2,1)}, bf16[1360,128]{1,0:T(8,128)(2,1)})) %all-reduce.9.cloned.1.call-update) | async-done | bytes 577552 | tf_op jit(solution)/shard_map/psum | solution.py:592
  (805 shorter events, 465.1 us)
Async XLA Ops:
  7.2 384.0 %all-gather.3.cloned.1.call-start = ((), (), s32[]{:S(2)}) async-start(), calls=%async_computation.4 | async-start | bytes 6193152 | tf_op jit(solution)/shard_map/all_gather | solution.py:386
  38.4 54.4 %copy-start.119 = (bf16[2,1536,256]{2,1,0:T(8,128)(2,1)S(1)}, bf16[2,1536,256]{2,1,0:T(8,128)(2,1)}, u32[]{:S(2)}) copy-start(bf16[2,1536,256]{2,1,0:T(8,128)(2,1)} %param.43) | copy-start | bytes 4718596
  105.5 169.1 %collective-permute-start.2 = (bf16[2,1536,768]{1,2,0:T(8,128)(2,1)}, bf16[2,1536,768]{1,2,0:T(8,128)(2,1)}, u32[]{:S(2)}, u32[]{:S(2)}) collective-permute-start(bf16[2,1536,768]{1,2,0:T(8,128)(2,1)} %pad_maximum_fusion), channel_id=1, source_target_pairs={{0,8},{4,12},{8,16},{12,20},{16,24},{20,28},{24,0},{28,4},{1,9},{5... | collective-permute-start | bytes 14155784 | tf_op jit(solution)/shard_map/ppermute | solution.py:63
  106.4 895.0 %reduce-scatter.3.cloned.1.call-start = ((), (), s32[]{:S(2)}) async-start(), calls=%async_computation.2 | async-start | bytes 2064384 | tf_op jit(solution)/shard_map/reduce_scatter | solution.py:591
  106.4 240.2 %collective-permute-start.5 = (bf16[2,1536,768]{1,2,0:T(8,128)(2,1)}, bf16[2,1536,768]{1,2,0:T(8,128)(2,1)}, u32[]{:S(2)}, u32[]{:S(2)}) collective-permute-start(bf16[2,1536,768]{1,2,0:T(8,128)(2,1)} %pad_maximum_fusion), channel_id=1, source_target_pairs={{0,4},{4,0},{8,12},{12,8},{16,20},{20,16},{24,28},{28,24},{1,5},{5... | collective-permute-start | bytes 14155784 | tf_op jit(solution)/shard_map/ppermute | solution.py:67
  120.7 168.9 %copy-start.109 = (f32[768,32]{0,1:T(8,128)}, f32[768,32]{0,1:T(8,128)S(1)}, u32[]{:S(2)}) copy-start(f32[768,32]{0,1:T(8,128)S(1)} %get-tuple-element.230) | copy-start | bytes 294916
  274.7 102.0 %collective-permute-start.3 = (bf16[2,1536,768]{1,2,0:T(8,128)(2,1)}, bf16[2,1536,768]{1,2,0:T(8,128)(2,1)}, u32[]{:S(2)}, u32[]{:S(2)}) collective-permute-start(bf16[2,1536,768]{1,2,0:T(8,128)(2,1)} %collective-permute-done.2), channel_id=1, source_target_pairs={{0,8},{4,12},{8,16},{12,20},{16,24},{20,28},{24,0},{28,4},{1,9},{5... | collective-permute-start | bytes 14155784 | tf_op jit(solution)/shard_map/ppermute | solution.py:63
  277.3 27.2 %collective-permute-start = (bf16[768,512]{1,0:T(8,128)(2,1)S(1)}, bf16[768,512]{1,0:T(8,128)(2,1)S(1)}, u32[]{:S(2)}, u32[]{:S(2)}) collective-permute-start(bf16[768,512]{1,0:T(8,128)(2,1)S(1)} %pad_maximum_fusion.1.ko_ref.vo_ref), channel_id=1, source_target_pairs={{0,2},{1,3},{4,6},{5,7},{8,10},{9,11},{12,14},{13,15},{16,18},{17,... | collective-permute-start | bytes 2359304 | tf_op jit(solution)/shard_map/ppermute | solution.py:451
  281.2 105.1 %collective-permute-start.6 = (bf16[2,1536,768]{1,2,0:T(8,128)(2,1)}, bf16[2,1536,768]{1,2,0:T(8,128)(2,1)}, u32[]{:S(2)}, u32[]{:S(2)}) collective-permute-start(bf16[2,1536,768]{1,2,0:T(8,128)(2,1)} %collective-permute-done.2), channel_id=1, source_target_pairs={{0,4},{4,0},{8,12},{12,8},{16,20},{20,16},{24,28},{28,24},{1,5},{5... | collective-permute-start | bytes 14155784 | tf_op jit(solution)/shard_map/ppermute | solution.py:67
  341.4 60.3 %copy-start = (bf16[768,768]{1,0:T(8,128)(2,1)}, bf16[768,768]{1,0:T(8,128)(2,1)S(1)}, u32[]{:S(2)}) copy-start(bf16[768,768]{1,0:T(8,128)(2,1)S(1)} %get-tuple-element.29.o_ref) | copy-start | bytes 3538948
  376.6 100.9 %collective-permute-start.4 = (bf16[2,1536,768]{1,2,0:T(8,128)(2,1)}, bf16[2,1536,768]{1,2,0:T(8,128)(2,1)}, u32[]{:S(2)}, u32[]{:S(2)}) collective-permute-start(bf16[2,1536,768]{1,2,0:T(8,128)(2,1)} %collective-permute-done.3), channel_id=1, source_target_pairs={{0,8},{4,12},{8,16},{12,20},{16,24},{20,28},{24,0},{28,4},{1,9},{5... | collective-permute-start | bytes 14155784 | tf_op jit(solution)/shard_map/ppermute | solution.py:63
  376.6 110.8 %collective-permute-start.7 = (bf16[2,1536,768]{1,2,0:T(8,128)(2,1)}, bf16[2,1536,768]{1,2,0:T(8,128)(2,1)}, u32[]{:S(2)}, u32[]{:S(2)}) collective-permute-start(bf16[2,1536,768]{1,2,0:T(8,128)(2,1)} %collective-permute-done.3), channel_id=1, source_target_pairs={{0,4},{4,0},{8,12},{12,8},{16,20},{20,16},{24,28},{28,24},{1,5},{5... | collective-permute-start | bytes 14155784 | tf_op jit(solution)/shard_map/ppermute | solution.py:67
  403.8 90.6 %collective-permute-start.1 = (f32[768,1536]{1,0:T(8,128)S(1)}, f32[768,1536]{1,0:T(8,128)}, u32[]{:S(2)}, u32[]{:S(2)}) collective-permute-start(f32[768,1536]{1,0:T(8,128)S(1)} %convolution_add_fusion), channel_id=1, source_target_pairs={{0,1},{1,0},{2,3},{3,2},{4,5},{5,4},{6,7},{7,6},{8,9},{9,8},{10,11... | collective-permute-start | bytes 14155784 | tf_op jit(solution)/shard_map/ppermute | solution.py:335
  477.5 106.3 %collective-permute-start.8 = (bf16[2,1536,768]{1,2,0:T(8,128)(2,1)}, bf16[2,1536,768]{1,2,0:T(8,128)(2,1)}, u32[]{:S(2)}, u32[]{:S(2)}) collective-permute-start(bf16[2,1536,768]{1,2,0:T(8,128)(2,1)} %collective-permute-done.4), channel_id=1, source_target_pairs={{0,4},{4,0},{8,12},{12,8},{16,20},{20,16},{24,28},{28,24},{1,5},{5... | collective-permute-start | bytes 14155784 | tf_op jit(solution)/shard_map/ppermute | solution.py:67
  600.2 1.3 collective-permute-start.11
  680.9 55.0 %copy-start.131 = (bf16[768,128]{1,0:T(8,128)(2,1)}, bf16[768,128]{1,0:T(8,128)(2,1)S(1)}, u32[]{:S(2)}) copy-start(bf16[768,128]{1,0:T(8,128)(2,1)S(1)} %fusion.107) | copy-start | bytes 589828
  681.2 58.5 %copy-start.129 = (bf16[768,128]{1,0:T(8,128)(2,1)}, bf16[768,128]{1,0:T(8,128)(2,1)S(1)}, u32[]{:S(2)}) copy-start(bf16[768,128]{1,0:T(8,128)(2,1)S(1)} %fusion.108) | copy-start | bytes 589828
  772.1 37.8 %collective-permute-start.10 = (f32[768,1536]{1,0:T(8,128)}, f32[768,1536]{1,0:T(8,128)}, u32[]{:S(2)}, u32[]{:S(2)}) collective-permute-start(f32[768,1536]{1,0:T(8,128)} %add_add_fusion.2), channel_id=1, source_target_pairs={{0,1},{1,0},{2,3},{3,2},{4,5},{5,4},{6,7},{7,6},{8,9},{9,8},{10,11... | collective-permute-start | bytes 14155784 | tf_op jit(solution)/shard_map/ppermute | solution.py:335
  799.3 21.8 %collective-permute-start.9 = (f32[768,1536]{1,0:T(8,128)}, f32[768,1536]{1,0:T(8,128)}, u32[]{:S(2)}, u32[]{:S(2)}) collective-permute-start(f32[768,1536]{1,0:T(8,128)} %fusion.12), channel_id=1, source_target_pairs={{0,1},{1,0},{2,3},{3,2},{4,5},{5,4},{6,7},{7,6},{8,9},{9,8},{10,11... | collective-permute-start | bytes 14155784 | tf_op jit(solution)/shard_map/ppermute | solution.py:335
  882.3 21.8 %collective-permute-start.12 = (bf16[768,512]{1,0:T(8,128)(2,1)}, bf16[768,512]{1,0:T(8,128)(2,1)}, u32[]{:S(2)}, u32[]{:S(2)}) collective-permute-start(bf16[768,512]{1,0:T(8,128)(2,1)} %pad_maximum_fusion.2), channel_id=1, source_target_pairs={{2,0},{3,1},{6,4},{7,5},{10,8},{11,9},{14,12},{15,13},{18,16},{19,... | collective-permute-start | bytes 2359304 | tf_op jit(solution)/shard_map/ppermute | solution.py:535
  932.5 143.7 %reduce-scatter.5.cloned.1.call-start = ((), (), s32[]{:S(2)}) async-start(), calls=%async_computation.3 | async-start | bytes 3133440 | tf_op jit(solution)/shard_map/reduce_scatter | solution.py:591
  978.9 131.6 %all-reduce.9.cloned.1.call-start = ((), (), s32[]{:S(2)}) async-start(), calls=%async_computation.5 | async-start | bytes 1155072 | tf_op jit(solution)/shard_map/psum | solution.py:592
  991.3 84.9 %copy-start.215 = (f32[768]{0:T(1024)S(1)}, f32[768]{0:T(1024)}, u32[]{:S(2)}) copy-start(f32[768]{0:T(1024)} %copy-done.214) | copy-start | bytes 9220
  991.3 8.0 collective-permute-start.13
  (228 other events, 1347.9 us)
Sparse Core Ops, SparseCore 0:
  106.5 156.2 all-gather.2
  932.6 66.7 reduce-scatter.2
  1003.3 72.7 reduce-scatter.4
  1078.6 31.9 all-reduce.8

commit v3 on v2

--- a/solution.py
+++ b/solution.py
@@ -52,33 +52,6 @@
 def levels(n):
     outer = 4 if n % 4 == 0 else n
     return outer, n // outer
-
-
-def spread(block):
-    n = lax.axis_size("fsdp")
-    outer, inner = levels(n)
-    me = lax.axis_index("fsdp")
-    held = [block]
-    for unused in range(outer - 1):
-        held.append(lax.ppermute(held[-1], "fsdp", [(i, (i + inner) % n) for i in range(n)]))
-    rows = [held]
-    turn = [(i, i // inner * inner + (i % inner + 1) % inner) for i in range(n)]
-    for unused in range(inner - 1):
-        rows.append([lax.ppermute(h, "fsdp", turn) for h in rows[-1]])
-    found = []
-    for dj, row in enumerate(rows):
-        for do, part in enumerate(row):
-            owner = (me // inner - do + outer) % outer * inner + (me % inner - dj + inner) % inner
-            found.append((owner, part))
-    return found
-
-
-def gathered(block):
-    n = lax.axis_size("fsdp")
-    whole = jnp.zeros((n,) + block.shape, block.dtype)
-    for owner, part in spread(block):
-        whole = lax.dynamic_update_index_in_dim(whole, part, owner, 0)
-    return whole
 
 
 def fill_bias(bias, start_ref, begin_ref, rows):
@@ -217,18 +190,155 @@
     )(start, begin, q, kv, kv, far, far, o, do, lse)
 
 
-def gather_kernel(n, count, *refs):
-    ins, outs = refs[:count], refs[count : 2 * count]
-    own_sem, z_send, z_recv, y_send, y_recv, x_send, x_recv = refs[2 * count :]
+def slab_of(rows, ctx):
+    edge = 3 * rows // 8 // 16 * 16
+    take = rows - edge
+    return pl.ds(pl.multiple_of(ctx * edge, 16), take), pl.ds(pl.multiple_of(ctx * take, 16), edge)
+
+
+def gather_kernel(n, layout, *refs):
+    total = sum(len(parts) for parts in layout)
+    count = len(layout)
+    ins, outs = refs[:total], refs[total : total + count]
+    own_sem, z_send, z_recv, y_send, y_recv, x_send, x_recv = refs[total + count :]
+    outer, inner = levels(n)
+    me = lax.axis_index("fsdp")
+    ctx = lax.axis_index("ctx")
+    tp = lax.axis_index("tp")
+    z, y = me // inner, me % inner
+    right = (z + 1) % outer * inner + y
+    left = (z + outer - 1) % outer * inner + y
+
+    def shard(do, dj):
+        return (z + outer - do) % outer * inner + (y + inner - dj) % inner
+
+    own = []
+    at = 0
+    for a, parts in enumerate(layout):
+        col = 0
+        for cols, split in parts:
+            src = ins[at].at[:, pl.ds(pl.multiple_of(tp * cols, LANES), cols)] if split else ins[at]
+            own.append(pltpu.make_async_copy(src, outs[a].at[me, :, pl.ds(col, cols)], own_sem.at[at]))
+            own[-1].start()
+            col += cols
+            at += 1
+
+    barrier = pltpu.get_barrier_semaphore()
+    peers = [right, left] + [z * inner + (y + dj) % inner for dj in range(1, inner)]
+    for peer in peers:
+        pl.semaphore_signal(barrier, inc=1, device_id={"fsdp": peer}, device_id_type=MESH)
+    pl.semaphore_signal(barrier, inc=1, device_id={"ctx": 1 - ctx}, device_id_type=MESH)
+    pl.semaphore_wait(barrier, len(peers) + 1)
+
+    def cut(a):
+        return 3 * outs[a].shape[1] // 8 >= 16
+
+    def taken(a, k):
+        if not cut(a):
+            return outs[a].at[k]
+        return outs[a].at[k, slab_of(outs[a].shape[1], ctx)[0]]
+
+    def remote(part, send, recv, to):
+        return pltpu.make_async_remote_copy(src_ref=part, dst_ref=part, send_sem=send, recv_sem=recv, device_id=to, device_id_type=MESH)
+
+    def z_copy(a, k):
+        return remote(taken(a, shard(k - 1, 0)), z_send.at[a, k - 1], z_recv.at[a, k - 1], {"fsdp": right})
+
+    def y_copy(a, do, dj):
+        to = {"fsdp": z * inner + (y + dj) % inner}
+        return remote(taken(a, shard(do, 0)), y_send.at[a, do, dj - 1], y_recv.at[a, do, dj - 1], to)
+
+    def x_copy(a, do, dj):
+        part = outs[a].at[shard(do, dj), slab_of(outs[a].shape[1], ctx)[1]]
+        return remote(part, x_send.at[a, do, dj], x_recv.at[a, do, dj], {"ctx": 1 - ctx})
+
+    started = []
+
+    def go(copy):
+        copy.start()
+        started.append(copy)
+
+    for c in own:
+        c.wait()
+    for a in range(count):
+        go(z_copy(a, 1))
+        for dj in range(1, inner):
+            go(y_copy(a, 0, dj))
+    for do in range(1, outer + 1):
+        for a in range(count):
+            if do < outer:
+                z_copy(a, do).wait_recv()
+                if do + 1 < outer:
+                    go(z_copy(a, do + 1))
+                for dj in range(1, inner):
+                    go(y_copy(a, do, dj))
+                if cut(a):
+                    go(x_copy(a, do, 0))
+        for a in range(count):
+            for dj in range(1, inner):
+                y_copy(a, do - 1, dj).wait_recv()
+                if cut(a):
+                    go(x_copy(a, do - 1, dj))
+    for a in range(count):
+        if cut(a):
+            for do in range(outer):
+                for dj in range(inner):
+                    if do or dj:
+                        x_copy(a, do, dj).wait_recv()
+    for c in started:
+        c.wait_send()
+
+
+def gather_packs(packs, collective_id):
+    n = lax.axis_size("fsdp")
+    outer, inner = levels(n)
+    count = len(packs)
+    layout = [[(cols, cols != a.shape[1]) for a, cols in parts] for parts in packs]
+    arrays = [a for parts in packs for a, cols in parts]
+    dma = pltpu.SemaphoreType.DMA
+    anywhere = pl.BlockSpec(memory_space=pl.ANY)
+    side = max(inner - 1, 1)
+    return pl.pallas_call(
+        functools.partial(gather_kernel, n, layout),
+        in_specs=[anywhere] * len(arrays),
+        out_specs=[anywhere] * count,
+        out_shape=[jax.ShapeDtypeStruct((n, parts[0][0].shape[0], sum(cols for a, cols in parts)), BF) for parts in packs],
+        scratch_shapes=[
+            dma((len(arrays),)), dma((count, outer - 1)), dma((count, outer - 1)),
+            dma((count, outer, side)), dma((count, outer, side)), dma((count, outer, inner)), dma((count, outer, inner)),
+        ],
+        compiler_params=pltpu.CompilerParams(collective_id=collective_id, has_side_effects=True),
+    )(*arrays)
+
+
+def moe_kernel(n, n2_ref, c_ref, gl_ref, ul_ref, al_ref, gates_ref, *refs):
+    own, near, side = refs[0:3], refs[3:6], refs[6:9]
+    moe_ref, dn2_ref, as_ref, gs_ref, us_ref, dgate_ref = refs[9:15]
+    bufs = refs[15:18]
+    wg, wu, wd, load_sem, z_send, z_recv, y_send, y_recv, x_send, x_recv = refs[18:]
     outer, inner = levels(n)
     me = lax.axis_index("fsdp")
     ctx = lax.axis_index("ctx")
     z, y = me // inner, me % inner
     right = (z + 1) % outer * inner + y
     left = (z + outer - 1) % outer * inner + y
+    local = own[0].shape[0]
+    rows = n2_ref.shape[0]
+    experts = gates_ref.shape[1]
+    chunks = [(j, a) for j in range(local) for a in range(3)]
 
     def shard(do, dj):
         return (z + outer - do) % outer * inner + (y + inner - dj) % inner
+
+    def held(do, dj):
+        if (do, dj) == (0, 0):
+            return own
+        if (do, dj) == (1, 0):
+            return near
+        if (do, dj) == (0, 1):
+            return side
+        at = shard(do, dj)
+        return [b.at[at] for b in bufs]
 
     barrier = pltpu.get_barrier_semaphore()
     peers = [right, left] + [z * inner + (y + dj) % inner for dj in range(1, inner)]
@@ -237,38 +347,30 @@
     pl.semaphore_signal(barrier, inc=1, device_id={"ctx": 1 - ctx}, device_id_type=MESH)
     pl.semaphore_wait(barrier, len(peers) + 1)
 
-    def slab(a):
-        third = ins[a].shape[0] // 3
-        if third % 16:
-            return pl.ds(0, ins[a].shape[0])
-        return pl.ds(pl.multiple_of(ctx * third, 16), 2 * third)
-
-    def tricked(a):
-        return ins[a].shape[0] // 3 % 16 == 0
-
-    def block(a, k, rows):
-        return ins[a].at[rows] if k is None else outs[a].at[k, rows]
-
-    def z_copy(a, k):
-        src = shard(k - 1, 0)
+    def remote(src, dst, send, recv, to):
         return pltpu.make_async_remote_copy(
-            src_ref=block(a, None if k == 1 else src, slab(a)), dst_ref=outs[a].at[src, slab(a)],
-            send_sem=z_send.at[a, k - 1], recv_sem=z_recv.at[a, k - 1], device_id={"fsdp": right}, device_id_type=MESH)
-
-    def y_copy(a, do, dj):
-        src = shard(do, 0)
-        return pltpu.make_async_remote_copy(
-            src_ref=block(a, None if do == 0 else src, slab(a)), dst_ref=outs[a].at[src, slab(a)],
-            send_sem=y_send.at[a, do, dj - 1], recv_sem=y_recv.at[a, do, dj - 1],
-            device_id={"fsdp": z * inner + (y + dj) % inner}, device_id_type=MESH)
-
-    def x_copy(a, do, dj):
-        src = shard(do, dj)
-        third = ins[a].shape[0] // 3
-        rows = pl.ds(pl.multiple_of(ctx * 2 * third, 16), third)
-        return pltpu.make_async_remote_copy(
-            src_ref=outs[a].at[src, rows], dst_ref=outs[a].at[src, rows],
-            send_sem=x_send.at[a, do, dj], recv_sem=x_recv.at[a, do, dj], device_id={"ctx": 1 - ctx}, device_id_type=MESH)
+            src_ref=src, dst_ref=dst, send_sem=send, recv_sem=recv, device_id=to, device_id_type=MESH
+        )
+
+    def z_copy(do, i):
+        j, a = chunks[i]
+        take, unused = slab_of(own[a].shape[1], ctx)
+        at = shard(do - 1, 0)
+        return remote(held(do - 1, 0)[a].at[j, take], bufs[a].at[at, j, take], z_send.at[do, i], z_recv.at[do, i], {"fsdp": right})
+
+    def y_copy(do, dj, i):
+        j, a = chunks[i]
+        take, unused = slab_of(own[a].shape[1], ctx)
+        at = shard(do, 0)
+        to = {"fsdp": z * inner + (y + dj) % inner}
+        return remote(held(do, 0)[a].at[j, take], bufs[a].at[at, j, take], y_send.at[do, dj, i], y_recv.at[do, dj, i], to)
+
+    def x_copy(do, dj, i):
+        j, a = chunks[i]
+        unused, edge = slab_of(own[a].shape[1], ctx)
+        at = shard(do, dj)
+        part = bufs[a].at[at, j, edge]
+        return remote(part, part, x_send.at[do, dj, i], x_recv.at[do, dj, i], {"ctx": 1 - ctx})
 
     started = []
 
@@ -276,70 +378,142 @@
         copy.start()
         started.append(copy)
 
-    own = [pltpu.make_async_copy(ins[a], outs[a].at[me], own_sem.at[a]) for a in range(count)]
-    for a in range(count):
-        go(z_copy(a, 1))
+    for ref in (moe_ref, dn2_ref, as_ref, gs_ref, us_ref, dgate_ref):
+        ref[...] = jnp.zeros_like(ref)
+
+    step = rows // 3
+
+    def compute(do, dj, j, slot):
+        e = shard(do, dj) * local + j
+
+        def block(b, carry):
+            at = pl.ds(pl.multiple_of(b * step, step), step)
+            xb = n2_ref[at, :]
+            cb = c_ref[at, :]
+            gv = dot(xb, wg[slot]) + gl_ref[at, :]
+            uv = dot(xb, wu[slot]) + ul_ref[at, :]
+            back = dot_t(cb, wd[slot]) + al_ref[at, :]
+            hit = lax.broadcasted_iota(jnp.int32, (step, experts), 1) == e
+            gate = jnp.sum(jnp.where(hit, gates_ref[at, :], 0.0), axis=1, keepdims=True)
+            sig = 1.0 / (1.0 + jnp.exp(-gv))
+            silu = gv * sig
+            act = silu * uv
+            col = jnp.sum(act * back, axis=1, keepdims=True)
+            dgate_ref[at, :] += jnp.where(hit, col, 0.0)
+            back = back * gate
+            act = (act * gate).astype(BF)
+            du = back * silu
+            dg = back * uv * (sig + silu * (1.0 - sig))
+            as_ref[at, :] += act.astype(F32)
+            gs_ref[at, :] += dg
+            us_ref[at, :] += du
+            moe_ref[at, :] += dot(act, wd[slot])
+            dn2_ref[at, :] += dot_t(dg.astype(BF), wg[slot]) + dot_t(du.astype(BF), wu[slot])
+            return carry
+
+        lax.fori_loop(0, 3, block, 0)
+
+    queue = []
+
+    def load(do, dj, j, slot):
+        found = []
+        for a, dst in enumerate((wg, wu, wd)):
+            copy = pltpu.make_async_copy(held(do, dj)[a].at[j], dst.at[slot], load_sem.at[slot, a])
+            copy.start()
+            found.append(copy)
+        return found
+
+    pending = []
+    turn = [0]
+
+    def run_next():
+        do, dj, j, slot, copies = pending.pop(0)
+        for c in copies:
+            c.wait()
+        compute(do, dj, j, slot)
+
+    def feed(do, dj, j):
+        if len(pending) == 2:
+            run_next()
+        slot = turn[0] % 2
+        turn[0] += 1
+        pending.append((do, dj, j, slot, load(do, dj, j, slot)))
+
+    def arrived(do, dj, j):
+        for i, (jj, a) in enumerate(chunks):
+            if jj == j:
+                x_copy(do, dj, i).wait_recv()
+
+    for i in range(len(chunks)):
+        go(z_copy(2, i))
         for dj in range(1, inner):
-            go(y_copy(a, 0, dj))
-    for c in own:
-        c.start()
-    for do in range(1, outer + 1):
-        if do < outer:
-            for a in range(count):
-                z_copy(a, do).wait_recv()
-                if do + 1 < outer:
-                    go(z_copy(a, do + 1))
+            go(y_copy(1, dj, i))
+        for dj in range(2, inner):
+            go(y_copy(0, dj, i))
+
+    ready = [(do, dj, j) for do, dj in ((0, 0), (1, 0), (0, 1)) for j in range(local)]
+    for r in range(outer - 1):
+        later = []
+        for i, (j, a) in enumerate(chunks):
+            if ready:
+                do, dj, jj = ready.pop(0)
+                if (do, dj) not in ((0, 0), (1, 0), (0, 1)):
+                    arrived(do, dj, jj)
+                feed(do, dj, jj)
+            if r + 2 < outer:
+                z_copy(r + 2, i).wait_recv()
+                if r + 3 < outer:
+                    go(z_copy(r + 3, i))
                 for dj in range(1, inner):
-                    go(y_copy(a, do, dj))
-                if tricked(a):
-                    go(x_copy(a, do, 0))
-        for a in range(count):
-            for dj in range(1, inner):
-                y_copy(a, do - 1, dj).wait_recv()
-                if tricked(a):
-                    go(x_copy(a, do - 1, dj))
-    for a in range(count):
-        if tricked(a):
-            for do in range(outer):
-                for dj in range(inner):
-                    if do or dj:
-                        x_copy(a, do, dj).wait_recv()
+                    go(y_copy(r + 2, dj, i))
+                go(x_copy(r + 2, 0, i))
+                if a == 2:
+                    later.append((r + 2, 0, j))
+            for do, dj in [(r + 1, dj) for dj in range(1, inner)] + ([(0, dj) for dj in range(2, inner)] if r == 0 else []):
+                y_copy(do, dj, i).wait_recv()
+                go(x_copy(do, dj, i))
+                if a == 2:
+                    later.append((do, dj, j))
+        ready = ready + later
+    for do, dj, j in ready:
+        arrived(do, dj, j)
+        feed(do, dj, j)
+    while pending:
+        run_next()
     for c in started:
         c.wait_send()
-    for c in own:
-        c.wait()
-
-
-def gather_now(arrays, collective_id):
+
+
+def moe_all(n2, cot, gate_low, up_low, act_low, gates, own, near, side, collective_id):
     n = lax.axis_size("fsdp")
     outer, inner = levels(n)
-    count = len(arrays)
+    rows, width = n2.shape
+    ff = gate_low.shape[1]
+    count = 3 * own[0].shape[0]
     dma = pltpu.SemaphoreType.DMA
-    return pl.pallas_call(
-        functools.partial(gather_kernel, n, count),
-        in_specs=[pl.BlockSpec(memory_space=pl.ANY)] * count,
-        out_specs=[pl.BlockSpec(memory_space=pl.ANY)] * count,
-        out_shape=[jax.ShapeDtypeStruct((n,) + a.shape, a.dtype) for a in arrays],
+    sd = jax.ShapeDtypeStruct
+    vm = pl.BlockSpec(memory_space=pltpu.VMEM)
+    anywhere = pl.BlockSpec(memory_space=pl.ANY)
+    outs = pl.pallas_call(
+        functools.partial(moe_kernel, n),
+        in_specs=[vm] * 6 + [anywhere] * 9,
+        out_specs=[vm] * 6 + [anywhere] * 3,
+        out_shape=[sd((rows, width), F32), sd((rows, width), F32), sd((rows, ff), F32), sd((rows, ff), F32), sd((rows, ff), F32), sd(gates.shape, F32)]
+        + [sd((n,) + a.shape, a.dtype) for a in own],
         scratch_shapes=[
-            dma((count,)), dma((count, outer - 1)), dma((count, outer - 1)),
-            dma((count, outer, max(inner - 1, 1))), dma((count, outer, max(inner - 1, 1))),
-            dma((count, outer, inner)), dma((count, outer, inner)),
+            pltpu.VMEM((2, width, ff), BF), pltpu.VMEM((2, width, ff), BF), pltpu.VMEM((2, ff, width), BF), dma((2, 3)),
+            dma((outer, count)), dma((outer, count)), dma((outer, inner, count)), dma((outer, inner, count)),
+            dma((outer, inner, count)), dma((outer, inner, count)),
         ],
-        compiler_params=pltpu.CompilerParams(collective_id=collective_id, has_side_effects=True),
-    )(*arrays)
+        compiler_params=pltpu.CompilerParams(collective_id=collective_id, has_side_effects=True, vmem_limit_bytes=56 << 20),
+    )(n2, cot, gate_low, up_low, act_low, gates, *own, *near, *side)
+    return outs[:6]
 
 
 def tp_sum(value):
     if lax.axis_size("tp") != 2:
         return lax.psum(value, "tp")
     return value + lax.ppermute(value, "tp", [(0, 1), (1, 0)])
-
-
-def tiles(matrix):
-    rows, cols = matrix.shape
-    if cols % LANES:
-        matrix = jnp.pad(matrix, ((0, 0), (0, LANES - cols % LANES)))
-    return [matrix[:, i : i + LANES] for i in range(0, matrix.shape[1], LANES)]
 
 
 def on_device(
@@ -363,58 +537,18 @@
     share = w_query.shape[0]
     low_rows = b_query.shape[0]
 
-    def tp_cols(matrix, size):
-        return lax.dynamic_slice_in_dim(matrix, tp_at * size, size, 1)
-
-    def packed_low(parts, height):
-        stack = jnp.concatenate(sum([tiles(p) for p in parts], []), axis=0)
-        blocks = -(-stack.shape[0] // height)
-        stack = jnp.pad(stack, ((0, blocks * height - stack.shape[0]), (0, 0)))
-        return [stack[i * height : (i + 1) * height] for i in range(blocks)]
-
-    first_low = [tp_cols(b_query, q_width), tp_cols(key_second_factor, kv_width), tp_cols(value_second_factor, kv_width)]
-    second_low = [tp_cols(b_gate, ff_width), tp_cols(b_up, ff_width), b_out, b_down, b_router]
-    base_one = [w_query, key_matrix, value_matrix, a_query, a_key, a_value]
-    pack_one = jnp.concatenate(base_one + packed_low(first_low, share), axis=1)
-    router_pad = jnp.pad(w_router, ((0, 0), (0, LANES - experts)))
-    base_two = [w_out.T, a_router, a_gate, a_up, router_pad, a_out]
-    pack_two = jnp.concatenate(base_two + packed_low(second_low + [a_down], share), axis=1)
-    expert_block = jnp.concatenate([w_gate, w_up, jnp.swapaxes(w_down, 1, 2)], axis=2)
-
-    (one,) = gather_now([pack_one], 0)
-    one, pack_two, expert_block = lax.optimization_barrier((one, pack_two, expert_block))
-    two = lax.all_gather(pack_two, "fsdp", axis=0, tiled=False)
-    expert_parts = spread(expert_block)
-
-    def unpack_low(whole, col, parts):
-        flat = whole[:, :, col:]
-        flat = flat.reshape(n, share, -1, LANES).transpose(0, 2, 1, 3).reshape(n, -1, LANES)
-        found = []
-        at = 0
-        for height, cols in parts:
-            count = -(-cols // LANES)
-            piece = flat[:, at : at + count * height].reshape(n, count, height, LANES)
-            found.append(piece.transpose(0, 2, 1, 3).reshape(n * height, count * LANES))
-            at += count * height
-        return found
-
+    pad = ((0, 0), (0, LANES - experts))
+    one, low_one = gather_packs(
+        [
+            [(a, a.shape[1]) for a in (w_query, key_matrix, value_matrix, a_query, a_key, a_value)],
+            [(b_query, q_width), (key_second_factor, kv_width), (value_second_factor, kv_width)],
+        ],
+        0,
+    )
+    qkv = q_width + 2 * kv_width
     w_one = one.reshape(n * share, -1)
-    cols_one = q_width + 2 * kv_width + 3 * ranks
-    query_b, key_b, value_b = unpack_low(one, cols_one, [(low_rows, q_width), (low_rows, kv_width), (low_rows, kv_width)])
-    w_two = two.reshape(n * share, -1)
-    cols_two = q_width + 5 * ranks
-    gate_b, up_b, out_b, down_b, router_b, down_a = unpack_low(
-        two,
-        cols_two,
-        [(low_rows, ff_width), (low_rows, ff_width), (low_rows, width), (low_rows, width), (low_rows, experts), (a_down.shape[0], ranks)],
-    )
-    out_wt = w_two[:, :q_width]
-    router_a = w_two[:, q_width : q_width + ranks]
-    gate_a = w_two[:, q_width + ranks : q_width + 2 * ranks]
-    up_a = w_two[:, q_width + 2 * ranks : q_width + 3 * ranks]
-    router_w = w_two[:, q_width + 3 * ranks : q_width + 4 * ranks]
-    out_a = lax.dynamic_slice_in_dim(w_two[:, q_width + 4 * ranks : q_width + 5 * ranks], tp_at * q_width, q_width, 0)
-    down_at = lax.dynamic_slice_in_dim(down_a, tp_at * ff_width, ff_width, 0)
+    low_one = low_one.reshape(n * low_rows, -1)
+    query_b, key_b, value_b = low_one[:, :q_width], low_one[:, q_width : q_width + kv_width], low_one[:, q_width + kv_width :]
 
     ends = jnp.cumsum(lengths[0])
     starts = ends - lengths[0]
@@ -436,8 +570,7 @@
 
     xfull = tokens.astype(F32)
     normed = rms_norm(xfull, attn_gain).astype(BF)
-    raw = dot(normed, w_one[:, :cols_one])
-    qkv = q_width + 2 * kv_width
+    raw = dot(normed, w_one)
     query_u = (raw[:, qkv : qkv + ranks] * mask).astype(BF)
     key_u = (raw[:, qkv + ranks : qkv + 2 * ranks] * mask).astype(BF)
     value_u = (raw[:, qkv + 2 * ranks : qkv + 3 * ranks] * mask).astype(BF)
@@ -448,8 +581,35 @@
         rotary_apply(query_pre.reshape(rows, -1, HEAD_SIZE), cosine_table, sine_table).reshape(rows, q_width).astype(BF)
     )
     key = rotary_apply(key_pre.reshape(rows, -1, HEAD_SIZE), cosine_table, sine_table).reshape(rows, kv_width).astype(BF)
-    far = lax.ppermute(jnp.concatenate([key, value_state], axis=1), "ctx", [(i, i + 1) for i in range(lax.axis_size("ctx") - 1)])
     kv = jnp.concatenate([key, value_state], axis=1)
+    far = lax.ppermute(kv, "ctx", [(i, i + 1) for i in range(lax.axis_size("ctx") - 1)])
+    w_out_t, kv = lax.optimization_barrier((w_out.T, kv))
+    two, low_two, down_a = gather_packs(
+        [
+            [(a, a.shape[1]) for a in (w_out_t, a_router, a_gate, a_up, jnp.pad(w_router, pad), a_out)],
+            [(b_gate, ff_width), (b_up, ff_width), (b_out, width), (b_down, width), (jnp.pad(b_router, pad), LANES)],
+            [(a_down, ranks)],
+        ],
+        1,
+    )
+    near_w = lax.optimization_barrier((w_gate, w_up, w_down, two))[:3]
+    outer, inner = levels(n)
+    ring = [(i, (i + inner) % n) for i in range(n)]
+    turn = [(i, i // inner * inner + (i % inner + 1) % inner) for i in range(n)]
+    near = [lax.ppermute(a, "fsdp", ring) for a in near_w]
+    beside = [lax.ppermute(a, "fsdp", turn) for a in near_w]
+    far, two = lax.optimization_barrier((far, two))
+    w_two = two.reshape(n * share, -1)
+    low_two = low_two.reshape(n * low_rows, -1)
+    gate_b, up_b = low_two[:, :ff_width], low_two[:, ff_width : 2 * ff_width]
+    out_b = low_two[:, 2 * ff_width : 2 * ff_width + width]
+    down_b = low_two[:, 2 * ff_width + width : 2 * ff_width + 2 * width]
+    router_b = low_two[:, 2 * ff_width + 2 * width :]
+    out_wt = w_two[:, :q_width]
+    router_a = w_two[:, q_width : q_width + ranks]
+    router_w = w_two[:, q_width + 3 * ranks : q_width + 4 * ranks]
+    out_a = lax.dynamic_slice_in_dim(w_two[:, q_width + 4 * ranks : q_width + 5 * ranks], tp_at * q_width, q_width, 0)
+    down_at = lax.dynamic_slice_in_dim(down_a.reshape(-1, ranks), tp_at * ff_width, ff_width, 0)
     begin_row = begin_local[None, :]
     start_at = jnp.reshape(start, (1,)).astype(jnp.int32)
     query_state = (query_state.astype(F32) * 0.125).astype(BF)
@@ -472,36 +632,9 @@
     up_low = dot(zin_up, up_b)
     down_back = dot_t(cot, down_b) * mask
     act_low = dot_t(down_back.astype(BF), down_at)
-    moe = jnp.zeros((rows, width), F32)
-    dn2 = jnp.zeros((rows, width), F32)
-    act_sum = jnp.zeros((rows, ff_width), F32)
-    dg_sum = jnp.zeros((rows, ff_width), F32)
-    du_sum = jnp.zeros((rows, ff_width), F32)
-    dgate = jnp.zeros((rows, experts), F32)
-    for owner, part in expert_parts:
-        for j in range(local_experts):
-            e = owner * local_experts + j
-            w_gu = part[j][:, : 2 * ff_width]
-            w_d = part[j][:, 2 * ff_width :]
-            g = lax.dynamic_slice_in_dim(gates, e, 1, 1)
-            pre = dot(normed_two, w_gu)
-            gv = pre[:, :ff_width] + gate_low
-            uv = pre[:, ff_width:] + up_low
-            sig = jax.nn.sigmoid(gv)
-            silu = gv * sig
-            act = silu * uv
-            back = dot(cot, w_d) + act_low
-            col = jnp.sum(act * back, axis=1, keepdims=True)
-            dgate = dgate + jnp.where(jnp.arange(experts)[None, :] == e, col, 0.0)
-            act_g = (act * g).astype(BF)
-            back = back * g
-            dg = (back * uv * sig * (1.0 + gv * (1.0 - sig))).astype(BF)
-            du = (back * silu).astype(BF)
-            moe = moe + dot_t(act_g, w_d)
-            dn2 = dn2 + dot_t(jnp.concatenate([dg, du], axis=1), w_gu)
-            act_sum = act_sum + act_g.astype(F32)
-            dg_sum = dg_sum + dg.astype(F32)
-            du_sum = du_sum + du.astype(F32)
+    moe, dn2, act_sum, dg_sum, du_sum, dgate = moe_all(
+        normed_two, cot, gate_low, up_low, act_low, gates, (w_gate, w_up, w_down), near, beside, 2
+    )
     down_low = (dot(act_sum.astype(BF), down_at) * mask).astype(BF)
     moe = moe + dot(down_low, down_b)
     output = (hidden + tp_sum(moe.astype(BF).astype(F32))).astype(BF)
@@ -513,9 +646,10 @@
     grad_bu = t_dot(zin_up, du_sum)
     gate_du = (dot_t(dg_sum, gate_b) * mask).astype(BF)
     up_du = (dot_t(du_sum, up_b) * mask).astype(BF)
-    dn2 = dn2 + dot_t(gate_du, gate_a) + dot_t(up_du, up_a)
-    grad_ag = t_dot(normed_two, gate_du)
-    grad_au = t_dot(normed_two, up_du)
+    gu_du = jnp.concatenate([gate_du, up_du], axis=1)
+    dn2 = dn2 + dot_t(gu_du, w_two[:, q_width + ranks : q_width + 3 * ranks])
+    grad_agu = t_dot(normed_two, gu_du)
+    grad_ag, grad_au = grad_agu[:, :ranks], grad_agu[:, ranks:]
     dn2, dgate = tp_sum(dn2), tp_sum(dgate)
     dlogits = (gates * (dgate - jnp.sum(gates * dgate, axis=-1, keepdims=True))).astype(BF)
     dlogits = jnp.pad(dlogits, ((0, 0), (0, LANES - experts)))
@@ -545,7 +679,7 @@
     key_du = (dot_t(dkey_pre, key_b) * mask).astype(BF)
     value_du = (dot_t(dvalue, value_b) * mask).astype(BF)
     everything = jnp.concatenate([dquery_pre, dkey_pre, dvalue, query_du, key_du, value_du], axis=1)
-    dn1 = dot_t(everything, w_one[:, :cols_one])
+    dn1 = dot_t(everything, w_one)
     grad_a3 = t_dot(normed, everything[:, qkv:])
     grad_bq = t_dot(query_u, dquery_pre)
     grad_bk = t_dot(key_u, dkey_pre)

time: 1140 us -> 894 us (0.78)
  Pallas kernels: 133 us -> 450 us
  matrix products: 326 us -> 88.5 us
  waiting for transfers between devices: 378 us -> 199 us
  local copies, waits for them, and re-layouts: 176 us -> 81.7 us
  other arithmetic: 85.5 us -> 44.2 us
    pallas_call x1 -> x3, Pallas kernels: 54.4 us -> 372 us  [the longest x1 232 us: moe_all(): pl.pallas_call(functools.partial(moe_kernel, n), in_specs=[vm] * 6 + [any...]
    dot_general x107 -> x41, matrix products: 326 us -> 88.5 us  [dot(): lax.dot_general(left, right, (dims, ((), ())), preferred_element_type=F32...]
    ppermute x8 -> x7, waiting for transfers between devices: 261 us -> 83 us  [the longest x3 83 us: on_device(): near = [lax.ppermute(a, 'fsdp', ring) for a in near_w]]
    unnamed x550 -> x206, local copies, waits for them, and re-layouts: 77.8 us -> 29.5 us
    squeeze x8 -> x0, local copies, waits for them, and re-layouts: 32.7 us -> none  [on_device(): w_gu = part[j][:, :2 * ff_width]]
    convert_element_type x5 -> x1, other arithmetic: 28.1 us -> 3.18 us  [on_device(): output = (hidden + tp_sum(moe.astype(BF).astype(F32))).astype(BF)]
  transfers between devices with their start and end apart: 18 -> 16, of which waited for: 11 -> 8; matrix products, arithmetic and copies ran while one was open for 25% -> 14% of each run, Pallas kernels for 3% -> 7%
where the time goes in v3:
time: 894 us; the launch traced here: 888 us
  Pallas kernels  450 us (50%)
  waiting for transfers between devices  199 us (22%)
  matrix products  88.5 us (10%)
  local copies, waits for them, and re-layouts  81.7 us (9%)
  other arithmetic  44.2 us (5%)
  between operations  15.5 us (2%)
  starting transfers between devices  9.23 us (1%)
    pallas_call x1, Pallas kernels, moe_all(): pl.pallas_call(functools.partial(moe_kernel, n), in_specs=[vm] * 6 + [any...  232 us
    pallas_call x2, Pallas kernels, gather_packs(): pl.pallas_call(functools.partial(gather_kernel, n, layout), in_specs=[any...  140 us
    dot_general x41, matrix products, dot(): lax.dot_general(left, right, (dims, ((), ())), preferred_element_type=F32...  88.5 us
    ppermute x3, waiting for transfers between devices, on_device(): near = [lax.ppermute(a, 'fsdp', ring) for a in near_w]  83 us
    reduce_scatter x2, waiting for transfers between devices, reduce_grads(): mine = lax.psum_scatter(flat, 'fsdp', scatter_dimension=0, tiled=False)  72.3 us
    pallas_call x1, Pallas kernels, attend_back(): pl.pallas_call(functools.partial(attend_back_kernel, group, q_blocks), gr...  43.9 us
    pallas_call x1, Pallas kernels, attend(): pl.pallas_call(functools.partial(attend_kernel, group, q_blocks), grid=(p...  34.8 us
    unnamed x206, local copies, waits for them, and re-layouts  29.5 us
  transfers between devices with their start and end apart: 16, of which 8 were waited for; matrix products, arithmetic and copies ran while one was open for 14% of the time, Pallas kernels for 7%

profile of v3, /device:TPU:0, one launch (start us, length us, event | category | flops | bytes accessed | tf_op | source)
XLA Modules:
  0.0 887.9 jit_solution(3953053884034355063)
XLA Ops:
  12.1 74.7 %shard_map.430 = (bf16[8,192,1664]{2,1,0:T(8,128)(2,1)}, bf16[8,16,1280]{2,1,0:T(8,128)(2,1)}) custom-call(bf16[192,768]{1,0:T(8,128)(2,1)} %refs_0_.2, bf16[192,256]{1,0:T(8,128)(2,1)} %refs_1_.3, bf16[192,256]{1,0:T(8,128)(2,1)} %refs_2_.3, bf16[192,128]{1,0:T(8,128)(2,1)} %refs_3_.2, bf16[192,128]{1,0:T(8,128)(2,1)} %refs_4_.1, bf16[192,128]{1,0:T(8,128)(2,1)} %refs_5_.2, ...), custom_call_target="tpu_custom_call" | custom-call | tf_op jit(solution)/shard_map/pallas_call | solution.py:301
  86.9 7.0 fusion.33
  101.1 3.7 slice_add_fusion
  114.1 65.0 %shard_map.431 = (bf16[8,192,1408]{2,1,0:T(8,128)(2,1)}, bf16[8,16,3712]{2,1,0:T(8,128)(2,1)}, bf16[8,64,128]{2,1,0:T(8,128)(2,1)}) custom-call(bf16[192,768]{1,0:T(8,128)(2,1)} %bitcast.190, bf16[192,128]{1,0:T(8,128)(2,1)} %refs_1_.4, bf16[192,128]{1,0:T(8,128)(2,1)} %refs_2_.4, bf16[192,128]{1,0:T(8,128)(2,1)} %refs_3_.3, bf16[192,128]{1,0:T(8,128)(2,1)} %pad.16.refs_4_, ...), custom_call_target="tpu_custom_call" | custom-call | tf_op jit(solution)/shard_map/pallas_call | solution.py:301
  182.4 34.8 %shard_map.432 = (bf16[768,768]{1,0:T(8,128)(2,1)S(1)}, f32[2,8,768]{2,1,0:T(8,128)S(1)}) custom-call(s32[1]{0:T(128)} %bitcast.start_ref, s32[1,768]{1,0:T(1,128)S(1)} %broadcast_in_dim.15.begin_ref, bf16[768,768]{1,0:T(8,128)(2,1)S(1)} %copy.159.q_ref, bf16[768,512]{1,0:T(8,128)(2,1)S(1)} %pad_maximum_fusion.1.ko_ref.vo_ref, ...), custom_call_target="tpu_custom_call" | custom-call | flops 3623878656 | bytes 8388608 | tf_op jit(solution)/shard_map/pallas_call | solution.py:107
  231.4 4.6 multiply_reduce_fusion.1
  236.1 26.0 %collective-permute-done.2.refs_3_ = bf16[2,1536,256]{2,1,0:T(8,128)(2,1)} collective-permute-done((bf16[2,1536,256]{2,1,0:T(8,128)(2,1)}, bf16[2,1536,256]{2,1,0:T(8,128)(2,1)}, u32[]{:S(2)}, u32[]{:S(2)}) %collective-permute-start.2) | collective-permute-done | bytes 1572896 | tf_op jit(solution)/shard_map/ppermute | solution.py:599
  264.2 3.7 fusion.13
  272.0 23.8 %collective-permute-done.3.refs_4_ = bf16[2,1536,256]{2,1,0:T(8,128)(2,1)} collective-permute-done((bf16[2,1536,256]{2,1,0:T(8,128)(2,1)}, bf16[2,1536,256]{2,1,0:T(8,128)(2,1)}, u32[]{:S(2)}, u32[]{:S(2)}) %collective-permute-start.3) | collective-permute-done | bytes 1572896 | tf_op jit(solution)/shard_map/ppermute | solution.py:599
  295.8 33.2 %collective-permute-done.4.refs_5_ = bf16[2,256,1536]{2,1,0:T(8,128)(2,1)S(1)} collective-permute-done((bf16[2,256,1536]{2,1,0:T(8,128)(2,1)S(1)}, bf16[2,256,1536]{2,1,0:T(8,128)(2,1)S(1)}, u32[]{:S(2)}, u32[]{:S(2)}) %collective-permute-start.4) | collective-permute-done | bytes 1572896 | tf_op jit(solution)/shard_map/ppermute | solution.py:599
  330.1 231.8 %shard_map.433 = (f32[768,1536]{1,0:T(8,128)}, f32[768,1536]{1,0:T(8,128)}, f32[768,256]{1,0:T(8,128)}, f32[768,256]{1,0:T(8,128)}, f32[768,256]{1,0:T(8,128)}, ...) custom-call(bf16[768,1536]{1,0:T(8,128)(2,1)} %copy-done.17, ...), custom_call_target="tpu_custom_call" | custom-call | tf_op jit(solution)/shard_map/pallas_call | solution.py:497
  567.6 3.2 add.160
  571.6 3.2 fusion.8
  584.3 6.8 multiply_reduce_fusion
  591.2 5.6 fusion
  602.4 43.9 %shard_map.434 = (f32[768,768]{1,0:T(8,128)}, f32[768,256]{1,0:T(8,128)}, f32[768,256]{1,0:T(8,128)}, bf16[768,256]{1,0:T(8,128)(2,1)}, bf16[768,256]{1,0:T(8,128)(2,1)}) custom-call(s32[1]{0:T(128)} %bitcast.start_ref, s32[1,768]{1,0:T(1,128)} %copy-done.4, bf16[768,768]{1,0:T(8,128)(2,1)} %copy-done.2, bf16[768,512]{1,0:T(8,128)(2,1)} %copy-done.3, ...), custom_call_target="tpu_custom_call" | custom-call | flops 9059696640 | bytes 16777216 | tf_op jit(solution)/shard_map/pallas_call | solution.py:178
  664.5 6.2 collective-permute-done.11
  717.5 3.2 fusion.7
  721.6 3.9 convolution_convert_fusion.3
  748.2 7.2 fusion.127
  755.5 7.9 collective-permute-done.12
  765.7 72.3 %reduce-scatter.5.cloned.1.call-done = bf16[1,1360,128]{2,1,0:T(8,128)(2,1)} async-done(((bf16[8,1360,128]{2,1,0:T(8,128)(2,1)}), bf16[1,1360,128]{2,1,0:T(8,128)(2,1)}) %reduce-scatter.5.cloned.1.call-update) | async-done | bytes 348176 | tf_op jit(solution)/shard_map/reduce_scatter | solution.py:725
  838.0 7.3 fusion.2
  845.3 27.2 %all-reduce.7.cloned.1.call-done = (bf16[896,128]{1,0:T(8,128)(2,1)}, bf16[1360,128]{1,0:T(8,128)(2,1)}) async-done(((bf16[896,128]{1,0:T(8,128)(2,1)}, bf16[1360,128]{1,0:T(8,128)(2,1)}), (bf16[896,128]{1,0:T(8,128)(2,1)}, bf16[1360,128]{1,0:T(8,128)(2,1)})) %all-reduce.7.cloned.1.call-update) | async-done | bytes 577552 | tf_op jit(solution)/shard_map/psum | solution.py:726
  (356 shorter events, 166.4 us)
Async XLA Ops:
  7.2 79.7 %copy-start.10 = (bf16[768,1536]{1,0:T(8,128)(2,1)S(1)}, bf16[768,1536]{1,0:T(8,128)(2,1)}, u32[]{:S(2)}) copy-start(bf16[768,1536]{1,0:T(8,128)(2,1)} %param.31) | copy-start | bytes 7077892
  7.2 79.7 %copy-start.73 = (f32[1536]{0:T(1024)S(1)}, f32[1536]{0:T(1024)}, u32[]{:S(2)}) copy-start(f32[1536]{0:T(1024)} %param.36) | copy-start | bytes 18436
  7.2 758.5 %reduce-scatter.3.cloned.1.call-start = ((), (), s32[]{:S(2)}) async-start(), calls=%async_computation.2 | async-start | bytes 2064384 | tf_op jit(solution)/shard_map/reduce_scatter | solution.py:725
  11.2 75.6 %copy-start.69 = (f32[768]{0:T(1024)}, f32[768]{0:T(1024)S(1)}, u32[]{:S(2)}) copy-start(f32[768]{0:T(1024)S(1)} %fusion.3) | copy-start | bytes 9220
  11.2 82.6 %copy-start.78 = (f32[768]{0:T(1024)}, f32[768]{0:T(1024)S(1)}, u32[]{:S(2)}) copy-start(f32[768]{0:T(1024)S(1)} %fusion.93) | copy-start | bytes 9220
  98.3 82.8 %copy-start.3 = (bf16[768,512]{1,0:T(8,128)(2,1)}, bf16[768,512]{1,0:T(8,128)(2,1)S(1)}, u32[]{:S(2)}) copy-start(bf16[768,512]{1,0:T(8,128)(2,1)S(1)} %pad_maximum_fusion.1.ko_ref.vo_ref) | copy-start | bytes 2359300
  98.3 80.8 %collective-permute-start = (bf16[768,512]{1,0:T(8,128)(2,1)S(1)}, bf16[768,512]{1,0:T(8,128)(2,1)S(1)}, u32[]{:S(2)}, u32[]{:S(2)}) collective-permute-start(bf16[768,512]{1,0:T(8,128)(2,1)S(1)} %pad_maximum_fusion.1.ko_ref.vo_ref), channel_id=1, source_target_pairs={{0,2},{1,3},{4,6},{5,7},{8,10},{9,11},{12,14},{13,15},{16,18},{17,... | collective-permute-start | bytes 2359304 | tf_op jit(solution)/shard_map/ppermute | solution.py:585
  112.7 104.4 %copy-start.2 = (bf16[768,768]{1,0:T(8,128)(2,1)}, bf16[768,768]{1,0:T(8,128)(2,1)S(1)}, u32[]{:S(2)}) copy-start(bf16[768,768]{1,0:T(8,128)(2,1)S(1)} %copy.159.q_ref) | copy-start | bytes 3538948
  112.7 104.4 %copy-start.4 = (s32[1,768]{1,0:T(1,128)}, s32[1,768]{1,0:T(1,128)S(1)}, u32[]{:S(2)}) copy-start(s32[1,768]{1,0:T(1,128)S(1)} %broadcast_in_dim.15.begin_ref) | copy-start | bytes 9220
  222.7 8.3 collective-permute-start.1
  222.7 39.4 %collective-permute-start.2 = (bf16[2,1536,256]{2,1,0:T(8,128)(2,1)}, bf16[2,1536,256]{2,1,0:T(8,128)(2,1)}, u32[]{:S(2)}, u32[]{:S(2)}) collective-permute-start(bf16[2,1536,256]{2,1,0:T(8,128)(2,1)} %refs_0_.3), channel_id=1, source_target_pairs={{0,8},{4,12},{8,16},{12,20},{16,24},{20,28},{24,0},{28,4},{1,9},{5... | collective-permute-start | bytes 4718600 | tf_op jit(solution)/shard_map/ppermute | solution.py:599
  222.9 107.3 %collective-permute-start.5 = (bf16[2,1536,256]{2,1,0:T(8,128)(2,1)}, bf16[2,1536,256]{2,1,0:T(8,128)(2,1)}, u32[]{:S(2)}, u32[]{:S(2)}) collective-permute-start(bf16[2,1536,256]{2,1,0:T(8,128)(2,1)} %refs_0_.3), channel_id=1, source_target_pairs={{0,4},{4,0},{8,12},{12,8},{16,20},{20,16},{24,28},{28,24},{1,5},{5... | collective-permute-start | bytes 4718600 | tf_op jit(solution)/shard_map/ppermute | solution.py:600
  224.4 71.4 %collective-permute-start.3 = (bf16[2,1536,256]{2,1,0:T(8,128)(2,1)}, bf16[2,1536,256]{2,1,0:T(8,128)(2,1)}, u32[]{:S(2)}, u32[]{:S(2)}) collective-permute-start(bf16[2,1536,256]{2,1,0:T(8,128)(2,1)} %refs_1_.5), channel_id=1, source_target_pairs={{0,8},{4,12},{8,16},{12,20},{16,24},{20,28},{24,0},{28,4},{1,9},{5... | collective-permute-start | bytes 4718600 | tf_op jit(solution)/shard_map/ppermute | solution.py:599
  224.4 105.7 %collective-permute-start.6 = (bf16[2,1536,256]{2,1,0:T(8,128)(2,1)}, bf16[2,1536,256]{2,1,0:T(8,128)(2,1)}, u32[]{:S(2)}, u32[]{:S(2)}) collective-permute-start(bf16[2,1536,256]{2,1,0:T(8,128)(2,1)} %refs_1_.5), channel_id=1, source_target_pairs={{0,4},{4,0},{8,12},{12,8},{16,20},{20,16},{24,28},{28,24},{1,5},{5... | collective-permute-start | bytes 4718600 | tf_op jit(solution)/shard_map/ppermute | solution.py:600
  231.0 98.0 %collective-permute-start.4 = (bf16[2,256,1536]{2,1,0:T(8,128)(2,1)S(1)}, bf16[2,256,1536]{2,1,0:T(8,128)(2,1)S(1)}, u32[]{:S(2)}, u32[]{:S(2)}) collective-permute-start(bf16[2,256,1536]{2,1,0:T(8,128)(2,1)S(1)} %copy-done.40), channel_id=1, source_target_pairs={{0,8},{4,12},{8,16},{12,20},{16,24},{20,28},{24,0},{28,4},{1,9},{5... | collective-permute-start | bytes 4718600 | tf_op jit(solution)/shard_map/ppermute | solution.py:599
  262.1 68.0 %collective-permute-start.7 = (bf16[2,256,1536]{2,1,0:T(8,128)(2,1)S(1)}, bf16[2,256,1536]{2,1,0:T(8,128)(2,1)}, u32[]{:S(2)}, u32[]{:S(2)}) collective-permute-start(bf16[2,256,1536]{2,1,0:T(8,128)(2,1)S(1)} %copy-done.40), channel_id=1, source_target_pairs={{0,4},{4,0},{8,12},{12,8},{16,20},{20,16},{24,28},{28,24},{1,5},{5... | collective-permute-start | bytes 4718600 | tf_op jit(solution)/shard_map/ppermute | solution.py:600
  570.8 13.4 %collective-permute-start.9 = (f32[768,1536]{1,0:T(8,128)}, f32[768,1536]{1,0:T(8,128)}, u32[]{:S(2)}, u32[]{:S(2)}) collective-permute-start(f32[768,1536]{1,0:T(8,128)} %add.160), channel_id=1, source_target_pairs={{0,1},{1,0},{2,3},{3,2},{4,5},{5,4},{6,7},{7,6},{8,9},{9,8},{10,11... | collective-permute-start | bytes 14155784 | tf_op jit(solution)/shard_map/ppermute | solution.py:516
  574.8 16.3 %collective-permute-start.8 = (f32[768,1536]{1,0:T(8,128)}, f32[768,1536]{1,0:T(8,128)}, u32[]{:S(2)}, u32[]{:S(2)}) collective-permute-start(f32[768,1536]{1,0:T(8,128)} %fusion.8), channel_id=1, source_target_pairs={{0,1},{1,0},{2,3},{3,2},{4,5},{5,4},{6,7},{7,6},{8,9},{9,8},{10,11... | collective-permute-start | bytes 14155784 | tf_op jit(solution)/shard_map/ppermute | solution.py:516
  575.3 5.1 collective-permute-start.10
  648.4 22.2 %collective-permute-start.11 = (bf16[768,512]{1,0:T(8,128)(2,1)}, bf16[768,512]{1,0:T(8,128)(2,1)}, u32[]{:S(2)}, u32[]{:S(2)}) collective-permute-start(bf16[768,512]{1,0:T(8,128)(2,1)} %pad_maximum_fusion.2), channel_id=1, source_target_pairs={{2,0},{3,1},{6,4},{7,5},{10,8},{11,9},{14,12},{15,13},{18,16},{19,... | collective-permute-start | bytes 2359304 | tf_op jit(solution)/shard_map/ppermute | solution.py:669
  697.0 140.9 %reduce-scatter.5.cloned.1.call-start = ((), (), s32[]{:S(2)}) async-start(), calls=%async_computation.3 | async-start | bytes 3133440 | tf_op jit(solution)/shard_map/reduce_scatter | solution.py:725
  740.3 132.2 %all-reduce.7.cloned.1.call-start = ((), (), s32[]{:S(2)}) async-start(), calls=%async_computation.4 | async-start | bytes 1155072 | tf_op jit(solution)/shard_map/psum | solution.py:726
  755.4 82.5 %copy-start.80 = (f32[768]{0:T(1024)S(1)}, f32[768]{0:T(1024)}, u32[]{:S(2)}) copy-start(f32[768]{0:T(1024)} %copy-done.78) | copy-start | bytes 9220
  755.4 8.0 collective-permute-start.12
  (83 other events, 609.5 us)
Sparse Core Ops, SparseCore 0:
  697.1 63.5 reduce-scatter.2
  764.6 73.2 reduce-scatter.4
  840.5 31.9 all-reduce.6

commit v4 on v3

--- a/solution.py
+++ b/solution.py
@@ -311,203 +311,167 @@
     )(*arrays)
 
 
-def moe_kernel(n, n2_ref, c_ref, gl_ref, ul_ref, al_ref, gates_ref, *refs):
-    own, near, side = refs[0:3], refs[3:6], refs[6:9]
-    moe_ref, dn2_ref, as_ref, gs_ref, us_ref, dgate_ref = refs[9:15]
-    bufs = refs[15:18]
-    wg, wu, wd, load_sem, z_send, z_recv, y_send, y_recv, x_send, x_recv = refs[18:]
-    outer, inner = levels(n)
-    me = lax.axis_index("fsdp")
-    ctx = lax.axis_index("ctx")
-    z, y = me // inner, me % inner
-    right = (z + 1) % outer * inner + y
-    left = (z + outer - 1) % outer * inner + y
-    local = own[0].shape[0]
-    rows = n2_ref.shape[0]
-    experts = gates_ref.shape[1]
-    chunks = [(j, a) for j in range(local) for a in range(3)]
-
-    def shard(do, dj):
-        return (z + outer - do) % outer * inner + (y + inner - dj) % inner
-
-    def held(do, dj):
-        if (do, dj) == (0, 0):
-            return own
-        if (do, dj) == (1, 0):
-            return near
-        if (do, dj) == (0, 1):
-            return side
-        at = shard(do, dj)
-        return [b.at[at] for b in bufs]
-
-    barrier = pltpu.get_barrier_semaphore()
-    peers = [right, left] + [z * inner + (y + dj) % inner for dj in range(1, inner)]
-    for peer in peers:
-        pl.semaphore_signal(barrier, inc=1, device_id={"fsdp": peer}, device_id_type=MESH)
-    pl.semaphore_signal(barrier, inc=1, device_id={"ctx": 1 - ctx}, device_id_type=MESH)
-    pl.semaphore_wait(barrier, len(peers) + 1)
-
-    def remote(src, dst, send, recv, to):
-        return pltpu.make_async_remote_copy(
-            src_ref=src, dst_ref=dst, send_sem=send, recv_sem=recv, device_id=to, device_id_type=MESH
-        )
-
-    def z_copy(do, i):
-        j, a = chunks[i]
-        take, unused = slab_of(own[a].shape[1], ctx)
-        at = shard(do - 1, 0)
-        return remote(held(do - 1, 0)[a].at[j, take], bufs[a].at[at, j, take], z_send.at[do, i], z_recv.at[do, i], {"fsdp": right})
-
-    def y_copy(do, dj, i):
-        j, a = chunks[i]
-        take, unused = slab_of(own[a].shape[1], ctx)
-        at = shard(do, 0)
-        to = {"fsdp": z * inner + (y + dj) % inner}
-        return remote(held(do, 0)[a].at[j, take], bufs[a].at[at, j, take], y_send.at[do, dj, i], y_recv.at[do, dj, i], to)
-
-    def x_copy(do, dj, i):
-        j, a = chunks[i]
-        unused, edge = slab_of(own[a].shape[1], ctx)
-        at = shard(do, dj)
-        part = bufs[a].at[at, j, edge]
-        return remote(part, part, x_send.at[do, dj, i], x_recv.at[do, dj, i], {"ctx": 1 - ctx})
-
-    started = []
-
-    def go(copy):
-        copy.start()
-        started.append(copy)
-
-    for ref in (moe_ref, dn2_ref, as_ref, gs_ref, us_ref, dgate_ref):
-        ref[...] = jnp.zeros_like(ref)
-
-    step = rows // 3
-
-    def compute(do, dj, j, slot):
-        e = shard(do, dj) * local + j
-
-        def block(b, carry):
-            at = pl.ds(pl.multiple_of(b * step, step), step)
-            xb = n2_ref[at, :]
-            cb = c_ref[at, :]
-            gv = dot(xb, wg[slot]) + gl_ref[at, :]
-            uv = dot(xb, wu[slot]) + ul_ref[at, :]
-            back = dot_t(cb, wd[slot]) + al_ref[at, :]
-            hit = lax.broadcasted_iota(jnp.int32, (step, experts), 1) == e
-            gate = jnp.sum(jnp.where(hit, gates_ref[at, :], 0.0), axis=1, keepdims=True)
-            sig = 1.0 / (1.0 + jnp.exp(-gv))
-            silu = gv * sig
-            act = silu * uv
-            col = jnp.sum(act * back, axis=1, keepdims=True)
-            dgate_ref[at, :] += jnp.where(hit, col, 0.0)
-            back = back * gate
-            act = (act * gate).astype(BF)
-            du = back * silu
-            dg = back * uv * (sig + silu * (1.0 - sig))
-            as_ref[at, :] += act.astype(F32)
-            gs_ref[at, :] += dg
-            us_ref[at, :] += du
-            moe_ref[at, :] += dot(act, wd[slot])
-            dn2_ref[at, :] += dot_t(dg.astype(BF), wg[slot]) + dot_t(du.astype(BF), wu[slot])
-            return carry
-
-        lax.fori_loop(0, 3, block, 0)
-
-    queue = []
-
-    def load(do, dj, j, slot):
-        found = []
-        for a, dst in enumerate((wg, wu, wd)):
-            copy = pltpu.make_async_copy(held(do, dj)[a].at[j], dst.at[slot], load_sem.at[slot, a])
-            copy.start()
-            found.append(copy)
-        return found
-
-    pending = []
-    turn = [0]
-
-    def run_next():
-        do, dj, j, slot, copies = pending.pop(0)
-        for c in copies:
-            c.wait()
-        compute(do, dj, j, slot)
-
-    def feed(do, dj, j):
-        if len(pending) == 2:
-            run_next()
-        slot = turn[0] % 2
-        turn[0] += 1
-        pending.append((do, dj, j, slot, load(do, dj, j, slot)))
-
-    def arrived(do, dj, j):
-        for i, (jj, a) in enumerate(chunks):
-            if jj == j:
-                x_copy(do, dj, i).wait_recv()
-
-    for i in range(len(chunks)):
-        go(z_copy(2, i))
-        for dj in range(1, inner):
-            go(y_copy(1, dj, i))
-        for dj in range(2, inner):
-            go(y_copy(0, dj, i))
-
-    ready = [(do, dj, j) for do, dj in ((0, 0), (1, 0), (0, 1)) for j in range(local)]
-    for r in range(outer - 1):
-        later = []
-        for i, (j, a) in enumerate(chunks):
-            if ready:
-                do, dj, jj = ready.pop(0)
-                if (do, dj) not in ((0, 0), (1, 0), (0, 1)):
-                    arrived(do, dj, jj)
-                feed(do, dj, jj)
-            if r + 2 < outer:
-                z_copy(r + 2, i).wait_recv()
-                if r + 3 < outer:
-                    go(z_copy(r + 3, i))
-                for dj in range(1, inner):
-                    go(y_copy(r + 2, dj, i))
-                go(x_copy(r + 2, 0, i))
-                if a == 2:
-                    later.append((r + 2, 0, j))
-            for do, dj in [(r + 1, dj) for dj in range(1, inner)] + ([(0, dj) for dj in range(2, inner)] if r == 0 else []):
-                y_copy(do, dj, i).wait_recv()
-                go(x_copy(do, dj, i))
-                if a == 2:
-                    later.append((do, dj, j))
-        ready = ready + later
-    for do, dj, j in ready:
-        arrived(do, dj, j)
-        feed(do, dj, j)
-    while pending:
-        run_next()
-    for c in started:
-        c.wait_send()
-
-
-def moe_all(n2, cot, gate_low, up_low, act_low, gates, own, near, side, collective_id):
-    n = lax.axis_size("fsdp")
-    outer, inner = levels(n)
-    rows, width = n2.shape
-    ff = gate_low.shape[1]
-    count = 3 * own[0].shape[0]
-    dma = pltpu.SemaphoreType.DMA
+def t_dot_k(left, right):
+    return dot(left, right, ((0,), (0,)))
+
+
+def expert_kernel(experts, count, ids_ref, t_ref, c_ref, *refs):
+    w_refs = refs[:count]
+    ga_ref, ua_ref, gb_ref, ub_ref, db_ref, da_ref = refs[count : count + 6]
+    prior = refs[count + 6 : count + 11]
+    early = refs[count + 11 : -9]
+    r_ref, m_ref = refs[-9:-7]
+    sums = refs[-7:-2]
+    moe_acc, dn2_acc = refs[-2:]
+    rows, width = c_ref.shape
+    ff = gb_ref.shape[1]
+    spare = r_ref.shape[1] - width
+    lanes = t_ref.shape[1] - width
+
+    @pl.when(pl.program_id(0) == 0)
+    def _():
+        for old, new in zip(prior, sums):
+            new[...] = old[...]
+
+    n2 = t_ref[:, :width]
+    cot = c_ref[...]
+    extra = t_ref[:, width:].astype(F32)
+    lane = lax.broadcasted_iota(jnp.int32, (rows, lanes), 1)
+    chosen = jnp.sum(jnp.where(lane == 2 * experts, extra, 0.0), axis=1, keepdims=True)
+    low_lane = lax.broadcasted_iota(jnp.int32, (rows, LANES), 1)
+    mask = ((low_lane // ADAPTER_RANK).astype(F32) == chosen).astype(F32)
+    zg = (dot(n2, ga_ref[...]) * mask).astype(BF)
+    zu = (dot(n2, ua_ref[...]) * mask).astype(BF)
+    gl = dot(zg, gb_ref[...])
+    ul = dot(zu, ub_ref[...])
+    down_back = (dot_t(cot, db_ref[...]) * mask).astype(BF)
+    al = dot_t(down_back, da_ref[...])
+    back_lane = lax.broadcasted_iota(jnp.int32, (rows, spare), 1)
+    dgate = jnp.zeros((rows, spare), F32)
+    act_sum = dg_sum = du_sum = None
+    for k in range(count):
+        e = ids_ref[k]
+        w = w_refs[k]
+        gate = jnp.sum(jnp.where((lane == e) | (lane == experts + e), extra, 0.0), axis=1, keepdims=True)
+        gv = dot(n2, w[:, :ff]) + gl
+        uv = dot(n2, w[:, ff : 2 * ff]) + ul
+        back = dot(cot, w[:, 2 * ff :]) + al
+        sig = 1.0 / (1.0 + jnp.exp(-gv))
+        silu = gv * sig
+        act = silu * uv
+        col = jnp.sum(act * back, axis=1, keepdims=True)
+        high = col.astype(BF).astype(F32)
+        at = e + ids_ref[count]
+        dgate = dgate + jnp.where(back_lane == at, high, 0.0) + jnp.where(back_lane == at + experts, col - high, 0.0)
+        back = back * gate
+        act = act * gate
+        du = back * silu
+        dg = back * uv * (sig + silu * (1.0 - sig))
+        act_sum = act if k == 0 else act_sum + act
+        dg_sum = dg if k == 0 else dg_sum + dg
+        du_sum = du if k == 0 else du_sum + du
+        moe = dot_t(act.astype(BF), w[:, 2 * ff :])
+        dn2 = dot_t(jnp.concatenate([dg.astype(BF), du.astype(BF)], axis=1), w[:, : 2 * ff])
+        if k == 0:
+            moe_acc[...] = moe
+            dn2_acc[...] = dn2
+        else:
+            moe_acc[...] += moe
+            dn2_acc[...] += dn2
+    act_sum, dg_sum, du_sum = act_sum.astype(BF), dg_sum.astype(BF), du_sum.astype(BF)
+    low = (dot(act_sum, da_ref[...]) * mask).astype(BF)
+    gdu = (dot_t(dg_sum, gb_ref[...]) * mask).astype(BF)
+    udu = (dot_t(du_sum, ub_ref[...]) * mask).astype(BF)
+    moe = moe_acc[...] + dot(low, db_ref[...])
+    dn2 = dn2_acc[...] + dot_t(gdu, ga_ref[...]) + dot_t(udu, ua_ref[...])
+    if early:
+        moe = moe + early[1][...].astype(F32)
+        dn2 = dn2 + early[0][:, :width].astype(F32)
+        dgate = dgate + early[0][:, width:].astype(F32)
+    m_ref[...] = moe.astype(BF)
+    r_ref[:, :width] = dn2.astype(BF)
+    r_ref[:, width:] = dgate.astype(BF)
+    bd_ref, ad_ref, bg_ref, bu_ref, a_ref = sums
+    bd_ref[...] += t_dot_k(low, cot)
+    ad_ref[...] += t_dot_k(act_sum, down_back)
+    bg_ref[...] += t_dot_k(zg, dg_sum)
+    bu_ref[...] += t_dot_k(zu, du_sum)
+    a_ref[...] += t_dot_k(n2, jnp.concatenate([gdu, udu], axis=1))
+
+
+def experts_on(ids, experts, spare, t, cot, weights, w_two, first, low_two, down_b, down_at, prior, early=()):
+    rows, width = cot.shape
+    ff = down_at.shape[0]
+    step = 256
     sd = jax.ShapeDtypeStruct
-    vm = pl.BlockSpec(memory_space=pltpu.VMEM)
-    anywhere = pl.BlockSpec(memory_space=pl.ANY)
+    whole = lambda a: pl.BlockSpec(a.shape, lambda i: (0, 0))
+    by_row = lambda cols: pl.BlockSpec((step, cols), lambda i: (i, 0))
+    column = lambda height, cols, at: pl.BlockSpec((height, cols), lambda i: (0, at))
+    low_rows = low_two.shape[0]
+    count = len(weights)
+    flops = 2 * rows * width * ff * 7 * count
     outs = pl.pallas_call(
-        functools.partial(moe_kernel, n),
-        in_specs=[vm] * 6 + [anywhere] * 9,
-        out_specs=[vm] * 6 + [anywhere] * 3,
-        out_shape=[sd((rows, width), F32), sd((rows, width), F32), sd((rows, ff), F32), sd((rows, ff), F32), sd((rows, ff), F32), sd(gates.shape, F32)]
-        + [sd((n,) + a.shape, a.dtype) for a in own],
-        scratch_shapes=[
-            pltpu.VMEM((2, width, ff), BF), pltpu.VMEM((2, width, ff), BF), pltpu.VMEM((2, ff, width), BF), dma((2, 3)),
-            dma((outer, count)), dma((outer, count)), dma((outer, inner, count)), dma((outer, inner, count)),
-            dma((outer, inner, count)), dma((outer, inner, count)),
-        ],
-        compiler_params=pltpu.CompilerParams(collective_id=collective_id, has_side_effects=True, vmem_limit_bytes=56 << 20),
-    )(n2, cot, gate_low, up_low, act_low, gates, *own, *near, *side)
-    return outs[:6]
+        functools.partial(expert_kernel, experts, count),
+        grid=(rows // step,),
+        in_specs=[pl.BlockSpec(memory_space=pltpu.SMEM), by_row(t.shape[1]), by_row(width)]
+        + [pl.BlockSpec(w.shape, lambda i: (0, 0), pipeline_mode=pl.Buffered(1)) for w in weights]
+        + [column(width, LANES, first), column(width, LANES, first + 1), column(low_rows, ff, 0), column(low_rows, ff, 1), whole(down_b), whole(down_at)]
+        + [whole(p) for p in prior] + [by_row(e.shape[1]) for e in early],
+        out_specs=[by_row(width + spare), by_row(width)] + [whole(p) for p in prior],
+        out_shape=[sd((rows, width + spare), BF), sd((rows, width), BF)] + [sd(p.shape, F32) for p in prior],
+        scratch_shapes=[pltpu.VMEM((step, width), F32), pltpu.VMEM((step, width), F32)],
+        input_output_aliases={3 + count + 6 + i: 2 + i for i in range(len(prior))},
+        compiler_params=pltpu.CompilerParams(vmem_limit_bytes=58 << 20),
+        cost_estimate=pl.CostEstimate(flops=flops, bytes_accessed=24 << 20, transcendentals=rows * ff * count),
+    )(ids, t, cot, *weights, w_two, w_two, low_two, low_two, down_b, down_at, *prior, *early)
+    return outs[0], outs[1], outs[2:]
+
+
+class Crossing:
+    def __init__(self):
+        self.n_ctx, self.n_tp = lax.axis_size("ctx"), lax.axis_size("tp")
+        self.tp_at = lax.axis_index("tp")
+
+    def pairs(self, by):
+        return [(c, (c + by) % self.n_ctx) for c in range(self.n_ctx)]
+
+    def half(self, block):
+        if self.n_tp != 2:
+            return block
+        size = block.shape[0] // 2
+        return lax.dynamic_slice_in_dim(block, self.tp_at * size, size, 0)
+
+    def other_half(self, block):
+        size = block.shape[0] // 2
+        return lax.dynamic_slice_in_dim(block, (1 - self.tp_at) * size, size, 0)
+
+    def joined(self, half):
+        if self.n_tp != 2:
+            return half
+        other = lax.ppermute(half, "tp", [(0, 1), (1, 0)])
+        size = half.shape[0]
+        whole = lax.dynamic_update_slice_in_dim(jnp.zeros((2 * size,) + half.shape[1:], half.dtype), half, self.tp_at * size, 0)
+        return lax.dynamic_update_slice_in_dim(whole, other, (1 - self.tp_at) * size, 0)
+
+    def fetch(self, block):
+        half = self.half(block)
+        return [lax.ppermute(half, "ctx", self.pairs(by)) for by in range(1, self.n_ctx)]
+
+    def summed_half(self, block):
+        if self.n_tp != 2:
+            return block.astype(F32)
+        return self.half(block).astype(F32) + lax.ppermute(self.other_half(block), "tp", [(0, 1), (1, 0)]).astype(F32)
+
+    def give(self, block, by):
+        return lax.ppermute(self.summed_half(block).astype(BF), "ctx", self.pairs(-by))
+
+    def total(self, own, parts):
+        found = self.summed_half(own)
+        for part in parts:
+            found = found + part.astype(F32)
+        if self.n_tp != 2:
+            return lax.psum(found, "tp")
+        return self.joined(found.astype(BF)).astype(F32)
 
 
 def tp_sum(value):
@@ -582,6 +546,29 @@
     )
     key = rotary_apply(key_pre.reshape(rows, -1, HEAD_SIZE), cosine_table, sine_table).reshape(rows, kv_width).astype(BF)
     kv = jnp.concatenate([key, value_state], axis=1)
+    cross = Crossing()
+    outer, inner = levels(n)
+    me = lax.axis_index("fsdp")
+    ring = [(i, (i + inner) % n) for i in range(n)]
+    turns = [[(i, i // inner * inner + (i % inner + dj) % inner) for i in range(n)] for dj in range(1, inner)]
+    local = local_experts // cross.n_ctx
+    mine = [lax.dynamic_slice_in_dim(a, ctx_at * local, local, 0) for a in (w_gate, w_up, w_down)]
+    block = jnp.concatenate([mine[0], mine[1], jnp.swapaxes(mine[2], 1, 2)], axis=2)
+    brought = {(0, 0): block}
+
+    def bring(do, after):
+        last = [brought[(do, 0)]] + [brought[(do - 1, dj)] for dj in range(1, inner) if do]
+        last, after = lax.optimization_barrier((last, after))
+        brought[(do, 0)] = last[0]
+        for dj, value in zip(range(1, inner), last[1:]):
+            brought[(do - 1, dj)] = value
+        if do + 1 < outer:
+            brought[(do + 1, 0)] = lax.ppermute(last[0], "fsdp", ring)
+        for dj in range(1, inner):
+            brought[(do, dj)] = lax.ppermute(last[0], "fsdp", turns[dj - 1])
+        return after
+
+    one = bring(0, one)
     far = lax.ppermute(kv, "ctx", [(i, i + 1) for i in range(lax.axis_size("ctx") - 1)])
     w_out_t, kv = lax.optimization_barrier((w_out.T, kv))
     two, low_two, down_a = gather_packs(
@@ -592,16 +579,12 @@
         ],
         1,
     )
-    near_w = lax.optimization_barrier((w_gate, w_up, w_down, two))[:3]
-    outer, inner = levels(n)
-    ring = [(i, (i + inner) % n) for i in range(n)]
-    turn = [(i, i // inner * inner + (i % inner + 1) % inner) for i in range(n)]
-    near = [lax.ppermute(a, "fsdp", ring) for a in near_w]
-    beside = [lax.ppermute(a, "fsdp", turn) for a in near_w]
+    two = bring(1, two)
+    cot = lax.optimization_barrier((out_cotangent, two))[0]
+    cot_halves = cross.fetch(cot)
     far, two = lax.optimization_barrier((far, two))
     w_two = two.reshape(n * share, -1)
     low_two = low_two.reshape(n * low_rows, -1)
-    gate_b, up_b = low_two[:, :ff_width], low_two[:, ff_width : 2 * ff_width]
     out_b = low_two[:, 2 * ff_width : 2 * ff_width + width]
     down_b = low_two[:, 2 * ff_width + width : 2 * ff_width + 2 * width]
     router_b = low_two[:, 2 * ff_width + 2 * width :]
@@ -614,43 +597,69 @@
     start_at = jnp.reshape(start, (1,)).astype(jnp.int32)
     query_state = (query_state.astype(F32) * 0.125).astype(BF)
     mixed_heads, log_total = attend(query_state, kv, far, begin_row, start_at)
+    mixed_heads = bring(2, mixed_heads)
+    cot_halves, mixed_heads = lax.optimization_barrier((cot_halves, mixed_heads))
     out_u = dot(mixed_heads, out_a) * mask
     attn_part = dot_t(mixed_heads, out_wt) + dot(out_u.astype(BF), out_b)
     hidden = xfull + tp_sum(attn_part)
     normed_two = rms_norm(hidden, ffn_gain).astype(BF)
-    lows = dot(normed_two, w_two[:, q_width : q_width + 4 * ranks])
+    lows = dot(normed_two, jnp.concatenate([router_a, router_w], axis=1))
     router_u = (lows[:, :ranks] * mask).astype(BF)
-    zin_gate = (lows[:, ranks : 2 * ranks] * mask).astype(BF)
-    zin_up = (lows[:, 2 * ranks : 3 * ranks] * mask).astype(BF)
-    logits = lows[:, 3 * ranks : 3 * ranks + experts] + dot(router_u, router_b)[:, :experts]
+    logits = lows[:, ranks : ranks + experts] + dot(router_u, router_b)[:, :experts]
     selected = jnp.any(routes[:, :, None] == jnp.arange(experts, dtype=jnp.int32)[None, None, :], axis=1)
     gates = jax.nn.softmax(jnp.where(selected, logits, -jnp.inf), axis=-1)
 
-    cot = out_cotangent
     dout = cot.astype(F32)
-    gate_low = dot(zin_gate, gate_b)
-    up_low = dot(zin_up, up_b)
-    down_back = dot_t(cot, down_b) * mask
-    act_low = dot_t(down_back.astype(BF), down_at)
-    moe, dn2, act_sum, dg_sum, du_sum, dgate = moe_all(
-        normed_two, cot, gate_low, up_low, act_low, gates, (w_gate, w_up, w_down), near, beside, 2
+    high = gates.astype(BF)
+    spare = -(-2 * experts * n_tp // LANES) * LANES
+    carried = jnp.concatenate(
+        [
+            normed_two,
+            high,
+            (gates - high.astype(F32)).astype(BF),
+            chosen_local[:, None].astype(BF),
+            jnp.zeros((rows, LANES - 2 * experts - 1), BF),
+        ],
+        axis=1,
     )
-    down_low = (dot(act_sum.astype(BF), down_at) * mask).astype(BF)
-    moe = moe + dot(down_low, down_b)
-    output = (hidden + tp_sum(moe.astype(BF).astype(F32))).astype(BF)
-    grad_bd = t_dot(down_low, cot)
-    grad_ad = t_dot(act_sum.astype(BF), down_back.astype(BF))
-    dg_sum = dg_sum.astype(BF)
-    du_sum = du_sum.astype(BF)
-    grad_bg = t_dot(zin_gate, dg_sum)
-    grad_bu = t_dot(zin_up, du_sum)
-    gate_du = (dot_t(dg_sum, gate_b) * mask).astype(BF)
-    up_du = (dot_t(du_sum, up_b) * mask).astype(BF)
-    gu_du = jnp.concatenate([gate_du, up_du], axis=1)
-    dn2 = dn2 + dot_t(gu_du, w_two[:, q_width + ranks : q_width + 3 * ranks])
-    grad_agu = t_dot(normed_two, gu_du)
+    halves = cross.fetch(carried)
+    for do in range(3, outer):
+        carried = bring(do, carried)
+    early = [(0, 0), (1, 0)] + [(0, dj) for dj in range(1, inner)] + [(2, 0)] + [(1, dj) for dj in range(1, inner)]
+    late = [(do, 0) for do in range(3, outer)] + [(do, dj) for do in range(2, outer) for dj in range(1, inner)]
+
+    def weights_of(keys):
+        ids = [((me // inner + outer - do) % outer * inner + (me % inner + inner - dj) % inner) * local_experts + ctx_at * local + j for do, dj in keys for j in range(local)]
+        return jnp.stack(ids + [tp_at * 2 * experts]).astype(jnp.int32), [brought[k][j] for k in keys for j in range(local)]
+
+    sums = [jnp.zeros(shape, F32) for shape in ((ranks, width), (ff_width, ranks), (ranks, ff_width), (ranks, ff_width), (width, 2 * ranks))]
+    at = q_width // LANES + 1
+    work = [(carried, cot)] + [(None, None)] * (cross.n_ctx - 1)
+    partial = []
+    ids, weights = weights_of(early)
+    for by in range(cross.n_ctx):
+        if by:
+            work[by] = (cross.joined(halves[by - 1]), cross.joined(cot_halves[by - 1]))
+        r, m, sums = experts_on(ids, experts, spare, *work[by], weights, w_two, at, low_two, down_b, down_at, sums)
+        if by == 0:
+            halves, cot_halves, r = lax.optimization_barrier((halves, cot_halves, r))
+        partial.append((r, m))
+    ids, weights = weights_of(late)
+    back_parts, moe_parts = [], []
+    for by in list(range(1, cross.n_ctx)) + [0]:
+        r, m, sums = experts_on(ids, experts, spare, *work[by], weights, w_two, at, low_two, down_b, down_at, sums, partial[by])
+        moe_parts.append(m)
+        if by:
+            half = cross.summed_half(r).astype(BF)
+            half, carried = lax.optimization_barrier((half, work[0][0]))
+            work[0] = (carried, cot)
+            back_parts.append(lax.ppermute(half, "ctx", cross.pairs(-by)))
+    r, back_parts = lax.optimization_barrier((r, back_parts))
+    back = cross.total(r, back_parts)
+    dn2 = back[:, :width]
+    dgate = jnp.sum(back[:, width : width + 2 * experts * n_tp].reshape(rows, 2 * n_tp, experts), axis=1)
+    grad_bd, grad_ad, grad_bg, grad_bu, grad_agu = sums
     grad_ag, grad_au = grad_agu[:, :ranks], grad_agu[:, ranks:]
-    dn2, dgate = tp_sum(dn2), tp_sum(dgate)
     dlogits = (gates * (dgate - jnp.sum(gates * dgate, axis=-1, keepdims=True))).astype(BF)
     dlogits = jnp.pad(dlogits, ((0, 0), (0, LANES - experts)))
     router_du = (dot_t(dlogits, router_b) * mask).astype(BF)
@@ -666,6 +675,9 @@
     dquery, dkey_own, dvalue_own, dkey_far, dvalue_far = attend_back(
         query_state, kv, far, begin_row, start_at, mixed_heads, dmixed, log_total
     )
+    moe_parts, dquery = lax.optimization_barrier((moe_parts, dquery))
+    moe = cross.total(moe_parts[-1], [cross.give(p, by) for by, p in zip(range(1, cross.n_ctx), moe_parts)])
+    output = (hidden + moe).astype(BF)
     far_back = lax.ppermute(
         jnp.concatenate([dkey_far, dvalue_far], axis=1),
         "ctx",

time: 894 us -> 790 us (0.88)
  Pallas kernels: 450 us -> 358 us
  local copies, waits for them, and re-layouts: 81.7 us -> 110 us
  matrix products: 88.5 us -> 60.8 us
  waiting for transfers between devices: 199 us -> 184 us
    pallas_call x1 -> x4, Pallas kernels: 232 us -> 127 us  [experts_on(): pl.pallas_call(functools.partial(expert_kernel, experts, count), grid=(ro...]
    dot_general x41 -> x27, matrix products: 88.5 us -> 60.8 us  [dot(): lax.dot_general(left, right, (dims, ((), ())), preferred_element_type=F32...]
    reduce_scatter x2, waiting for transfers between devices: 72.3 us -> 49.8 us  [reduce_grads(): mine = lax.psum_scatter(flat, 'fsdp', scatter_dimension=0, tiled=False)]
    pallas_call x2, Pallas kernels: 140 us -> 152 us  [gather_packs(): pl.pallas_call(functools.partial(gather_kernel, n, layout), in_specs=[any...]
    dynamic_slice x1 -> x9, local copies, waits for them, and re-layouts: 0.08 us -> 11.8 us  [the longest x4 5.6 us: other_half(): return lax.dynamic_slice_in_dim(block, (1 - self.tp_at) * size, size, 0)]
    unnamed x206 -> x187, local copies, waits for them, and re-layouts: 29.5 us -> 37.3 us
    ppermute x6 -> x19, waiting for transfers between devices: 83 us -> 87 us  [the longest x3 32.8 us: bring(): brought[do + 1, 0] = lax.ppermute(last[0], 'fsdp', ring)]
  transfers between devices with their start and end apart: 16 -> 26, of which waited for: 8 -> 16; matrix products, arithmetic and copies ran while one was open for 14% -> 16% of each run, Pallas kernels for 7% -> 27%
where the time goes in v4:
time: 790 us; the launch traced here: 783 us
  Pallas kernels  358 us (45%)
  waiting for transfers between devices  184 us (23%)
  local copies, waits for them, and re-layouts  110 us (14%)
  matrix products  60.8 us (8%)
  other arithmetic  40.8 us (5%)
  between operations  15.6 us (2%)
  starting transfers between devices  14 us (2%)
    pallas_call x2, Pallas kernels, gather_packs(): pl.pallas_call(functools.partial(gather_kernel, n, layout), in_specs=[any...  152 us
    pallas_call x4, Pallas kernels, experts_on(): pl.pallas_call(functools.partial(expert_kernel, experts, count), grid=(ro...  127 us
    dot_general x27, matrix products, dot(): lax.dot_general(left, right, (dims, ((), ())), preferred_element_type=F32...  60.8 us
    reduce_scatter x2, waiting for transfers between devices, reduce_grads(): mine = lax.psum_scatter(flat, 'fsdp', scatter_dimension=0, tiled=False)  49.8 us
    pallas_call x1, Pallas kernels, attend_back(): pl.pallas_call(functools.partial(attend_back_kernel, group, q_blocks), gr...  44.2 us
    unnamed x187, local copies, waits for them, and re-layouts  37.3 us
    pallas_call x1, Pallas kernels, attend(): pl.pallas_call(functools.partial(attend_kernel, group, q_blocks), grid=(p...  34.8 us
    ppermute x3, waiting for transfers between devices, bring(): brought[do + 1, 0] = lax.ppermute(last[0], 'fsdp', ring)  32.8 us
  transfers between devices with their start and end apart: 26, of which 16 were waited for; matrix products, arithmetic and copies ran while one was open for 16% of the time, Pallas kernels for 27%

profile of v4, /device:TPU:0, one launch (start us, length us, event | category | flops | bytes accessed | tf_op | source)
XLA Modules:
  0.0 783.0 jit_solution(8955914391013792421)
XLA Ops:
  12.0 74.7 %shard_map.430 = (bf16[8,192,1664]{2,1,0:T(8,128)(2,1)}, bf16[8,16,1280]{2,1,0:T(8,128)(2,1)}) custom-call(bf16[192,768]{1,0:T(8,128)(2,1)} %refs_0_.1, bf16[192,256]{1,0:T(8,128)(2,1)} %refs_1_.2, bf16[192,256]{1,0:T(8,128)(2,1)} %refs_2_.2, bf16[192,128]{1,0:T(8,128)(2,1)} %refs_3_.2, bf16[192,128]{1,0:T(8,128)(2,1)} %refs_4_.1, bf16[192,128]{1,0:T(8,128)(2,1)} %refs_5_.2, ...), custom_call_target="tpu_custom_call" | custom-call | tf_op jit(solution)/shard_map/pallas_call | solution.py:301
  90.5 7.7 fusion.29
  105.7 77.8 %shard_map.431 = (bf16[8,192,1408]{2,1,0:T(8,128)(2,1)}, bf16[8,16,3712]{2,1,0:T(8,128)(2,1)}, bf16[8,64,128]{2,1,0:T(8,128)(2,1)}) custom-call(bf16[192,768]{1,0:T(8,128)(2,1)} %bitcast.210, bf16[192,128]{1,0:T(8,128)(2,1)} %refs_1_.3, bf16[192,128]{1,0:T(8,128)(2,1)} %refs_2_.3, bf16[192,128]{1,0:T(8,128)(2,1)} %refs_3_.3, bf16[192,128]{1,0:T(8,128)(2,1)} %pad.16.refs_4_, ...), custom_call_target="tpu_custom_call" | custom-call | tf_op jit(solution)/shard_map/pallas_call | solution.py:301
  201.3 5.2 collective-permute-done.5.kf_ref.vf_ref
  208.5 34.8 %shard_map.432 = (bf16[768,768]{1,0:T(8,128)(2,1)S(1)}, f32[2,8,768]{2,1,0:T(8,128)S(1)}) custom-call(s32[1]{0:T(128)} %bitcast.11.start_ref, s32[1,768]{1,0:T(1,128)S(1)} %broadcast_in_dim.19.begin_ref, bf16[768,768]{1,0:T(8,128)(2,1)S(1)} %copy.259.q_ref, bf16[768,512]{1,0:T(8,128)(2,1)S(1)} %pad_maximum_fusion.2.ko_ref.vo_ref, ...), custom_call_target="tpu_custom_call" | custom-call | flops 3623878656 | bytes 8388608 | tf_op jit(solution)/shard_map/pallas_call | solution.py:107
  246.6 5.8 convolution_add_fusion
  256.3 4.3 collective-permute-done.6
  260.6 5.3 multiply_reduce_fusion.1
  271.3 5.4 concatenate.48.t_ref
  278.0 32.8 %collective-permute-done.8 = bf16[1,1536,768]{2,1,0:T(8,128)(2,1)} collective-permute-done((bf16[1,1536,768]{2,1,0:T(8,128)(2,1)}, bf16[1,1536,768]{2,1,0:T(8,128)(2,1)}, u32[]{:S(2)}, u32[]{:S(2)}) %collective-permute-start.8) | collective-permute-done | bytes 2359328 | tf_op jit(solution)/shard_map/ppermute | solution.py:566
  317.5 35.7 %shard_map.433 = (bf16[768,1664]{1,0:T(8,128)(2,1)}, bf16[768,1536]{1,0:T(8,128)(2,1)}, f32[128,1536]{1,0:T(8,128)}, f32[256,128]{1,0:T(8,128)}, f32[128,256]{1,...) custom-call(s32[6]{0:T(128)} %stack.44.ids_ref, ...), custom_call_target="tpu_custom_call", output_to_operand_aliasing={{2}: (14, {}), {3}: (15, {}), {4}: (16, {}), {5}: (17, {}),... | custom-call | flops 21139292160 | bytes 25165824 | tf_op jit(solution)/shard_map/pallas_call | solution.py:413
  361.2 36.1 %shard_map.434 = (bf16[768,1664]{1,0:T(8,128)(2,1)}, bf16[768,1536]{1,0:T(8,128)(2,1)}, f32[128,1536]{1,0:T(8,128)}, f32[256,128]{1,0:T(8,128)}, f32[128,256]{1,...) custom-call(s32[6]{0:T(128)} %stack.44.ids_ref, ...), custom_call_target="tpu_custom_call", output_to_operand_aliasing={{2}: (14, {}), {3}: (15, {}), {4}: (16, {}), {5}: (17, {}),... | custom-call | flops 21139292160 | bytes 25165824 | tf_op jit(solution)/shard_map/pallas_call | solution.py:413
  397.3 10.7 %collective-permute-done.12 = bf16[1,1536,768]{2,1,0:T(8,128)(2,1)} collective-permute-done((bf16[1,1536,768]{2,1,0:T(8,128)(2,1)}, bf16[1,1536,768]{2,1,0:T(8,128)(2,1)}, u32[]{:S(2)}, u32[]{:S(2)}) %collective-permute-start.12) | collective-permute-done | bytes 2359328 | tf_op jit(solution)/shard_map/ppermute | solution.py:568
  408.0 27.4 %shard_map.435 = (bf16[768,1664]{1,0:T(8,128)(2,1)}, bf16[768,1536]{1,0:T(8,128)(2,1)}, f32[128,1536]{1,0:T(8,128)}, f32[256,128]{1,0:T(8,128)}, f32[128,256]{1,...) custom-call(s32[4]{0:T(128)} %pad_add_fusion.ids_ref, ...), custom_call_target="tpu_custom_call", output_to_operand_aliasing={{2}: (12, {}), {3}: (13, {}), {4}: (14, {}), {5}: (15, {}),... | custom-call | flops 12683575296 | bytes 25165824 | tf_op jit(solution)/shard_map/pallas_call | solution.py:413
  440.4 27.7 %shard_map.436 = (bf16[768,1664]{1,0:T(8,128)(2,1)}, bf16[768,1536]{1,0:T(8,128)(2,1)}, f32[128,1536]{1,0:T(8,128)}, f32[256,128]{1,0:T(8,128)}, f32[128,256]{1,...) custom-call(s32[4]{0:T(128)} %pad_add_fusion.ids_ref, ...), custom_call_target="tpu_custom_call", output_to_operand_aliasing={{2}: (12, {}), {3}: (13, {}), {4}: (14, {}), {5}: (15, {}),... | custom-call | flops 12683575296 | bytes 25165824 | tf_op jit(solution)/shard_map/pallas_call | solution.py:413
  494.4 4.7 add_convert_fusion.5.do_ref
  499.1 44.2 %shard_map.437 = (f32[768,768]{1,0:T(8,128)}, f32[768,256]{1,0:T(8,128)}, f32[768,256]{1,0:T(8,128)}, bf16[768,256]{1,0:T(8,128)(2,1)}, bf16[768,256]{1,0:T(8,128)(2,1)}) custom-call(s32[1]{0:T(128)} %bitcast.11.start_ref, s32[1,768]{1,0:T(1,128)} %copy-done.6, bf16[768,768]{1,0:T(8,128)(2,1)} %copy-done.4, bf16[768,512]{1,0:T(8,128)(2,1)} %copy-done.5, ...), custom_call_target="tpu_custom_call" | custom-call | flops 9059696640 | bytes 16777216 | tf_op jit(solution)/shard_map/pallas_call | solution.py:178
  556.1 10.9 %collective-permute-done.21 = bf16[768,512]{1,0:T(8,128)(2,1)} collective-permute-done((bf16[768,512]{1,0:T(8,128)(2,1)}, bf16[768,512]{1,0:T(8,128)(2,1)}, u32[]{:S(2)}, u32[]{:S(2)}) %collective-permute-start.21) | collective-permute-done | bytes 786464 | tf_op jit(solution)/shard_map/ppermute | solution.py:681
  631.4 7.6 fusion.100
  644.0 4.8 collective-permute-done.17
  648.8 23.6 %collective-permute-done.19 = bf16[384,1536]{1,0:T(8,128)(2,1)S(1)} collective-permute-done((bf16[384,1536]{1,0:T(8,128)(2,1)S(1)}, bf16[384,1536]{1,0:T(8,128)(2,1)S(1)}, u32[]{:S(2)}, u32[]{:S(2)}) %collective-permute-start.19) | collective-permute-done | bytes 1179680 | tf_op jit(solution)/shard_map/ppermute | solution.py:466
  680.5 49.8 %reduce-scatter.5.cloned.1.call-done = bf16[1,1360,128]{2,1,0:T(8,128)(2,1)} async-done(((bf16[8,1360,128]{2,1,0:T(8,128)(2,1)}), bf16[1,1360,128]{2,1,0:T(8,128)(2,1)}) %reduce-scatter.5.cloned.1.call-update) | async-done | bytes 348176 | tf_op jit(solution)/shard_map/reduce_scatter | solution.py:737
  730.4 8.1 %fusion.2 = bf16[768,1536]{1,0:T(8,128)(2,1)} fusion(f32[768,1536]{1,0:T(8,128)} %copy-done.11, bf16[768,1536]{1,0:T(8,128)(2,1)} %param.31, f32[768]{0:T(1024)S(1)} %multiply_multiply_fusion, f32[768]{0:T(1024)S(1)} %copy-done.72, f32[1536]{0:T(1024)S(1)} %copy-done.67, f32[768,1536]{1,0:T(8,128)} %copy-done.15, f32[768,1536]{1,0:T(8,128)} %copy-done.16), kind=kLoop, calls=%fused_computation.9 | loop fusion | flops 10616832 | bytes 18886656 | tf_op jit(solution)/shard_map/convert_element_type | solution.py:700
  738.4 26.5 %all-reduce.7.cloned.1.call-done = (bf16[896,128]{1,0:T(8,128)(2,1)}, bf16[1360,128]{1,0:T(8,128)(2,1)}) async-done(((bf16[896,128]{1,0:T(8,128)(2,1)}, bf16[1360,128]{1,0:T(8,128)(2,1)}), (bf16[896,128]{1,0:T(8,128)(2,1)}, bf16[1360,128]{1,0:T(8,128)(2,1)})) %all-reduce.7.cloned.1.call-update) | async-done | bytes 577552 | tf_op jit(solution)/shard_map/psum | solution.py:738
  (393 shorter events, 195.9 us)
Async XLA Ops:
  7.2 673.3 %reduce-scatter.3.cloned.1.call-start = ((), (), s32[]{:S(2)}) async-start(), calls=%async_computation.2 | async-start | bytes 2064384 | tf_op jit(solution)/shard_map/reduce_scatter | solution.py:737
  86.7 96.7 %collective-permute-start = (bf16[1,1536,768]{2,1,0:T(8,128)(2,1)}, bf16[1,1536,768]{2,1,0:T(8,128)(2,1)}, u32[]{:S(2)}, u32[]{:S(2)}) collective-permute-start(bf16[1,1536,768]{2,1,0:T(8,128)(2,1)} %pad_maximum_fusion), channel_id=1, source_target_pairs={{0,8},{4,12},{8,16},{12,20},{16,24},{20,28},{24,0},{28,4},{1,9},{5... | collective-permute-start | bytes 7077896 | tf_op jit(solution)/shard_map/ppermute | solution.py:566
  87.3 96.2 %collective-permute-start.1 = (bf16[1,1536,768]{2,1,0:T(8,128)(2,1)}, bf16[1,1536,768]{2,1,0:T(8,128)(2,1)}, u32[]{:S(2)}, u32[]{:S(2)}) collective-permute-start(bf16[1,1536,768]{2,1,0:T(8,128)(2,1)} %pad_maximum_fusion), channel_id=1, source_target_pairs={{0,4},{4,0},{8,12},{12,8},{16,20},{20,16},{24,28},{28,24},{1,5},{5... | collective-permute-start | bytes 7077896 | tf_op jit(solution)/shard_map/ppermute | solution.py:568
  183.5 61.7 %collective-permute-start.3 = (bf16[1,1536,768]{2,1,0:T(8,128)(2,1)}, bf16[1,1536,768]{2,1,0:T(8,128)(2,1)}, u32[]{:S(2)}, u32[]{:S(2)}) collective-permute-start(bf16[1,1536,768]{2,1,0:T(8,128)(2,1)} %collective-permute-done), channel_id=1, source_target_pairs={{0,8},{4,12},{8,16},{12,20},{16,24},{20,28},{24,0},{28,4},{1,9},{5... | collective-permute-start | bytes 7077896 | tf_op jit(solution)/shard_map/ppermute | solution.py:566
  183.6 61.6 %collective-permute-start.4 = (bf16[1,1536,768]{2,1,0:T(8,128)(2,1)}, bf16[1,1536,768]{2,1,0:T(8,128)(2,1)}, u32[]{:S(2)}, u32[]{:S(2)}) collective-permute-start(bf16[1,1536,768]{2,1,0:T(8,128)(2,1)} %collective-permute-done), channel_id=1, source_target_pairs={{0,4},{4,0},{8,12},{12,8},{16,20},{20,16},{24,28},{28,24},{1,5},{5... | collective-permute-start | bytes 7077896 | tf_op jit(solution)/shard_map/ppermute | solution.py:568
  185.1 21.4 %collective-permute-start.5 = (bf16[768,512]{1,0:T(8,128)(2,1)S(1)}, bf16[768,512]{1,0:T(8,128)(2,1)S(1)}, u32[]{:S(2)}, u32[]{:S(2)}) collective-permute-start(bf16[768,512]{1,0:T(8,128)(2,1)S(1)} %pad_maximum_fusion.2.ko_ref.vo_ref), channel_id=1, source_target_pairs={{0,2},{1,3},{4,6},{5,7},{8,10},{9,11},{12,14},{13,15},{16,18},{17,... | collective-permute-start | bytes 2359304 | tf_op jit(solution)/shard_map/ppermute | solution.py:572
  198.1 47.1 %collective-permute-start.2 = (bf16[384,1536]{1,0:T(8,128)(2,1)}, bf16[384,1536]{1,0:T(8,128)(2,1)}, u32[]{:S(2)}, u32[]{:S(2)}) collective-permute-start(bf16[384,1536]{1,0:T(8,128)(2,1)} %constant_dynamic-slice_fusion.6), channel_id=1, source_target_pairs={{0,2},{2,0},{1,3},{3,1},{4,6},{6,4},{5,7},{7,5},{8,10},{10,8},{9,1... | collective-permute-start | bytes 3538952 | tf_op jit(solution)/shard_map/ppermute | solution.py:458
  252.4 8.3 %collective-permute-start.6 = (f32[768,1536]{1,0:T(8,128)}, f32[768,1536]{1,0:T(8,128)}, u32[]{:S(2)}, u32[]{:S(2)}) collective-permute-start(f32[768,1536]{1,0:T(8,128)} %convolution_add_fusion), channel_id=1, source_target_pairs={{0,1},{1,0},{2,3},{3,2},{4,5},{5,4},{6,7},{7,6},{8,9},{9,8},{10,11... | collective-permute-start | bytes 14155784 | tf_op jit(solution)/shard_map/ppermute | solution.py:480
  254.9 56.0 %collective-permute-start.8 = (bf16[1,1536,768]{2,1,0:T(8,128)(2,1)}, bf16[1,1536,768]{2,1,0:T(8,128)(2,1)}, u32[]{:S(2)}, u32[]{:S(2)}) collective-permute-start(bf16[1,1536,768]{2,1,0:T(8,128)(2,1)} %collective-permute-done.3), channel_id=1, source_target_pairs={{0,8},{4,12},{8,16},{12,20},{16,24},{20,28},{24,0},{28,4},{1,9},{5... | collective-permute-start | bytes 7077896 | tf_op jit(solution)/shard_map/ppermute | solution.py:566
  254.9 56.0 %collective-permute-start.9 = (bf16[1,1536,768]{2,1,0:T(8,128)(2,1)}, bf16[1,1536,768]{2,1,0:T(8,128)(2,1)}, u32[]{:S(2)}, u32[]{:S(2)}) collective-permute-start(bf16[1,1536,768]{2,1,0:T(8,128)(2,1)} %collective-permute-done.3), channel_id=1, source_target_pairs={{0,4},{4,0},{8,12},{12,8},{16,20},{20,16},{24,28},{28,24},{1,5},{5... | collective-permute-start | bytes 7077896 | tf_op jit(solution)/shard_map/ppermute | solution.py:568
  310.8 42.4 %collective-permute-start.7 = (bf16[384,1664]{1,0:T(8,128)(2,1)S(1)}, bf16[384,1664]{1,0:T(8,128)(2,1)S(1)}, u32[]{:S(2)}, u32[]{:S(2)}) collective-permute-start(bf16[384,1664]{1,0:T(8,128)(2,1)S(1)} %constant_dynamic-slice_fusion.5), channel_id=1, source_target_pairs={{0,2},{2,0},{1,3},{3,1},{4,6},{6,4},{5,7},{7,5},{8,10},{10,8},{9,1... | collective-permute-start | bytes 3833864 | tf_op jit(solution)/shard_map/ppermute | solution.py:458
  353.3 4.0 collective-permute-start.11
  353.3 4.8 collective-permute-start.10
  354.4 53.5 %collective-permute-start.12 = (bf16[1,1536,768]{2,1,0:T(8,128)(2,1)}, bf16[1,1536,768]{2,1,0:T(8,128)(2,1)}, u32[]{:S(2)}, u32[]{:S(2)}) collective-permute-start(bf16[1,1536,768]{2,1,0:T(8,128)(2,1)} %collective-permute-done.8), channel_id=1, source_target_pairs={{0,4},{4,0},{8,12},{12,8},{16,20},{20,16},{24,28},{28,24},{1,5},{5... | collective-permute-start | bytes 7077896 | tf_op jit(solution)/shard_map/ppermute | solution.py:568
  436.9 3.1 collective-permute-start.13
  440.3 30.2 %collective-permute-start.14 = (bf16[384,1664]{1,0:T(8,128)(2,1)S(1)}, bf16[384,1664]{1,0:T(8,128)(2,1)S(1)}, u32[]{:S(2)}, u32[]{:S(2)}) collective-permute-start(bf16[384,1664]{1,0:T(8,128)(2,1)S(1)} %add_convert_fusion.2), channel_id=1, source_target_pairs={{0,2},{2,0},{1,3},{3,1},{4,6},{6,4},{5,7},{7,5},{8,10},{10,8},{9,1... | collective-permute-start | bytes 3833864 | tf_op jit(solution)/shard_map/ppermute | solution.py:656
  472.1 3.1 collective-permute-start.15
  545.3 21.8 %collective-permute-start.21 = (bf16[768,512]{1,0:T(8,128)(2,1)}, bf16[768,512]{1,0:T(8,128)(2,1)}, u32[]{:S(2)}, u32[]{:S(2)}) collective-permute-start(bf16[768,512]{1,0:T(8,128)(2,1)} %pad_maximum_fusion.3), channel_id=1, source_target_pairs={{2,0},{3,1},{6,4},{7,5},{10,8},{11,9},{14,12},{15,13},{18,16},{19,... | collective-permute-start | bytes 2359304 | tf_op jit(solution)/shard_map/ppermute | solution.py:681
  589.4 140.9 %reduce-scatter.5.cloned.1.call-start = ((), (), s32[]{:S(2)}) async-start(), calls=%async_computation.3 | async-start | bytes 3133440 | tf_op jit(solution)/shard_map/reduce_scatter | solution.py:737
  616.1 23.6 %collective-permute-start.18 = (bf16[384,1536]{1,0:T(8,128)(2,1)}, bf16[384,1536]{1,0:T(8,128)(2,1)}, u32[]{:S(2)}, u32[]{:S(2)}) collective-permute-start(bf16[384,1536]{1,0:T(8,128)(2,1)} %constant_dynamic-slice_fusion), channel_id=1, source_target_pairs={{0,1},{1,0},{2,3},{3,2},{4,5},{5,4},{6,7},{7,6},{8,9},{9,8},{10,11... | collective-permute-start | bytes 3538952 | tf_op jit(solution)/shard_map/ppermute | solution.py:463
  626.5 138.5 %all-reduce.7.cloned.1.call-start = ((), (), s32[]{:S(2)}) async-start(), calls=%async_computation.4 | async-start | bytes 1155072 | tf_op jit(solution)/shard_map/psum | solution.py:738
  639.0 39.3 %collective-permute-start.22 = (f32[768,1536]{1,0:T(8,128)S(1)}, f32[768,1536]{1,0:T(8,128)S(1)}, u32[]{:S(2)}, u32[]{:S(2)}) collective-permute-start(f32[768,1536]{1,0:T(8,128)S(1)} %fusion.100), channel_id=1, source_target_pairs={{0,1},{1,0},{2,3},{3,2},{4,5},{5,4},{6,7},{7,6},{8,9},{9,8},{10,11... | collective-permute-start | bytes 14155784 | tf_op jit(solution)/shard_map/ppermute | solution.py:480
  639.6 9.1 %collective-permute-start.17 = (bf16[384,1536]{1,0:T(8,128)(2,1)S(1)}, bf16[384,1536]{1,0:T(8,128)(2,1)S(1)}, u32[]{:S(2)}, u32[]{:S(2)}) collective-permute-start(bf16[384,1536]{1,0:T(8,128)(2,1)S(1)} %constant_dynamic-slice_fusion.1), channel_id=1, source_target_pairs={{0,1},{1,0},{2,3},{3,2},{4,5},{5,4},{6,7},{7,6},{8,9},{9,8},{10,11... | collective-permute-start | bytes 3538952 | tf_op jit(solution)/shard_map/ppermute | solution.py:463
  643.9 28.4 %collective-permute-start.19 = (bf16[384,1536]{1,0:T(8,128)(2,1)S(1)}, bf16[384,1536]{1,0:T(8,128)(2,1)S(1)}, u32[]{:S(2)}, u32[]{:S(2)}) collective-permute-start(bf16[384,1536]{1,0:T(8,128)(2,1)S(1)} %add_convert_fusion.4), channel_id=1, source_target_pairs={{0,2},{2,0},{1,3},{3,1},{4,6},{6,4},{5,7},{7,5},{8,10},{10,8},{9,1... | collective-permute-start | bytes 3538952 | tf_op jit(solution)/shard_map/ppermute | solution.py:466
  (83 other events, 861.0 us)
Sparse Core Ops, SparseCore 0:
  589.5 63.8 reduce-scatter.2
  657.4 72.9 reduce-scatter.4
  732.9 32.0 all-reduce.6

commit v5 on v4

--- a/solution.py
+++ b/solution.py
@@ -196,15 +196,12 @@
     return pl.ds(pl.multiple_of(ctx * edge, 16), take), pl.ds(pl.multiple_of(ctx * take, 16), edge)
 
 
-def gather_kernel(n, layout, *refs):
-    total = sum(len(parts) for parts in layout)
-    count = len(layout)
-    ins, outs = refs[:total], refs[total : total + count]
-    own_sem, z_send, z_recv, y_send, y_recv, x_send, x_recv = refs[total + count :]
+def gather_kernel(n, count, *refs):
+    ins, outs = refs[:count], refs[count : 2 * count]
+    own_sem, z_send, z_recv, y_send, y_recv, x_send, x_recv = refs[2 * count :]
     outer, inner = levels(n)
     me = lax.axis_index("fsdp")
     ctx = lax.axis_index("ctx")
-    tp = lax.axis_index("tp")
     z, y = me // inner, me % inner
     right = (z + 1) % outer * inner + y
     left = (z + outer - 1) % outer * inner + y
@@ -212,17 +209,7 @@
     def shard(do, dj):
         return (z + outer - do) % outer * inner + (y + inner - dj) % inner
 
-    own = []
-    at = 0
-    for a, parts in enumerate(layout):
-        col = 0
-        for cols, split in parts:
-            src = ins[at].at[:, pl.ds(pl.multiple_of(tp * cols, LANES), cols)] if split else ins[at]
-            own.append(pltpu.make_async_copy(src, outs[a].at[me, :, pl.ds(col, cols)], own_sem.at[at]))
-            own[-1].start()
-            col += cols
-            at += 1
-
+    own = [pltpu.make_async_copy(ins[a], outs[a].at[me], own_sem.at[a]) for a in range(count)]
     barrier = pltpu.get_barrier_semaphore()
     peers = [right, left] + [z * inner + (y + dj) % inner for dj in range(1, inner)]
     for peer in peers:
@@ -238,15 +225,21 @@
             return outs[a].at[k]
         return outs[a].at[k, slab_of(outs[a].shape[1], ctx)[0]]
 
-    def remote(part, send, recv, to):
-        return pltpu.make_async_remote_copy(src_ref=part, dst_ref=part, send_sem=send, recv_sem=recv, device_id=to, device_id_type=MESH)
+    def remote(part, send, recv, to, src=None):
+        src = part if src is None else src
+        return pltpu.make_async_remote_copy(src_ref=src, dst_ref=part, send_sem=send, recv_sem=recv, device_id=to, device_id_type=MESH)
+
+    def from_own(a):
+        return ins[a].at[slab_of(ins[a].shape[0], ctx)[0]] if cut(a) else ins[a]
 
     def z_copy(a, k):
-        return remote(taken(a, shard(k - 1, 0)), z_send.at[a, k - 1], z_recv.at[a, k - 1], {"fsdp": right})
+        src = from_own(a) if k == 1 else None
+        return remote(taken(a, shard(k - 1, 0)), z_send.at[a, k - 1], z_recv.at[a, k - 1], {"fsdp": right}, src)
 
     def y_copy(a, do, dj):
         to = {"fsdp": z * inner + (y + dj) % inner}
-        return remote(taken(a, shard(do, 0)), y_send.at[a, do, dj - 1], y_recv.at[a, do, dj - 1], to)
+        src = from_own(a) if do == 0 else None
+        return remote(taken(a, shard(do, 0)), y_send.at[a, do, dj - 1], y_recv.at[a, do, dj - 1], to, src)
 
     def x_copy(a, do, dj):
         part = outs[a].at[shard(do, dj), slab_of(outs[a].shape[1], ctx)[1]]
@@ -258,12 +251,12 @@
         copy.start()
         started.append(copy)
 
-    for c in own:
-        c.wait()
     for a in range(count):
         go(z_copy(a, 1))
         for dj in range(1, inner):
             go(y_copy(a, 0, dj))
+    for c in own:
+        c.start()
     for do in range(1, outer + 1):
         for a in range(count):
             if do < outer:
@@ -287,24 +280,29 @@
                         x_copy(a, do, dj).wait_recv()
     for c in started:
         c.wait_send()
+    for c in own:
+        c.wait()
 
 
 def gather_packs(packs, collective_id):
     n = lax.axis_size("fsdp")
     outer, inner = levels(n)
     count = len(packs)
-    layout = [[(cols, cols != a.shape[1]) for a, cols in parts] for parts in packs]
-    arrays = [a for parts in packs for a, cols in parts]
+    tp_at = lax.axis_index("tp")
+    arrays = []
+    for parts in packs:
+        cut = [a if cols == a.shape[1] else lax.dynamic_slice_in_dim(a, tp_at * cols, cols, 1) for a, cols in parts]
+        arrays.append(jnp.concatenate(cut, axis=1) if len(cut) > 1 else cut[0])
     dma = pltpu.SemaphoreType.DMA
     anywhere = pl.BlockSpec(memory_space=pl.ANY)
     side = max(inner - 1, 1)
     return pl.pallas_call(
-        functools.partial(gather_kernel, n, layout),
-        in_specs=[anywhere] * len(arrays),
+        functools.partial(gather_kernel, n, count),
+        in_specs=[anywhere] * count,
         out_specs=[anywhere] * count,
-        out_shape=[jax.ShapeDtypeStruct((n, parts[0][0].shape[0], sum(cols for a, cols in parts)), BF) for parts in packs],
+        out_shape=[jax.ShapeDtypeStruct((n,) + a.shape, a.dtype) for a in arrays],
         scratch_shapes=[
-            dma((len(arrays),)), dma((count, outer - 1)), dma((count, outer - 1)),
+            dma((count,)), dma((count, outer - 1)), dma((count, outer - 1)),
             dma((count, outer, side)), dma((count, outer, side)), dma((count, outer, inner)), dma((count, outer, inner)),
         ],
         compiler_params=pltpu.CompilerParams(collective_id=collective_id, has_side_effects=True),
@@ -462,16 +460,299 @@
             return block.astype(F32)
         return self.half(block).astype(F32) + lax.ppermute(self.other_half(block), "tp", [(0, 1), (1, 0)]).astype(F32)
 
-    def give(self, block, by):
-        return lax.ppermute(self.summed_half(block).astype(BF), "ctx", self.pairs(-by))
-
-    def total(self, own, parts):
+    def swapped(self, blocks):
+        if self.n_tp != 2:
+            return [jnp.zeros_like(b) for b in blocks]
+        return [lax.ppermute(self.other_half(b), "tp", [(0, 1), (1, 0)]) for b in blocks]
+
+    def halves_of_total(self, own, parts):
         found = self.summed_half(own)
         for part in parts:
             found = found + part.astype(F32)
         if self.n_tp != 2:
-            return lax.psum(found, "tp")
-        return self.joined(found.astype(BF)).astype(F32)
+            found = lax.psum(found, "tp").astype(BF)
+            size = found.shape[0] // 2
+            return found[:size], found[size:], 0
+        found = found.astype(BF)
+        return found, lax.ppermute(found, "tp", [(0, 1), (1, 0)]), self.tp_at
+
+
+def put_rows(pack, value, at, height):
+    for f in range(pack.shape[0]):
+        pack[f, pl.ds(at, height), :] = value[f * height : (f + 1) * height, :]
+
+
+def put_cols(pack, value, at, height, first):
+    for i in range(value.shape[1] // LANES):
+        for f in range(pack.shape[0]):
+            spot = pl.ds(pl.multiple_of(at + (first + i) * height, 8), height)
+            pack[f, spot, :] = value[f * height : (f + 1) * height, i * LANES : (i + 1) * LANES]
+
+
+def adapter_mask(chosen_ref):
+    rows = chosen_ref.shape[0]
+    return (lax.broadcasted_iota(jnp.int32, (rows, LANES), 1) // ADAPTER_RANK == chosen_ref[...]).astype(F32)
+
+
+def qkv_back_kernel(n_tp, low_rows, share, tp_ref, dq_ref, dko_ref, dvo_ref, fb_ref, cos_ref, sin_ref, n1_ref, u_ref, chosen_ref, w_ref, lb_ref, dn1_ref, pack_ref, a_acc, b_acc):
+    q_width, kv_width = dq_ref.shape[1], dko_ref.shape[1]
+    ranks = LANES
+    rows = dq_ref.shape[0]
+    step = pl.program_id(0)
+    mask = adapter_mask(chosen_ref)
+    head = lax.broadcasted_iota(jnp.int32, (rows, LANES), 1) % HEAD_SIZE < HEAD_SIZE // 2
+
+    def turned_back(v):
+        swapped = jnp.where(head, pltpu.roll(v, LANES - HEAD_SIZE // 2, 1), pltpu.roll(v, HEAD_SIZE // 2, 1))
+        return (v * cos_ref[...] - swapped * sin_ref[...]).astype(BF)
+
+    dq = [turned_back(dq_ref[:, i : i + LANES]) for i in range(0, q_width, LANES)]
+    dk = [turned_back(dko_ref[:, i : i + LANES] + fb_ref[:, i : i + LANES].astype(F32)) for i in range(0, kv_width, LANES)]
+    dv = (dvo_ref[...] + fb_ref[:, kv_width:].astype(F32)).astype(BF)
+    dq = jnp.concatenate(dq, axis=1)
+    dk = jnp.concatenate(dk, axis=1) if len(dk) > 1 else dk[0]
+    lows = []
+    at = 0
+    for d in (dq, dk, dv):
+        lows.append((dot_t(d, lb_ref[:, at : at + d.shape[1]]) * mask).astype(BF))
+        at += d.shape[1]
+    lows = jnp.concatenate(lows, axis=1)
+    dn1_ref[...] = dot_t(jnp.concatenate([dq, dk, dv, lows], axis=1), w_ref[...]).astype(BF)
+    n1 = n1_ref[...]
+    parts = [
+        (a_acc, slice(0, 3 * ranks), t_dot_k(n1, lows)),
+        (b_acc, slice(0, q_width), t_dot_k(u_ref[:, :ranks], dq)),
+        (b_acc, slice(q_width, q_width + kv_width), t_dot_k(u_ref[:, ranks : 2 * ranks], dk)),
+        (b_acc, slice(q_width + kv_width, q_width + 2 * kv_width), t_dot_k(u_ref[:, 2 * ranks :], dv)),
+    ]
+
+    @pl.when(step == 0)
+    def _():
+        for acc, cols, value in parts:
+            acc[:, cols] = value
+
+    @pl.when(step > 0)
+    def _():
+        for acc, cols, value in parts:
+            acc[:, cols] += value
+
+    @pl.when(step == pl.num_programs(0) - 1)
+    def _():
+        pack_ref[...] = jnp.zeros_like(pack_ref)
+        at, col = 0, 0
+        for i, cols in enumerate((q_width, kv_width, kv_width)):
+            put_rows(pack_ref, a_acc[:, i * ranks : (i + 1) * ranks], at, share)
+            at += share
+            put_cols(pack_ref, b_acc[:, col : col + cols], at, low_rows, tp_ref[0] * (cols // LANES))
+            at += cols * n_tp // LANES * low_rows
+            col += cols
+
+
+def qkv_back(n, n_tp, low_rows, share, tp_at, dq, dko, dvo, fb, cos, sin, n1, u3, chosen, w_one, low_one, height):
+    rows, q_width = dq.shape
+    width = n1.shape[1]
+    step = 256
+    by_row = lambda a: pl.BlockSpec((step, a.shape[1]), lambda i: (i, 0))
+    whole = lambda a: pl.BlockSpec(a.shape, lambda i: (0, 0), pipeline_mode=pl.Buffered(1))
+    sd = jax.ShapeDtypeStruct
+    return pl.pallas_call(
+        functools.partial(qkv_back_kernel, n_tp, low_rows, share),
+        grid=(rows // step,),
+        in_specs=[pl.BlockSpec(memory_space=pltpu.SMEM)] + [by_row(a) for a in (dq, dko, dvo, fb, cos, sin, n1, u3, chosen)] + [whole(w_one), whole(low_one)],
+        out_specs=[pl.BlockSpec((step, width), lambda i: (i, 0)), pl.BlockSpec((n, height, LANES), lambda i: (0, 0, 0))],
+        out_shape=[sd((rows, width), BF), sd((n, height, LANES), F32)],
+        scratch_shapes=[pltpu.VMEM((width, 3 * LANES), F32), pltpu.VMEM((LANES, low_one.shape[1]), F32)],
+        compiler_params=pltpu.CompilerParams(vmem_limit_bytes=50 << 20),
+        cost_estimate=pl.CostEstimate(flops=4 * rows * width * w_one.shape[1], bytes_accessed=24 << 20, transcendentals=0),
+    )(tp_at, dq, dko, dvo, fb, cos, sin, n1, u3, chosen, w_one, low_one)
+
+
+def mid_back_kernel(n, n_tp, experts, share, low_rows, sel_ref, mine_ref, other_ref, h_ref, c_ref, t_ref, o_ref, ou_ref, ru_ref, chosen_ref, gain_ref,
+                    w_ref, low_ref, oa_ref, bd_ref, ad_ref, bg_ref, bu_ref, agu_ref, dh_ref, do_ref, pack_ref, ar_acc, ao_acc, bo_acc, br_acc):
+    width = h_ref.shape[1]
+    q_width = o_ref.shape[1]
+    ff = bg_ref.shape[1]
+    spare = mine_ref.shape[1] - width
+    step = pl.program_id(0)
+    mask = adapter_mask(chosen_ref)
+    picked = step == sel_ref[0]
+
+    def fold(height, top):
+        lane = lax.broadcasted_iota(jnp.int32, (height, LANES), 0)
+        return ((lane % experts == lax.broadcasted_iota(jnp.int32, (height, LANES), 1)) & (lane < top)).astype(BF)
+
+    back = jnp.where(picked, mine_ref[:, :width].astype(F32), other_ref[:, :width].astype(F32))
+    tail = jnp.where(picked, mine_ref[:, width:].astype(F32), other_ref[:, width:].astype(F32)).astype(BF)
+    dgate = dot(tail, fold(spare, 2 * experts * n_tp))
+    gates = dot(t_ref[:, width:], fold(LANES, 2 * experts))
+    n2 = t_ref[:, :width]
+    router_a, router_w = w_ref[:, q_width : q_width + LANES], w_ref[:, q_width + 3 * LANES : q_width + 4 * LANES]
+    out_b, router_b = low_ref[:, 2 * ff : 2 * ff + width], low_ref[:, 2 * ff + 2 * width :]
+    dlog = (gates * (dgate - jnp.sum(gates * dgate, axis=1, keepdims=True))).astype(BF)
+    rdu = (dot_t(dlog, router_b) * mask).astype(BF)
+    dn2 = back + dot_t(dlog, router_w) + dot_t(rdu, router_a)
+    h = h_ref[...]
+    r = lax.rsqrt(jnp.mean(h * h, axis=1, keepdims=True) + norm_eps)
+    gd = dn2 * gain_ref[...]
+    dh = c_ref[...].astype(F32) + r * gd - h * (r * r * r * jnp.mean(gd * h, axis=1, keepdims=True))
+    dh_ref[...] = dh
+    dattn = dh.astype(BF)
+    odu = (dot_t(dattn, out_b) * mask).astype(BF)
+    do_ref[...] = (dot(dattn, w_ref[:, :q_width]) + dot_t(odu, oa_ref[...])).astype(BF)
+    parts = [
+        (ar_acc, t_dot_k(n2, rdu)),
+        (ao_acc, t_dot_k(o_ref[...], odu)),
+        (bo_acc, t_dot_k(ou_ref[...], dattn)),
+        (br_acc, t_dot_k(ru_ref[...], dlog)),
+    ]
+
+    @pl.when(step == 0)
+    def _():
+        for acc, value in parts:
+            acc[...] = value
+
+    @pl.when(step > 0)
+    def _():
+        for acc, value in parts:
+            acc[...] += value
+
+    @pl.when(step == pl.num_programs(0) - 1)
+    def _():
+        pack_ref[...] = jnp.zeros_like(pack_ref)
+        tp = sel_ref[1]
+        first = (tp == 0).astype(F32)
+        own = n // n_tp
+        at = 0
+        for k in range(own):
+            pack_ref[tp * own + k, pl.ds(at, share), :] = ao_acc[k * share : (k + 1) * share, :]
+        at += share
+        put_cols(pack_ref, bo_acc, at, low_rows, 0)
+        at += width // LANES * low_rows
+        ar_acc[...] = ar_acc[...] * first
+        put_rows(pack_ref, ar_acc, at, share)
+        at += share
+        br_acc[...] = br_acc[...] * first
+        put_cols(pack_ref, br_acc, at, low_rows, 0)
+        at += low_rows
+        for i, ref in enumerate((bg_ref, bu_ref)):
+            put_rows(pack_ref, agu_ref[:, i * LANES : (i + 1) * LANES], at, share)
+            at += share
+            put_cols(pack_ref, ref, at, low_rows, tp * (ff // LANES))
+            at += ff * n_tp // LANES * low_rows
+        size = ad_ref.shape[0] // own
+        for k in range(own):
+            pack_ref[tp * own + k, pl.ds(at, size), :] = ad_ref[k * size : (k + 1) * size, :]
+        at += size
+        put_cols(pack_ref, bd_ref, at, low_rows, 0)
+
+
+def mid_back(n, n_tp, experts, share, low_rows, sel, mine, other, hidden, cot, carried, mixed, out_u, router_u, chosen, gain, w_two, low_two, out_a, sums, height):
+    rows, width = hidden.shape
+    q_width = mixed.shape[1]
+    step = rows // 2
+    sd = jax.ShapeDtypeStruct
+    by_row = lambda a: pl.BlockSpec((step, a.shape[1]), lambda i: (i, 0))
+    whole = lambda a: pl.BlockSpec(a.shape, lambda i: (0, 0), pipeline_mode=pl.Buffered(1))
+    return pl.pallas_call(
+        functools.partial(mid_back_kernel, n, n_tp, experts, share, low_rows),
+        grid=(2,),
+        in_specs=[pl.BlockSpec(memory_space=pltpu.SMEM), whole(mine), whole(other)]
+        + [by_row(a) for a in (hidden, cot, carried, mixed, out_u, router_u, chosen)]
+        + [whole(a) for a in (gain, w_two, low_two, out_a, *sums)],
+        out_specs=[by_row(hidden), by_row(mixed), pl.BlockSpec((n, height, LANES), lambda i: (0, 0, 0))],
+        out_shape=[sd((rows, width), F32), sd((rows, q_width), BF), sd((n, height, LANES), F32)],
+        scratch_shapes=[pltpu.VMEM((width, LANES), F32), pltpu.VMEM((q_width, LANES), F32), pltpu.VMEM((LANES, width), F32), pltpu.VMEM((LANES, LANES), F32)],
+        compiler_params=pltpu.CompilerParams(vmem_limit_bytes=58 << 20),
+        cost_estimate=pl.CostEstimate(flops=8 * rows * width * q_width, bytes_accessed=32 << 20, transcendentals=0),
+    )(sel, mine, other, hidden, cot, carried, mixed, out_u, router_u, chosen, gain, w_two, low_two, out_a, *sums)
+
+
+def reduce_kernel(n, pack_ref, side_ref, out_ref, side_out, side_in, side_snd, snd1, rcv1, acc, snd2, rcv2, acc2, snd3, rcv3, fin, sems, send3, recv3):
+    me = lax.axis_index("fsdp")
+    ctx = lax.axis_index("ctx")
+    tp = lax.axis_index("tp")
+    half = pack_ref.shape[1] // 2
+    part = half // 2
+    barrier = pltpu.get_barrier_semaphore()
+    pl.semaphore_signal(barrier, inc=1, device_id={"tp": 1 - tp}, device_id_type=MESH)
+    pl.semaphore_signal(barrier, inc=1, device_id={"ctx": 1 - ctx}, device_id_type=MESH)
+    for k in range(1, n):
+        pl.semaphore_signal(barrier, inc=1, device_id={"fsdp": (me + k) % n}, device_id_type=MESH)
+    snd1[...] = pack_ref[:, pl.ds(pl.multiple_of((1 - tp) * half, 16), half), :].astype(BF)
+    pl.semaphore_wait(barrier, n + 1)
+
+    def swap(src, dst, i, to):
+        copy = pltpu.make_async_remote_copy(src_ref=src, dst_ref=dst, send_sem=sems.at[0, i], recv_sem=sems.at[1, i], device_id=to, device_id_type=MESH)
+        copy.start()
+        return copy
+
+    copy = swap(snd1, rcv1, 0, {"tp": 1 - tp})
+    side = swap(side_ref, side_in.at[0], 4, {"tp": 1 - tp})
+    copy.wait()
+    acc[...] = pack_ref[:, pl.ds(pl.multiple_of(tp * half, 16), half), :] + rcv1[...].astype(F32)
+    snd2[...] = acc[:, pl.ds(pl.multiple_of((1 - ctx) * part, 16), part), :].astype(BF)
+    copy = swap(snd2, rcv2, 1, {"ctx": 1 - ctx})
+    side.wait()
+    side_snd[...] = (side_ref[...].astype(F32) + side_in[0].astype(F32)).astype(BF)
+    side = swap(side_snd, side_in.at[1], 5, {"ctx": 1 - ctx})
+    copy.wait()
+    acc2[...] = acc[:, pl.ds(pl.multiple_of(ctx * part, 16), part), :] + rcv2[...].astype(F32)
+    snd3[...] = acc2[...].astype(BF)
+
+    def ship(k):
+        to = (me + k) % n
+        return pltpu.make_async_remote_copy(
+            src_ref=snd3.at[to], dst_ref=rcv3.at[me], send_sem=send3.at[k], recv_sem=recv3.at[k], device_id={"fsdp": to}, device_id_type=MESH
+        )
+
+    def came(k):
+        return pltpu.make_async_remote_copy(
+            src_ref=snd3.at[me], dst_ref=rcv3.at[(me + n - k) % n], send_sem=send3.at[k], recv_sem=recv3.at[k],
+            device_id={"fsdp": (me + k) % n}, device_id_type=MESH,
+        )
+
+    for k in range(1, n):
+        ship(k).start()
+    total = acc2[me]
+    for k in range(1, n):
+        came(k).wait_recv()
+        total = total + rcv3[(me + n - k) % n].astype(F32)
+    for k in range(1, n):
+        ship(k).wait_send()
+    spot = tp * 2 + ctx
+    fin[spot] = total.astype(BF)
+    copy = swap(fin.at[spot], fin.at[spot], 2, {"ctx": 1 - ctx})
+    copy.wait()
+    both = fin.at[pl.ds(tp * 2, 2)]
+    copy = swap(both, both, 3, {"tp": 1 - tp})
+    copy.wait()
+    for i in range(4):
+        out_ref[pl.ds(i * part, part), :] = fin[i].astype(F32)
+    side.wait()
+    side_out[...] = side_snd[...].astype(F32) + side_in[1].astype(F32)
+
+
+def reduce_pack(pack, side, collective_id):
+    n, height = pack.shape[:2]
+    if lax.axis_size("tp") != 2 or lax.axis_size("ctx") != 2 or height % 64 or side.shape[0] % 16:
+        mine = lax.psum_scatter(pack.astype(BF), "fsdp", scatter_dimension=0, tiled=False)
+        return lax.psum(mine, ("ctx", "tp")).astype(F32), lax.psum(side, ("ctx", "tp")).astype(F32)
+    half, part = height // 2, height // 4
+    vm = pltpu.VMEM
+    dma = pltpu.SemaphoreType.DMA
+    return pl.pallas_call(
+        functools.partial(reduce_kernel, n),
+        in_specs=[pl.BlockSpec(memory_space=vm)] * 2,
+        out_specs=[pl.BlockSpec(memory_space=vm)] * 2,
+        out_shape=[jax.ShapeDtypeStruct((height, LANES), F32), jax.ShapeDtypeStruct(side.shape, F32)],
+        scratch_shapes=[
+            vm((2,) + side.shape, BF), vm(side.shape, BF), vm((n, half, LANES), BF), vm((n, half, LANES), BF), vm((n, half, LANES), F32),
+            vm((n, part, LANES), BF), vm((n, part, LANES), BF), vm((n, part, LANES), F32),
+            vm((n, part, LANES), BF), vm((n, part, LANES), BF), vm((4, part, LANES), BF),
+            dma((2, 6)), dma((n,)), dma((n,)),
+        ],
+        compiler_params=pltpu.CompilerParams(collective_id=collective_id, has_side_effects=True, vmem_limit_bytes=48 << 20),
+    )(pack, side)
 
 
 def tp_sum(value):
@@ -609,7 +890,6 @@
     selected = jnp.any(routes[:, :, None] == jnp.arange(experts, dtype=jnp.int32)[None, None, :], axis=1)
     gates = jax.nn.softmax(jnp.where(selected, logits, -jnp.inf), axis=-1)
 
-    dout = cot.astype(F32)
     high = gates.astype(BF)
     spare = -(-2 * experts * n_tp // LANES) * LANES
     carried = jnp.concatenate(
@@ -623,8 +903,6 @@
         axis=1,
     )
     halves = cross.fetch(carried)
-    for do in range(3, outer):
-        carried = bring(do, carried)
     early = [(0, 0), (1, 0)] + [(0, dj) for dj in range(1, inner)] + [(2, 0)] + [(1, dj) for dj in range(1, inner)]
     late = [(do, 0) for do in range(3, outer)] + [(do, dj) for do in range(2, outer) for dj in range(1, inner)]
 
@@ -642,6 +920,8 @@
             work[by] = (cross.joined(halves[by - 1]), cross.joined(cot_halves[by - 1]))
         r, m, sums = experts_on(ids, experts, spare, *work[by], weights, w_two, at, low_two, down_b, down_at, sums)
         if by == 0:
+            for do in range(3, outer):
+                r = bring(do, r)
             halves, cot_halves, r = lax.optimization_barrier((halves, cot_halves, r))
         partial.append((r, m))
     ids, weights = weights_of(late)
@@ -655,98 +935,60 @@
             work[0] = (carried, cot)
             back_parts.append(lax.ppermute(half, "ctx", cross.pairs(-by)))
     r, back_parts = lax.optimization_barrier((r, back_parts))
-    back = cross.total(r, back_parts)
-    dn2 = back[:, :width]
-    dgate = jnp.sum(back[:, width : width + 2 * experts * n_tp].reshape(rows, 2 * n_tp, experts), axis=1)
-    grad_bd, grad_ad, grad_bg, grad_bu, grad_agu = sums
-    grad_ag, grad_au = grad_agu[:, :ranks], grad_agu[:, ranks:]
-    dlogits = (gates * (dgate - jnp.sum(gates * dgate, axis=-1, keepdims=True))).astype(BF)
-    dlogits = jnp.pad(dlogits, ((0, 0), (0, LANES - experts)))
-    router_du = (dot_t(dlogits, router_b) * mask).astype(BF)
-    dn2 = dn2 + dot_t(dlogits, router_w) + dot_t(router_du, router_a)
-    grad_br = t_dot(router_u, dlogits)[:, :experts]
-    grad_ar = t_dot(normed_two, router_du)
-    dhidden = dout + norm_back(hidden, ffn_gain, dn2)
-    dattn = dhidden.astype(BF)
-    out_du = (dot_t(dattn, out_b) * mask).astype(BF)
-    dmixed = (dot(dattn, out_wt) + dot_t(out_du, out_a)).astype(BF)
-    grad_bo = t_dot(out_u.astype(BF), dattn)
-    grad_ao = t_dot(mixed_heads, out_du)
+    mine_half, other, first = cross.halves_of_total(r, back_parts)
+    swapped = cross.swapped(moe_parts)
+    early_shapes = [
+        (share, ranks), (low_rows, width), (share, ranks), (low_rows, experts), (share, ranks), (low_rows, ff_width * n_tp),
+        (share, ranks), (low_rows, ff_width * n_tp), (a_down.shape[0], ranks), (low_rows, width),
+    ]
+    height = sum(-(-cols // LANES) * tall for tall, cols in early_shapes)
+    sel = jnp.stack([jnp.asarray(first, jnp.int32), tp_at.astype(jnp.int32)])
+    dhidden, dmixed, early_pack = mid_back(
+        n, n_tp, experts, share, low_rows, sel, mine_half, other, hidden, cot, carried, mixed_heads, out_u.astype(BF), router_u,
+        chosen_local[:, None], ffn_gain[None, :], w_two, low_two, out_a, sums, height,
+    )
+    early_pack, dmixed, swapped = lax.optimization_barrier((early_pack.astype(BF), dmixed, swapped))
+    moe_halves = [cross.half(p).astype(F32) + q.astype(F32) for p, q in zip(moe_parts, swapped)]
+    moe_got = [lax.ppermute(p.astype(BF), "ctx", cross.pairs(-by)) for by, p in zip(range(1, cross.n_ctx), moe_halves)]
+    early_sum = lax.psum_scatter(early_pack, "fsdp", scatter_dimension=0, tiled=False)
     dquery, dkey_own, dvalue_own, dkey_far, dvalue_far = attend_back(
         query_state, kv, far, begin_row, start_at, mixed_heads, dmixed, log_total
     )
-    moe_parts, dquery = lax.optimization_barrier((moe_parts, dquery))
-    moe = cross.total(moe_parts[-1], [cross.give(p, by) for by, p in zip(range(1, cross.n_ctx), moe_parts)])
+    moe_got, dquery = lax.optimization_barrier((moe_got, dquery))
+    moe = moe_halves[-1]
+    for part in moe_got:
+        moe = moe + part.astype(F32)
+    moe = cross.joined(moe.astype(BF)).astype(F32) if n_tp == 2 else lax.psum(moe, "tp")
     output = (hidden + moe).astype(BF)
     far_back = lax.ppermute(
         jnp.concatenate([dkey_far, dvalue_far], axis=1),
         "ctx",
         [(i + 1, i) for i in range(lax.axis_size("ctx") - 1)],
-    ).astype(F32)
-    dkey = dkey_own + far_back[:, :kv_width]
-    dvalue = (dvalue_own + far_back[:, kv_width:]).astype(BF)
-    dquery_pre = rotary_apply(dquery.reshape(rows, -1, HEAD_SIZE), cosine_table, -sine_table).reshape(rows, q_width).astype(BF)
-    dkey_pre = rotary_apply(dkey.reshape(rows, -1, HEAD_SIZE), cosine_table, -sine_table).reshape(rows, kv_width).astype(BF)
-    query_du = (dot_t(dquery_pre, query_b) * mask).astype(BF)
-    key_du = (dot_t(dkey_pre, key_b) * mask).astype(BF)
-    value_du = (dot_t(dvalue, value_b) * mask).astype(BF)
-    everything = jnp.concatenate([dquery_pre, dkey_pre, dvalue, query_du, key_du, value_du], axis=1)
-    dn1 = dot_t(everything, w_one)
-    grad_a3 = t_dot(normed, everything[:, qkv:])
-    grad_bq = t_dot(query_u, dquery_pre)
-    grad_bk = t_dot(key_u, dkey_pre)
-    grad_bv = t_dot(value_u, dvalue)
-    dn1 = tp_sum(dn1)
+    )
+    height = 3 * share + low_rows * n_tp * qkv // LANES
+    cosine_wide = jnp.tile(cosine_table[:, 0, :], (1, 2 * LANES // HEAD_SIZE))
+    sine_wide = jnp.tile(jnp.concatenate([-sine_table[:, 0, :], sine_table[:, 0, :]], axis=1), (1, LANES // HEAD_SIZE))
+    dn1, pack = qkv_back(
+        n, n_tp, low_rows, share, jnp.reshape(tp_at, (1,)).astype(jnp.int32), dquery, dkey_own, dvalue_own, far_back,
+        cosine_wide, sine_wide, normed, jnp.concatenate([query_u, key_u, value_u], axis=1), chosen_local[:, None], w_one, low_one, height,
+    )
+    early_sum, dn1, pack = lax.optimization_barrier((early_sum, dn1, pack))
+    late, early_sum = reduce_pack(pack, early_sum, 2)
+    dn1 = tp_sum(dn1.astype(F32)) if n_tp != 2 else dn1.astype(F32) + lax.ppermute(dn1, "tp", [(0, 1), (1, 0)]).astype(F32)
     grad_tokens = (dhidden + norm_back(xfull, attn_gain, dn1)).astype(BF)
 
-    def place_cols(piece, full_cols):
-        blank = jnp.zeros((piece.shape[0], full_cols), F32)
-        return lax.dynamic_update_slice_in_dim(blank, piece, tp_at * piece.shape[1], 1)
-
-    def place_rows(piece, full_rows):
-        blank = jnp.zeros((full_rows, piece.shape[1]), F32)
-        return lax.dynamic_update_slice_in_dim(blank, piece, tp_at * piece.shape[0], 0)
-
-    only_first = (tp_at == 0).astype(F32)
-    grads = (
-        grad_a3[:, :ranks],
-        place_cols(grad_bq, q_width * n_tp),
-        grad_a3[:, ranks : 2 * ranks],
-        place_cols(grad_bk, kv_width * n_tp),
-        grad_a3[:, 2 * ranks :],
-        place_cols(grad_bv, kv_width * n_tp),
-        place_rows(grad_ao, q_width * n_tp),
-        grad_bo,
-        grad_ar * only_first,
-        grad_br * only_first,
-        grad_ag,
-        place_cols(grad_bg, ff_width * n_tp),
-        grad_au,
-        place_cols(grad_bu, ff_width * n_tp),
-        place_rows(grad_ad, ff_width * n_tp),
-        grad_bd,
-    )
-    def reduce_grads(some):
-        flat = []
-        for g in some:
-            height, cols = g.shape[0] // n, g.shape[1]
-            count = -(-cols // LANES)
-            g = jnp.pad(g.astype(BF), ((0, 0), (0, count * LANES - cols)))
-            flat.append(g.reshape(n, height, count, LANES).transpose(0, 2, 1, 3).reshape(n, count * height, LANES))
-        flat = jnp.concatenate(flat, axis=1)
-        mine = lax.psum_scatter(flat, "fsdp", scatter_dimension=0, tiled=False)
-        mine = lax.psum(mine, ("ctx", "tp")).astype(F32)
+    def unpack(mine, shapes):
         found = []
         at = 0
-        for g in some:
-            height, cols = g.shape[0] // n, g.shape[1]
+        for height, cols in shapes:
             count = -(-cols // LANES)
             piece = mine[at : at + count * height].reshape(count, height, LANES).transpose(1, 0, 2).reshape(height, count * LANES)
             found.append(piece[:, :cols])
             at += count * height
         return found
 
-    final = reduce_grads(grads[:6]) + reduce_grads(grads[6:])
+    first_shapes = [(share, ranks), (low_rows, q_width * n_tp), (share, ranks), (low_rows, kv_width * n_tp), (share, ranks), (low_rows, kv_width * n_tp)]
+    final = unpack(late, first_shapes) + unpack(early_sum, early_shapes)
     return (output, grad_tokens, *final)
 
 

time: 790 us -> 605 us (0.77)
  waiting for transfers between devices: 184 us -> 43.2 us
  local copies, waits for them, and re-layouts: 110 us -> 62.2 us
  matrix products: 60.8 us -> 22.5 us
  Pallas kernels: 358 us -> 396 us
    reduce_scatter x2 -> x1, waiting for transfers between devices: 49.8 us -> 0.01 us  [on_device(): lax.psum_scatter(early_pack, 'fsdp', scatter_dimension=0, tiled=False)]
    pallas_call x2 -> x5, Pallas kernels: 152 us -> 191 us  [the longest x2 126 us: gather_packs(): pl.pallas_call(functools.partial(gather_kernel, n, count), in_specs=[anyw...]
    dot_general x27 -> x9, matrix products: 60.8 us -> 22.5 us  [dot(): lax.dot_general(left, right, (dims, ((), ())), preferred_element_type=F32...]
    ppermute x3, waiting for transfers between devices: 32.8 us -> 0.01 us  [bring(): brought[do + 1, 0] = lax.ppermute(last[0], 'fsdp', ring)]
    psum x1 -> x0, waiting for transfers between devices: 26.5 us -> none  [reduce_grads(): mine = lax.psum(mine, ('ctx', 'tp')).astype(F32)]
    ppermute x1 -> x5, waiting for transfers between devices: 23.6 us -> 0.01 us  [the longest x2 0.01 us: swapped(): lax.ppermute(self.other_half(b), 'tp', [(0, 1), (1, 0)])]
    unnamed x187 -> x169, local copies, waits for them, and re-layouts: 37.3 us -> 16.3 us
  transfers between devices with their start and end apart: 26 -> 24, of which waited for: 16 -> 8; matrix products, arithmetic and copies ran while one was open for 16% -> 16% of each run, Pallas kernels for 27% -> 53%
where the time goes in v5:
time: 605 us; the launch traced here: 598 us
  Pallas kernels  396 us (65%)
  local copies, waits for them, and re-layouts  62.2 us (10%)
  waiting for transfers between devices  43.2 us (7%)
  other arithmetic  42.7 us (7%)
  matrix products  22.5 us (4%)
  between operations  16 us (3%)
  starting transfers between devices  15.1 us (2%)
    pallas_call x4, Pallas kernels, experts_on(): pl.pallas_call(functools.partial(expert_kernel, experts, count), grid=(ro...  127 us
    pallas_call x2, Pallas kernels, gather_packs(): pl.pallas_call(functools.partial(gather_kernel, n, count), in_specs=[anyw...  126 us
    pallas_call x1, Pallas kernels, attend_back(): pl.pallas_call(functools.partial(attend_back_kernel, group, q_blocks), gr...  43.6 us
    pallas_call x1, Pallas kernels, attend(): pl.pallas_call(functools.partial(attend_kernel, group, q_blocks), grid=(p...  34.8 us
    pallas_call x1, Pallas kernels, reduce_pack(): pl.pallas_call(functools.partial(reduce_kernel, n), in_specs=[pl.BlockSpe...  31.5 us
    dot_general x9, matrix products, dot(): lax.dot_general(left, right, (dims, ((), ())), preferred_element_type=F32...  22.5 us
    pallas_call x1, Pallas kernels, mid_back(): pl.pallas_call(functools.partial(mid_back_kernel, n, n_tp, experts, share...  19.6 us
    unnamed x169, local copies, waits for them, and re-layouts  16.3 us
  transfers between devices with their start and end apart: 24, of which 8 were waited for; matrix products, arithmetic and copies ran while one was open for 16% of the time, Pallas kernels for 53%

profile of v5, /device:TPU:0, one launch (start us, length us, event | category | flops | bytes accessed | tf_op | source)
XLA Modules:
  0.0 598.2 jit_solution(3441270604354326171)
XLA Ops:
  11.9 53.1 %shard_map.430 = (bf16[8,192,1664]{2,1,0:T(8,128)(2,1)}, bf16[8,16,1280]{2,1,0:T(8,128)(2,1)}) custom-call(bf16[192,1664]{1,0:T(8,128)(2,1)} %copy-done.34, bf16[16,1280]{1,0:T(8,128)(2,1)} %pad_maximum_fusion.6.refs_1_), custom_call_target="tpu_custom_call" | custom-call | tf_op jit(solution)/shard_map/pallas_call | solution.py:299
  76.2 8.7 %fusion.42 = f32[768,1664]{1,0:T(8,128)} fusion(bf16[768,1536]{1,0:T(8,128)(2,1)S(1)} %fusion.4.n1_ref, bf16[1536,1664]{1,0:T(8,128)(2,1)} %bitcast.157), kind=kOutput, calls=%fused_computation.142 | convolution fusion | flops 3925868544 | bytes 12582912 | tf_op jit(solution)/shard_map/dot_general | solution.py:22
  93.0 72.5 %shard_map.431 = (bf16[8,192,1408]{2,1,0:T(8,128)(2,1)}, bf16[8,16,3712]{2,1,0:T(8,128)(2,1)}, bf16[8,64,128]{2,1,0:T(8,128)(2,1)}) custom-call(bf16[192,1408]{1,0:T(8,128)(2,1)} %copy-done.35, bf16[16,3712]{1,0:T(8,128)(2,1)} %copy-done.45, bf16[64,128]{1,0:T(8,128)(2,1)} %refs_2_.1), custom_call_target="tpu_custom_call" | custom-call | tf_op jit(solution)/shard_map/pallas_call | solution.py:299
  167.1 3.3 collective-permute-start.5
  170.4 3.5 slice_add_fusion
  182.8 5.4 collective-permute-done.5.kf_ref.vf_ref
  190.8 34.8 %shard_map.432 = (bf16[768,768]{1,0:T(8,128)(2,1)S(1)}, f32[2,8,768]{2,1,0:T(8,128)S(1)}) custom-call(s32[1]{0:T(128)} %bitcast.11.start_ref, s32[1,768]{1,0:T(1,128)S(1)} %broadcast_in_dim.21.begin_ref, bf16[768,768]{1,0:T(8,128)(2,1)S(1)} %copy.145.q_ref, bf16[768,512]{1,0:T(8,128)(2,1)S(1)} %pad_maximum_fusion.1.ko_ref.vo_ref, ...), custom_call_target="tpu_custom_call" | custom-call | flops 3623878656 | bytes 8388608 | tf_op jit(solution)/shard_map/pallas_call | solution.py:107
  227.0 4.3 convolution_add_fusion
  235.0 4.6 collective-permute-done.6
  239.6 5.3 multiply_reduce_fusion
  250.5 5.4 concatenate.50.t_ref
  264.0 35.8 %shard_map.433 = (bf16[768,1664]{1,0:T(8,128)(2,1)}, bf16[768,1536]{1,0:T(8,128)(2,1)}, f32[128,1536]{1,0:T(8,128)}, f32[256,128]{1,0:T(8,128)}, f32[128,256]{1,...) custom-call(s32[6]{0:T(128)} %stack.51.ids_ref, ...), custom_call_target="tpu_custom_call", output_to_operand_aliasing={{2}: (14, {}), {3}: (15, {}), {4}: (16, {}), {5}: (17, {}),... | custom-call | flops 21139292160 | bytes 25165824 | tf_op jit(solution)/shard_map/pallas_call | solution.py:411
  309.1 36.1 %shard_map.434 = (bf16[768,1664]{1,0:T(8,128)(2,1)}, bf16[768,1536]{1,0:T(8,128)(2,1)}, f32[128,1536]{1,0:T(8,128)}, f32[256,128]{1,0:T(8,128)}, f32[128,256]{1,...) custom-call(s32[6]{0:T(128)} %stack.51.ids_ref, ...), custom_call_target="tpu_custom_call", output_to_operand_aliasing={{2}: (14, {}), {3}: (15, {}), {4}: (16, {}), {5}: (17, {}),... | custom-call | flops 21139292160 | bytes 25165824 | tf_op jit(solution)/shard_map/pallas_call | solution.py:411
  345.3 9.2 %collective-permute-done.12 = bf16[1,1536,768]{2,1,0:T(8,128)(2,1)} collective-permute-done((bf16[1,1536,768]{2,1,0:T(8,128)(2,1)}, bf16[1,1536,768]{2,1,0:T(8,128)(2,1)}, u32[]{:S(2)}, u32[]{:S(2)}) %collective-permute-start.12) | collective-permute-done | bytes 2359328 | tf_op jit(solution)/shard_map/ppermute | solution.py:849
  354.5 27.5 %shard_map.435 = (bf16[768,1664]{1,0:T(8,128)(2,1)}, bf16[768,1536]{1,0:T(8,128)(2,1)}, f32[128,1536]{1,0:T(8,128)}, f32[256,128]{1,0:T(8,128)}, f32[128,256]{1,...) custom-call(s32[4]{0:T(128)} %pad_add_fusion.ids_ref, ...), custom_call_target="tpu_custom_call", output_to_operand_aliasing={{2}: (12, {}), {3}: (13, {}), {4}: (14, {}), {5}: (15, {}),... | custom-call | flops 12683575296 | bytes 25165824 | tf_op jit(solution)/shard_map/pallas_call | solution.py:411
  387.1 27.5 %shard_map.436 = (bf16[768,1664]{1,0:T(8,128)(2,1)}, bf16[768,1536]{1,0:T(8,128)(2,1)}, f32[128,1536]{1,0:T(8,128)}, f32[256,128]{1,0:T(8,128)}, f32[128,256]{1,...) custom-call(s32[4]{0:T(128)} %pad_add_fusion.ids_ref, ...), custom_call_target="tpu_custom_call", output_to_operand_aliasing={{2}: (12, {}), {3}: (13, {}), {4}: (14, {}), {5}: (15, {}),... | custom-call | flops 12683575296 | bytes 25165824 | tf_op jit(solution)/shard_map/pallas_call | solution.py:411
  428.6 19.6 %shard_map.437 = (f32[768,1536]{1,0:T(8,128)}, bf16[768,768]{1,0:T(8,128)(2,1)}, f32[8,1360,128]{2,1,0:T(8,128)}) custom-call(s32[2]{0:T(128)} %pad_add_fusion.1.sel_ref, bf16[384,1664]{1,0:T(8,128)(2,1)} %copy-done.36, bf16[384,1664]{1,0:T(8,128)(2,1)} %copy-done.71, f32[768,1536]{1,0:T(8,128)} %copy-done.15, bf16[768,1536]{1,0:T(8,128)(2,1)} %c_ref.2, ...), custom_call_target="tpu_custom_call" | custom-call | flops 7247757312 | bytes 33554432 | tf_op jit(solution)/shard_map/pallas_call | solution.py:656
  448.3 4.4 convert_element_type.158
  455.0 43.6 %shard_map.438 = (f32[768,768]{1,0:T(8,128)}, f32[768,256]{1,0:T(8,128)}, f32[768,256]{1,0:T(8,128)}, bf16[768,256]{1,0:T(8,128)(2,1)}, bf16[768,256]{1,0:T(8,128)(2,1)}) custom-call(s32[1]{0:T(128)} %bitcast.11.start_ref, s32[1,768]{1,0:T(1,128)} %copy-done.8, bf16[768,768]{1,0:T(8,128)(2,1)} %copy-done.3, bf16[768,512]{1,0:T(8,128)(2,1)} %copy-done.4, ...), custom_call_target="tpu_custom_call" | custom-call | flops 9059696640 | bytes 16777216 | tf_op jit(solution)/shard_map/pallas_call | solution.py:178
  507.5 15.2 %collective-permute-done.21.fb_ref = bf16[768,512]{1,0:T(8,128)(2,1)} collective-permute-done((bf16[768,512]{1,0:T(8,128)(2,1)}, bf16[768,512]{1,0:T(8,128)(2,1)}, u32[]{:S(2)}, u32[]{:S(2)}) %collective-permute-start.21) | collective-permute-done | bytes 786464 | tf_op jit(solution)/shard_map/ppermute | solution.py:963
  523.8 14.3 %shard_map.439 = (bf16[768,1536]{1,0:T(8,128)(2,1)}, f32[8,896,128]{2,1,0:T(8,128)}) custom-call(s32[1]{0:T(128)} %bitcast.34.tp_ref, f32[768,768]{1,0:T(8,128)} %get-tuple-element.166.dq_ref, f32[768,256]{1,0:T(8,128)S(1)} %copy-done.11, f32[768,256]{1,0:T(8,128)S(1)} %copy-done.12, bf16[768,512]{1,0:T(8,128)(2,1)} %collective-permute-done.21.fb_ref, ...), custom_call_target="tpu_custom_call" | custom-call | flops 7851737088 | bytes 25165824 | tf_op jit(solution)/shard_map/pallas_call | solution.py:558
  540.6 5.4 add_convert_fusion
  546.0 31.5 %shard_map.440 = (f32[896,128]{1,0:T(8,128)S(1)}, f32[1360,128]{1,0:T(8,128)S(1)}) custom-call(f32[8,896,128]{2,1,0:T(8,128)S(1)} %copy-done.2, bf16[1360,128]{1,0:T(8,128)(2,1)S(1)} %bitcast.99), custom_call_target="tpu_custom_call" | custom-call | tf_op jit(solution)/shard_map/pallas_call | solution.py:743
  586.1 4.7 fusion.1
  (313 shorter events, 106.3 us)
Async XLA Ops:
  7.3 530.9 %reduce-scatter.2.cloned.1.call-start = ((), (), s32[]{:S(2)}) async-start(), calls=%async_computation.1 | async-start | bytes 3133440 | tf_op jit(solution)/shard_map/reduce_scatter | solution.py:953
  68.1 97.4 %collective-permute-start = (bf16[1,1536,768]{2,1,0:T(8,128)(2,1)}, bf16[1,1536,768]{2,1,0:T(8,128)(2,1)}, u32[]{:S(2)}, u32[]{:S(2)}) collective-permute-start(bf16[1,1536,768]{2,1,0:T(8,128)(2,1)} %pad_maximum_fusion), channel_id=1, source_target_pairs={{0,8},{4,12},{8,16},{12,20},{16,24},{20,28},{24,0},{28,4},{1,9},{5... | collective-permute-start | bytes 7077896 | tf_op jit(solution)/shard_map/ppermute | solution.py:847
  69.4 96.1 %collective-permute-start.1 = (bf16[1,1536,768]{2,1,0:T(8,128)(2,1)}, bf16[1,1536,768]{2,1,0:T(8,128)(2,1)}, u32[]{:S(2)}, u32[]{:S(2)}) collective-permute-start(bf16[1,1536,768]{2,1,0:T(8,128)(2,1)} %pad_maximum_fusion), channel_id=1, source_target_pairs={{0,4},{4,0},{8,12},{12,8},{16,20},{20,16},{24,28},{28,24},{1,5},{5... | collective-permute-start | bytes 7077896 | tf_op jit(solution)/shard_map/ppermute | solution.py:849
  165.5 60.2 %collective-permute-start.3 = (bf16[1,1536,768]{2,1,0:T(8,128)(2,1)}, bf16[1,1536,768]{2,1,0:T(8,128)(2,1)}, u32[]{:S(2)}, u32[]{:S(2)}) collective-permute-start(bf16[1,1536,768]{2,1,0:T(8,128)(2,1)} %collective-permute-done), channel_id=1, source_target_pairs={{0,8},{4,12},{8,16},{12,20},{16,24},{20,28},{24,0},{28,4},{1,9},{5... | collective-permute-start | bytes 7077896 | tf_op jit(solution)/shard_map/ppermute | solution.py:847
  165.6 60.1 %collective-permute-start.4 = (bf16[1,1536,768]{2,1,0:T(8,128)(2,1)}, bf16[1,1536,768]{2,1,0:T(8,128)(2,1)}, u32[]{:S(2)}, u32[]{:S(2)}) collective-permute-start(bf16[1,1536,768]{2,1,0:T(8,128)(2,1)} %collective-permute-done), channel_id=1, source_target_pairs={{0,4},{4,0},{8,12},{12,8},{16,20},{20,16},{24,28},{28,24},{1,5},{5... | collective-permute-start | bytes 7077896 | tf_op jit(solution)/shard_map/ppermute | solution.py:849
  167.1 21.1 %collective-permute-start.5 = (bf16[768,512]{1,0:T(8,128)(2,1)S(1)}, bf16[768,512]{1,0:T(8,128)(2,1)S(1)}, u32[]{:S(2)}, u32[]{:S(2)}) collective-permute-start(bf16[768,512]{1,0:T(8,128)(2,1)S(1)} %pad_maximum_fusion.1.ko_ref.vo_ref), channel_id=1, source_target_pairs={{0,2},{1,3},{4,6},{5,7},{8,10},{9,11},{12,14},{13,15},{16,18},{17,... | collective-permute-start | bytes 2359304 | tf_op jit(solution)/shard_map/ppermute | solution.py:853
  179.5 46.1 %collective-permute-start.2 = (bf16[384,1536]{1,0:T(8,128)(2,1)}, bf16[384,1536]{1,0:T(8,128)(2,1)}, u32[]{:S(2)}, u32[]{:S(2)}) collective-permute-start(bf16[384,1536]{1,0:T(8,128)(2,1)} %constant_dynamic-slice_fusion.7), channel_id=1, source_target_pairs={{0,2},{2,0},{1,3},{3,1},{4,6},{6,4},{5,7},{7,5},{8,10},{10,8},{9,1... | collective-permute-start | bytes 3538952 | tf_op jit(solution)/shard_map/ppermute | solution.py:456
  231.3 8.3 %collective-permute-start.6 = (f32[768,1536]{1,0:T(8,128)}, f32[768,1536]{1,0:T(8,128)}, u32[]{:S(2)}, u32[]{:S(2)}) collective-permute-start(f32[768,1536]{1,0:T(8,128)} %convolution_add_fusion), channel_id=1, source_target_pairs={{0,1},{1,0},{2,3},{3,2},{4,5},{5,4},{6,7},{7,6},{8,9},{9,8},{10,11... | collective-permute-start | bytes 14155784 | tf_op jit(solution)/shard_map/ppermute | solution.py:761
  233.8 66.0 %collective-permute-start.8 = (bf16[1,1536,768]{2,1,0:T(8,128)(2,1)}, bf16[1,1536,768]{2,1,0:T(8,128)(2,1)}, u32[]{:S(2)}, u32[]{:S(2)}) collective-permute-start(bf16[1,1536,768]{2,1,0:T(8,128)(2,1)} %collective-permute-done.3), channel_id=1, source_target_pairs={{0,8},{4,12},{8,16},{12,20},{16,24},{20,28},{24,0},{28,4},{1,9},{5... | collective-permute-start | bytes 7077896 | tf_op jit(solution)/shard_map/ppermute | solution.py:847
  234.0 65.7 %collective-permute-start.9 = (bf16[1,1536,768]{2,1,0:T(8,128)(2,1)}, bf16[1,1536,768]{2,1,0:T(8,128)(2,1)}, u32[]{:S(2)}, u32[]{:S(2)}) collective-permute-start(bf16[1,1536,768]{2,1,0:T(8,128)(2,1)} %collective-permute-done.3), channel_id=1, source_target_pairs={{0,4},{4,0},{8,12},{12,8},{16,20},{20,16},{24,28},{28,24},{1,5},{5... | collective-permute-start | bytes 7077896 | tf_op jit(solution)/shard_map/ppermute | solution.py:849
  257.2 42.5 %collective-permute-start.7 = (bf16[384,1664]{1,0:T(8,128)(2,1)S(1)}, bf16[384,1664]{1,0:T(8,128)(2,1)S(1)}, u32[]{:S(2)}, u32[]{:S(2)}) collective-permute-start(bf16[384,1664]{1,0:T(8,128)(2,1)S(1)} %constant_dynamic-slice_fusion.5), channel_id=1, source_target_pairs={{0,2},{2,0},{1,3},{3,1},{4,6},{6,4},{5,7},{7,5},{8,10},{10,8},{9,1... | collective-permute-start | bytes 3833864 | tf_op jit(solution)/shard_map/ppermute | solution.py:456
  299.8 4.1 collective-permute-start.11
  299.9 5.5 collective-permute-start.10
  300.9 53.5 %collective-permute-start.12 = (bf16[1,1536,768]{2,1,0:T(8,128)(2,1)}, bf16[1,1536,768]{2,1,0:T(8,128)(2,1)}, u32[]{:S(2)}, u32[]{:S(2)}) collective-permute-start(bf16[1,1536,768]{2,1,0:T(8,128)(2,1)} %collective-permute-done.8), channel_id=1, source_target_pairs={{0,4},{4,0},{8,12},{12,8},{16,20},{20,16},{24,28},{28,24},{1,5},{5... | collective-permute-start | bytes 7077896 | tf_op jit(solution)/shard_map/ppermute | solution.py:849
  383.5 3.1 collective-permute-start.13
  386.9 30.2 %collective-permute-start.14 = (bf16[384,1664]{1,0:T(8,128)(2,1)S(1)}, bf16[384,1664]{1,0:T(8,128)(2,1)S(1)}, u32[]{:S(2)}, u32[]{:S(2)}) collective-permute-start(bf16[384,1664]{1,0:T(8,128)(2,1)S(1)} %add_convert_fusion.2), channel_id=1, source_target_pairs={{0,2},{2,0},{1,3},{3,1},{4,6},{6,4},{5,7},{7,5},{8,10},{10,8},{9,1... | collective-permute-start | bytes 3833864 | tf_op jit(solution)/shard_map/ppermute | solution.py:936
  418.5 3.1 collective-permute-start.15
  422.1 5.5 collective-permute-start.16
  422.3 30.4 %collective-permute-start.17 = (bf16[384,1536]{1,0:T(8,128)(2,1)S(1)}, bf16[384,1536]{1,0:T(8,128)(2,1)}, u32[]{:S(2)}, u32[]{:S(2)}) collective-permute-start(bf16[384,1536]{1,0:T(8,128)(2,1)S(1)} %constant_dynamic-slice_fusion.1), channel_id=1, source_target_pairs={{0,1},{1,0},{2,3},{3,2},{4,5},{5,4},{6,7},{7,6},{8,9},{9,8},{10,11... | collective-permute-start | bytes 3538952 | tf_op jit(solution)/shard_map/ppermute | solution.py:466
  425.3 27.4 %collective-permute-start.18 = (bf16[384,1536]{1,0:T(8,128)(2,1)}, bf16[384,1536]{1,0:T(8,128)(2,1)}, u32[]{:S(2)}, u32[]{:S(2)}) collective-permute-start(bf16[384,1536]{1,0:T(8,128)(2,1)} %constant_dynamic-slice_fusion), channel_id=1, source_target_pairs={{0,1},{1,0},{2,3},{3,2},{4,5},{5,4},{6,7},{7,6},{8,9},{9,8},{10,11... | collective-permute-start | bytes 3538952 | tf_op jit(solution)/shard_map/ppermute | solution.py:466
  454.7 47.9 %collective-permute-start.19 = (bf16[384,1536]{1,0:T(8,128)(2,1)S(1)}, bf16[384,1536]{1,0:T(8,128)(2,1)S(1)}, u32[]{:S(2)}, u32[]{:S(2)}) collective-permute-start(bf16[384,1536]{1,0:T(8,128)(2,1)S(1)} %add_convert_fusion.4), channel_id=1, source_target_pairs={{0,2},{2,0},{1,3},{3,1},{4,6},{6,4},{5,7},{7,5},{8,10},{10,8},{9,1... | collective-permute-start | bytes 3538952 | tf_op jit(solution)/shard_map/ppermute | solution.py:952
  500.9 21.7 %collective-permute-start.21 = (bf16[768,512]{1,0:T(8,128)(2,1)}, bf16[768,512]{1,0:T(8,128)(2,1)}, u32[]{:S(2)}, u32[]{:S(2)}) collective-permute-start(bf16[768,512]{1,0:T(8,128)(2,1)} %pad_maximum_fusion.2), channel_id=1, source_target_pairs={{2,0},{3,1},{6,4},{7,5},{10,8},{11,9},{14,12},{15,13},{18,16},{19,... | collective-permute-start | bytes 2359304 | tf_op jit(solution)/shard_map/ppermute | solution.py:963
  505.7 32.5 %collective-permute-start.20 = (bf16[384,1536]{1,0:T(8,128)(2,1)}, bf16[384,1536]{1,0:T(8,128)(2,1)}, u32[]{:S(2)}, u32[]{:S(2)}) collective-permute-start(bf16[384,1536]{1,0:T(8,128)(2,1)} %get-tuple-element.181), channel_id=1, source_target_pairs={{0,1},{1,0},{2,3},{3,2},{4,5},{5,4},{6,7},{7,6},{8,9},{9,8},{10,11... | collective-permute-start | bytes 3538952 | tf_op jit(solution)/shard_map/ppermute | solution.py:449
  538.2 46.7 %collective-permute-start.22 = (bf16[768,1536]{1,0:T(8,128)(2,1)}, bf16[768,1536]{1,0:T(8,128)(2,1)S(1)}, u32[]{:S(2)}, u32[]{:S(2)}) collective-permute-start(bf16[768,1536]{1,0:T(8,128)(2,1)} %get-tuple-element.173), channel_id=1, source_target_pairs={{0,1},{1,0},{2,3},{3,2},{4,5},{5,4},{6,7},{7,6},{8,9},{9,8},{10,11... | collective-permute-start | bytes 7077896 | tf_op jit(solution)/shard_map/ppermute | solution.py:977
  (75 other events, 873.8 us)
Sparse Core Ops, SparseCore 0:
  452.9 74.1 reduce-scatter.1

commit v6 on v5

--- a/solution.py
+++ b/solution.py
@@ -37,16 +37,6 @@
 def norm_back(values, gain, grad):
     unused, pull = jax.vjp(lambda inner: rms_norm(inner, gain), values)
     return pull(grad)[0]
-
-
-def rotary_apply(values, cosine_table, sine_table):
-    half = values.shape[-1] // 2
-    first = values[..., :half]
-    second = values[..., half:]
-    return jnp.concatenate(
-        [first * cosine_table - second * sine_table, first * sine_table + second * cosine_table],
-        axis=-1,
-    )
 
 
 def levels(n):
@@ -196,9 +186,10 @@
     return pl.ds(pl.multiple_of(ctx * edge, 16), take), pl.ds(pl.multiple_of(ctx * take, 16), edge)
 
 
-def gather_kernel(n, count, *refs):
-    ins, outs = refs[:count], refs[count : 2 * count]
-    own_sem, z_send, z_recv, y_send, y_recv, x_send, x_recv = refs[2 * count :]
+def gather_kernel(n, count, extra, *refs):
+    total = count + extra
+    ins, outs = refs[:total], refs[total : 2 * total]
+    own_sem, z_send, z_recv, y_send, y_recv, x_send, x_recv, extra_sem = refs[2 * total :]
     outer, inner = levels(n)
     me = lax.axis_index("fsdp")
     ctx = lax.axis_index("ctx")
@@ -251,6 +242,15 @@
         copy.start()
         started.append(copy)
 
+    straight = [
+        pltpu.make_async_remote_copy(
+            src_ref=ins[count + i], dst_ref=outs[count + i], send_sem=extra_sem.at[0, i], recv_sem=extra_sem.at[1, i],
+            device_id={"ctx": 1 - ctx}, device_id_type=MESH,
+        )
+        for i in range(extra)
+    ]
+    for c in straight:
+        c.start()
     for a in range(count):
         go(z_copy(a, 1))
         for dj in range(1, inner):
@@ -280,11 +280,13 @@
                         x_copy(a, do, dj).wait_recv()
     for c in started:
         c.wait_send()
+    for c in straight:
+        c.wait()
     for c in own:
         c.wait()
 
 
-def gather_packs(packs, collective_id):
+def gather_packs(packs, extra, collective_id):
     n = lax.axis_size("fsdp")
     outer, inner = levels(n)
     count = len(packs)
@@ -297,16 +299,18 @@
     anywhere = pl.BlockSpec(memory_space=pl.ANY)
     side = max(inner - 1, 1)
     return pl.pallas_call(
-        functools.partial(gather_kernel, n, count),
-        in_specs=[anywhere] * count,
-        out_specs=[anywhere] * count,
-        out_shape=[jax.ShapeDtypeStruct((n,) + a.shape, a.dtype) for a in arrays],
+        functools.partial(gather_kernel, n, count, len(extra)),
+        in_specs=[anywhere] * (count + len(extra)),
+        out_specs=[anywhere] * (count + len(extra)),
+        out_shape=[jax.ShapeDtypeStruct((n,) + a.shape, a.dtype) for a in arrays]
+        + [jax.ShapeDtypeStruct(a.shape, a.dtype) for a in extra],
         scratch_shapes=[
             dma((count,)), dma((count, outer - 1)), dma((count, outer - 1)),
             dma((count, outer, side)), dma((count, outer, side)), dma((count, outer, inner)), dma((count, outer, inner)),
+            dma((2, max(len(extra), 1))),
         ],
         compiler_params=pltpu.CompilerParams(collective_id=collective_id, has_side_effects=True),
-    )(*arrays)
+    )(*arrays, *extra)
 
 
 def t_dot_k(left, right):
@@ -479,14 +483,14 @@
 
 def put_rows(pack, value, at, height):
     for f in range(pack.shape[0]):
-        pack[f, pl.ds(at, height), :] = value[f * height : (f + 1) * height, :]
+        pack[f, pl.ds(at, height), :] = value[f * height : (f + 1) * height, :].astype(pack.dtype)
 
 
 def put_cols(pack, value, at, height, first):
     for i in range(value.shape[1] // LANES):
         for f in range(pack.shape[0]):
-            spot = pl.ds(pl.multiple_of(at + (first + i) * height, 8), height)
-            pack[f, spot, :] = value[f * height : (f + 1) * height, i * LANES : (i + 1) * LANES]
+            spot = pl.ds(pl.multiple_of(at + (first + i) * height, 8 if height % 16 else 16), height)
+            pack[f, spot, :] = value[f * height : (f + 1) * height, i * LANES : (i + 1) * LANES].astype(pack.dtype)
 
 
 def adapter_mask(chosen_ref):
@@ -565,6 +569,83 @@
         compiler_params=pltpu.CompilerParams(vmem_limit_bytes=50 << 20),
         cost_estimate=pl.CostEstimate(flops=4 * rows * width * w_one.shape[1], bytes_accessed=24 << 20, transcendentals=0),
     )(tp_at, dq, dko, dvo, fb, cos, sin, n1, u3, chosen, w_one, low_one)
+
+
+def normed_rows(v, gain):
+    return v * lax.rsqrt(jnp.mean(v * v, axis=1, keepdims=True) + norm_eps) * gain
+
+
+def turned(v, cos, sin):
+    head = lax.broadcasted_iota(jnp.int32, v.shape, 1) % HEAD_SIZE < HEAD_SIZE // 2
+    swapped = jnp.where(head, pltpu.roll(v, LANES - HEAD_SIZE // 2, 1), pltpu.roll(v, HEAD_SIZE // 2, 1))
+    return v * cos + swapped * sin
+
+
+def kv_kernel(q_width, x_ref, chosen_ref, cos_ref, sin_ref, gain_ref, w_ref, low_ref, n1_ref, u_ref, kv_ref):
+    kv_width = kv_ref.shape[1] // 2
+    mask = adapter_mask(chosen_ref)
+    n1 = normed_rows(x_ref[...].astype(F32), gain_ref[...]).astype(BF)
+    n1_ref[...] = n1
+    raw = dot(n1, w_ref[:, q_width:])
+    lows = (raw[:, 2 * kv_width :] * jnp.concatenate([mask] * 3, axis=1)).astype(BF)
+    u_ref[...] = lows
+    key = raw[:, :kv_width] + dot(lows[:, LANES : 2 * LANES], low_ref[:, q_width : q_width + kv_width])
+    for i in range(0, kv_width, LANES):
+        kv_ref[:, i : i + LANES] = turned(key[:, i : i + LANES], cos_ref[...], sin_ref[...]).astype(BF)
+    value = raw[:, kv_width : 2 * kv_width] + dot(lows[:, 2 * LANES :], low_ref[:, q_width + kv_width :])
+    kv_ref[:, kv_width:] = value.astype(BF)
+
+
+def q_kernel(n1_ref, u_ref, cos_ref, sin_ref, w_ref, low_ref, q_ref):
+    q_width = q_ref.shape[1]
+    q = dot(n1_ref[...], w_ref[:, :q_width]) + dot(u_ref[:, :LANES], low_ref[:, :q_width])
+    for i in range(0, q_width, LANES):
+        q_ref[:, i : i + LANES] = (turned(q[:, i : i + LANES], cos_ref[...], sin_ref[...]) * 0.125).astype(BF)
+
+
+def out_kernel(o_ref, chosen_ref, w_ref, oa_ref, low_ref, part_ref, u_ref):
+    q_width, width = o_ref.shape[1], part_ref.shape[1]
+    ff2 = low_ref.shape[1] - 2 * width - LANES
+    o = o_ref[...]
+    u = (dot(o, oa_ref[...]) * adapter_mask(chosen_ref)).astype(BF)
+    u_ref[...] = u
+    part_ref[...] = (dot_t(o, w_ref[:, :q_width]) + dot(u, low_ref[:, ff2 : ff2 + width])).astype(BF)
+
+
+def route_kernel(experts, q_width, x_ref, one_ref, other_ref, chosen_ref, routes_ref, gain_ref, w_ref, low_ref, h_ref, t_ref, u_ref):
+    width = h_ref.shape[1]
+    rows = h_ref.shape[0]
+    h = x_ref[...].astype(F32) + (one_ref[...].astype(F32) + other_ref[...].astype(F32))
+    h_ref[...] = h
+    n2 = normed_rows(h, gain_ref[...]).astype(BF)
+    t_ref[:, :width] = n2
+    u = (dot(n2, w_ref[:, q_width : q_width + LANES]) * adapter_mask(chosen_ref)).astype(BF)
+    u_ref[...] = u
+    logits = dot(n2, w_ref[:, q_width + 3 * LANES : q_width + 4 * LANES]) + dot(u, low_ref[:, low_ref.shape[1] - LANES :])
+    lane = lax.broadcasted_iota(jnp.int32, (rows, LANES), 1)
+    selected = lane == routes_ref[:, 0:1]
+    for k in range(1, routes_ref.shape[1]):
+        selected = selected | (lane == routes_ref[:, k : k + 1])
+    top = jnp.max(jnp.where(selected, logits, -jnp.inf), axis=1, keepdims=True)
+    gates = jnp.where(selected, jnp.exp(jnp.where(selected, logits - top, 0.0)), 0.0)
+    gates = gates / jnp.sum(gates, axis=1, keepdims=True)
+    high = gates.astype(BF).astype(F32)
+    extra = high + pltpu.roll(gates - high, experts, 1) + jnp.where(lane == 2 * experts, chosen_ref[...].astype(F32), 0.0)
+    t_ref[:, width:] = extra.astype(BF)
+
+
+def by_rows(kernel, step, rowed, whole, outs, flops):
+    rows = rowed[0].shape[0]
+    block = lambda cols: pl.BlockSpec((step, cols), lambda i: (i, 0))
+    return pl.pallas_call(
+        kernel,
+        grid=(rows // step,),
+        in_specs=[block(a.shape[1]) for a in rowed] + [pl.BlockSpec(a.shape, lambda i: (0, 0), pipeline_mode=pl.Buffered(1)) for a in whole],
+        out_specs=[block(cols) for cols, kind in outs],
+        out_shape=[jax.ShapeDtypeStruct((rows, cols), kind) for cols, kind in outs],
+        compiler_params=pltpu.CompilerParams(vmem_limit_bytes=48 << 20),
+        cost_estimate=pl.CostEstimate(flops=flops, bytes_accessed=1 << 20, transcendentals=0),
+    )(*rowed, *whole)
 
 
 def mid_back_kernel(n, n_tp, experts, share, low_rows, sel_ref, mine_ref, other_ref, h_ref, c_ref, t_ref, o_ref, ou_ref, ru_ref, chosen_ref, gain_ref,
@@ -624,7 +705,7 @@
         own = n // n_tp
         at = 0
         for k in range(own):
-            pack_ref[tp * own + k, pl.ds(at, share), :] = ao_acc[k * share : (k + 1) * share, :]
+            pack_ref[tp * own + k, pl.ds(at, share), :] = ao_acc[k * share : (k + 1) * share, :].astype(pack_ref.dtype)
         at += share
         put_cols(pack_ref, bo_acc, at, low_rows, 0)
         at += width // LANES * low_rows
@@ -641,7 +722,7 @@
             at += ff * n_tp // LANES * low_rows
         size = ad_ref.shape[0] // own
         for k in range(own):
-            pack_ref[tp * own + k, pl.ds(at, size), :] = ad_ref[k * size : (k + 1) * size, :]
+            pack_ref[tp * own + k, pl.ds(at, size), :] = ad_ref[k * size : (k + 1) * size, :].astype(pack_ref.dtype)
         at += size
         put_cols(pack_ref, bd_ref, at, low_rows, 0)
 
@@ -660,7 +741,7 @@
         + [by_row(a) for a in (hidden, cot, carried, mixed, out_u, router_u, chosen)]
         + [whole(a) for a in (gain, w_two, low_two, out_a, *sums)],
         out_specs=[by_row(hidden), by_row(mixed), pl.BlockSpec((n, height, LANES), lambda i: (0, 0, 0))],
-        out_shape=[sd((rows, width), F32), sd((rows, q_width), BF), sd((n, height, LANES), F32)],
+        out_shape=[sd((rows, width), F32), sd((rows, q_width), BF), sd((n, height, LANES), F32 if low_rows % 16 else BF)],
         scratch_shapes=[pltpu.VMEM((width, LANES), F32), pltpu.VMEM((q_width, LANES), F32), pltpu.VMEM((LANES, width), F32), pltpu.VMEM((LANES, LANES), F32)],
         compiler_params=pltpu.CompilerParams(vmem_limit_bytes=58 << 20),
         cost_estimate=pl.CostEstimate(flops=8 * rows * width * q_width, bytes_accessed=32 << 20, transcendentals=0),
@@ -788,12 +869,12 @@
             [(a, a.shape[1]) for a in (w_query, key_matrix, value_matrix, a_query, a_key, a_value)],
             [(b_query, q_width), (key_second_factor, kv_width), (value_second_factor, kv_width)],
         ],
+        (),
         0,
     )
     qkv = q_width + 2 * kv_width
     w_one = one.reshape(n * share, -1)
     low_one = low_one.reshape(n * low_rows, -1)
-    query_b, key_b, value_b = low_one[:, :q_width], low_one[:, q_width : q_width + kv_width], low_one[:, q_width + kv_width :]
 
     ends = jnp.cumsum(lengths[0])
     starts = ends - lengths[0]
@@ -806,27 +887,17 @@
     query_index = start + jnp.arange(rows, dtype=jnp.int32)
     begin_local = lax.dynamic_slice_in_dim(begin, start, rows)
     chosen_local = lax.dynamic_slice_in_dim(chosen, start, rows)
-    mask = (chosen_local[:, None] == (jnp.arange(ranks, dtype=jnp.int32) // ADAPTER_RANK)[None, :]).astype(F32)
-    half = HEAD_SIZE // 2
-    freq = 10000.0 ** (-jnp.arange(half, dtype=F32) / half)
+    freq = 10000.0 ** (-jnp.arange(HEAD_SIZE // 2, dtype=F32) / (HEAD_SIZE // 2))
     angles = (query_index - begin_local).astype(F32)[:, None] * freq[None, :]
-    cosine_table = jnp.cos(angles)[:, None, :]
-    sine_table = jnp.sin(angles)[:, None, :]
-
-    xfull = tokens.astype(F32)
-    normed = rms_norm(xfull, attn_gain).astype(BF)
-    raw = dot(normed, w_one)
-    query_u = (raw[:, qkv : qkv + ranks] * mask).astype(BF)
-    key_u = (raw[:, qkv + ranks : qkv + 2 * ranks] * mask).astype(BF)
-    value_u = (raw[:, qkv + 2 * ranks : qkv + 3 * ranks] * mask).astype(BF)
-    query_pre = raw[:, :q_width] + dot(query_u, query_b)
-    key_pre = raw[:, q_width : q_width + kv_width] + dot(key_u, key_b)
-    value_state = (raw[:, q_width + kv_width : qkv] + dot(value_u, value_b)).astype(BF)
-    query_state = (
-        rotary_apply(query_pre.reshape(rows, -1, HEAD_SIZE), cosine_table, sine_table).reshape(rows, q_width).astype(BF)
+    cosine, sine = jnp.cos(angles), jnp.sin(angles)
+    cosine_wide = jnp.tile(cosine, (1, 2 * LANES // HEAD_SIZE))
+    sine_wide = jnp.tile(jnp.concatenate([-sine, sine], axis=1), (1, LANES // HEAD_SIZE))
+    chosen_col = chosen_local[:, None]
+    gain_one, gain_two = attn_gain[None, :], ffn_gain[None, :]
+    normed, low_u, kv = by_rows(
+        functools.partial(kv_kernel, q_width), 256, (tokens, chosen_col, cosine_wide, sine_wide), (gain_one, w_one, low_one),
+        ((width, BF), (3 * ranks, BF), (2 * kv_width, BF)), 2 * rows * width * (w_one.shape[1] - q_width),
     )
-    key = rotary_apply(key_pre.reshape(rows, -1, HEAD_SIZE), cosine_table, sine_table).reshape(rows, kv_width).astype(BF)
-    kv = jnp.concatenate([key, value_state], axis=1)
     cross = Crossing()
     outer, inner = levels(n)
     me = lax.axis_index("fsdp")
@@ -850,57 +921,43 @@
         return after
 
     one = bring(0, one)
-    far = lax.ppermute(kv, "ctx", [(i, i + 1) for i in range(lax.axis_size("ctx") - 1)])
-    w_out_t, kv = lax.optimization_barrier((w_out.T, kv))
-    two, low_two, down_a = gather_packs(
+    (query_state,) = by_rows(
+        q_kernel, 256, (normed, low_u, cosine_wide, sine_wide), (w_one, low_one), ((q_width, BF),), 2 * rows * width * q_width
+    )
+    w_out, w_router, b_router, query_state = lax.optimization_barrier((w_out, w_router, b_router, query_state))
+    two, low_two, down_a, far = gather_packs(
         [
-            [(a, a.shape[1]) for a in (w_out_t, a_router, a_gate, a_up, jnp.pad(w_router, pad), a_out)],
+            [(a, a.shape[1]) for a in (w_out.T, a_router, a_gate, a_up, jnp.pad(w_router, pad), a_out)],
             [(b_gate, ff_width), (b_up, ff_width), (b_out, width), (b_down, width), (jnp.pad(b_router, pad), LANES)],
             [(a_down, ranks)],
         ],
+        (kv,),
         1,
     )
-    two = bring(1, two)
     cot = lax.optimization_barrier((out_cotangent, two))[0]
     cot_halves = cross.fetch(cot)
-    far, two = lax.optimization_barrier((far, two))
+    far = bring(1, far)
     w_two = two.reshape(n * share, -1)
     low_two = low_two.reshape(n * low_rows, -1)
-    out_b = low_two[:, 2 * ff_width : 2 * ff_width + width]
     down_b = low_two[:, 2 * ff_width + width : 2 * ff_width + 2 * width]
-    router_b = low_two[:, 2 * ff_width + 2 * width :]
-    out_wt = w_two[:, :q_width]
-    router_a = w_two[:, q_width : q_width + ranks]
-    router_w = w_two[:, q_width + 3 * ranks : q_width + 4 * ranks]
     out_a = lax.dynamic_slice_in_dim(w_two[:, q_width + 4 * ranks : q_width + 5 * ranks], tp_at * q_width, q_width, 0)
     down_at = lax.dynamic_slice_in_dim(down_a.reshape(-1, ranks), tp_at * ff_width, ff_width, 0)
     begin_row = begin_local[None, :]
     start_at = jnp.reshape(start, (1,)).astype(jnp.int32)
-    query_state = (query_state.astype(F32) * 0.125).astype(BF)
     mixed_heads, log_total = attend(query_state, kv, far, begin_row, start_at)
     mixed_heads = bring(2, mixed_heads)
     cot_halves, mixed_heads = lax.optimization_barrier((cot_halves, mixed_heads))
-    out_u = dot(mixed_heads, out_a) * mask
-    attn_part = dot_t(mixed_heads, out_wt) + dot(out_u.astype(BF), out_b)
-    hidden = xfull + tp_sum(attn_part)
-    normed_two = rms_norm(hidden, ffn_gain).astype(BF)
-    lows = dot(normed_two, jnp.concatenate([router_a, router_w], axis=1))
-    router_u = (lows[:, :ranks] * mask).astype(BF)
-    logits = lows[:, ranks : ranks + experts] + dot(router_u, router_b)[:, :experts]
-    selected = jnp.any(routes[:, :, None] == jnp.arange(experts, dtype=jnp.int32)[None, None, :], axis=1)
-    gates = jax.nn.softmax(jnp.where(selected, logits, -jnp.inf), axis=-1)
-
-    high = gates.astype(BF)
+    attn_part, out_u = by_rows(
+        out_kernel, 256, (mixed_heads, chosen_col), (w_two, out_a, low_two), ((width, BF), (ranks, BF)), 0
+    )
+    if n_tp == 2:
+        attn_other = lax.ppermute(attn_part, "tp", [(0, 1), (1, 0)])
+    else:
+        attn_part, attn_other = lax.psum(attn_part.astype(F32), "tp"), jnp.zeros_like(attn_part)
     spare = -(-2 * experts * n_tp // LANES) * LANES
-    carried = jnp.concatenate(
-        [
-            normed_two,
-            high,
-            (gates - high.astype(F32)).astype(BF),
-            chosen_local[:, None].astype(BF),
-            jnp.zeros((rows, LANES - 2 * experts - 1), BF),
-        ],
-        axis=1,
+    hidden, carried, router_u = by_rows(
+        functools.partial(route_kernel, experts, q_width), 256, (tokens, attn_part, attn_other, chosen_col, routes), (gain_two, w_two, low_two),
+        ((width, F32), (width + LANES, BF), (ranks, BF)), 0,
     )
     halves = cross.fetch(carried)
     early = [(0, 0), (1, 0)] + [(0, dj) for dj in range(1, inner)] + [(2, 0)] + [(1, dj) for dj in range(1, inner)]
@@ -944,8 +1001,8 @@
     height = sum(-(-cols // LANES) * tall for tall, cols in early_shapes)
     sel = jnp.stack([jnp.asarray(first, jnp.int32), tp_at.astype(jnp.int32)])
     dhidden, dmixed, early_pack = mid_back(
-        n, n_tp, experts, share, low_rows, sel, mine_half, other, hidden, cot, carried, mixed_heads, out_u.astype(BF), router_u,
-        chosen_local[:, None], ffn_gain[None, :], w_two, low_two, out_a, sums, height,
+        n, n_tp, experts, share, low_rows, sel, mine_half, other, hidden, cot, carried, mixed_heads, out_u, router_u,
+        chosen_col, gain_two, w_two, low_two, out_a, sums, height,
     )
     early_pack, dmixed, swapped = lax.optimization_barrier((early_pack.astype(BF), dmixed, swapped))
     moe_halves = [cross.half(p).astype(F32) + q.astype(F32) for p, q in zip(moe_parts, swapped)]
@@ -966,16 +1023,14 @@
         [(i + 1, i) for i in range(lax.axis_size("ctx") - 1)],
     )
     height = 3 * share + low_rows * n_tp * qkv // LANES
-    cosine_wide = jnp.tile(cosine_table[:, 0, :], (1, 2 * LANES // HEAD_SIZE))
-    sine_wide = jnp.tile(jnp.concatenate([-sine_table[:, 0, :], sine_table[:, 0, :]], axis=1), (1, LANES // HEAD_SIZE))
     dn1, pack = qkv_back(
         n, n_tp, low_rows, share, jnp.reshape(tp_at, (1,)).astype(jnp.int32), dquery, dkey_own, dvalue_own, far_back,
-        cosine_wide, sine_wide, normed, jnp.concatenate([query_u, key_u, value_u], axis=1), chosen_local[:, None], w_one, low_one, height,
+        cosine_wide, sine_wide, normed, low_u, chosen_col, w_one, low_one, height,
     )
     early_sum, dn1, pack = lax.optimization_barrier((early_sum, dn1, pack))
     late, early_sum = reduce_pack(pack, early_sum, 2)
     dn1 = tp_sum(dn1.astype(F32)) if n_tp != 2 else dn1.astype(F32) + lax.ppermute(dn1, "tp", [(0, 1), (1, 0)]).astype(F32)
-    grad_tokens = (dhidden + norm_back(xfull, attn_gain, dn1)).astype(BF)
+    grad_tokens = (dhidden + norm_back(tokens.astype(F32), attn_gain, dn1)).astype(BF)
 
     def unpack(mine, shapes):
         found = []

time: 605 us -> 585 us (0.967)
  Pallas kernels: 396 us -> 424 us
  matrix products: 22.5 us -> 0 us
  other arithmetic: 42.7 us -> 23.2 us
    pallas_call x2 -> x6, Pallas kernels: 126 us -> 154 us  [the longest x2 125 us: gather_packs(): pl.pallas_call(functools.partial(gather_kernel, n, count, len(extra)), in...]
    dot_general x9 -> x0, matrix products: 22.5 us -> none  [dot(): lax.dot_general(left, right, (dims, ((), ())), preferred_element_type=F32...]
    convert_element_type x8 -> x1, other arithmetic: 15 us -> 4.74 us  [on_device(): (dhidden + norm_back(tokens.astype(F32), attn_gain, dn1)).astype(BF)]
    ppermute x2 -> x1, waiting for transfers between devices: 9.96 us -> 0.01 us  [on_device(): attn_other = lax.ppermute(attn_part, 'tp', [(0, 1), (1, 0)])]
    ppermute x3, waiting for transfers between devices: 0.01 us -> 9.61 us  [bring(): brought[do + 1, 0] = lax.ppermute(last[0], 'fsdp', ring)]
    unnamed x169 -> x129, local copies, waits for them, and re-layouts: 16.3 us -> 22.7 us
  transfers between devices with their start and end apart: 24 -> 23, of which waited for: 8 -> 6; matrix products, arithmetic and copies ran while one was open for 16% -> 9% of each run, Pallas kernels for 53% -> 59%
where the time goes in v6:
time: 585 us; the launch traced here: 575 us
  Pallas kernels  424 us (72%)
  local copies, waits for them, and re-layouts  58.6 us (10%)
  waiting for transfers between devices  39.1 us (7%)
  other arithmetic  23.2 us (4%)
  between operations  15.5 us (3%)
  starting transfers between devices  14.3 us (2%)
    pallas_call x4, Pallas kernels, experts_on(): pl.pallas_call(functools.partial(expert_kernel, experts, count), grid=(ro...  127 us
    pallas_call x2, Pallas kernels, gather_packs(): pl.pallas_call(functools.partial(gather_kernel, n, count, len(extra)), in...  125 us
    pallas_call x1, Pallas kernels, attend_back(): pl.pallas_call(functools.partial(attend_back_kernel, group, q_blocks), gr...  43.6 us
    pallas_call x1, Pallas kernels, attend(): pl.pallas_call(functools.partial(attend_kernel, group, q_blocks), grid=(p...  34.9 us
    pallas_call x1, Pallas kernels, reduce_pack(): pl.pallas_call(functools.partial(reduce_kernel, n), in_specs=[pl.BlockSpe...  31.4 us
    pallas_call x4, Pallas kernels, by_rows(): pl.pallas_call(kernel, grid=(rows // step,), in_specs=[block(a.shape[1])...  29.1 us
    unnamed x129, local copies, waits for them, and re-layouts  22.7 us
    pallas_call x1, Pallas kernels, mid_back(): pl.pallas_call(functools.partial(mid_back_kernel, n, n_tp, experts, share...  18.7 us
  transfers between devices with their start and end apart: 23, of which 6 were waited for; matrix products, arithmetic and copies ran while one was open for 9% of the time, Pallas kernels for 59%

profile of v6, /device:TPU:0, one launch (start us, length us, event | category | flops | bytes accessed | tf_op | source)
XLA Modules:
  0.0 574.9 jit_solution(8222336194117533754)
XLA Ops:
  11.8 53.1 %shard_map.430 = (bf16[8,192,1664]{2,1,0:T(8,128)(2,1)}, bf16[8,16,1280]{2,1,0:T(8,128)(2,1)}) custom-call(bf16[192,1664]{1,0:T(8,128)(2,1)} %copy-done.37, bf16[16,1280]{1,0:T(8,128)(2,1)} %pad_maximum_fusion.3.refs_1_), custom_call_target="tpu_custom_call" | custom-call | tf_op jit(solution)/shard_map/pallas_call | solution.py:301
  71.4 7.2 %shard_map.431 = (bf16[768,1536]{1,0:T(8,128)(2,1)S(1)}, bf16[768,384]{1,0:T(8,128)(2,1)S(1)}, bf16[768,512]{1,0:T(8,128)(2,1)S(1)}) custom-call(bf16[768,1536]{1,0:T(8,128)(2,1)} %x_ref.3, s32[768,1]{1,0:T(8,128)S(1)} %broadcast_in_dim.45.chosen_ref, f32[768,128]{1,0:T(8,128)S(1)} %copy.101.cos_ref, f32[768,128]{1,0:T(8,128)S(1)} %copy.102.sin_ref, ...), custom_call_target="tpu_custom_call" | custom-call | flops 2113929216 | bytes 1048576 | tf_op jit(solution)/shard_map/pallas_call | solution.py:640
  79.5 6.2 %shard_map.432.q_ref = bf16[768,768]{1,0:T(8,128)(2,1)S(1)} custom-call(bf16[768,1536]{1,0:T(8,128)(2,1)S(1)} %get-tuple-element.109.n1_ref, bf16[768,384]{1,0:T(8,128)(2,1)S(1)} %get-tuple-element.110.u_ref, f32[768,128]{1,0:T(8,128)S(1)} %copy.101.cos_ref, f32[768,128]{1,0:T(8,128)S(1)} %copy.102.sin_ref, bf16[1536,1664]{1,0:T(8,128)(2,1)} %bitcast.102, ...), custom_call_target="tpu_custom_call" | custom-call | flops 1811939328 | bytes 1048576 | tf_op jit(solution)/shard_map/pallas_call | solution.py:640
  93.4 72.0 %shard_map.433 = (bf16[8,192,1408]{2,1,0:T(8,128)(2,1)}, bf16[8,16,3712]{2,1,0:T(8,128)(2,1)}, bf16[8,64,128]{2,1,0:T(8,128)(2,1)}, bf16[768,512]{1,0:T(8,128)(2,1)}) custom-call(bf16[192,1408]{1,0:T(8,128)(2,1)} %copy-done.38, bf16[16,3712]{1,0:T(8,128)(2,1)} %copy-done.40, bf16[64,128]{1,0:T(8,128)(2,1)} %refs_2_.1, bf16[768,512]{1,0:T(8,128)(2,1)} %copy-done.16), custom_call_target="tpu_custom_call" | custom-call | tf_op jit(solution)/shard_map/pallas_call | solution.py:301
  170.8 34.9 %shard_map.434 = (bf16[768,768]{1,0:T(8,128)(2,1)S(1)}, f32[2,8,768]{2,1,0:T(8,128)S(1)}) custom-call(s32[1]{0:T(128)} %bitcast.11.start_ref, s32[1,768]{1,0:T(1,128)S(1)} %broadcast_in_dim.38.begin_ref, bf16[768,768]{1,0:T(8,128)(2,1)S(1)} %shard_map.432.q_ref, bf16[768,512]{1,0:T(8,128)(2,1)S(1)} %copy-done.17, bf16[768,512]{1,0:T(8,128)(2,1)S(1)} %copy-done.17, ...), custom_call_target="tpu_custom_call" | custom-call | flops 3623878656 | bytes 8388608 | tf_op jit(solution)/shard_map/pallas_call | solution.py:97
  206.4 9.6 %collective-permute-done.3 = bf16[1,1536,768]{2,1,0:T(8,128)(2,1)} collective-permute-done((bf16[1,1536,768]{2,1,0:T(8,128)(2,1)}, bf16[1,1536,768]{2,1,0:T(8,128)(2,1)}, u32[]{:S(2)}, u32[]{:S(2)}) %collective-permute-start.3) | collective-permute-done | bytes 2359328 | tf_op jit(solution)/shard_map/ppermute | solution.py:918
  216.0 6.7 %shard_map.435 = (bf16[768,1536]{1,0:T(8,128)(2,1)}, bf16[768,128]{1,0:T(8,128)(2,1)S(1)}) custom-call(bf16[768,768]{1,0:T(8,128)(2,1)S(1)} %get-tuple-element.124.o_ref, s32[768,1]{1,0:T(8,128)S(1)} %broadcast_in_dim.45.chosen_ref, bf16[1536,1408]{1,0:T(8,128)(2,1)} %bitcast.105, bf16[768,128]{1,0:T(8,128)(2,1)S(1)} %constant_dynamic-slice_fusion.6.oa_ref, ...), custom_call_target="tpu_custom_call" | custom-call | bytes 1048576 | tf_op jit(solution)/shard_map/pallas_call | solution.py:640
  232.2 9.0 %shard_map.436 = (f32[768,1536]{1,0:T(8,128)}, bf16[768,1664]{1,0:T(8,128)(2,1)}, bf16[768,128]{1,0:T(8,128)(2,1)S(1)}) custom-call(bf16[768,1536]{1,0:T(8,128)(2,1)S(1)} %copy-done.2, bf16[768,1536]{1,0:T(8,128)(2,1)} %get-tuple-element.126.one_ref, bf16[768,1536]{1,0:T(8,128)(2,1)} %collective-permute-done.5.other_ref, ...), custom_call_target="tpu_custom_call" | custom-call | bytes 1048576 | tf_op jit(solution)/shard_map/pallas_call | solution.py:640
  247.7 35.8 %shard_map.437 = (bf16[768,1664]{1,0:T(8,128)(2,1)}, bf16[768,1536]{1,0:T(8,128)(2,1)}, f32[128,1536]{1,0:T(8,128)}, f32[256,128]{1,0:T(8,128)}, f32[128,256]{1,...) custom-call(s32[6]{0:T(128)} %stack.51.ids_ref, ...), custom_call_target="tpu_custom_call", output_to_operand_aliasing={{2}: (14, {}), {3}: (15, {}), {4}: (16, {}), {5}: (17, {}),... | custom-call | flops 21139292160 | bytes 25165824 | tf_op jit(solution)/shard_map/pallas_call | solution.py:415
  294.5 36.2 %shard_map.438 = (bf16[768,1664]{1,0:T(8,128)(2,1)}, bf16[768,1536]{1,0:T(8,128)(2,1)}, f32[128,1536]{1,0:T(8,128)}, f32[256,128]{1,0:T(8,128)}, f32[128,256]{1,...) custom-call(s32[6]{0:T(128)} %stack.51.ids_ref, ...), custom_call_target="tpu_custom_call", output_to_operand_aliasing={{2}: (14, {}), {3}: (15, {}), {4}: (16, {}), {5}: (17, {}),... | custom-call | flops 21139292160 | bytes 25165824 | tf_op jit(solution)/shard_map/pallas_call | solution.py:415
  330.7 7.5 %collective-permute-done.11 = bf16[1,1536,768]{2,1,0:T(8,128)(2,1)} collective-permute-done((bf16[1,1536,768]{2,1,0:T(8,128)(2,1)}, bf16[1,1536,768]{2,1,0:T(8,128)(2,1)}, u32[]{:S(2)}, u32[]{:S(2)}) %collective-permute-start.11) | collective-permute-done | bytes 2359328 | tf_op jit(solution)/shard_map/ppermute | solution.py:920
  338.2 27.5 %shard_map.439 = (bf16[768,1664]{1,0:T(8,128)(2,1)}, bf16[768,1536]{1,0:T(8,128)(2,1)}, f32[128,1536]{1,0:T(8,128)}, f32[256,128]{1,0:T(8,128)}, f32[128,256]{1,...) custom-call(s32[4]{0:T(128)} %pad_add_fusion.ids_ref, ...), custom_call_target="tpu_custom_call", output_to_operand_aliasing={{2}: (12, {}), {3}: (13, {}), {4}: (14, {}), {5}: (15, {}),... | custom-call | flops 12683575296 | bytes 25165824 | tf_op jit(solution)/shard_map/pallas_call | solution.py:415
  367.4 3.0 collective-permute-done.12
  372.1 27.5 %shard_map.440 = (bf16[768,1664]{1,0:T(8,128)(2,1)}, bf16[768,1536]{1,0:T(8,128)(2,1)}, f32[128,1536]{1,0:T(8,128)}, f32[256,128]{1,0:T(8,128)}, f32[128,256]{1,...) custom-call(s32[4]{0:T(128)} %pad_add_fusion.ids_ref, ...), custom_call_target="tpu_custom_call", output_to_operand_aliasing={{2}: (12, {}), {3}: (13, {}), {4}: (14, {}), {5}: (15, {}),... | custom-call | flops 12683575296 | bytes 25165824 | tf_op jit(solution)/shard_map/pallas_call | solution.py:415
  402.3 3.0 collective-permute-done.14
  410.8 18.7 %shard_map.441 = (f32[768,1536]{1,0:T(8,128)}, bf16[768,768]{1,0:T(8,128)(2,1)}, bf16[8,1360,128]{2,1,0:T(8,128)(2,1)}) custom-call(s32[2]{0:T(128)} %pad_add_fusion.1.sel_ref, bf16[384,1664]{1,0:T(8,128)(2,1)} %copy-done.39, bf16[384,1664]{1,0:T(8,128)(2,1)} %copy-done.52, f32[768,1536]{1,0:T(8,128)} %get-tuple-element.127.h_ref, bf16[768,1536]{1,0:T(8,128)(2,1)} %c_ref.2, ...), custom_call_target="tpu_custom_call" | custom-call | flops 7247757312 | bytes 33554432 | tf_op jit(solution)/shard_map/pallas_call | solution.py:737
  432.9 43.6 %shard_map.442 = (f32[768,768]{1,0:T(8,128)}, f32[768,256]{1,0:T(8,128)}, f32[768,256]{1,0:T(8,128)}, bf16[768,256]{1,0:T(8,128)(2,1)}, bf16[768,256]{1,0:T(8,128)(2,1)}) custom-call(s32[1]{0:T(128)} %bitcast.11.start_ref, s32[1,768]{1,0:T(1,128)} %copy-done.22, bf16[768,768]{1,0:T(8,128)(2,1)} %copy-done.13, bf16[768,512]{1,0:T(8,128)(2,1)} %copy-done.16, ...), custom_call_target="tpu_custom_call" | custom-call | flops 9059696640 | bytes 16777216 | tf_op jit(solution)/shard_map/pallas_call | solution.py:168
  481.1 3.3 constant_dynamic-update-slice_fusion.16
  484.4 14.9 %collective-permute-done.20.fb_ref = bf16[768,512]{1,0:T(8,128)(2,1)S(1)} collective-permute-done((bf16[768,512]{1,0:T(8,128)(2,1)S(1)}, bf16[768,512]{1,0:T(8,128)(2,1)S(1)}, u32[]{:S(2)}, u32[]{:S(2)}) %collective-permute-start.20) | collective-permute-done | bytes 786464 | tf_op jit(solution)/shard_map/ppermute | solution.py:1020
  500.2 14.3 %shard_map.443 = (bf16[768,1536]{1,0:T(8,128)(2,1)}, f32[8,896,128]{2,1,0:T(8,128)}) custom-call(s32[1]{0:T(128)} %bitcast.32.tp_ref, f32[768,768]{1,0:T(8,128)} %get-tuple-element.184.dq_ref, f32[768,256]{1,0:T(8,128)S(1)} %copy-done.26, f32[768,256]{1,0:T(8,128)S(1)} %copy-done.27, bf16[768,512]{1,0:T(8,128)(2,1)} %copy-done.53, ...), custom_call_target="tpu_custom_call" | custom-call | flops 7851737088 | bytes 25165824 | tf_op jit(solution)/shard_map/pallas_call | solution.py:562
  514.6 2.4 constant_dynamic-update-slice_fusion.15
  517.0 5.4 add_convert_fusion
  522.4 31.4 %shard_map.444 = (f32[896,128]{1,0:T(8,128)S(1)}, f32[1360,128]{1,0:T(8,128)S(1)}) custom-call(f32[8,896,128]{2,1,0:T(8,128)S(1)} %copy-done.8, bf16[1360,128]{1,0:T(8,128)(2,1)S(1)} %bitcast.100), custom_call_target="tpu_custom_call" | custom-call | tf_op jit(solution)/shard_map/pallas_call | solution.py:824
  562.8 4.7 fusion.3
  (241 shorter events, 81.6 us)
Async XLA Ops:
  7.3 507.2 %reduce-scatter.2.cloned.1.call-start = ((), (), s32[]{:S(2)}) async-start(), calls=%async_computation.1 | async-start | bytes 3133440 | tf_op jit(solution)/shard_map/reduce_scatter | solution.py:1010
  68.0 97.4 %collective-permute-start.1 = (bf16[1,1536,768]{2,1,0:T(8,128)(2,1)}, bf16[1,1536,768]{2,1,0:T(8,128)(2,1)}, u32[]{:S(2)}, u32[]{:S(2)}) collective-permute-start(bf16[1,1536,768]{2,1,0:T(8,128)(2,1)} %pad_maximum_fusion), channel_id=1, source_target_pairs={{0,8},{4,12},{8,16},{12,20},{16,24},{20,28},{24,0},{28,4},{1,9},{5... | collective-permute-start | bytes 7077896 | tf_op jit(solution)/shard_map/ppermute | solution.py:918
  69.3 96.1 %collective-permute-start.2 = (bf16[1,1536,768]{2,1,0:T(8,128)(2,1)}, bf16[1,1536,768]{2,1,0:T(8,128)(2,1)}, u32[]{:S(2)}, u32[]{:S(2)}) collective-permute-start(bf16[1,1536,768]{2,1,0:T(8,128)(2,1)} %pad_maximum_fusion), channel_id=1, source_target_pairs={{0,4},{4,0},{8,12},{12,8},{16,20},{20,16},{24,28},{28,24},{1,5},{5... | collective-permute-start | bytes 7077896 | tf_op jit(solution)/shard_map/ppermute | solution.py:920
  71.4 158.6 %copy-start.4 = (s32[768,1]{1,0:T(8,128)}, s32[768,1]{1,0:T(8,128)S(1)}, u32[]{:S(2)}) copy-start(s32[768,1]{1,0:T(8,128)S(1)} %broadcast_in_dim.45.chosen_ref) | copy-start | bytes 9220
  165.4 50.5 %collective-permute-start.3 = (bf16[1,1536,768]{2,1,0:T(8,128)(2,1)}, bf16[1,1536,768]{2,1,0:T(8,128)(2,1)}, u32[]{:S(2)}, u32[]{:S(2)}) collective-permute-start(bf16[1,1536,768]{2,1,0:T(8,128)(2,1)} %collective-permute-done.1), channel_id=1, source_target_pairs={{0,8},{4,12},{8,16},{12,20},{16,24},{20,28},{24,0},{28,4},{1,9},{5... | collective-permute-start | bytes 7077896 | tf_op jit(solution)/shard_map/ppermute | solution.py:918
  165.5 50.5 %collective-permute-start.4 = (bf16[1,1536,768]{2,1,0:T(8,128)(2,1)}, bf16[1,1536,768]{2,1,0:T(8,128)(2,1)}, u32[]{:S(2)}, u32[]{:S(2)}) collective-permute-start(bf16[1,1536,768]{2,1,0:T(8,128)(2,1)} %collective-permute-done.1), channel_id=1, source_target_pairs={{0,4},{4,0},{8,12},{12,8},{16,20},{20,16},{24,28},{28,24},{1,5},{5... | collective-permute-start | bytes 7077896 | tf_op jit(solution)/shard_map/ppermute | solution.py:920
  168.5 47.5 %collective-permute-start = (bf16[384,1536]{1,0:T(8,128)(2,1)S(1)}, bf16[384,1536]{1,0:T(8,128)(2,1)}, u32[]{:S(2)}, u32[]{:S(2)}) collective-permute-start(bf16[384,1536]{1,0:T(8,128)(2,1)S(1)} %constant_dynamic-slice_fusion.10), channel_id=1, source_target_pairs={{0,2},{2,0},{1,3},{3,1},{4,6},{6,4},{5,7},{7,5},{8,10},{10,8},{9,1... | collective-permute-start | bytes 3538952 | tf_op jit(solution)/shard_map/ppermute | solution.py:460
  223.4 6.6 %collective-permute-start.5 = (bf16[768,1536]{1,0:T(8,128)(2,1)}, bf16[768,1536]{1,0:T(8,128)(2,1)}, u32[]{:S(2)}, u32[]{:S(2)}) collective-permute-start(bf16[768,1536]{1,0:T(8,128)(2,1)} %get-tuple-element.126.one_ref), channel_id=1, source_target_pairs={{0,1},{1,0},{2,3},{3,2},{4,5},{5,4},{6,7},{7,6},{8,9},{9,8},{10,11... | collective-permute-start | bytes 7077896 | tf_op jit(solution)/shard_map/ppermute | solution.py:954
  227.2 56.2 %collective-permute-start.7 = (bf16[1,1536,768]{2,1,0:T(8,128)(2,1)}, bf16[1,1536,768]{2,1,0:T(8,128)(2,1)}, u32[]{:S(2)}, u32[]{:S(2)}) collective-permute-start(bf16[1,1536,768]{2,1,0:T(8,128)(2,1)} %collective-permute-done.3), channel_id=1, source_target_pairs={{0,8},{4,12},{8,16},{12,20},{16,24},{20,28},{24,0},{28,4},{1,9},{5... | collective-permute-start | bytes 7077896 | tf_op jit(solution)/shard_map/ppermute | solution.py:918
  227.4 56.1 %collective-permute-start.8 = (bf16[1,1536,768]{2,1,0:T(8,128)(2,1)}, bf16[1,1536,768]{2,1,0:T(8,128)(2,1)}, u32[]{:S(2)}, u32[]{:S(2)}) collective-permute-start(bf16[1,1536,768]{2,1,0:T(8,128)(2,1)} %collective-permute-done.3), channel_id=1, source_target_pairs={{0,4},{4,0},{8,12},{12,8},{16,20},{20,16},{24,28},{28,24},{1,5},{5... | collective-permute-start | bytes 7077896 | tf_op jit(solution)/shard_map/ppermute | solution.py:920
  242.7 40.8 %collective-permute-start.6 = (bf16[384,1664]{1,0:T(8,128)(2,1)S(1)}, bf16[384,1664]{1,0:T(8,128)(2,1)}, u32[]{:S(2)}, u32[]{:S(2)}) collective-permute-start(bf16[384,1664]{1,0:T(8,128)(2,1)S(1)} %constant_dynamic-slice_fusion.5), channel_id=1, source_target_pairs={{0,2},{2,0},{1,3},{3,1},{4,6},{6,4},{5,7},{7,5},{8,10},{10,8},{9,1... | collective-permute-start | bytes 3833864 | tf_op jit(solution)/shard_map/ppermute | solution.py:460
  283.5 5.8 %collective-permute-start.10 = (bf16[384,1536]{1,0:T(8,128)(2,1)}, bf16[384,1536]{1,0:T(8,128)(2,1)}, u32[]{:S(2)}, u32[]{:S(2)}) collective-permute-start(bf16[384,1536]{1,0:T(8,128)(2,1)} %collective-permute-done), channel_id=1, source_target_pairs={{0,1},{1,0},{2,3},{3,2},{4,5},{5,4},{6,7},{7,6},{8,9},{9,8},{10,11... | collective-permute-start | bytes 3538952 | tf_op jit(solution)/shard_map/ppermute | solution.py:453
  283.6 7.1 %collective-permute-start.9 = (bf16[384,1664]{1,0:T(8,128)(2,1)}, bf16[384,1664]{1,0:T(8,128)(2,1)}, u32[]{:S(2)}, u32[]{:S(2)}) collective-permute-start(bf16[384,1664]{1,0:T(8,128)(2,1)} %collective-permute-done.6), channel_id=1, source_target_pairs={{0,1},{1,0},{2,3},{3,2},{4,5},{5,4},{6,7},{7,6},{8,9},{9,8},{10,11... | collective-permute-start | bytes 3833864 | tf_op jit(solution)/shard_map/ppermute | solution.py:453
  284.6 53.5 %collective-permute-start.11 = (bf16[1,1536,768]{2,1,0:T(8,128)(2,1)}, bf16[1,1536,768]{2,1,0:T(8,128)(2,1)}, u32[]{:S(2)}, u32[]{:S(2)}) collective-permute-start(bf16[1,1536,768]{2,1,0:T(8,128)(2,1)} %collective-permute-done.7), channel_id=1, source_target_pairs={{0,4},{4,0},{8,12},{12,8},{16,20},{20,16},{24,28},{28,24},{1,5},{5... | collective-permute-start | bytes 7077896 | tf_op jit(solution)/shard_map/ppermute | solution.py:920
  367.3 3.1 collective-permute-start.12
  370.7 30.2 %collective-permute-start.13 = (bf16[384,1664]{1,0:T(8,128)(2,1)S(1)}, bf16[384,1664]{1,0:T(8,128)(2,1)S(1)}, u32[]{:S(2)}, u32[]{:S(2)}) collective-permute-start(bf16[384,1664]{1,0:T(8,128)(2,1)S(1)} %add_convert_fusion.2), channel_id=1, source_target_pairs={{0,2},{2,0},{1,3},{3,1},{4,6},{6,4},{5,7},{7,5},{8,10},{10,8},{9,1... | collective-permute-start | bytes 3833864 | tf_op jit(solution)/shard_map/ppermute | solution.py:993
  402.3 3.1 collective-permute-start.14
  405.8 3.9 collective-permute-start.15
  406.1 23.4 %collective-permute-start.16 = (bf16[384,1536]{1,0:T(8,128)(2,1)S(1)}, bf16[384,1536]{1,0:T(8,128)(2,1)}, u32[]{:S(2)}, u32[]{:S(2)}) collective-permute-start(bf16[384,1536]{1,0:T(8,128)(2,1)S(1)} %constant_dynamic-slice_fusion.1), channel_id=1, source_target_pairs={{0,1},{1,0},{2,3},{3,2},{4,5},{5,4},{6,7},{7,6},{8,9},{9,8},{10,11... | collective-permute-start | bytes 3538952 | tf_op jit(solution)/shard_map/ppermute | solution.py:470
  409.0 20.5 %collective-permute-start.17 = (bf16[384,1536]{1,0:T(8,128)(2,1)}, bf16[384,1536]{1,0:T(8,128)(2,1)}, u32[]{:S(2)}, u32[]{:S(2)}) collective-permute-start(bf16[384,1536]{1,0:T(8,128)(2,1)} %constant_dynamic-slice_fusion), channel_id=1, source_target_pairs={{0,1},{1,0},{2,3},{3,2},{4,5},{5,4},{6,7},{7,6},{8,9},{9,8},{10,11... | collective-permute-start | bytes 3538952 | tf_op jit(solution)/shard_map/ppermute | solution.py:470
  431.4 48.1 %collective-permute-start.18 = (bf16[384,1536]{1,0:T(8,128)(2,1)S(1)}, bf16[384,1536]{1,0:T(8,128)(2,1)S(1)}, u32[]{:S(2)}, u32[]{:S(2)}) collective-permute-start(bf16[384,1536]{1,0:T(8,128)(2,1)S(1)} %add_convert_fusion.4), channel_id=1, source_target_pairs={{0,2},{2,0},{1,3},{3,1},{4,6},{6,4},{5,7},{7,5},{8,10},{10,8},{9,1... | collective-permute-start | bytes 3538952 | tf_op jit(solution)/shard_map/ppermute | solution.py:1009
  477.9 21.4 %collective-permute-start.20 = (bf16[768,512]{1,0:T(8,128)(2,1)S(1)}, bf16[768,512]{1,0:T(8,128)(2,1)S(1)}, u32[]{:S(2)}, u32[]{:S(2)}) collective-permute-start(bf16[768,512]{1,0:T(8,128)(2,1)S(1)} %pad_maximum_fusion.1), channel_id=1, source_target_pairs={{2,0},{3,1},{6,4},{7,5},{10,8},{11,9},{14,12},{15,13},{18,16},{19,... | collective-permute-start | bytes 2359304 | tf_op jit(solution)/shard_map/ppermute | solution.py:1020
  484.3 30.2 %collective-permute-start.19 = (bf16[384,1536]{1,0:T(8,128)(2,1)}, bf16[384,1536]{1,0:T(8,128)(2,1)}, u32[]{:S(2)}, u32[]{:S(2)}) collective-permute-start(bf16[384,1536]{1,0:T(8,128)(2,1)} %get-tuple-element.201), channel_id=1, source_target_pairs={{0,1},{1,0},{2,3},{3,2},{4,5},{5,4},{6,7},{7,6},{8,9},{9,8},{10,11... | collective-permute-start | bytes 3538952 | tf_op jit(solution)/shard_map/ppermute | solution.py:453
  514.5 46.6 %collective-permute-start.21 = (bf16[768,1536]{1,0:T(8,128)(2,1)}, bf16[768,1536]{1,0:T(8,128)(2,1)S(1)}, u32[]{:S(2)}, u32[]{:S(2)}) collective-permute-start(bf16[768,1536]{1,0:T(8,128)(2,1)} %get-tuple-element.191), channel_id=1, source_target_pairs={{0,1},{1,0},{2,3},{3,2},{4,5},{5,4},{6,7},{7,6},{8,9},{9,8},{10,11... | collective-permute-start | bytes 7077896 | tf_op jit(solution)/shard_map/ppermute | solution.py:1032
  (54 other events, 569.5 us)
Sparse Core Ops, SparseCore 0:
  429.6 74.8 reduce-scatter.1

commit v7 on v6

--- a/solution.py
+++ b/solution.py
@@ -108,30 +108,42 @@
     )(start, begin, q, kv, kv, far, far)
 
 
-def attend_back_kernel(group, q_blocks, start_ref, begin_ref, q_ref, ko_ref, vo_ref, kf_ref, vf_ref, o_ref, do_ref, lse_ref,
-                       dq_ref, dko_ref, dvo_ref, dkf_ref, dvf_ref, bias, ks, vs, kts, qs, dos, dqts, dks, dvs, deltas):
+def attend_back_kernel(group, q_blocks, far, *refs):
+    if far:
+        start_ref, begin_ref, q_ref, k_ref, v_ref, o_ref, do_ref, lse_ref = refs[:8]
+        dq_far = None
+    else:
+        start_ref, begin_ref, q_ref, k_ref, v_ref, o_ref, do_ref, lse_ref, dq_far = refs[:9]
+    dq_ref, dk_ref, dv_ref, bias, ks, vs, kts, qs, dos, dqts, dks, dvs, deltas = refs[-13:]
     rows = q_ref.shape[0]
     width = rows // q_blocks
     heads = 2 * group
+
     @pl.when(pl.program_id(0) == 0)
     def _():
-        fill_bias(bias, start_ref, begin_ref, rows)
-    split_heads(kf_ref, ks, 2, rows, 0)
-    split_heads(ko_ref, ks, 2, rows, rows)
-    split_heads(vf_ref, vs, 2, rows, 0)
-    split_heads(vo_ref, vs, 2, rows, rows)
+        first = start_ref[0] - rows if far else start_ref[0]
+        for at in range(0, rows, width):
+            key = first + at + lax.broadcasted_iota(jnp.int32, (width, rows), 0)
+            query = start_ref[0] + lax.broadcasted_iota(jnp.int32, (width, rows), 1)
+            ok = (key <= query) & (key >= begin_ref[...]) & (key >= 0)
+            bias[pl.ds(at, width), :] = jnp.where(ok, 0.0, -1e30)
+
+    split_heads(k_ref, ks, 2, rows, 0)
+    split_heads(v_ref, vs, 2, rows, 0)
     split_heads(q_ref, qs, heads, rows, 0)
     split_heads(do_ref, dos, heads, rows, 0)
-    kts[:, pl.ds(0, rows)] = kf_ref[...].astype(F32).T.astype(BF)
-    kts[:, pl.ds(rows, rows)] = ko_ref[...].astype(F32).T.astype(BF)
+    kts[...] = k_ref[...].astype(F32).T.astype(BF)
     cols = heads * HEAD_SIZE
-    pick = (lax.broadcasted_iota(jnp.int32, (8, cols), 1) // HEAD_SIZE == lax.broadcasted_iota(jnp.int32, (8, cols), 0)).astype(F32)
+    pick = (
+        lax.broadcasted_iota(jnp.int32, (8, cols), 1) // HEAD_SIZE == lax.broadcasted_iota(jnp.int32, (8, cols), 0)
+    ).astype(F32)
     prod = o_ref[...].astype(F32) * do_ref[...].astype(F32)
     deltas[...] = dot(pick, prod, ((1,), (1,)), lax.Precision.HIGHEST)
     dks[...] = jnp.zeros_like(dks)
     dvs[...] = jnp.zeros_like(dvs)
     for b in range(q_blocks):
-        keys = rows + (b + 1) * width
+        keys = rows if far else (b + 1) * width
+
         def one(h, _):
             g = h // group
             at = pl.ds(b * width, width)
@@ -146,38 +158,44 @@
             kt = kts[pl.ds(pl.multiple_of(g * HEAD_SIZE, HEAD_SIZE), HEAD_SIZE), pl.ds(0, keys)]
             dqts[pl.ds(pl.multiple_of(h * HEAD_SIZE, HEAD_SIZE), HEAD_SIZE), at] = dot(kt, ds) * 0.125
             return 0
+
         lax.fori_loop(0, heads, one, 0)
     for j in range(group):
-        dq_ref[:, j * LANES : (j + 1) * LANES] = dqts[pl.ds(j * LANES, LANES), :].T
+        at = slice(j * LANES, (j + 1) * LANES)
+        part = dqts[pl.ds(j * LANES, LANES), :].T
+        dq_ref[:, at] = part if far else part + dq_far[:, at]
     for g in range(2):
         at = slice(g * HEAD_SIZE, (g + 1) * HEAD_SIZE)
-        dkf_ref[:, at] = dks[g, pl.ds(0, rows), :].astype(BF)
-        dko_ref[:, at] = dks[g, pl.ds(rows, rows), :]
-        dvf_ref[:, at] = dvs[g, pl.ds(0, rows), :].astype(BF)
-        dvo_ref[:, at] = dvs[g, pl.ds(rows, rows), :]
-
-
-def attend_back(q, kv, far, begin, start, o, do, lse, q_blocks=3):
+        dk_ref[:, at] = dks[g].astype(dk_ref.dtype)
+        dv_ref[:, at] = dvs[g].astype(dv_ref.dtype)
+
+
+def attend_back(q, keys, begin, start, o, do, lse, dq_far=None, q_blocks=3):
+    far = dq_far is None
     rows, q_width = q.shape
-    kv_width = kv.shape[1] // 2
+    kv_width = keys.shape[1] // 2
     pairs = kv_width // LANES
     group = q_width // kv_width
     spec = lambda off: pl.BlockSpec((rows, LANES), lambda i: (0, i + off))
     wide = pl.BlockSpec((rows, group * LANES), lambda i: (0, i))
     sd = jax.ShapeDtypeStruct
+    kind = BF if far else F32
+    vm = pltpu.VMEM
     return pl.pallas_call(
-        functools.partial(attend_back_kernel, group, q_blocks),
+        functools.partial(attend_back_kernel, group, q_blocks, far),
         grid=(pairs,),
-        in_specs=[pl.BlockSpec(memory_space=pltpu.SMEM), pl.BlockSpec((1, rows), lambda i: (0, 0)),
-                  wide, spec(0), spec(pairs), spec(0), spec(pairs), wide, wide, pl.BlockSpec((1, 8, rows), lambda i: (i, 0, 0))],
-        out_specs=[wide, spec(0), spec(0), spec(0), spec(0)],
-        out_shape=[sd((rows, q_width), F32), sd((rows, kv_width), F32), sd((rows, kv_width), F32), sd((rows, kv_width), BF), sd((rows, kv_width), BF)],
-        scratch_shapes=[pltpu.VMEM((2 * rows, rows), F32), pltpu.VMEM((2, 2 * rows, HEAD_SIZE), BF), pltpu.VMEM((2, 2 * rows, HEAD_SIZE), BF), pltpu.VMEM((LANES, 2 * rows), BF),
-                        pltpu.VMEM((2 * group, rows, HEAD_SIZE), BF), pltpu.VMEM((2 * group, rows, HEAD_SIZE), BF), pltpu.VMEM((2 * group * HEAD_SIZE, rows), F32),
-                        pltpu.VMEM((2, 2 * rows, HEAD_SIZE), F32), pltpu.VMEM((2, 2 * rows, HEAD_SIZE), F32), pltpu.VMEM((8, rows), F32)],
+        in_specs=[pl.BlockSpec(memory_space=pltpu.SMEM), pl.BlockSpec((1, rows), lambda i: (0, 0)), wide, spec(0), spec(pairs), wide, wide]
+        + [pl.BlockSpec((1, 8, rows), lambda i: (i, 0, 0))] + ([] if far else [wide]),
+        out_specs=[wide, spec(0), spec(0)],
+        out_shape=[sd((rows, q_width), F32), sd((rows, kv_width), kind), sd((rows, kv_width), kind)],
+        scratch_shapes=[
+            vm((rows, rows), F32), vm((2, rows, HEAD_SIZE), BF), vm((2, rows, HEAD_SIZE), BF), vm((LANES, rows), BF),
+            vm((2 * group, rows, HEAD_SIZE), BF), vm((2 * group, rows, HEAD_SIZE), BF), vm((2 * group * HEAD_SIZE, rows), F32),
+            vm((2, rows, HEAD_SIZE), F32), vm((2, rows, HEAD_SIZE), F32), vm((8, rows), F32),
+        ],
         compiler_params=pltpu.CompilerParams(vmem_limit_bytes=56 << 20),
-        cost_estimate=pl.CostEstimate(flops=20 * rows * rows * q_width, bytes_accessed=16 << 20, transcendentals=2 * rows * rows * 12),
-    )(start, begin, q, kv, kv, far, far, o, do, lse)
+        cost_estimate=pl.CostEstimate(flops=12 * rows * rows * q_width, bytes_accessed=16 << 20, transcendentals=rows * rows * 12),
+    )(start, begin, q, keys, keys, o, do, lse, *(() if far else (dq_far,)))
 
 
 def slab_of(rows, ctx):
@@ -317,40 +335,18 @@
     return dot(left, right, ((0,), (0,)))
 
 
-def expert_kernel(experts, count, ids_ref, t_ref, c_ref, *refs):
-    w_refs = refs[:count]
-    ga_ref, ua_ref, gb_ref, ub_ref, db_ref, da_ref = refs[count : count + 6]
-    prior = refs[count + 6 : count + 11]
-    early = refs[count + 11 : -9]
-    r_ref, m_ref = refs[-9:-7]
-    sums = refs[-7:-2]
-    moe_acc, dn2_acc = refs[-2:]
+def expert_loop(experts, ids_ref, t_ref, c_ref, w_refs, lows, kept, moe_acc, dn2_acc, spare):
     rows, width = c_ref.shape
-    ff = gb_ref.shape[1]
-    spare = r_ref.shape[1] - width
-    lanes = t_ref.shape[1] - width
-
-    @pl.when(pl.program_id(0) == 0)
-    def _():
-        for old, new in zip(prior, sums):
-            new[...] = old[...]
-
+    count = len(w_refs)
+    ff = lows[0].shape[1]
+    gl, ul, al = lows
     n2 = t_ref[:, :width]
     cot = c_ref[...]
     extra = t_ref[:, width:].astype(F32)
-    lane = lax.broadcasted_iota(jnp.int32, (rows, lanes), 1)
-    chosen = jnp.sum(jnp.where(lane == 2 * experts, extra, 0.0), axis=1, keepdims=True)
-    low_lane = lax.broadcasted_iota(jnp.int32, (rows, LANES), 1)
-    mask = ((low_lane // ADAPTER_RANK).astype(F32) == chosen).astype(F32)
-    zg = (dot(n2, ga_ref[...]) * mask).astype(BF)
-    zu = (dot(n2, ua_ref[...]) * mask).astype(BF)
-    gl = dot(zg, gb_ref[...])
-    ul = dot(zu, ub_ref[...])
-    down_back = (dot_t(cot, db_ref[...]) * mask).astype(BF)
-    al = dot_t(down_back, da_ref[...])
+    lane = lax.broadcasted_iota(jnp.int32, extra.shape, 1)
     back_lane = lax.broadcasted_iota(jnp.int32, (rows, spare), 1)
     dgate = jnp.zeros((rows, spare), F32)
-    act_sum = dg_sum = du_sum = None
+    act_sum, dg_sum, du_sum = kept
     for k in range(count):
         e = ids_ref[k]
         w = w_refs[k]
@@ -369,9 +365,9 @@
         act = act * gate
         du = back * silu
         dg = back * uv * (sig + silu * (1.0 - sig))
-        act_sum = act if k == 0 else act_sum + act
-        dg_sum = dg if k == 0 else dg_sum + dg
-        du_sum = du if k == 0 else du_sum + du
+        act_sum = act if act_sum is None else act_sum + act
+        dg_sum = dg if dg_sum is None else dg_sum + dg
+        du_sum = du if du_sum is None else du_sum + du
         moe = dot_t(act.astype(BF), w[:, 2 * ff :])
         dn2 = dot_t(jnp.concatenate([dg.astype(BF), du.astype(BF)], axis=1), w[:, : 2 * ff])
         if k == 0:
@@ -380,53 +376,108 @@
         else:
             moe_acc[...] += moe
             dn2_acc[...] += dn2
+    return dgate, act_sum, dg_sum, du_sum
+
+
+def row_mask(experts, t_ref, width):
+    extra = t_ref[:, width:].astype(F32)
+    lane = lax.broadcasted_iota(jnp.int32, extra.shape, 1)
+    chosen = jnp.sum(jnp.where(lane == 2 * experts, extra, 0.0), axis=1, keepdims=True)
+    low_lane = lax.broadcasted_iota(jnp.int32, (extra.shape[0], LANES), 1)
+    return ((low_lane // ADAPTER_RANK).astype(F32) == chosen).astype(F32)
+
+
+def first_experts_kernel(experts, count, ids_ref, t_ref, c_ref, *refs):
+    w_refs = refs[:count]
+    ga_ref, ua_ref, gb_ref, ub_ref, db_ref, da_ref, r_ref, m_ref, wide_ref, thin_ref, moe_acc, dn2_acc = refs[count:]
+    width = c_ref.shape[1]
+    mask = row_mask(experts, t_ref, width)
+    n2 = t_ref[:, :width]
+    zg = (dot(n2, ga_ref[...]) * mask).astype(BF)
+    zu = (dot(n2, ua_ref[...]) * mask).astype(BF)
+    down_back = (dot_t(c_ref[...], db_ref[...]) * mask).astype(BF)
+    lows = (dot(zg, gb_ref[...]), dot(zu, ub_ref[...]), dot_t(down_back, da_ref[...]))
+    dgate, *sums = expert_loop(experts, ids_ref, t_ref, c_ref, w_refs, lows, (None, None, None), moe_acc, dn2_acc, r_ref.shape[1] - width)
+    thin_ref[...] = jnp.concatenate([zg, zu, down_back], axis=1)
+    wide_ref[...] = jnp.concatenate([*lows, *sums], axis=1)
+    m_ref[...] = moe_acc[...].astype(BF)
+    r_ref[:, :width] = dn2_acc[...].astype(BF)
+    r_ref[:, width:] = dgate.astype(BF)
+
+
+def last_experts_kernel(experts, count, ids_ref, t_ref, c_ref, *refs):
+    w_refs = refs[:count]
+    ga_ref, ua_ref, gb_ref, ub_ref, db_ref, da_ref = refs[count : count + 6]
+    prior = refs[count + 6 : count + 11]
+    r1_ref, m1_ref, wide_ref, thin_ref, r_ref, m_ref = refs[count + 11 : count + 17]
+    sums = refs[count + 17 : count + 22]
+    moe_acc, dn2_acc = refs[count + 22 :]
+    width = c_ref.shape[1]
+    ff = gb_ref.shape[1]
+
+    @pl.when(pl.program_id(0) == 0)
+    def _():
+        for old, new in zip(prior, sums):
+            new[...] = old[...]
+
+    mask = row_mask(experts, t_ref, width)
+    parts = [wide_ref[:, i * ff : (i + 1) * ff] for i in range(6)]
+    dgate, act_sum, dg_sum, du_sum = expert_loop(
+        experts, ids_ref, t_ref, c_ref, w_refs, parts[:3], parts[3:], moe_acc, dn2_acc, r_ref.shape[1] - width
+    )
+    zg, zu, down_back = thin_ref[:, :LANES], thin_ref[:, LANES : 2 * LANES], thin_ref[:, 2 * LANES :]
     act_sum, dg_sum, du_sum = act_sum.astype(BF), dg_sum.astype(BF), du_sum.astype(BF)
     low = (dot(act_sum, da_ref[...]) * mask).astype(BF)
     gdu = (dot_t(dg_sum, gb_ref[...]) * mask).astype(BF)
     udu = (dot_t(du_sum, ub_ref[...]) * mask).astype(BF)
-    moe = moe_acc[...] + dot(low, db_ref[...])
+    m_ref[...] = (moe_acc[...] + dot(low, db_ref[...]) + m1_ref[...].astype(F32)).astype(BF)
     dn2 = dn2_acc[...] + dot_t(gdu, ga_ref[...]) + dot_t(udu, ua_ref[...])
-    if early:
-        moe = moe + early[1][...].astype(F32)
-        dn2 = dn2 + early[0][:, :width].astype(F32)
-        dgate = dgate + early[0][:, width:].astype(F32)
-    m_ref[...] = moe.astype(BF)
-    r_ref[:, :width] = dn2.astype(BF)
-    r_ref[:, width:] = dgate.astype(BF)
+    r_ref[:, :width] = (dn2 + r1_ref[:, :width].astype(F32)).astype(BF)
+    r_ref[:, width:] = (dgate + r1_ref[:, width:].astype(F32)).astype(BF)
     bd_ref, ad_ref, bg_ref, bu_ref, a_ref = sums
+    cot = c_ref[...]
     bd_ref[...] += t_dot_k(low, cot)
     ad_ref[...] += t_dot_k(act_sum, down_back)
     bg_ref[...] += t_dot_k(zg, dg_sum)
     bu_ref[...] += t_dot_k(zu, du_sum)
-    a_ref[...] += t_dot_k(n2, jnp.concatenate([gdu, udu], axis=1))
-
-
-def experts_on(ids, experts, spare, t, cot, weights, w_two, first, low_two, down_b, down_at, prior, early=()):
+    a_ref[...] += t_dot_k(t_ref[:, :width], jnp.concatenate([gdu, udu], axis=1))
+
+
+def experts_on(ids, experts, spare, t, cot, weights, w_two, first, low_two, down_b, down_at, prior=(), early=()):
     rows, width = cot.shape
     ff = down_at.shape[0]
     step = 256
     sd = jax.ShapeDtypeStruct
     whole = lambda a: pl.BlockSpec(a.shape, lambda i: (0, 0))
+    once = lambda a: pl.BlockSpec(a.shape, lambda i: (0, 0), pipeline_mode=pl.Buffered(1))
     by_row = lambda cols: pl.BlockSpec((step, cols), lambda i: (i, 0))
     column = lambda height, cols, at: pl.BlockSpec((height, cols), lambda i: (0, at))
     low_rows = low_two.shape[0]
     count = len(weights)
     flops = 2 * rows * width * ff * 7 * count
+    out_specs = [by_row(width + spare), by_row(width)]
+    out_shape = [sd((rows, width + spare), BF), sd((rows, width), BF)]
+    if early:
+        out_specs += [whole(p) for p in prior]
+        out_shape += [sd(p.shape, F32) for p in prior]
+    else:
+        out_specs += [by_row(6 * ff), by_row(3 * LANES)]
+        out_shape += [sd((rows, 6 * ff), F32), sd((rows, 3 * LANES), BF)]
     outs = pl.pallas_call(
-        functools.partial(expert_kernel, experts, count),
+        functools.partial(last_experts_kernel if early else first_experts_kernel, experts, count),
         grid=(rows // step,),
         in_specs=[pl.BlockSpec(memory_space=pltpu.SMEM), by_row(t.shape[1]), by_row(width)]
-        + [pl.BlockSpec(w.shape, lambda i: (0, 0), pipeline_mode=pl.Buffered(1)) for w in weights]
+        + [once(w) for w in weights]
         + [column(width, LANES, first), column(width, LANES, first + 1), column(low_rows, ff, 0), column(low_rows, ff, 1), whole(down_b), whole(down_at)]
-        + [whole(p) for p in prior] + [by_row(e.shape[1]) for e in early],
-        out_specs=[by_row(width + spare), by_row(width)] + [whole(p) for p in prior],
-        out_shape=[sd((rows, width + spare), BF), sd((rows, width), BF)] + [sd(p.shape, F32) for p in prior],
+        + [once(p) for p in prior] + [by_row(e.shape[1]) for e in early],
+        out_specs=out_specs,
+        out_shape=out_shape,
         scratch_shapes=[pltpu.VMEM((step, width), F32), pltpu.VMEM((step, width), F32)],
         input_output_aliases={3 + count + 6 + i: 2 + i for i in range(len(prior))},
         compiler_params=pltpu.CompilerParams(vmem_limit_bytes=58 << 20),
         cost_estimate=pl.CostEstimate(flops=flops, bytes_accessed=24 << 20, transcendentals=rows * ff * count),
     )(ids, t, cot, *weights, w_two, w_two, low_two, low_two, down_b, down_at, *prior, *early)
-    return outs[0], outs[1], outs[2:]
+    return outs
 
 
 class Crossing:
@@ -945,11 +996,11 @@
     begin_row = begin_local[None, :]
     start_at = jnp.reshape(start, (1,)).astype(jnp.int32)
     mixed_heads, log_total = attend(query_state, kv, far, begin_row, start_at)
-    mixed_heads = bring(2, mixed_heads)
     cot_halves, mixed_heads = lax.optimization_barrier((cot_halves, mixed_heads))
     attn_part, out_u = by_rows(
         out_kernel, 256, (mixed_heads, chosen_col), (w_two, out_a, low_two), ((width, BF), (ranks, BF)), 0
     )
+    attn_part = bring(2, attn_part)
     if n_tp == 2:
         attn_other = lax.ppermute(attn_part, "tp", [(0, 1), (1, 0)])
     else:
@@ -975,16 +1026,16 @@
     for by in range(cross.n_ctx):
         if by:
             work[by] = (cross.joined(halves[by - 1]), cross.joined(cot_halves[by - 1]))
-        r, m, sums = experts_on(ids, experts, spare, *work[by], weights, w_two, at, low_two, down_b, down_at, sums)
+        r, m, wide, thin = experts_on(ids, experts, spare, *work[by], weights, w_two, at, low_two, down_b, down_at)
         if by == 0:
             for do in range(3, outer):
                 r = bring(do, r)
             halves, cot_halves, r = lax.optimization_barrier((halves, cot_halves, r))
-        partial.append((r, m))
+        partial.append((r, m, wide, thin))
     ids, weights = weights_of(late)
     back_parts, moe_parts = [], []
     for by in list(range(1, cross.n_ctx)) + [0]:
-        r, m, sums = experts_on(ids, experts, spare, *work[by], weights, w_two, at, low_two, down_b, down_at, sums, partial[by])
+        r, m, *sums = experts_on(ids, experts, spare, *work[by], weights, w_two, at, low_two, down_b, down_at, sums, partial[by])
         moe_parts.append(m)
         if by:
             half = cross.summed_half(r).astype(BF)
@@ -1008,20 +1059,17 @@
     moe_halves = [cross.half(p).astype(F32) + q.astype(F32) for p, q in zip(moe_parts, swapped)]
     moe_got = [lax.ppermute(p.astype(BF), "ctx", cross.pairs(-by)) for by, p in zip(range(1, cross.n_ctx), moe_halves)]
     early_sum = lax.psum_scatter(early_pack, "fsdp", scatter_dimension=0, tiled=False)
-    dquery, dkey_own, dvalue_own, dkey_far, dvalue_far = attend_back(
-        query_state, kv, far, begin_row, start_at, mixed_heads, dmixed, log_total
+    dq_far, dkey_far, dvalue_far = attend_back(query_state, far, begin_row, start_at, mixed_heads, dmixed, log_total)
+    far_back = lax.ppermute(
+        jnp.concatenate([dkey_far, dvalue_far], axis=1), "ctx", [(i + 1, i) for i in range(lax.axis_size("ctx") - 1)]
     )
-    moe_got, dquery = lax.optimization_barrier((moe_got, dquery))
+    dquery, dkey_own, dvalue_own = attend_back(query_state, kv, begin_row, start_at, mixed_heads, dmixed, log_total, dq_far)
+    far_back, moe_got, dquery = lax.optimization_barrier((far_back, moe_got, dquery))
     moe = moe_halves[-1]
     for part in moe_got:
         moe = moe + part.astype(F32)
     moe = cross.joined(moe.astype(BF)).astype(F32) if n_tp == 2 else lax.psum(moe, "tp")
     output = (hidden + moe).astype(BF)
-    far_back = lax.ppermute(
-        jnp.concatenate([dkey_far, dvalue_far], axis=1),
-        "ctx",
-        [(i + 1, i) for i in range(lax.axis_size("ctx") - 1)],
-    )
     height = 3 * share + low_rows * n_tp * qkv // LANES
     dn1, pack = qkv_back(
         n, n_tp, low_rows, share, jnp.reshape(tp_at, (1,)).astype(jnp.int32), dquery, dkey_own, dvalue_own, far_back,

time: 585 us -> 576 us (0.985)
  waiting for transfers between devices: 39.1 us -> 32.2 us
    ppermute x1, waiting for transfers between devices: 14.9 us -> 0.01 us  [on_device(): lax.ppermute(jnp.concatenate([dkey_far, dvalue_far], axis=1), 'ctx', [(i...]
    pallas_call x5 -> x6, Pallas kernels: 171 us -> 168 us  [the longest x4 112 us: experts_on(): pl.pallas_call(functools.partial(last_experts_kernel if early else first_...]
  transfers between devices with their start and end apart: 23 -> 23, of which waited for: 6 -> 6; matrix products, arithmetic and copies ran while one was open for 9% -> 8% of each run, Pallas kernels for 59% -> 61%
where the time goes in v7:
time: 576 us; the launch traced here: 566 us
  Pallas kernels  422 us (73%)
  local copies, waits for them, and re-layouts  59.8 us (10%)
  waiting for transfers between devices  32.2 us (6%)
  other arithmetic  23.1 us (4%)
  between operations  15.4 us (3%)
  starting transfers between devices  13.4 us (2%)
    pallas_call x2, Pallas kernels, gather_packs(): pl.pallas_call(functools.partial(gather_kernel, n, count, len(extra)), in...  125 us
    pallas_call x4, Pallas kernels, experts_on(): pl.pallas_call(functools.partial(last_experts_kernel if early else first_...  112 us
    pallas_call x2, Pallas kernels, attend_back(): pl.pallas_call(functools.partial(attend_back_kernel, group, q_blocks, far...  56.2 us
    pallas_call x1, Pallas kernels, attend(): pl.pallas_call(functools.partial(attend_kernel, group, q_blocks), grid=(p...  34.9 us
    pallas_call x1, Pallas kernels, reduce_pack(): pl.pallas_call(functools.partial(reduce_kernel, n), in_specs=[pl.BlockSpe...  31.3 us
    pallas_call x4, Pallas kernels, by_rows(): pl.pallas_call(kernel, grid=(rows // step,), in_specs=[block(a.shape[1])...  29.4 us
    unnamed x129, local copies, waits for them, and re-layouts  24.9 us
    pallas_call x1, Pallas kernels, mid_back(): pl.pallas_call(functools.partial(mid_back_kernel, n, n_tp, experts, share...  18.5 us
  transfers between devices with their start and end apart: 23, of which 6 were waited for; matrix products, arithmetic and copies ran while one was open for 8% of the time, Pallas kernels for 61%

profile of v7, /device:TPU:0, one launch (start us, length us, event | category | flops | bytes accessed | tf_op | source)
XLA Modules:
  0.0 565.8 jit_solution(13491392966714146230)
XLA Ops:
  11.8 53.1 %shard_map.430 = (bf16[8,192,1664]{2,1,0:T(8,128)(2,1)}, bf16[8,16,1280]{2,1,0:T(8,128)(2,1)}) custom-call(bf16[192,1664]{1,0:T(8,128)(2,1)} %copy-done.37, bf16[16,1280]{1,0:T(8,128)(2,1)} %pad_maximum_fusion.3.refs_1_), custom_call_target="tpu_custom_call" | custom-call | tf_op jit(solution)/shard_map/pallas_call | solution.py:319
  71.4 7.2 %shard_map.431 = (bf16[768,1536]{1,0:T(8,128)(2,1)S(1)}, bf16[768,384]{1,0:T(8,128)(2,1)S(1)}, bf16[768,512]{1,0:T(8,128)(2,1)S(1)}) custom-call(bf16[768,1536]{1,0:T(8,128)(2,1)} %x_ref.3, s32[768,1]{1,0:T(8,128)S(1)} %broadcast_in_dim.45.chosen_ref, f32[768,128]{1,0:T(8,128)S(1)} %copy.92.cos_ref, f32[768,128]{1,0:T(8,128)S(1)} %copy.93.sin_ref, ...), custom_call_target="tpu_custom_call" | custom-call | flops 2113929216 | bytes 1048576 | tf_op jit(solution)/shard_map/pallas_call | solution.py:691
  79.5 6.2 %shard_map.432.q_ref.refs_2_ = bf16[768,768]{1,0:T(8,128)(2,1)S(1)} custom-call(bf16[768,1536]{1,0:T(8,128)(2,1)S(1)} %get-tuple-element.106.n1_ref, bf16[768,384]{1,0:T(8,128)(2,1)S(1)} %get-tuple-element.107.u_ref, f32[768,128]{1,0:T(8,128)S(1)} %copy.92.cos_ref, f32[768,128]{1,0:T(8,128)S(1)} %copy.93.sin_ref, bf16[1536,1664]{1,0:T(8,128)(2,1)} %bitcast.102, ...), custom_call_target="tpu_custom_call" | custom-call | flops 1811939328 | bytes 1048576 | tf_op jit(solution)/shard_map/pallas_call | solution.py:691
  93.2 72.1 %shard_map.433 = (bf16[8,192,1408]{2,1,0:T(8,128)(2,1)}, bf16[8,16,3712]{2,1,0:T(8,128)(2,1)}, bf16[8,64,128]{2,1,0:T(8,128)(2,1)}, bf16[768,512]{1,0:T(8,128)(2,1)}) custom-call(bf16[192,1408]{1,0:T(8,128)(2,1)} %copy-done.38, bf16[16,3712]{1,0:T(8,128)(2,1)} %copy-done.40, bf16[64,128]{1,0:T(8,128)(2,1)} %refs_2_.1, bf16[768,512]{1,0:T(8,128)(2,1)} %copy-done.16), custom_call_target="tpu_custom_call" | custom-call | tf_op jit(solution)/shard_map/pallas_call | solution.py:319
  170.8 34.9 %shard_map.434 = (bf16[768,768]{1,0:T(8,128)(2,1)S(1)}, f32[2,8,768]{2,1,0:T(8,128)S(1)}) custom-call(s32[1]{0:T(128)} %bitcast.11.start_ref.refs_0_, s32[1,768]{1,0:T(1,128)S(1)} %broadcast_in_dim.38.begin_ref.refs_1_, bf16[768,768]{1,0:T(8,128)(2,1)S(1)} %shard_map.432.q_ref.refs_2_, bf16[768,512]{1,0:T(8,128)(2,1)S(1)} %copy-done.17, ...), custom_call_target="tpu_custom_call" | custom-call | flops 3623878656 | bytes 8388608 | tf_op jit(solution)/shard_map/pallas_call | solution.py:97
  206.4 7.0 %shard_map.435 = (bf16[768,1536]{1,0:T(8,128)(2,1)}, bf16[768,128]{1,0:T(8,128)(2,1)S(1)}) custom-call(bf16[768,768]{1,0:T(8,128)(2,1)S(1)} %get-tuple-element.119.o_ref.refs_5_, s32[768,1]{1,0:T(8,128)S(1)} %broadcast_in_dim.45.chosen_ref, bf16[1536,1408]{1,0:T(8,128)(2,1)} %bitcast.105, bf16[768,128]{1,0:T(8,128)(2,1)S(1)} %constant_dynamic-slice_fusion.6.oa_ref, ...), custom_call_target="tpu_custom_call" | custom-call | bytes 1048576 | tf_op jit(solution)/shard_map/pallas_call | solution.py:691
  224.8 9.1 %shard_map.436 = (f32[768,1536]{1,0:T(8,128)}, bf16[768,1664]{1,0:T(8,128)(2,1)}, bf16[768,128]{1,0:T(8,128)(2,1)S(1)}) custom-call(bf16[768,1536]{1,0:T(8,128)(2,1)S(1)} %copy-done.2, bf16[768,1536]{1,0:T(8,128)(2,1)} %get-tuple-element.122.one_ref, bf16[768,1536]{1,0:T(8,128)(2,1)} %collective-permute-done.5.other_ref, ...), custom_call_target="tpu_custom_call" | custom-call | bytes 1048576 | tf_op jit(solution)/shard_map/pallas_call | solution.py:691
  236.6 31.2 %shard_map.437 = (bf16[768,1664]{1,0:T(8,128)(2,1)}, bf16[768,1536]{1,0:T(8,128)(2,1)}, f32[768,1536]{1,0:T(8,128)}, bf16[768,384]{1,0:T(8,128)(2,1)}) custom-call(s32[6]{0:T(128)} %stack.51.ids_ref, bf16[768,1664]{1,0:T(8,128)(2,1)} %get-tuple-element.141.t_ref, bf16[768,1536]{1,0:T(8,128)(2,1)} %c_ref.2, bf16[1536,768]{1,0:T(8,128)(2,1)} %bitcast.23.refs_0_, ...), custom_call_target="tpu_custom_call" | custom-call | flops 21139292160 | bytes 25165824 | tf_op jit(solution)/shard_map/pallas_call | solution.py:466
  267.8 7.9 %collective-permute-done.7 = bf16[1,1536,768]{2,1,0:T(8,128)(2,1)} collective-permute-done((bf16[1,1536,768]{2,1,0:T(8,128)(2,1)}, bf16[1,1536,768]{2,1,0:T(8,128)(2,1)}, u32[]{:S(2)}, u32[]{:S(2)}) %collective-permute-start.7) | collective-permute-done | bytes 2359328 | tf_op jit(solution)/shard_map/ppermute | solution.py:969
  286.9 31.4 %shard_map.438 = (bf16[768,1664]{1,0:T(8,128)(2,1)}, bf16[768,1536]{1,0:T(8,128)(2,1)}, f32[768,1536]{1,0:T(8,128)}, bf16[768,384]{1,0:T(8,128)(2,1)}) custom-call(s32[6]{0:T(128)} %stack.51.ids_ref, bf16[768,1664]{1,0:T(8,128)(2,1)} %copy-done.31, bf16[768,1536]{1,0:T(8,128)(2,1)} %copy-done.33, bf16[1536,768]{1,0:T(8,128)(2,1)} %bitcast.23.refs_0_, ...), custom_call_target="tpu_custom_call" | custom-call | flops 21139292160 | bytes 25165824 | tf_op jit(solution)/shard_map/pallas_call | solution.py:466
  318.3 12.1 %collective-permute-done.11 = bf16[1,1536,768]{2,1,0:T(8,128)(2,1)} collective-permute-done((bf16[1,1536,768]{2,1,0:T(8,128)(2,1)}, bf16[1,1536,768]{2,1,0:T(8,128)(2,1)}, u32[]{:S(2)}, u32[]{:S(2)}) %collective-permute-start.11) | collective-permute-done | bytes 2359328 | tf_op jit(solution)/shard_map/ppermute | solution.py:971
  334.6 24.8 %shard_map.439 = (bf16[768,1664]{1,0:T(8,128)(2,1)}, bf16[768,1536]{1,0:T(8,128)(2,1)}, f32[128,1536]{1,0:T(8,128)}, f32[256,128]{1,0:T(8,128)}, f32[128,256]{1,...) custom-call(s32[4]{0:T(128)} %pad_add_fusion.ids_ref, ...), custom_call_target="tpu_custom_call", output_to_operand_aliasing={{2}: (12, {}), {3}: (13, {}), {4}: (14, {}), {5}: (15, {}),... | custom-call | flops 12683575296 | bytes 25165824 | tf_op jit(solution)/shard_map/pallas_call | solution.py:466
  361.0 3.0 collective-permute-done.12
  365.4 24.7 %shard_map.440 = (bf16[768,1664]{1,0:T(8,128)(2,1)}, bf16[768,1536]{1,0:T(8,128)(2,1)}, f32[128,1536]{1,0:T(8,128)}, f32[256,128]{1,0:T(8,128)}, f32[128,256]{1,...) custom-call(s32[4]{0:T(128)} %pad_add_fusion.ids_ref, ...), custom_call_target="tpu_custom_call", output_to_operand_aliasing={{2}: (12, {}), {3}: (13, {}), {4}: (14, {}), {5}: (15, {}),... | custom-call | flops 12683575296 | bytes 25165824 | tf_op jit(solution)/shard_map/pallas_call | solution.py:466
  390.1 4.3 collective-permute-done.13
  395.9 3.0 collective-permute-done.14
  404.4 18.5 %shard_map.441 = (f32[768,1536]{1,0:T(8,128)}, bf16[768,768]{1,0:T(8,128)(2,1)}, bf16[8,1360,128]{2,1,0:T(8,128)(2,1)}) custom-call(s32[2]{0:T(128)} %pad_add_fusion.1.sel_ref, bf16[384,1664]{1,0:T(8,128)(2,1)} %copy-done.39, bf16[384,1664]{1,0:T(8,128)(2,1)} %copy-done.52, f32[768,1536]{1,0:T(8,128)} %get-tuple-element.123.h_ref, bf16[768,1536]{1,0:T(8,128)(2,1)} %c_ref.2, ...), custom_call_target="tpu_custom_call" | custom-call | flops 7247757312 | bytes 33554432 | tf_op jit(solution)/shard_map/pallas_call | solution.py:788
  426.1 30.1 %shard_map.442 = (f32[768,768]{1,0:T(8,128)}, bf16[768,256]{1,0:T(8,128)(2,1)}, bf16[768,256]{1,0:T(8,128)(2,1)}) custom-call(s32[1]{0:T(128)} %bitcast.11.start_ref.refs_0_, s32[1,768]{1,0:T(1,128)} %copy-done.22, bf16[768,768]{1,0:T(8,128)(2,1)} %copy-done.13, bf16[768,512]{1,0:T(8,128)(2,1)} %get-tuple-element.117.kf_ref.vf_ref.refs_3_.refs_4_, ...), custom_call_target="tpu_custom_call" | custom-call | flops 5435817984 | bytes 16777216 | tf_op jit(solution)/shard_map/pallas_call | solution.py:184
  458.6 26.1 %shard_map.443 = (f32[768,768]{1,0:T(8,128)}, f32[768,256]{1,0:T(8,128)}, f32[768,256]{1,0:T(8,128)}) custom-call(s32[1]{0:T(128)} %bitcast.11.start_ref.refs_0_, s32[1,768]{1,0:T(1,128)} %copy-done.22, bf16[768,768]{1,0:T(8,128)(2,1)} %copy-done.13, bf16[768,512]{1,0:T(8,128)(2,1)} %copy-done.16, bf16[768,512]{1,0:T(8,128)(2,1)} %copy-done.16, ...), custom_call_target="tpu_custom_call" | custom-call | flops 5435817984 | bytes 16777216 | tf_op jit(solution)/shard_map/pallas_call | solution.py:184
  487.5 3.3 constant_dynamic-update-slice_fusion.16
  490.9 14.3 %shard_map.444 = (bf16[768,1536]{1,0:T(8,128)(2,1)}, f32[8,896,128]{2,1,0:T(8,128)}) custom-call(s32[1]{0:T(128)} %bitcast.32.tp_ref, f32[768,768]{1,0:T(8,128)} %get-tuple-element.177.dq_ref, f32[768,256]{1,0:T(8,128)S(1)} %copy-done.26, f32[768,256]{1,0:T(8,128)S(1)} %copy-done.27, bf16[768,512]{1,0:T(8,128)(2,1)} %copy-done.53, ...), custom_call_target="tpu_custom_call" | custom-call | flops 7851737088 | bytes 25165824 | tf_op jit(solution)/shard_map/pallas_call | solution.py:613
  508.1 5.4 add_convert_fusion
  513.5 31.3 %shard_map.445 = (f32[896,128]{1,0:T(8,128)S(1)}, f32[1360,128]{1,0:T(8,128)S(1)}) custom-call(f32[8,896,128]{2,1,0:T(8,128)S(1)} %copy-done.8, bf16[1360,128]{1,0:T(8,128)(2,1)S(1)} %bitcast.100), custom_call_target="tpu_custom_call" | custom-call | tf_op jit(solution)/shard_map/pallas_call | solution.py:875
  553.8 4.7 fusion.3
  (242 shorter events, 84.8 us)
Async XLA Ops:
  7.3 497.9 %reduce-scatter.2.cloned.1.call-start = ((), (), s32[]{:S(2)}) async-start(), calls=%async_computation.1 | async-start | bytes 3133440 | tf_op jit(solution)/shard_map/reduce_scatter | solution.py:1061
  68.0 97.4 %collective-permute-start = (bf16[1,1536,768]{2,1,0:T(8,128)(2,1)}, bf16[1,1536,768]{2,1,0:T(8,128)(2,1)}, u32[]{:S(2)}, u32[]{:S(2)}) collective-permute-start(bf16[1,1536,768]{2,1,0:T(8,128)(2,1)} %pad_maximum_fusion), channel_id=1, source_target_pairs={{0,8},{4,12},{8,16},{12,20},{16,24},{20,28},{24,0},{28,4},{1,9},{5... | collective-permute-start | bytes 7077896 | tf_op jit(solution)/shard_map/ppermute | solution.py:969
  69.3 96.1 %collective-permute-start.1 = (bf16[1,1536,768]{2,1,0:T(8,128)(2,1)}, bf16[1,1536,768]{2,1,0:T(8,128)(2,1)}, u32[]{:S(2)}, u32[]{:S(2)}) collective-permute-start(bf16[1,1536,768]{2,1,0:T(8,128)(2,1)} %pad_maximum_fusion), channel_id=1, source_target_pairs={{0,4},{4,0},{8,12},{12,8},{16,20},{20,16},{24,28},{28,24},{1,5},{5... | collective-permute-start | bytes 7077896 | tf_op jit(solution)/shard_map/ppermute | solution.py:971
  71.4 151.2 %copy-start.4 = (s32[768,1]{1,0:T(8,128)}, s32[768,1]{1,0:T(8,128)S(1)}, u32[]{:S(2)}) copy-start(s32[768,1]{1,0:T(8,128)S(1)} %broadcast_in_dim.45.chosen_ref) | copy-start | bytes 9220
  165.4 50.5 %collective-permute-start.2 = (bf16[1,1536,768]{2,1,0:T(8,128)(2,1)}, bf16[1,1536,768]{2,1,0:T(8,128)(2,1)}, u32[]{:S(2)}, u32[]{:S(2)}) collective-permute-start(bf16[1,1536,768]{2,1,0:T(8,128)(2,1)} %collective-permute-done), channel_id=1, source_target_pairs={{0,8},{4,12},{8,16},{12,20},{16,24},{20,28},{24,0},{28,4},{1,9},{5... | collective-permute-start | bytes 7077896 | tf_op jit(solution)/shard_map/ppermute | solution.py:969
  165.5 50.5 %collective-permute-start.3 = (bf16[1,1536,768]{2,1,0:T(8,128)(2,1)}, bf16[1,1536,768]{2,1,0:T(8,128)(2,1)}, u32[]{:S(2)}, u32[]{:S(2)}) collective-permute-start(bf16[1,1536,768]{2,1,0:T(8,128)(2,1)} %collective-permute-done), channel_id=1, source_target_pairs={{0,4},{4,0},{8,12},{12,8},{16,20},{20,16},{24,28},{28,24},{1,5},{5... | collective-permute-start | bytes 7077896 | tf_op jit(solution)/shard_map/ppermute | solution.py:971
  168.5 37.9 %collective-permute-start.4 = (bf16[384,1536]{1,0:T(8,128)(2,1)S(1)}, bf16[384,1536]{1,0:T(8,128)(2,1)}, u32[]{:S(2)}, u32[]{:S(2)}) collective-permute-start(bf16[384,1536]{1,0:T(8,128)(2,1)S(1)} %constant_dynamic-slice_fusion.7), channel_id=1, source_target_pairs={{0,2},{2,0},{1,3},{3,1},{4,6},{6,4},{5,7},{7,5},{8,10},{10,8},{9,1... | collective-permute-start | bytes 3538952 | tf_op jit(solution)/shard_map/ppermute | solution.py:511
  216.0 6.6 %collective-permute-start.5 = (bf16[768,1536]{1,0:T(8,128)(2,1)}, bf16[768,1536]{1,0:T(8,128)(2,1)}, u32[]{:S(2)}, u32[]{:S(2)}) collective-permute-start(bf16[768,1536]{1,0:T(8,128)(2,1)} %get-tuple-element.122.one_ref), channel_id=1, source_target_pairs={{0,1},{1,0},{2,3},{3,2},{4,5},{5,4},{6,7},{7,6},{8,9},{9,8},{10,11... | collective-permute-start | bytes 7077896 | tf_op jit(solution)/shard_map/ppermute | solution.py:1005
  219.7 56.0 %collective-permute-start.7 = (bf16[1,1536,768]{2,1,0:T(8,128)(2,1)}, bf16[1,1536,768]{2,1,0:T(8,128)(2,1)}, u32[]{:S(2)}, u32[]{:S(2)}) collective-permute-start(bf16[1,1536,768]{2,1,0:T(8,128)(2,1)} %collective-permute-done.2), channel_id=1, source_target_pairs={{0,8},{4,12},{8,16},{12,20},{16,24},{20,28},{24,0},{28,4},{1,9},{5... | collective-permute-start | bytes 7077896 | tf_op jit(solution)/shard_map/ppermute | solution.py:969
  219.9 55.8 %collective-permute-start.8 = (bf16[1,1536,768]{2,1,0:T(8,128)(2,1)}, bf16[1,1536,768]{2,1,0:T(8,128)(2,1)}, u32[]{:S(2)}, u32[]{:S(2)}) collective-permute-start(bf16[1,1536,768]{2,1,0:T(8,128)(2,1)} %collective-permute-done.2), channel_id=1, source_target_pairs={{0,4},{4,0},{8,12},{12,8},{16,20},{20,16},{24,28},{28,24},{1,5},{5... | collective-permute-start | bytes 7077896 | tf_op jit(solution)/shard_map/ppermute | solution.py:971
  235.9 39.8 %collective-permute-start.6 = (bf16[384,1664]{1,0:T(8,128)(2,1)S(1)}, bf16[384,1664]{1,0:T(8,128)(2,1)}, u32[]{:S(2)}, u32[]{:S(2)}) collective-permute-start(bf16[384,1664]{1,0:T(8,128)(2,1)S(1)} %constant_dynamic-slice_fusion.5), channel_id=1, source_target_pairs={{0,2},{2,0},{1,3},{3,1},{4,6},{6,4},{5,7},{7,5},{8,10},{10,8},{9,1... | collective-permute-start | bytes 3833864 | tf_op jit(solution)/shard_map/ppermute | solution.py:511
  275.7 5.4 collective-permute-start.10
  275.7 8.2 %collective-permute-start.9 = (bf16[384,1664]{1,0:T(8,128)(2,1)}, bf16[384,1664]{1,0:T(8,128)(2,1)}, u32[]{:S(2)}, u32[]{:S(2)}) collective-permute-start(bf16[384,1664]{1,0:T(8,128)(2,1)} %collective-permute-done.6), channel_id=1, source_target_pairs={{0,1},{1,0},{2,3},{3,2},{4,5},{5,4},{6,7},{7,6},{8,9},{9,8},{10,11... | collective-permute-start | bytes 3833864 | tf_op jit(solution)/shard_map/ppermute | solution.py:504
  276.8 53.5 %collective-permute-start.11 = (bf16[1,1536,768]{2,1,0:T(8,128)(2,1)}, bf16[1,1536,768]{2,1,0:T(8,128)(2,1)}, u32[]{:S(2)}, u32[]{:S(2)}) collective-permute-start(bf16[1,1536,768]{2,1,0:T(8,128)(2,1)} %collective-permute-done.7), channel_id=1, source_target_pairs={{0,4},{4,0},{8,12},{12,8},{16,20},{20,16},{24,28},{28,24},{1,5},{5... | collective-permute-start | bytes 7077896 | tf_op jit(solution)/shard_map/ppermute | solution.py:971
  360.9 3.1 collective-permute-start.12
  364.3 30.2 %collective-permute-start.13 = (bf16[384,1664]{1,0:T(8,128)(2,1)S(1)}, bf16[384,1664]{1,0:T(8,128)(2,1)S(1)}, u32[]{:S(2)}, u32[]{:S(2)}) collective-permute-start(bf16[384,1664]{1,0:T(8,128)(2,1)S(1)} %add_convert_fusion.2), channel_id=1, source_target_pairs={{0,2},{2,0},{1,3},{3,1},{4,6},{6,4},{5,7},{7,5},{8,10},{10,8},{9,1... | collective-permute-start | bytes 3833864 | tf_op jit(solution)/shard_map/ppermute | solution.py:1044
  395.9 3.1 collective-permute-start.14
  399.4 4.0 collective-permute-start.15
  399.7 23.2 %collective-permute-start.16 = (bf16[384,1536]{1,0:T(8,128)(2,1)S(1)}, bf16[384,1536]{1,0:T(8,128)(2,1)}, u32[]{:S(2)}, u32[]{:S(2)}) collective-permute-start(bf16[384,1536]{1,0:T(8,128)(2,1)S(1)} %constant_dynamic-slice_fusion.1), channel_id=1, source_target_pairs={{0,1},{1,0},{2,3},{3,2},{4,5},{5,4},{6,7},{7,6},{8,9},{9,8},{10,11... | collective-permute-start | bytes 3538952 | tf_op jit(solution)/shard_map/ppermute | solution.py:521
  402.6 20.3 %collective-permute-start.17 = (bf16[384,1536]{1,0:T(8,128)(2,1)}, bf16[384,1536]{1,0:T(8,128)(2,1)}, u32[]{:S(2)}, u32[]{:S(2)}) collective-permute-start(bf16[384,1536]{1,0:T(8,128)(2,1)} %constant_dynamic-slice_fusion), channel_id=1, source_target_pairs={{0,1},{1,0},{2,3},{3,2},{4,5},{5,4},{6,7},{7,6},{8,9},{9,8},{10,11... | collective-permute-start | bytes 3538952 | tf_op jit(solution)/shard_map/ppermute | solution.py:521
  424.9 59.8 %collective-permute-start.19 = (bf16[384,1536]{1,0:T(8,128)(2,1)S(1)}, bf16[384,1536]{1,0:T(8,128)(2,1)S(1)}, u32[]{:S(2)}, u32[]{:S(2)}) collective-permute-start(bf16[384,1536]{1,0:T(8,128)(2,1)S(1)} %add_convert_fusion.4), channel_id=1, source_target_pairs={{0,2},{2,0},{1,3},{3,1},{4,6},{6,4},{5,7},{7,5},{8,10},{10,8},{9,1... | collective-permute-start | bytes 3538952 | tf_op jit(solution)/shard_map/ppermute | solution.py:1060
  457.3 27.4 %collective-permute-start.18 = (bf16[768,512]{1,0:T(8,128)(2,1)S(1)}, bf16[768,512]{1,0:T(8,128)(2,1)S(1)}, u32[]{:S(2)}, u32[]{:S(2)}) collective-permute-start(bf16[768,512]{1,0:T(8,128)(2,1)S(1)} %pad_maximum_fusion.1), channel_id=1, source_target_pairs={{2,0},{3,1},{6,4},{7,5},{10,8},{11,9},{14,12},{15,13},{18,16},{19,... | collective-permute-start | bytes 2359304 | tf_op jit(solution)/shard_map/ppermute | solution.py:1063
  490.8 14.9 %collective-permute-start.20 = (bf16[384,1536]{1,0:T(8,128)(2,1)}, bf16[384,1536]{1,0:T(8,128)(2,1)}, u32[]{:S(2)}, u32[]{:S(2)}) collective-permute-start(bf16[384,1536]{1,0:T(8,128)(2,1)} %get-tuple-element.193), channel_id=1, source_target_pairs={{0,1},{1,0},{2,3},{3,2},{4,5},{5,4},{6,7},{7,6},{8,9},{9,8},{10,11... | collective-permute-start | bytes 3538952 | tf_op jit(solution)/shard_map/ppermute | solution.py:504
  505.2 46.9 %collective-permute-start.21 = (bf16[768,1536]{1,0:T(8,128)(2,1)}, bf16[768,1536]{1,0:T(8,128)(2,1)S(1)}, u32[]{:S(2)}, u32[]{:S(2)}) collective-permute-start(bf16[768,1536]{1,0:T(8,128)(2,1)} %get-tuple-element.183), channel_id=1, source_target_pairs={{0,1},{1,0},{2,3},{3,2},{4,5},{5,4},{6,7},{7,6},{8,9},{9,8},{10,11... | collective-permute-start | bytes 7077896 | tf_op jit(solution)/shard_map/ppermute | solution.py:1080
  (54 other events, 466.0 us)
Sparse Core Ops, SparseCore 0:
  423.1 72.3 reduce-scatter.1

commit v8 on v7

--- a/solution.py
+++ b/solution.py
@@ -1013,6 +1013,8 @@
     halves = cross.fetch(carried)
     early = [(0, 0), (1, 0)] + [(0, dj) for dj in range(1, inner)] + [(2, 0)] + [(1, dj) for dj in range(1, inner)]
     late = [(do, 0) for do in range(3, outer)] + [(do, dj) for do in range(2, outer) for dj in range(1, inner)]
+    last = [k for k in late if k[0] == outer - 1 and k[1]]
+    between = [k for k in late if k not in last]
 
     def weights_of(keys):
         ids = [((me // inner + outer - do) % outer * inner + (me % inner + inner - dj) % inner) * local_experts + ctx_at * local + j for do, dj in keys for j in range(local)]
@@ -1022,8 +1024,8 @@
     at = q_width // LANES + 1
     work = [(carried, cot)] + [(None, None)] * (cross.n_ctx - 1)
     partial = []
-    ids, weights = weights_of(early)
     for by in range(cross.n_ctx):
+        ids, weights = weights_of(early + between if by else early)
         if by:
             work[by] = (cross.joined(halves[by - 1]), cross.joined(cot_halves[by - 1]))
         r, m, wide, thin = experts_on(ids, experts, spare, *work[by], weights, w_two, at, low_two, down_b, down_at)
@@ -1032,9 +1034,9 @@
                 r = bring(do, r)
             halves, cot_halves, r = lax.optimization_barrier((halves, cot_halves, r))
         partial.append((r, m, wide, thin))
-    ids, weights = weights_of(late)
     back_parts, moe_parts = [], []
     for by in list(range(1, cross.n_ctx)) + [0]:
+        ids, weights = weights_of(last if by else late)
         r, m, *sums = experts_on(ids, experts, spare, *work[by], weights, w_two, at, low_two, down_b, down_at, sums, partial[by])
         moe_parts.append(m)
         if by:

time: 576 us -> 563 us (0.977)
  local copies, waits for them, and re-layouts: 59.8 us -> 50 us
  waiting for transfers between devices: 32.2 us -> 24.2 us
    ppermute x4, waiting for transfers between devices: 12.1 us -> 4.26 us  [bring(): brought[do, dj] = lax.ppermute(last[0], 'fsdp', turns[dj - 1])]
    unnamed x129 -> x163, local copies, waits for them, and re-layouts: 24.9 us -> 18.8 us
  transfers between devices with their start and end apart: 23 -> 23, of which waited for: 6 -> 8; matrix products, arithmetic and copies ran while one was open for 8% -> 7% of each run, Pallas kernels for 61% -> 65%
where the time goes in v8:
time: 563 us; the launch traced here: 553 us
  Pallas kernels  426 us (76%)
  local copies, waits for them, and re-layouts  50 us (9%)
  waiting for transfers between devices  24.2 us (4%)
  other arithmetic  23.7 us (4%)
  between operations  15.7 us (3%)
  starting transfers between devices  14 us (2%)
    pallas_call x2, Pallas kernels, gather_packs(): pl.pallas_call(functools.partial(gather_kernel, n, count, len(extra)), in...  129 us
    pallas_call x4, Pallas kernels, experts_on(): pl.pallas_call(functools.partial(last_experts_kernel if early else first_...  112 us
    pallas_call x2, Pallas kernels, attend_back(): pl.pallas_call(functools.partial(attend_back_kernel, group, q_blocks, far...  56.2 us
    pallas_call x1, Pallas kernels, attend(): pl.pallas_call(functools.partial(attend_kernel, group, q_blocks), grid=(p...  34.8 us
    pallas_call x1, Pallas kernels, reduce_pack(): pl.pallas_call(functools.partial(reduce_kernel, n), in_specs=[pl.BlockSpe...  31.3 us
    pallas_call x4, Pallas kernels, by_rows(): pl.pallas_call(kernel, grid=(rows // step,), in_specs=[block(a.shape[1])...  29.7 us
    unnamed x163, local copies, waits for them, and re-layouts  18.8 us
    pallas_call x1, Pallas kernels, mid_back(): pl.pallas_call(functools.partial(mid_back_kernel, n, n_tp, experts, share...  18.7 us
  transfers between devices with their start and end apart: 23, of which 8 were waited for; matrix products, arithmetic and copies ran while one was open for 7% of the time, Pallas kernels for 65%

profile of v8, /device:TPU:0, one launch (start us, length us, event | category | flops | bytes accessed | tf_op | source)
XLA Modules:
  0.0 553.2 jit_solution(4992038285548717092)
XLA Ops:
  11.2 53.1 %shard_map.430 = (bf16[8,192,1664]{2,1,0:T(8,128)(2,1)}, bf16[8,16,1280]{2,1,0:T(8,128)(2,1)}) custom-call(bf16[192,1664]{1,0:T(8,128)(2,1)} %copy-done.42, bf16[16,1280]{1,0:T(8,128)(2,1)} %pad_maximum_fusion.3.refs_1_), custom_call_target="tpu_custom_call" | custom-call | tf_op jit(solution)/shard_map/pallas_call | solution.py:319
  70.9 7.2 %shard_map.431 = (bf16[768,1536]{1,0:T(8,128)(2,1)S(1)}, bf16[768,384]{1,0:T(8,128)(2,1)S(1)}, bf16[768,512]{1,0:T(8,128)(2,1)S(1)}) custom-call(bf16[768,1536]{1,0:T(8,128)(2,1)} %x_ref.3, s32[768,1]{1,0:T(8,128)S(1)} %broadcast_in_dim.45.chosen_ref, f32[768,128]{1,0:T(8,128)S(1)} %copy.92.cos_ref, f32[768,128]{1,0:T(8,128)S(1)} %copy.93.sin_ref, ...), custom_call_target="tpu_custom_call" | custom-call | flops 2113929216 | bytes 1048576 | tf_op jit(solution)/shard_map/pallas_call | solution.py:691
  79.1 6.0 %shard_map.432.q_ref.refs_2_ = bf16[768,768]{1,0:T(8,128)(2,1)S(1)} custom-call(bf16[768,1536]{1,0:T(8,128)(2,1)S(1)} %get-tuple-element.106.n1_ref, bf16[768,384]{1,0:T(8,128)(2,1)S(1)} %get-tuple-element.107.u_ref, f32[768,128]{1,0:T(8,128)S(1)} %copy.92.cos_ref, f32[768,128]{1,0:T(8,128)S(1)} %copy.93.sin_ref, bf16[1536,1664]{1,0:T(8,128)(2,1)} %bitcast.114, ...), custom_call_target="tpu_custom_call" | custom-call | flops 1811939328 | bytes 1048576 | tf_op jit(solution)/shard_map/pallas_call | solution.py:691
  89.4 75.4 %shard_map.433 = (bf16[8,192,1408]{2,1,0:T(8,128)(2,1)}, bf16[8,16,3712]{2,1,0:T(8,128)(2,1)}, bf16[8,64,128]{2,1,0:T(8,128)(2,1)}, bf16[768,512]{1,0:T(8,128)(2,1)}) custom-call(bf16[192,1408]{1,0:T(8,128)(2,1)} %copy-done.43, bf16[16,3712]{1,0:T(8,128)(2,1)} %copy-done.48, bf16[64,128]{1,0:T(8,128)(2,1)} %refs_2_.1, bf16[768,512]{1,0:T(8,128)(2,1)} %copy-done.21), custom_call_target="tpu_custom_call" | custom-call | tf_op jit(solution)/shard_map/pallas_call | solution.py:319
  170.3 34.8 %shard_map.434 = (bf16[768,768]{1,0:T(8,128)(2,1)S(1)}, f32[2,8,768]{2,1,0:T(8,128)S(1)}) custom-call(s32[1]{0:T(128)} %bitcast.11.start_ref.refs_0_, s32[1,768]{1,0:T(1,128)S(1)} %broadcast_in_dim.38.begin_ref.refs_1_, bf16[768,768]{1,0:T(8,128)(2,1)S(1)} %shard_map.432.q_ref.refs_2_, bf16[768,512]{1,0:T(8,128)(2,1)S(1)} %copy-done.22, ...), custom_call_target="tpu_custom_call" | custom-call | flops 3623878656 | bytes 8388608 | tf_op jit(solution)/shard_map/pallas_call | solution.py:97
  205.9 7.5 %shard_map.435 = (bf16[768,1536]{1,0:T(8,128)(2,1)}, bf16[768,128]{1,0:T(8,128)(2,1)S(1)}) custom-call(bf16[768,768]{1,0:T(8,128)(2,1)S(1)} %get-tuple-element.119.o_ref.refs_5_, s32[768,1]{1,0:T(8,128)S(1)} %copy-done.6, bf16[1536,1408]{1,0:T(8,128)(2,1)} %bitcast.102, bf16[768,128]{1,0:T(8,128)(2,1)S(1)} %constant_dynamic-slice_fusion.6.oa_ref, ...), custom_call_target="tpu_custom_call" | custom-call | bytes 1048576 | tf_op jit(solution)/shard_map/pallas_call | solution.py:691
  222.3 9.0 %shard_map.436 = (f32[768,1536]{1,0:T(8,128)}, bf16[768,1664]{1,0:T(8,128)(2,1)}, bf16[768,128]{1,0:T(8,128)(2,1)S(1)}) custom-call(bf16[768,1536]{1,0:T(8,128)(2,1)S(1)} %copy-done.2, bf16[768,1536]{1,0:T(8,128)(2,1)} %get-tuple-element.122.one_ref, bf16[768,1536]{1,0:T(8,128)(2,1)} %collective-permute-done.5.other_ref, s32[768,1]{1,0:T(8,128)S(1)} %copy-done.7, ...), custom_call_target="tpu_custom_call" | custom-call | bytes 1048576 | tf_op jit(solution)/shard_map/pallas_call | solution.py:691
  234.6 31.1 %shard_map.437 = (bf16[768,1664]{1,0:T(8,128)(2,1)}, bf16[768,1536]{1,0:T(8,128)(2,1)}, f32[768,1536]{1,0:T(8,128)}, bf16[768,384]{1,0:T(8,128)(2,1)}) custom-call(s32[6]{0:T(128)} %stack.68.ids_ref, bf16[768,1664]{1,0:T(8,128)(2,1)} %get-tuple-element.141.t_ref, bf16[768,1536]{1,0:T(8,128)(2,1)} %c_ref.2, bf16[1536,768]{1,0:T(8,128)(2,1)} %bitcast.23.refs_0_, ...), custom_call_target="tpu_custom_call" | custom-call | flops 21139292160 | bytes 25165824 | tf_op jit(solution)/shard_map/pallas_call | solution.py:466
  265.6 8.1 %collective-permute-done.7 = bf16[1,1536,768]{2,1,0:T(8,128)(2,1)} collective-permute-done((bf16[1,1536,768]{2,1,0:T(8,128)(2,1)}, bf16[1,1536,768]{2,1,0:T(8,128)(2,1)}, u32[]{:S(2)}, u32[]{:S(2)}) %collective-permute-start.7) | collective-permute-done | bytes 2359328 | tf_op jit(solution)/shard_map/ppermute | solution.py:969
  283.8 41.0 %shard_map.438 = (bf16[768,1664]{1,0:T(8,128)(2,1)}, bf16[768,1536]{1,0:T(8,128)(2,1)}, f32[768,1536]{1,0:T(8,128)}, bf16[768,384]{1,0:T(8,128)(2,1)}) custom-call(s32[8]{0:T(128)} %stack.69.ids_ref, bf16[768,1664]{1,0:T(8,128)(2,1)} %copy-done.34, bf16[768,1536]{1,0:T(8,128)(2,1)} %copy-done.35, bf16[1536,768]{1,0:T(8,128)(2,1)} %bitcast.23.refs_0_, ...), custom_call_target="tpu_custom_call" | custom-call | flops 29595009024 | bytes 25165824 | tf_op jit(solution)/shard_map/pallas_call | solution.py:466
  324.8 4.3 collective-permute-done.11
  333.2 15.3 %shard_map.439 = (bf16[768,1664]{1,0:T(8,128)(2,1)}, bf16[768,1536]{1,0:T(8,128)(2,1)}, f32[128,1536]{1,0:T(8,128)}, f32[256,128]{1,0:T(8,128)}, f32[128,256]{1,...) custom-call(s32[2]{0:T(128)} %pad_add_fusion.1.ids_ref, ...), custom_call_target="tpu_custom_call", output_to_operand_aliasing={{2}: (10, {}), {3}: (11, {}), {4}: (12, {}), {5}: (13, {}),... | custom-call | flops 4227858432 | bytes 25165824 | tf_op jit(solution)/shard_map/pallas_call | solution.py:466
  350.2 3.0 collective-permute-done.12
  355.2 24.6 %shard_map.440 = (bf16[768,1664]{1,0:T(8,128)(2,1)}, bf16[768,1536]{1,0:T(8,128)(2,1)}, f32[128,1536]{1,0:T(8,128)}, f32[256,128]{1,0:T(8,128)}, f32[128,256]{1,...) custom-call(s32[4]{0:T(128)} %pad_add_fusion.ids_ref, ...), custom_call_target="tpu_custom_call", output_to_operand_aliasing={{2}: (12, {}), {3}: (13, {}), {4}: (14, {}), {5}: (15, {}),... | custom-call | flops 12683575296 | bytes 25165824 | tf_op jit(solution)/shard_map/pallas_call | solution.py:466
  379.9 3.8 collective-permute-done.13
  385.2 3.0 collective-permute-done.14
  392.8 18.7 %shard_map.441 = (f32[768,1536]{1,0:T(8,128)}, bf16[768,768]{1,0:T(8,128)(2,1)}, bf16[8,1360,128]{2,1,0:T(8,128)(2,1)}) custom-call(s32[2]{0:T(128)} %pad_add_fusion.2.sel_ref, bf16[384,1664]{1,0:T(8,128)(2,1)} %copy-done.44, bf16[384,1664]{1,0:T(8,128)(2,1)} %copy-done.69, f32[768,1536]{1,0:T(8,128)} %get-tuple-element.123.h_ref, bf16[768,1536]{1,0:T(8,128)(2,1)} %c_ref.2, ...), custom_call_target="tpu_custom_call" | custom-call | flops 7247757312 | bytes 33554432 | tf_op jit(solution)/shard_map/pallas_call | solution.py:788
  414.6 30.1 %shard_map.442 = (f32[768,768]{1,0:T(8,128)}, bf16[768,256]{1,0:T(8,128)(2,1)}, bf16[768,256]{1,0:T(8,128)(2,1)}) custom-call(s32[1]{0:T(128)} %bitcast.11.start_ref.refs_0_, s32[1,768]{1,0:T(1,128)} %copy-done.27, bf16[768,768]{1,0:T(8,128)(2,1)} %copy-done.18, bf16[768,512]{1,0:T(8,128)(2,1)} %get-tuple-element.117.kf_ref.vf_ref.refs_3_.refs_4_, ...), custom_call_target="tpu_custom_call" | custom-call | flops 5435817984 | bytes 16777216 | tf_op jit(solution)/shard_map/pallas_call | solution.py:184
  447.2 26.1 %shard_map.443 = (f32[768,768]{1,0:T(8,128)}, f32[768,256]{1,0:T(8,128)}, f32[768,256]{1,0:T(8,128)}) custom-call(s32[1]{0:T(128)} %bitcast.11.start_ref.refs_0_, s32[1,768]{1,0:T(1,128)} %copy-done.27, bf16[768,768]{1,0:T(8,128)(2,1)} %copy-done.18, bf16[768,512]{1,0:T(8,128)(2,1)} %copy-done.21, bf16[768,512]{1,0:T(8,128)(2,1)} %copy-done.21, ...), custom_call_target="tpu_custom_call" | custom-call | flops 5435817984 | bytes 16777216 | tf_op jit(solution)/shard_map/pallas_call | solution.py:184
  476.2 3.3 constant_dynamic-update-slice_fusion.16
  479.5 14.3 %shard_map.444 = (bf16[768,1536]{1,0:T(8,128)(2,1)}, f32[8,896,128]{2,1,0:T(8,128)}) custom-call(s32[1]{0:T(128)} %bitcast.32.tp_ref, f32[768,768]{1,0:T(8,128)} %get-tuple-element.177.dq_ref, f32[768,256]{1,0:T(8,128)S(1)} %copy-done.31, f32[768,256]{1,0:T(8,128)S(1)} %copy-done.32, bf16[768,512]{1,0:T(8,128)(2,1)} %copy-done.70, ...), custom_call_target="tpu_custom_call" | custom-call | flops 7851737088 | bytes 25165824 | tf_op jit(solution)/shard_map/pallas_call | solution.py:613
  495.5 5.4 add_convert_fusion
  500.9 31.3 %shard_map.445 = (f32[896,128]{1,0:T(8,128)S(1)}, f32[1360,128]{1,0:T(8,128)S(1)}) custom-call(f32[8,896,128]{2,1,0:T(8,128)S(1)} %copy-done.9, bf16[1360,128]{1,0:T(8,128)(2,1)S(1)} %bitcast.100), custom_call_target="tpu_custom_call" | custom-call | tf_op jit(solution)/shard_map/pallas_call | solution.py:875
  541.1 4.7 fusion.3
  (278 shorter events, 76.3 us)
Async XLA Ops:
  7.3 486.6 %reduce-scatter.2.cloned.1.call-start = ((), (), s32[]{:S(2)}) async-start(), calls=%async_computation.1 | async-start | bytes 3133440 | tf_op jit(solution)/shard_map/reduce_scatter | solution.py:1063
  67.5 97.4 %collective-permute-start = (bf16[1,1536,768]{2,1,0:T(8,128)(2,1)}, bf16[1,1536,768]{2,1,0:T(8,128)(2,1)}, u32[]{:S(2)}, u32[]{:S(2)}) collective-permute-start(bf16[1,1536,768]{2,1,0:T(8,128)(2,1)} %pad_maximum_fusion), channel_id=1, source_target_pairs={{0,8},{4,12},{8,16},{12,20},{16,24},{20,28},{24,0},{28,4},{1,9},{5... | collective-permute-start | bytes 7077896 | tf_op jit(solution)/shard_map/ppermute | solution.py:969
  68.7 96.1 %collective-permute-start.1 = (bf16[1,1536,768]{2,1,0:T(8,128)(2,1)}, bf16[1,1536,768]{2,1,0:T(8,128)(2,1)}, u32[]{:S(2)}, u32[]{:S(2)}) collective-permute-start(bf16[1,1536,768]{2,1,0:T(8,128)(2,1)} %pad_maximum_fusion), channel_id=1, source_target_pairs={{0,4},{4,0},{8,12},{12,8},{16,20},{20,16},{24,28},{28,24},{1,5},{5... | collective-permute-start | bytes 7077896 | tf_op jit(solution)/shard_map/ppermute | solution.py:971
  87.4 82.9 %copy-start.18 = (bf16[768,768]{1,0:T(8,128)(2,1)}, bf16[768,768]{1,0:T(8,128)(2,1)S(1)}, u32[]{:S(2)}) copy-start(bf16[768,768]{1,0:T(8,128)(2,1)S(1)} %shard_map.432.q_ref.refs_2_) | copy-start | bytes 3538948
  164.9 50.5 %collective-permute-start.2 = (bf16[1,1536,768]{2,1,0:T(8,128)(2,1)}, bf16[1,1536,768]{2,1,0:T(8,128)(2,1)}, u32[]{:S(2)}, u32[]{:S(2)}) collective-permute-start(bf16[1,1536,768]{2,1,0:T(8,128)(2,1)} %collective-permute-done), channel_id=1, source_target_pairs={{0,8},{4,12},{8,16},{12,20},{16,24},{20,28},{24,0},{28,4},{1,9},{5... | collective-permute-start | bytes 7077896 | tf_op jit(solution)/shard_map/ppermute | solution.py:969
  164.9 50.5 %collective-permute-start.3 = (bf16[1,1536,768]{2,1,0:T(8,128)(2,1)}, bf16[1,1536,768]{2,1,0:T(8,128)(2,1)}, u32[]{:S(2)}, u32[]{:S(2)}) collective-permute-start(bf16[1,1536,768]{2,1,0:T(8,128)(2,1)} %collective-permute-done), channel_id=1, source_target_pairs={{0,4},{4,0},{8,12},{12,8},{16,20},{20,16},{24,28},{28,24},{1,5},{5... | collective-permute-start | bytes 7077896 | tf_op jit(solution)/shard_map/ppermute | solution.py:971
  167.9 37.9 %collective-permute-start.4 = (bf16[384,1536]{1,0:T(8,128)(2,1)S(1)}, bf16[384,1536]{1,0:T(8,128)(2,1)S(1)}, u32[]{:S(2)}, u32[]{:S(2)}) collective-permute-start(bf16[384,1536]{1,0:T(8,128)(2,1)S(1)} %constant_dynamic-slice_fusion.7), channel_id=1, source_target_pairs={{0,2},{2,0},{1,3},{3,1},{4,6},{6,4},{5,7},{7,5},{8,10},{10,8},{9,1... | collective-permute-start | bytes 3538952 | tf_op jit(solution)/shard_map/ppermute | solution.py:511
  215.4 4.9 collective-permute-start.5
  217.8 56.0 %collective-permute-start.7 = (bf16[1,1536,768]{2,1,0:T(8,128)(2,1)}, bf16[1,1536,768]{2,1,0:T(8,128)(2,1)}, u32[]{:S(2)}, u32[]{:S(2)}) collective-permute-start(bf16[1,1536,768]{2,1,0:T(8,128)(2,1)} %collective-permute-done.2), channel_id=1, source_target_pairs={{0,8},{4,12},{8,16},{12,20},{16,24},{20,28},{24,0},{28,4},{1,9},{5... | collective-permute-start | bytes 7077896 | tf_op jit(solution)/shard_map/ppermute | solution.py:969
  218.0 55.8 %collective-permute-start.8 = (bf16[1,1536,768]{2,1,0:T(8,128)(2,1)}, bf16[1,1536,768]{2,1,0:T(8,128)(2,1)}, u32[]{:S(2)}, u32[]{:S(2)}) collective-permute-start(bf16[1,1536,768]{2,1,0:T(8,128)(2,1)} %collective-permute-done.2), channel_id=1, source_target_pairs={{0,4},{4,0},{8,12},{12,8},{16,20},{20,16},{24,28},{28,24},{1,5},{5... | collective-permute-start | bytes 7077896 | tf_op jit(solution)/shard_map/ppermute | solution.py:971
  233.4 40.3 %collective-permute-start.6 = (bf16[384,1664]{1,0:T(8,128)(2,1)S(1)}, bf16[384,1664]{1,0:T(8,128)(2,1)}, u32[]{:S(2)}, u32[]{:S(2)}) collective-permute-start(bf16[384,1664]{1,0:T(8,128)(2,1)S(1)} %constant_dynamic-slice_fusion.5), channel_id=1, source_target_pairs={{0,2},{2,0},{1,3},{3,1},{4,6},{6,4},{5,7},{7,5},{8,10},{10,8},{9,1... | collective-permute-start | bytes 3833864 | tf_op jit(solution)/shard_map/ppermute | solution.py:511
  273.7 4.8 collective-permute-start.10
  273.8 6.1 %collective-permute-start.9 = (bf16[384,1664]{1,0:T(8,128)(2,1)}, bf16[384,1664]{1,0:T(8,128)(2,1)}, u32[]{:S(2)}, u32[]{:S(2)}) collective-permute-start(bf16[384,1664]{1,0:T(8,128)(2,1)} %collective-permute-done.6), channel_id=1, source_target_pairs={{0,1},{1,0},{2,3},{3,2},{4,5},{5,4},{6,7},{7,6},{8,9},{9,8},{10,11... | collective-permute-start | bytes 3833864 | tf_op jit(solution)/shard_map/ppermute | solution.py:504
  275.5 53.5 %collective-permute-start.11 = (bf16[1,1536,768]{2,1,0:T(8,128)(2,1)}, bf16[1,1536,768]{2,1,0:T(8,128)(2,1)}, u32[]{:S(2)}, u32[]{:S(2)}) collective-permute-start(bf16[1,1536,768]{2,1,0:T(8,128)(2,1)} %collective-permute-done.7), channel_id=1, source_target_pairs={{0,4},{4,0},{8,12},{12,8},{16,20},{20,16},{24,28},{28,24},{1,5},{5... | collective-permute-start | bytes 7077896 | tf_op jit(solution)/shard_map/ppermute | solution.py:971
  350.1 3.1 collective-permute-start.12
  353.5 30.2 %collective-permute-start.13 = (bf16[384,1664]{1,0:T(8,128)(2,1)S(1)}, bf16[384,1664]{1,0:T(8,128)(2,1)S(1)}, u32[]{:S(2)}, u32[]{:S(2)}) collective-permute-start(bf16[384,1664]{1,0:T(8,128)(2,1)S(1)} %add_convert_fusion.2), channel_id=1, source_target_pairs={{0,2},{2,0},{1,3},{3,1},{4,6},{6,4},{5,7},{7,5},{8,10},{10,8},{9,1... | collective-permute-start | bytes 3833864 | tf_op jit(solution)/shard_map/ppermute | solution.py:1046
  385.1 3.1 collective-permute-start.14
  388.6 3.1 collective-permute-start.15
  388.9 22.6 %collective-permute-start.16 = (bf16[384,1536]{1,0:T(8,128)(2,1)S(1)}, bf16[384,1536]{1,0:T(8,128)(2,1)}, u32[]{:S(2)}, u32[]{:S(2)}) collective-permute-start(bf16[384,1536]{1,0:T(8,128)(2,1)S(1)} %constant_dynamic-slice_fusion.1), channel_id=1, source_target_pairs={{0,1},{1,0},{2,3},{3,2},{4,5},{5,4},{6,7},{7,6},{8,9},{9,8},{10,11... | collective-permute-start | bytes 3538952 | tf_op jit(solution)/shard_map/ppermute | solution.py:521
  390.8 20.7 %collective-permute-start.17 = (bf16[384,1536]{1,0:T(8,128)(2,1)S(1)}, bf16[384,1536]{1,0:T(8,128)(2,1)}, u32[]{:S(2)}, u32[]{:S(2)}) collective-permute-start(bf16[384,1536]{1,0:T(8,128)(2,1)S(1)} %constant_dynamic-slice_fusion), channel_id=1, source_target_pairs={{0,1},{1,0},{2,3},{3,2},{4,5},{5,4},{6,7},{7,6},{8,9},{9,8},{10,11... | collective-permute-start | bytes 3538952 | tf_op jit(solution)/shard_map/ppermute | solution.py:521
  413.5 59.9 %collective-permute-start.19 = (bf16[384,1536]{1,0:T(8,128)(2,1)S(1)}, bf16[384,1536]{1,0:T(8,128)(2,1)S(1)}, u32[]{:S(2)}, u32[]{:S(2)}) collective-permute-start(bf16[384,1536]{1,0:T(8,128)(2,1)S(1)} %add_convert_fusion.4), channel_id=1, source_target_pairs={{0,2},{2,0},{1,3},{3,1},{4,6},{6,4},{5,7},{7,5},{8,10},{10,8},{9,1... | collective-permute-start | bytes 3538952 | tf_op jit(solution)/shard_map/ppermute | solution.py:1062
  445.9 27.5 %collective-permute-start.18 = (bf16[768,512]{1,0:T(8,128)(2,1)S(1)}, bf16[768,512]{1,0:T(8,128)(2,1)S(1)}, u32[]{:S(2)}, u32[]{:S(2)}) collective-permute-start(bf16[768,512]{1,0:T(8,128)(2,1)S(1)} %pad_maximum_fusion.1), channel_id=1, source_target_pairs={{2,0},{3,1},{6,4},{7,5},{10,8},{11,9},{14,12},{15,13},{18,16},{19,... | collective-permute-start | bytes 2359304 | tf_op jit(solution)/shard_map/ppermute | solution.py:1065
  479.5 14.9 %collective-permute-start.20 = (bf16[384,1536]{1,0:T(8,128)(2,1)}, bf16[384,1536]{1,0:T(8,128)(2,1)S(1)}, u32[]{:S(2)}, u32[]{:S(2)}) collective-permute-start(bf16[384,1536]{1,0:T(8,128)(2,1)} %get-tuple-element.193), channel_id=1, source_target_pairs={{0,1},{1,0},{2,3},{3,2},{4,5},{5,4},{6,7},{7,6},{8,9},{9,8},{10,11... | collective-permute-start | bytes 3538952 | tf_op jit(solution)/shard_map/ppermute | solution.py:504
  493.9 45.6 %collective-permute-start.21 = (bf16[768,1536]{1,0:T(8,128)(2,1)}, bf16[768,1536]{1,0:T(8,128)(2,1)S(1)}, u32[]{:S(2)}, u32[]{:S(2)}) collective-permute-start(bf16[768,1536]{1,0:T(8,128)(2,1)} %get-tuple-element.183), channel_id=1, source_target_pairs={{0,1},{1,0},{2,3},{3,2},{4,5},{5,4},{6,7},{7,6},{8,9},{9,8},{10,11... | collective-permute-start | bytes 7077896 | tf_op jit(solution)/shard_map/ppermute | solution.py:1082
  (71 other events, 571.4 us)
Sparse Core Ops, SparseCore 0:
  411.7 72.2 reduce-scatter.1

commit v9 on v8

--- a/solution.py
+++ b/solution.py
@@ -405,20 +405,20 @@
     r_ref[:, width:] = dgate.astype(BF)
 
 
-def last_experts_kernel(experts, count, ids_ref, t_ref, c_ref, *refs):
+def last_experts_kernel(experts, count, before, ids_ref, t_ref, c_ref, *refs):
     w_refs = refs[:count]
     ga_ref, ua_ref, gb_ref, ub_ref, db_ref, da_ref = refs[count : count + 6]
-    prior = refs[count + 6 : count + 11]
-    r1_ref, m1_ref, wide_ref, thin_ref, r_ref, m_ref = refs[count + 11 : count + 17]
-    sums = refs[count + 17 : count + 22]
-    moe_acc, dn2_acc = refs[count + 22 :]
+    prior = refs[count + 6 : count + 6 + before]
+    r1_ref, m1_ref, wide_ref, thin_ref, r_ref, m_ref = refs[-13:-7]
+    sums = refs[-7:-2]
+    moe_acc, dn2_acc = refs[-2:]
     width = c_ref.shape[1]
     ff = gb_ref.shape[1]
 
     @pl.when(pl.program_id(0) == 0)
     def _():
-        for old, new in zip(prior, sums):
-            new[...] = old[...]
+        for i, new in enumerate(sums):
+            new[...] = prior[i][...] if before else jnp.zeros_like(new)
 
     mask = row_mask(experts, t_ref, width)
     parts = [wide_ref[:, i * ff : (i + 1) * ff] for i in range(6)]
@@ -458,13 +458,14 @@
     out_specs = [by_row(width + spare), by_row(width)]
     out_shape = [sd((rows, width + spare), BF), sd((rows, width), BF)]
     if early:
-        out_specs += [whole(p) for p in prior]
-        out_shape += [sd(p.shape, F32) for p in prior]
+        shapes = [(LANES, width), (ff, LANES), (LANES, ff), (LANES, ff), (width, 2 * LANES)]
+        out_specs += [pl.BlockSpec(shape, lambda i: (0, 0)) for shape in shapes]
+        out_shape += [sd(shape, F32) for shape in shapes]
     else:
         out_specs += [by_row(6 * ff), by_row(3 * LANES)]
         out_shape += [sd((rows, 6 * ff), F32), sd((rows, 3 * LANES), BF)]
     outs = pl.pallas_call(
-        functools.partial(last_experts_kernel if early else first_experts_kernel, experts, count),
+        functools.partial(last_experts_kernel, experts, count, len(prior)) if early else functools.partial(first_experts_kernel, experts, count),
         grid=(rows // step,),
         in_specs=[pl.BlockSpec(memory_space=pltpu.SMEM), by_row(t.shape[1]), by_row(width)]
         + [once(w) for w in weights]
@@ -1020,7 +1021,7 @@
         ids = [((me // inner + outer - do) % outer * inner + (me % inner + inner - dj) % inner) * local_experts + ctx_at * local + j for do, dj in keys for j in range(local)]
         return jnp.stack(ids + [tp_at * 2 * experts]).astype(jnp.int32), [brought[k][j] for k in keys for j in range(local)]
 
-    sums = [jnp.zeros(shape, F32) for shape in ((ranks, width), (ff_width, ranks), (ranks, ff_width), (ranks, ff_width), (width, 2 * ranks))]
+    sums = ()
     at = q_width // LANES + 1
     work = [(carried, cot)] + [(None, None)] * (cross.n_ctx - 1)
     partial = []

time: 563 us -> 558 us (level)
  no operation moved by 1% of the time
where the time goes in v9:
time: 558 us; the launch traced here: 548 us
  Pallas kernels  425 us (76%)
  local copies, waits for them, and re-layouts  45.7 us (8%)
  waiting for transfers between devices  24.2 us (4%)
  other arithmetic  23.7 us (4%)
  between operations  15.7 us (3%)
  starting transfers between devices  14 us (3%)
    pallas_call x2, Pallas kernels, gather_packs(): pl.pallas_call(functools.partial(gather_kernel, n, count, len(extra)), in...  129 us
    pallas_call x4, Pallas kernels, experts_on(): pl.pallas_call(functools.partial(last_experts_kernel, experts, count, len...  111 us
    pallas_call x2, Pallas kernels, attend_back(): pl.pallas_call(functools.partial(attend_back_kernel, group, q_blocks, far...  56.2 us
    pallas_call x1, Pallas kernels, attend(): pl.pallas_call(functools.partial(attend_kernel, group, q_blocks), grid=(p...  34.8 us
    pallas_call x1, Pallas kernels, reduce_pack(): pl.pallas_call(functools.partial(reduce_kernel, n), in_specs=[pl.BlockSpe...  31.3 us
    pallas_call x4, Pallas kernels, by_rows(): pl.pallas_call(kernel, grid=(rows // step,), in_specs=[block(a.shape[1])...  29.7 us
    pallas_call x1, Pallas kernels, mid_back(): pl.pallas_call(functools.partial(mid_back_kernel, n, n_tp, experts, share...  18.8 us
    unnamed x163, local copies, waits for them, and re-layouts  18.6 us
  transfers between devices with their start and end apart: 23, of which 8 were waited for; matrix products, arithmetic and copies ran while one was open for 7% of the time, Pallas kernels for 65%

profile of v9, /device:TPU:0, one launch (start us, length us, event | category | flops | bytes accessed | tf_op | source)
XLA Modules:
  0.0 548.0 jit_solution(14660553728123223318)
XLA Ops:
  11.2 53.1 %shard_map.430 = (bf16[8,192,1664]{2,1,0:T(8,128)(2,1)}, bf16[8,16,1280]{2,1,0:T(8,128)(2,1)}) custom-call(bf16[192,1664]{1,0:T(8,128)(2,1)} %copy-done.42, bf16[16,1280]{1,0:T(8,128)(2,1)} %pad_maximum_fusion.3.refs_1_), custom_call_target="tpu_custom_call" | custom-call | tf_op jit(solution)/shard_map/pallas_call | solution.py:319
  70.9 7.2 %shard_map.431 = (bf16[768,1536]{1,0:T(8,128)(2,1)S(1)}, bf16[768,384]{1,0:T(8,128)(2,1)S(1)}, bf16[768,512]{1,0:T(8,128)(2,1)S(1)}) custom-call(bf16[768,1536]{1,0:T(8,128)(2,1)} %x_ref.3, s32[768,1]{1,0:T(8,128)S(1)} %broadcast_in_dim.33.chosen_ref, f32[768,128]{1,0:T(8,128)S(1)} %copy.87.cos_ref, f32[768,128]{1,0:T(8,128)S(1)} %copy.88.sin_ref, ...), custom_call_target="tpu_custom_call" | custom-call | flops 2113929216 | bytes 1048576 | tf_op jit(solution)/shard_map/pallas_call | solution.py:692
  79.1 6.0 %shard_map.432.q_ref.refs_2_ = bf16[768,768]{1,0:T(8,128)(2,1)S(1)} custom-call(bf16[768,1536]{1,0:T(8,128)(2,1)S(1)} %get-tuple-element.106.n1_ref, bf16[768,384]{1,0:T(8,128)(2,1)S(1)} %get-tuple-element.107.u_ref, f32[768,128]{1,0:T(8,128)S(1)} %copy.87.cos_ref, f32[768,128]{1,0:T(8,128)S(1)} %copy.88.sin_ref, bf16[1536,1664]{1,0:T(8,128)(2,1)} %bitcast.114, ...), custom_call_target="tpu_custom_call" | custom-call | flops 1811939328 | bytes 1048576 | tf_op jit(solution)/shard_map/pallas_call | solution.py:692
  89.4 75.5 %shard_map.433 = (bf16[8,192,1408]{2,1,0:T(8,128)(2,1)}, bf16[8,16,3712]{2,1,0:T(8,128)(2,1)}, bf16[8,64,128]{2,1,0:T(8,128)(2,1)}, bf16[768,512]{1,0:T(8,128)(2,1)}) custom-call(bf16[192,1408]{1,0:T(8,128)(2,1)} %copy-done.43, bf16[16,3712]{1,0:T(8,128)(2,1)} %copy-done.48, bf16[64,128]{1,0:T(8,128)(2,1)} %refs_2_.1, bf16[768,512]{1,0:T(8,128)(2,1)} %copy-done.21), custom_call_target="tpu_custom_call" | custom-call | tf_op jit(solution)/shard_map/pallas_call | solution.py:319
  170.3 34.8 %shard_map.434 = (bf16[768,768]{1,0:T(8,128)(2,1)S(1)}, f32[2,8,768]{2,1,0:T(8,128)S(1)}) custom-call(s32[1]{0:T(128)} %bitcast.11.start_ref.refs_0_, s32[1,768]{1,0:T(1,128)S(1)} %broadcast_in_dim.14.begin_ref.refs_1_, bf16[768,768]{1,0:T(8,128)(2,1)S(1)} %shard_map.432.q_ref.refs_2_, bf16[768,512]{1,0:T(8,128)(2,1)S(1)} %copy-done.22, ...), custom_call_target="tpu_custom_call" | custom-call | flops 3623878656 | bytes 8388608 | tf_op jit(solution)/shard_map/pallas_call | solution.py:97
  205.9 7.5 %shard_map.435 = (bf16[768,1536]{1,0:T(8,128)(2,1)}, bf16[768,128]{1,0:T(8,128)(2,1)S(1)}) custom-call(bf16[768,768]{1,0:T(8,128)(2,1)S(1)} %get-tuple-element.119.o_ref.refs_5_, s32[768,1]{1,0:T(8,128)S(1)} %copy-done.6, bf16[1536,1408]{1,0:T(8,128)(2,1)} %bitcast.102, bf16[768,128]{1,0:T(8,128)(2,1)S(1)} %constant_dynamic-slice_fusion.6.oa_ref, ...), custom_call_target="tpu_custom_call" | custom-call | bytes 1048576 | tf_op jit(solution)/shard_map/pallas_call | solution.py:692
  222.3 9.0 %shard_map.436 = (f32[768,1536]{1,0:T(8,128)}, bf16[768,1664]{1,0:T(8,128)(2,1)}, bf16[768,128]{1,0:T(8,128)(2,1)S(1)}) custom-call(bf16[768,1536]{1,0:T(8,128)(2,1)S(1)} %copy-done.2, bf16[768,1536]{1,0:T(8,128)(2,1)} %get-tuple-element.122.one_ref, bf16[768,1536]{1,0:T(8,128)(2,1)} %collective-permute-done.5.other_ref, s32[768,1]{1,0:T(8,128)S(1)} %copy-done.7, ...), custom_call_target="tpu_custom_call" | custom-call | bytes 1048576 | tf_op jit(solution)/shard_map/pallas_call | solution.py:692
  234.6 31.0 %shard_map.437 = (bf16[768,1664]{1,0:T(8,128)(2,1)}, bf16[768,1536]{1,0:T(8,128)(2,1)}, f32[768,1536]{1,0:T(8,128)}, bf16[768,384]{1,0:T(8,128)(2,1)}) custom-call(s32[6]{0:T(128)} %stack.68.ids_ref, bf16[768,1664]{1,0:T(8,128)(2,1)} %get-tuple-element.141.t_ref, bf16[768,1536]{1,0:T(8,128)(2,1)} %c_ref.2, bf16[1536,768]{1,0:T(8,128)(2,1)} %bitcast.23.refs_0_, ...), custom_call_target="tpu_custom_call" | custom-call | flops 21139292160 | bytes 25165824 | tf_op jit(solution)/shard_map/pallas_call | solution.py:467
  265.6 8.1 %collective-permute-done.7 = bf16[1,1536,768]{2,1,0:T(8,128)(2,1)} collective-permute-done((bf16[1,1536,768]{2,1,0:T(8,128)(2,1)}, bf16[1,1536,768]{2,1,0:T(8,128)(2,1)}, u32[]{:S(2)}, u32[]{:S(2)}) %collective-permute-start.7) | collective-permute-done | bytes 2359328 | tf_op jit(solution)/shard_map/ppermute | solution.py:970
  283.7 41.0 %shard_map.438 = (bf16[768,1664]{1,0:T(8,128)(2,1)}, bf16[768,1536]{1,0:T(8,128)(2,1)}, f32[768,1536]{1,0:T(8,128)}, bf16[768,384]{1,0:T(8,128)(2,1)}) custom-call(s32[8]{0:T(128)} %stack.69.ids_ref, bf16[768,1664]{1,0:T(8,128)(2,1)} %copy-done.34, bf16[768,1536]{1,0:T(8,128)(2,1)} %copy-done.36, bf16[1536,768]{1,0:T(8,128)(2,1)} %bitcast.23.refs_0_, ...), custom_call_target="tpu_custom_call" | custom-call | flops 29595009024 | bytes 25165824 | tf_op jit(solution)/shard_map/pallas_call | solution.py:467
  324.8 4.2 collective-permute-done.11
  329.0 14.4 %shard_map.439 = (bf16[768,1664]{1,0:T(8,128)(2,1)}, bf16[768,1536]{1,0:T(8,128)(2,1)}, f32[128,1536]{1,0:T(8,128)}, f32[256,128]{1,0:T(8,128)}, f32[128,256]{1,...) custom-call(s32[2]{0:T(128)} %pad_add_fusion.1.ids_ref, bf16[768,1664]{1,0:T(8,128)(2,1)} %copy-done.34, ...), custom_call_target="tpu_custom_call" | custom-call | flops 4227858432 | bytes 25165824 | tf_op jit(solution)/shard_map/pallas_call | solution.py:467
  345.0 3.0 collective-permute-done.12
  350.1 24.5 %shard_map.440 = (bf16[768,1664]{1,0:T(8,128)(2,1)}, bf16[768,1536]{1,0:T(8,128)(2,1)}, f32[128,1536]{1,0:T(8,128)}, f32[256,128]{1,0:T(8,128)}, f32[128,256]{1,...) custom-call(s32[4]{0:T(128)} %pad_add_fusion.ids_ref, ...), custom_call_target="tpu_custom_call", output_to_operand_aliasing={{2}: (12, {}), {3}: (13, {}), {4}: (14, {}), {5}: (15, {}),... | custom-call | flops 12683575296 | bytes 25165824 | tf_op jit(solution)/shard_map/pallas_call | solution.py:467
  374.6 3.9 collective-permute-done.13
  380.0 3.0 collective-permute-done.14
  387.6 18.8 %shard_map.441 = (f32[768,1536]{1,0:T(8,128)}, bf16[768,768]{1,0:T(8,128)(2,1)}, bf16[8,1360,128]{2,1,0:T(8,128)(2,1)}) custom-call(s32[2]{0:T(128)} %pad_add_fusion.2.sel_ref, bf16[384,1664]{1,0:T(8,128)(2,1)} %copy-done.44, bf16[384,1664]{1,0:T(8,128)(2,1)} %copy-done.69, f32[768,1536]{1,0:T(8,128)} %get-tuple-element.123.h_ref, bf16[768,1536]{1,0:T(8,128)(2,1)} %c_ref.2, ...), custom_call_target="tpu_custom_call" | custom-call | flops 7247757312 | bytes 33554432 | tf_op jit(solution)/shard_map/pallas_call | solution.py:789
  409.5 30.1 %shard_map.442 = (f32[768,768]{1,0:T(8,128)}, bf16[768,256]{1,0:T(8,128)(2,1)}, bf16[768,256]{1,0:T(8,128)(2,1)}) custom-call(s32[1]{0:T(128)} %bitcast.11.start_ref.refs_0_, s32[1,768]{1,0:T(1,128)} %copy-done.27, bf16[768,768]{1,0:T(8,128)(2,1)} %copy-done.18, bf16[768,512]{1,0:T(8,128)(2,1)} %get-tuple-element.117.kf_ref.vf_ref.refs_3_.refs_4_, ...), custom_call_target="tpu_custom_call" | custom-call | flops 5435817984 | bytes 16777216 | tf_op jit(solution)/shard_map/pallas_call | solution.py:184
  442.0 26.1 %shard_map.443 = (f32[768,768]{1,0:T(8,128)}, f32[768,256]{1,0:T(8,128)}, f32[768,256]{1,0:T(8,128)}) custom-call(s32[1]{0:T(128)} %bitcast.11.start_ref.refs_0_, s32[1,768]{1,0:T(1,128)} %copy-done.27, bf16[768,768]{1,0:T(8,128)(2,1)} %copy-done.18, bf16[768,512]{1,0:T(8,128)(2,1)} %copy-done.21, bf16[768,512]{1,0:T(8,128)(2,1)} %copy-done.21, ...), custom_call_target="tpu_custom_call" | custom-call | flops 5435817984 | bytes 16777216 | tf_op jit(solution)/shard_map/pallas_call | solution.py:184
  471.0 3.3 constant_dynamic-update-slice_fusion.16
  474.3 14.3 %shard_map.444 = (bf16[768,1536]{1,0:T(8,128)(2,1)}, f32[8,896,128]{2,1,0:T(8,128)}) custom-call(s32[1]{0:T(128)} %bitcast.32.tp_ref, f32[768,768]{1,0:T(8,128)} %get-tuple-element.177.dq_ref, f32[768,256]{1,0:T(8,128)S(1)} %copy-done.31, f32[768,256]{1,0:T(8,128)S(1)} %copy-done.32, bf16[768,512]{1,0:T(8,128)(2,1)} %copy-done.70, ...), custom_call_target="tpu_custom_call" | custom-call | flops 7851737088 | bytes 25165824 | tf_op jit(solution)/shard_map/pallas_call | solution.py:614
  490.3 5.4 add_convert_fusion
  495.7 31.3 %shard_map.445 = (f32[896,128]{1,0:T(8,128)S(1)}, f32[1360,128]{1,0:T(8,128)S(1)}) custom-call(f32[8,896,128]{2,1,0:T(8,128)S(1)} %copy-done.9, bf16[1360,128]{1,0:T(8,128)(2,1)S(1)} %bitcast.100), custom_call_target="tpu_custom_call" | custom-call | tf_op jit(solution)/shard_map/pallas_call | solution.py:876
  535.9 4.7 fusion.3
  (273 shorter events, 72.0 us)
Async XLA Ops:
  7.3 481.3 %reduce-scatter.2.cloned.1.call-start = ((), (), s32[]{:S(2)}) async-start(), calls=%async_computation.1 | async-start | bytes 3133440 | tf_op jit(solution)/shard_map/reduce_scatter | solution.py:1064
  67.5 97.4 %collective-permute-start = (bf16[1,1536,768]{2,1,0:T(8,128)(2,1)}, bf16[1,1536,768]{2,1,0:T(8,128)(2,1)}, u32[]{:S(2)}, u32[]{:S(2)}) collective-permute-start(bf16[1,1536,768]{2,1,0:T(8,128)(2,1)} %pad_maximum_fusion), channel_id=1, source_target_pairs={{0,8},{4,12},{8,16},{12,20},{16,24},{20,28},{24,0},{28,4},{1,9},{5... | collective-permute-start | bytes 7077896 | tf_op jit(solution)/shard_map/ppermute | solution.py:970
  68.7 96.1 %collective-permute-start.1 = (bf16[1,1536,768]{2,1,0:T(8,128)(2,1)}, bf16[1,1536,768]{2,1,0:T(8,128)(2,1)}, u32[]{:S(2)}, u32[]{:S(2)}) collective-permute-start(bf16[1,1536,768]{2,1,0:T(8,128)(2,1)} %pad_maximum_fusion), channel_id=1, source_target_pairs={{0,4},{4,0},{8,12},{12,8},{16,20},{20,16},{24,28},{28,24},{1,5},{5... | collective-permute-start | bytes 7077896 | tf_op jit(solution)/shard_map/ppermute | solution.py:972
  87.4 82.9 %copy-start.18 = (bf16[768,768]{1,0:T(8,128)(2,1)}, bf16[768,768]{1,0:T(8,128)(2,1)S(1)}, u32[]{:S(2)}) copy-start(bf16[768,768]{1,0:T(8,128)(2,1)S(1)} %shard_map.432.q_ref.refs_2_) | copy-start | bytes 3538948
  164.9 50.5 %collective-permute-start.2 = (bf16[1,1536,768]{2,1,0:T(8,128)(2,1)}, bf16[1,1536,768]{2,1,0:T(8,128)(2,1)}, u32[]{:S(2)}, u32[]{:S(2)}) collective-permute-start(bf16[1,1536,768]{2,1,0:T(8,128)(2,1)} %collective-permute-done), channel_id=1, source_target_pairs={{0,8},{4,12},{8,16},{12,20},{16,24},{20,28},{24,0},{28,4},{1,9},{5... | collective-permute-start | bytes 7077896 | tf_op jit(solution)/shard_map/ppermute | solution.py:970
  164.9 50.5 %collective-permute-start.3 = (bf16[1,1536,768]{2,1,0:T(8,128)(2,1)}, bf16[1,1536,768]{2,1,0:T(8,128)(2,1)}, u32[]{:S(2)}, u32[]{:S(2)}) collective-permute-start(bf16[1,1536,768]{2,1,0:T(8,128)(2,1)} %collective-permute-done), channel_id=1, source_target_pairs={{0,4},{4,0},{8,12},{12,8},{16,20},{20,16},{24,28},{28,24},{1,5},{5... | collective-permute-start | bytes 7077896 | tf_op jit(solution)/shard_map/ppermute | solution.py:972
  167.9 37.9 %collective-permute-start.4 = (bf16[384,1536]{1,0:T(8,128)(2,1)S(1)}, bf16[384,1536]{1,0:T(8,128)(2,1)S(1)}, u32[]{:S(2)}, u32[]{:S(2)}) collective-permute-start(bf16[384,1536]{1,0:T(8,128)(2,1)S(1)} %constant_dynamic-slice_fusion.7), channel_id=1, source_target_pairs={{0,2},{2,0},{1,3},{3,1},{4,6},{6,4},{5,7},{7,5},{8,10},{10,8},{9,1... | collective-permute-start | bytes 3538952 | tf_op jit(solution)/shard_map/ppermute | solution.py:512
  215.4 4.9 collective-permute-start.5
  217.7 56.0 %collective-permute-start.7 = (bf16[1,1536,768]{2,1,0:T(8,128)(2,1)}, bf16[1,1536,768]{2,1,0:T(8,128)(2,1)}, u32[]{:S(2)}, u32[]{:S(2)}) collective-permute-start(bf16[1,1536,768]{2,1,0:T(8,128)(2,1)} %collective-permute-done.2), channel_id=1, source_target_pairs={{0,8},{4,12},{8,16},{12,20},{16,24},{20,28},{24,0},{28,4},{1,9},{5... | collective-permute-start | bytes 7077896 | tf_op jit(solution)/shard_map/ppermute | solution.py:970
  217.9 55.8 %collective-permute-start.8 = (bf16[1,1536,768]{2,1,0:T(8,128)(2,1)}, bf16[1,1536,768]{2,1,0:T(8,128)(2,1)}, u32[]{:S(2)}, u32[]{:S(2)}) collective-permute-start(bf16[1,1536,768]{2,1,0:T(8,128)(2,1)} %collective-permute-done.2), channel_id=1, source_target_pairs={{0,4},{4,0},{8,12},{12,8},{16,20},{20,16},{24,28},{28,24},{1,5},{5... | collective-permute-start | bytes 7077896 | tf_op jit(solution)/shard_map/ppermute | solution.py:972
  233.4 40.3 %collective-permute-start.6 = (bf16[384,1664]{1,0:T(8,128)(2,1)S(1)}, bf16[384,1664]{1,0:T(8,128)(2,1)}, u32[]{:S(2)}, u32[]{:S(2)}) collective-permute-start(bf16[384,1664]{1,0:T(8,128)(2,1)S(1)} %constant_dynamic-slice_fusion.5), channel_id=1, source_target_pairs={{0,2},{2,0},{1,3},{3,1},{4,6},{6,4},{5,7},{7,5},{8,10},{10,8},{9,1... | collective-permute-start | bytes 3833864 | tf_op jit(solution)/shard_map/ppermute | solution.py:512
  273.7 4.8 collective-permute-start.10
  273.8 6.1 %collective-permute-start.9 = (bf16[384,1664]{1,0:T(8,128)(2,1)}, bf16[384,1664]{1,0:T(8,128)(2,1)}, u32[]{:S(2)}, u32[]{:S(2)}) collective-permute-start(bf16[384,1664]{1,0:T(8,128)(2,1)} %collective-permute-done.6), channel_id=1, source_target_pairs={{0,1},{1,0},{2,3},{3,2},{4,5},{5,4},{6,7},{7,6},{8,9},{9,8},{10,11... | collective-permute-start | bytes 3833864 | tf_op jit(solution)/shard_map/ppermute | solution.py:505
  275.5 53.5 %collective-permute-start.11 = (bf16[1,1536,768]{2,1,0:T(8,128)(2,1)}, bf16[1,1536,768]{2,1,0:T(8,128)(2,1)}, u32[]{:S(2)}, u32[]{:S(2)}) collective-permute-start(bf16[1,1536,768]{2,1,0:T(8,128)(2,1)} %collective-permute-done.7), channel_id=1, source_target_pairs={{0,4},{4,0},{8,12},{12,8},{16,20},{20,16},{24,28},{28,24},{1,5},{5... | collective-permute-start | bytes 7077896 | tf_op jit(solution)/shard_map/ppermute | solution.py:972
  345.0 3.1 collective-permute-start.12
  348.3 30.2 %collective-permute-start.13 = (bf16[384,1664]{1,0:T(8,128)(2,1)S(1)}, bf16[384,1664]{1,0:T(8,128)(2,1)S(1)}, u32[]{:S(2)}, u32[]{:S(2)}) collective-permute-start(bf16[384,1664]{1,0:T(8,128)(2,1)S(1)} %add_convert_fusion.2), channel_id=1, source_target_pairs={{0,2},{2,0},{1,3},{3,1},{4,6},{6,4},{5,7},{7,5},{8,10},{10,8},{9,1... | collective-permute-start | bytes 3833864 | tf_op jit(solution)/shard_map/ppermute | solution.py:1047
  379.9 3.1 collective-permute-start.14
  383.5 3.1 collective-permute-start.15
  383.8 22.6 %collective-permute-start.16 = (bf16[384,1536]{1,0:T(8,128)(2,1)S(1)}, bf16[384,1536]{1,0:T(8,128)(2,1)}, u32[]{:S(2)}, u32[]{:S(2)}) collective-permute-start(bf16[384,1536]{1,0:T(8,128)(2,1)S(1)} %constant_dynamic-slice_fusion.1), channel_id=1, source_target_pairs={{0,1},{1,0},{2,3},{3,2},{4,5},{5,4},{6,7},{7,6},{8,9},{9,8},{10,11... | collective-permute-start | bytes 3538952 | tf_op jit(solution)/shard_map/ppermute | solution.py:522
  385.7 20.7 %collective-permute-start.17 = (bf16[384,1536]{1,0:T(8,128)(2,1)S(1)}, bf16[384,1536]{1,0:T(8,128)(2,1)}, u32[]{:S(2)}, u32[]{:S(2)}) collective-permute-start(bf16[384,1536]{1,0:T(8,128)(2,1)S(1)} %constant_dynamic-slice_fusion), channel_id=1, source_target_pairs={{0,1},{1,0},{2,3},{3,2},{4,5},{5,4},{6,7},{7,6},{8,9},{9,8},{10,11... | collective-permute-start | bytes 3538952 | tf_op jit(solution)/shard_map/ppermute | solution.py:522
  408.3 59.9 %collective-permute-start.19 = (bf16[384,1536]{1,0:T(8,128)(2,1)S(1)}, bf16[384,1536]{1,0:T(8,128)(2,1)S(1)}, u32[]{:S(2)}, u32[]{:S(2)}) collective-permute-start(bf16[384,1536]{1,0:T(8,128)(2,1)S(1)} %add_convert_fusion.4), channel_id=1, source_target_pairs={{0,2},{2,0},{1,3},{3,1},{4,6},{6,4},{5,7},{7,5},{8,10},{10,8},{9,1... | collective-permute-start | bytes 3538952 | tf_op jit(solution)/shard_map/ppermute | solution.py:1063
  440.7 27.4 %collective-permute-start.18 = (bf16[768,512]{1,0:T(8,128)(2,1)S(1)}, bf16[768,512]{1,0:T(8,128)(2,1)S(1)}, u32[]{:S(2)}, u32[]{:S(2)}) collective-permute-start(bf16[768,512]{1,0:T(8,128)(2,1)S(1)} %pad_maximum_fusion.1), channel_id=1, source_target_pairs={{2,0},{3,1},{6,4},{7,5},{10,8},{11,9},{14,12},{15,13},{18,16},{19,... | collective-permute-start | bytes 2359304 | tf_op jit(solution)/shard_map/ppermute | solution.py:1066
  474.3 14.9 %collective-permute-start.20 = (bf16[384,1536]{1,0:T(8,128)(2,1)}, bf16[384,1536]{1,0:T(8,128)(2,1)S(1)}, u32[]{:S(2)}, u32[]{:S(2)}) collective-permute-start(bf16[384,1536]{1,0:T(8,128)(2,1)} %get-tuple-element.193), channel_id=1, source_target_pairs={{0,1},{1,0},{2,3},{3,2},{4,5},{5,4},{6,7},{7,6},{8,9},{9,8},{10,11... | collective-permute-start | bytes 3538952 | tf_op jit(solution)/shard_map/ppermute | solution.py:505
  488.6 45.6 %collective-permute-start.21 = (bf16[768,1536]{1,0:T(8,128)(2,1)}, bf16[768,1536]{1,0:T(8,128)(2,1)S(1)}, u32[]{:S(2)}, u32[]{:S(2)}) collective-permute-start(bf16[768,1536]{1,0:T(8,128)(2,1)} %get-tuple-element.183), channel_id=1, source_target_pairs={{0,1},{1,0},{2,3},{3,2},{4,5},{5,4},{6,7},{7,6},{8,9},{9,8},{10,11... | collective-permute-start | bytes 7077896 | tf_op jit(solution)/shard_map/ppermute | solution.py:1083
  (71 other events, 570.7 us)
Sparse Core Ops, SparseCore 0:
  406.5 72.3 reduce-scatter.1
